TPU v7x, 32 devices: a whole 2x2x4 slice. The times are simulated.
32 devices in a mesh: groups: 2 (over x), box: 16 (over z, y, core).
Axes of the slice: x: 2, y: 2, z: 4, core: 2. Of those that a mesh axis runs over, the one named last changes fastest.
Arguments:
- source_weights: float32 [2, 81, 65536], P(None, None, ('groups', 'box')), parts along dimension 2, may hold values from -2 to 2
- wave_vectors: float32 [4, 2, 65536], P(None, None, ('groups', 'box')), parts along dimension 2, may hold values from -8 to 8
- source_centers: float32 [4, 2, 65536], P(None, None, ('groups', 'box')), parts along dimension 2, may hold values from -1 to 1
- phase_coef: float32 [4, 3], replicated, may hold values from 0.5 to 1.5
- phase_kind: int32 [65536], P(('groups', 'box')), parts along dimension 0, may hold values from 0 to 3
Outputs:
- target_coef: float32 [2, 81, 65536], P(None, None, ('groups', 'box')), parts along dimension 2
There are 2 independent parts, one for each index of `groups`. A program takes and returns all parts, laid end to end along the dimension named above; an argument that names none is the same for every part. Nothing has to cross between parts.
All inputs are finite; a program needn't handle non-finite values.
Results may differ from a plain program's by a relative error of at most 0.0003.
Values sent between devices are 32-bit elements; how exact they have to be, the bound alone decides.
No kernel may reach another device: no remote copies, remote signals or barrier semaphores. Data moves between devices by JAX's collectives and lax.ppermute only.
A program may use at most 64 MiB of HBM per device.

v0:
```python
import math

import jax
import jax.numpy as jnp
from jax import lax
from jax.sharding import PartitionSpec as P

CHEB = 9
KINDS = 4
LEVELS = 4


def partner_2(value, axis, distance):
    mask = 2**distance
    pairs = [(source, source ^ mask) for source in range(lax.axis_size(axis))]
    return lax.ppermute(value, axis, pairs)


def chebyshev_nodes():
    return jnp.cos(math.pi * (2.0 * jnp.arange(CHEB, dtype=jnp.float32) + 1.0) / (2.0 * CHEB))


def lagrange_matrix(targets):
    node_values = chebyshev_nodes()
    row_list = []
    for t_index in range(CHEB):
        factor_product = jnp.ones_like(targets)
        for other_node in range(CHEB):
            if other_node != t_index:
                factor_product = (
                    factor_product
                    * (targets - node_values[other_node])
                    / (node_values[t_index] - node_values[other_node])
                )
        row_list.append(factor_product)
    return jnp.stack(row_list)


def child_matrix(which_child, along_first):
    node_values = chebyshev_nodes()
    one_dim = lagrange_matrix((node_values + 2.0 * which_child - 1.0) / 2.0)
    identity = jnp.eye(CHEB, dtype=jnp.float32)
    if along_first:
        return jnp.kron(one_dim, identity)
    return jnp.kron(identity, one_dim)


def box_phase(first_coord, second_coord, wave_block, center_block, box_coefs, half_size):
    point_one = center_block[0][None, :] + half_size * first_coord[:, None]
    point_two = center_block[1][None, :] + half_size * second_coord[:, None]
    root_term = box_coefs[0] * jnp.sqrt(
        (box_coefs[1] * wave_block[0]) ** 2 + wave_block[1] ** 2 + 1.0
    )
    return (
        2.0
        * math.pi
        * (
            point_one * wave_block[0]
            + point_two * wave_block[1]
            + root_term * (1.0 + box_coefs[2] * point_one * point_one)
        )
    )


def combine(child_zero, child_one, wave_block, center_block, box_coefs, level_index):
    node_values = chebyshev_nodes()
    first_coord = jnp.repeat(node_values, CHEB)
    second_coord = jnp.tile(node_values, CHEB)
    half_size = 2.0 ** (level_index - LEVELS)
    along_first = level_index % 2 == 0
    summed = None
    for which_child, values in ((0, child_zero), (1, child_one)):
        shifted = (node_values + 2.0 * which_child - 1.0) / 2.0
        if along_first:
            coord_first = jnp.repeat(shifted, CHEB)
            coord_second = second_coord
        else:
            coord_first = first_coord
            coord_second = jnp.tile(shifted, CHEB)
        phases = box_phase(
            coord_first, coord_second, wave_block, center_block, box_coefs, half_size
        )
        cosine = jnp.cos(phases)
        sine_part = jnp.sin(phases)
        real_part = cosine * values[0] + sine_part * values[1]
        imag_part = cosine * values[1] - sine_part * values[0]
        interpolated = jnp.einsum(
            "ts,rsb->rtb",
            child_matrix(which_child, along_first),
            jnp.stack([real_part, imag_part]),
            precision=lax.Precision.HIGHEST,
        )
        summed = interpolated if summed is None else summed + interpolated
    phases = box_phase(first_coord, second_coord, wave_block, center_block, box_coefs, half_size)
    cosine = jnp.cos(phases)
    sine_part = jnp.sin(phases)
    return jnp.stack(
        [cosine * summed[0] - sine_part * summed[1], cosine * summed[1] + sine_part * summed[0]]
    )


def lookup_coefs(phase_kind, phase_coef):
    picked = jnp.zeros((3, phase_kind.shape[-1]), jnp.float32)
    for kind_index in range(KINDS):
        picked = (
            picked
            + jnp.where(phase_kind == kind_index, 1.0, 0.0)[None, :]
            * phase_coef[kind_index][:, None]
        )
    return picked


def on_device(source_weights, wave_vectors, source_centers, phase_coef, phase_kind):
    axis_count = lax.axis_size("box")
    log_axis = axis_count.bit_length() - 1
    box_coefs = lookup_coefs(phase_kind, phase_coef)
    current = source_weights
    device = lax.axis_index("box")
    for level_index in range(LEVELS):
        device_bit = log_axis - 1 - level_index
        partner = partner_2(current, "box", device_bit)
        own_bit = device >> device_bit & 1
        child_zero = jnp.where(own_bit == 0, current, partner)
        child_one = jnp.where(own_bit == 0, partner, current)
        current = combine(
            child_zero,
            child_one,
            wave_vectors[level_index],
            source_centers[level_index],
            box_coefs,
            level_index,
        )
    return lax.all_to_all(current, "box", split_axis=2, concat_axis=2, tiled=True)


def solution(mesh):
    in_specs = (
        P(None, None, ("groups", "box")),
        P(None, None, ("groups", "box")),
        P(None, None, ("groups", "box")),
        P(),
        P(("groups", "box")),
    )
    out_specs = P(None, None, ("groups", "box"))
    return jax.shard_map(
        on_device, mesh=mesh, in_specs=in_specs, out_specs=out_specs, check_vma=False
    )
```

profile of v0, /device:TPU:0, one launch (start us, length us, event | category | flops | bytes accessed | tf_op | source)
XLA Modules:
  0.0 329.9 jit_solution(18298757701007675824)
XLA Ops:
  0.0 4.0 %collective-permute-start = (f32[2,81,2048]{2,0,1:T(2,128)}, f32[2,81,2048]{2,0,1:T(2,128)}, u32[]{:S(2)}, u32[]{:S(2)}) collective-permute-start(f32[2,81,2048]{2,0,1:T(2,128)} %param.5), channel_id=1, source_target_pairs={{0,8},{1,9},{2,10},{3,11},{4,12},{5,13},{6,14},{7,15},{8,0},{9,1},... | collective-permute-start | bytes 3981320 | tf_op jit(solution)/shard_map/ppermute | solution.py:16
  98.8 5.1 %fusion.125 = (f32[1,9]{1,0:T(1,128)S(1)}, f32[1,9]{1,0:T(1,128)S(1)}) fusion(f32[]{:T(128)S(6)} %sub.1194, f32[]{:T(128)S(6)} %sub.1191, f32[]{:T(128)S(6)} %sub.1188, f32[]{:T(128)S(6)} %sub.1185, f32[]{:T(128)S(6)} %sub.1182, f32[]{:T(128)S(6)} %sub.1179, f32[]{:T(128)S(6)} %sub.1176, f32[]{:T(128)S(6)} %sub.1173, f32[]{:T(128)} %bitcast.33, ...), kind=kLoop, calls=%fused_computation.343 | loop fusion | flops 477 | bytes 136 | tf_op jit(solution)/shard_map/div | solution.py:31
  103.9 5.1 %fusion.126 = (f32[1,9]{1,0:T(1,128)S(1)}, f32[1,9]{1,0:T(1,128)S(1)}) fusion(f32[]{:T(128)S(6)} %sub.1204, f32[]{:T(128)S(6)} %sub.1203, f32[]{:T(128)S(6)} %sub.1202, f32[]{:T(128)S(6)} %sub.1201, f32[]{:T(128)S(6)} %sub.1200, f32[]{:T(128)S(6)} %sub.1199, f32[]{:T(128)S(6)} %sub.1198, f32[]{:T(128)S(6)} %sub.1197, f32[]{:T(128)} %bitcast.35, ...), kind=kLoop, calls=%fused_computation.344 | loop fusion | flops 477 | bytes 136 | tf_op jit(solution)/shard_map/div | solution.py:31
  109.0 5.1 %fusion.127 = (f32[1,9]{1,0:T(1,128)S(1)}, f32[1,9]{1,0:T(1,128)S(1)}) fusion(f32[]{:T(128)S(6)} %sub.1212, f32[]{:T(128)S(6)} %sub.1211, f32[]{:T(128)S(6)} %sub.1210, f32[]{:T(128)S(6)} %sub.1209, f32[]{:T(128)S(6)} %sub.1208, f32[]{:T(128)S(6)} %sub.1207, f32[]{:T(128)S(6)} %sub.1206, f32[]{:T(128)S(6)} %sub.1205, f32[]{:T(128)} %bitcast.33, ...), kind=kLoop, calls=%fused_computation.345 | loop fusion | flops 477 | bytes 136 | tf_op jit(solution)/shard_map/div | solution.py:31
  114.1 5.1 %fusion.128 = (f32[1,9]{1,0:T(1,128)S(1)}, f32[1,9]{1,0:T(1,128)S(1)}) fusion(f32[]{:T(128)S(6)} %sub.1220, f32[]{:T(128)S(6)} %sub.1219, f32[]{:T(128)S(6)} %sub.1218, f32[]{:T(128)S(6)} %sub.1217, f32[]{:T(128)S(6)} %sub.1216, f32[]{:T(128)S(6)} %sub.1215, f32[]{:T(128)S(6)} %sub.1214, f32[]{:T(128)S(6)} %sub.1213, f32[]{:T(128)} %bitcast.33, ...), kind=kLoop, calls=%fused_computation.346 | loop fusion | flops 477 | bytes 136 | tf_op jit(solution)/shard_map/div | solution.py:31
  119.2 5.1 %fusion.129 = (f32[1,9]{1,0:T(1,128)S(1)}, f32[1,9]{1,0:T(1,128)S(1)}) fusion(f32[]{:T(128)S(6)} %sub.1228, f32[]{:T(128)S(6)} %sub.1227, f32[]{:T(128)S(6)} %sub.1226, f32[]{:T(128)S(6)} %sub.1225, f32[]{:T(128)S(6)} %sub.1224, f32[]{:T(128)S(6)} %sub.1223, f32[]{:T(128)S(6)} %sub.1222, f32[]{:T(128)S(6)} %sub.1221, f32[]{:T(128)} %bitcast.33, ...), kind=kLoop, calls=%fused_computation.347 | loop fusion | flops 477 | bytes 136 | tf_op jit(solution)/shard_map/div | solution.py:31
  124.3 5.1 %fusion.130 = (f32[1,9]{1,0:T(1,128)S(1)}, f32[1,9]{1,0:T(1,128)S(1)}) fusion(f32[]{:T(128)S(6)} %sub.1236, f32[]{:T(128)S(6)} %sub.1235, f32[]{:T(128)S(6)} %sub.1234, f32[]{:T(128)S(6)} %sub.1233, f32[]{:T(128)S(6)} %sub.1232, f32[]{:T(128)S(6)} %sub.1231, f32[]{:T(128)S(6)} %sub.1230, f32[]{:T(128)S(6)} %sub.1229, f32[]{:T(128)} %bitcast.33, ...), kind=kLoop, calls=%fused_computation.348 | loop fusion | flops 477 | bytes 136 | tf_op jit(solution)/shard_map/div | solution.py:31
  129.4 5.1 %fusion.131 = (f32[1,9]{1,0:T(1,128)S(1)}, f32[1,9]{1,0:T(1,128)S(1)}) fusion(f32[]{:T(128)S(6)} %sub.1244, f32[]{:T(128)S(6)} %sub.1243, f32[]{:T(128)S(6)} %sub.1242, f32[]{:T(128)S(6)} %sub.1241, f32[]{:T(128)S(6)} %sub.1240, f32[]{:T(128)S(6)} %sub.1239, f32[]{:T(128)S(6)} %sub.1238, f32[]{:T(128)S(6)} %sub.1237, f32[]{:T(128)} %bitcast.33, ...), kind=kLoop, calls=%fused_computation.349 | loop fusion | flops 477 | bytes 136 | tf_op jit(solution)/shard_map/div | solution.py:31
  134.5 5.1 %fusion.132 = (f32[1,9]{1,0:T(1,128)S(1)}, f32[1,9]{1,0:T(1,128)S(1)}) fusion(f32[]{:T(128)S(6)} %sub.1252, f32[]{:T(128)S(6)} %sub.1251, f32[]{:T(128)S(6)} %sub.1250, f32[]{:T(128)S(6)} %sub.1249, f32[]{:T(128)S(6)} %sub.1248, f32[]{:T(128)S(6)} %sub.1247, f32[]{:T(128)S(6)} %sub.1246, f32[]{:T(128)S(6)} %sub.1245, f32[]{:T(128)} %bitcast.33, ...), kind=kLoop, calls=%fused_computation.350 | loop fusion | flops 477 | bytes 136 | tf_op jit(solution)/shard_map/div | solution.py:31
  139.7 5.2 %fusion.133 = (f32[1,9]{1,0:T(1,128)S(1)}, f32[1,9]{1,0:T(1,128)S(1)}) fusion(f32[]{:T(128)S(6)} %sub.1260, f32[]{:T(128)S(6)} %sub.1259, f32[]{:T(128)S(6)} %sub.1258, f32[]{:T(128)S(6)} %sub.1257, f32[]{:T(128)S(6)} %sub.1256, f32[]{:T(128)S(6)} %sub.1255, f32[]{:T(128)S(6)} %sub.1254, f32[]{:T(128)S(6)} %sub.1253, f32[]{:T(128)} %bitcast.33, ...), kind=kLoop, calls=%fused_computation.351 | loop fusion | flops 477 | bytes 136 | tf_op jit(solution)/shard_map/div | solution.py:31
  146.0 3.2 copy_select_fusion.6
  149.2 6.5 %multiply_add_fusion.10 = (f32[1,81,2048]{2,1,0:T(8,128)S(1)}, f32[1,81,2048]{2,1,0:T(8,128)S(1)}, f32[1,81,2048]{2,1,0:T(8,128)S(1)}, f32[1,81,2048]{2,1,0:T(8,128)S(1)}) fusion(f32[2,81,2048]{2,1,0:T(8,128)S(1)} %get-tuple-element.11, f32[81]{0:T(128)S(1)} %mul.3754, f32[2048]{0:T(1024)S(1)} %bitcast.156, f32[2048]{0:T(1024)S(1)} %bitcast.152, ...), kind=kLoop, calls=%fused_computation.145 | loop fusion | flops 5308416 | bytes 5358540 | tf_op jit(solution)/shard_map/add | solution.py:85
  157.1 1.4 fusion.3
  158.6 3.0 multiply_subtract_fusion.9
  161.7 2.1 copy.14
  163.8 1.6 collective-permute-start.1
  166.3 28.3 %collective-permute-done.1 = f32[2,81,2048]{2,0,1:T(2,128)} collective-permute-done((f32[2,81,2048]{2,0,1:T(2,128)}, f32[2,81,2048]{2,0,1:T(2,128)}, u32[]{:S(2)}, u32[]{:S(2)}) %collective-permute-start.1) | collective-permute-done | bytes 1327136 | tf_op jit(solution)/shard_map/ppermute | solution.py:16
  194.7 2.1 copy_select_fusion.4
  196.8 6.1 %multiply_add_fusion.7 = (f32[1,81,2048]{2,1,0:T(8,128)S(1)}, f32[1,81,2048]{2,1,0:T(8,128)S(1)}, f32[1,81,2048]{2,1,0:T(8,128)S(1)}, f32[1,81,2048]{2,1,0:T(8,128)S(1)}) fusion(f32[2,81,2048]{2,1,0:T(8,128)S(1)} %get-tuple-element.9, f32[81]{0:T(128)S(1)} %mul.3843, f32[2048]{0:T(1024)S(1)} %bitcast.150, f32[2048]{0:T(1024)S(1)} %bitcast.146, ...), kind=kLoop, calls=%fused_computation.139 | loop fusion | flops 4644864 | bytes 5358540 | tf_op jit(solution)/shard_map/add | solution.py:85
  204.3 1.4 fusion.2
  205.8 3.0 multiply_subtract_fusion.6
  208.9 2.1 copy.17
  211.0 1.5 collective-permute-start.2
  213.2 27.6 %collective-permute-done.2 = f32[2,81,2048]{2,0,1:T(2,128)S(1)} collective-permute-done((f32[2,81,2048]{2,0,1:T(2,128)}, f32[2,81,2048]{2,0,1:T(2,128)S(1)}, u32[]{:S(2)}, u32[]{:S(2)}) %collective-permute-start.2) | collective-permute-done | bytes 1327136 | tf_op jit(solution)/shard_map/ppermute | solution.py:16
  241.7 6.2 %multiply_add_fusion.4 = (f32[1,81,2048]{2,1,0:T(8,128)S(1)}, f32[1,81,2048]{2,1,0:T(8,128)S(1)}, f32[1,81,2048]{2,1,0:T(8,128)S(1)}, f32[1,81,2048]{2,1,0:T(8,128)S(1)}) fusion(f32[2,81,2048]{2,1,0:T(8,128)S(1)} %get-tuple-element.7, f32[81]{0:T(128)S(1)} %mul.3862, f32[2048]{0:T(1024)S(1)} %bitcast.144, f32[2048]{0:T(1024)S(1)} %bitcast.140, ...), kind=kLoop, calls=%fused_computation.133 | loop fusion | flops 5308416 | bytes 5358540 | tf_op jit(solution)/shard_map/add | solution.py:85
  250.8 3.0 multiply_subtract_fusion.3
  253.9 2.1 copy.20
  256.6 2.7 collective-permute-done.3
  260.1 6.1 %multiply_add_fusion.1 = (f32[1,81,2048]{2,1,0:T(8,128)S(1)}, f32[1,81,2048]{2,1,0:T(8,128)S(1)}, f32[1,81,2048]{2,1,0:T(8,128)S(1)}, f32[1,81,2048]{2,1,0:T(8,128)S(1)}) fusion(f32[2,81,2048]{2,1,0:T(8,128)S(1)} %get-tuple-element.5, f32[81]{0:T(128)S(1)} %mul.3881, f32[2048]{0:T(1024)S(1)} %bitcast.116, f32[2048]{0:T(1024)S(1)} %bitcast.134, ...), kind=kLoop, calls=%fused_computation.127 | loop fusion | flops 4644864 | bytes 5358540 | tf_op jit(solution)/shard_map/add | solution.py:85
  269.1 3.0 multiply_subtract_fusion
  273.4 51.1 %all_to_all.5 = f32[2,81,2048]{1,0,2:T(2,128)} all-to-all(f32[2,81,2048]{1,0,2:T(2,128)S(1)} %copy.23), channel_id=1, replica_groups=mesh['groups'=2,'box'=16] {'box'}, dimensions={2} | all-to-all | bytes 2654208 | tf_op jit(solution)/shard_map/all_to_all | solution.py:133
  324.5 4.9 %copy.24 = f32[2,81,2048]{2,0,1:T(2,128)} copy(f32[2,81,2048]{1,0,2:T(2,128)} %all_to_all.5) | data formatting | bytes 2654208 | tf_op jit(solution)/shard_map/all_to_all | solution.py:133
  (77 shorter events, 19.0 us)
Async XLA Ops:
  0.0 146.0 %collective-permute-start = (f32[2,81,2048]{2,0,1:T(2,128)}, f32[2,81,2048]{2,0,1:T(2,128)}, u32[]{:S(2)}, u32[]{:S(2)}) collective-permute-start(f32[2,81,2048]{2,0,1:T(2,128)} %param.5), channel_id=1, source_target_pairs={{0,8},{1,9},{2,10},{3,11},{4,12},{5,13},{6,14},{7,15},{8,0},{9,1},... | collective-permute-start | bytes 3981320 | tf_op jit(solution)/shard_map/ppermute | solution.py:16
  145.0 0.8 copy-start
  163.8 30.9 %collective-permute-start.1 = (f32[2,81,2048]{2,0,1:T(2,128)}, f32[2,81,2048]{2,0,1:T(2,128)}, u32[]{:S(2)}, u32[]{:S(2)}) collective-permute-start(f32[2,81,2048]{2,0,1:T(2,128)} %copy.14), channel_id=1, source_target_pairs={{0,4},{1,5},{2,6},{3,7},{4,0},{5,1},{6,2},{7,3},{8,12},{9,13},{10,... | collective-permute-start | bytes 3981320 | tf_op jit(solution)/shard_map/ppermute | solution.py:16
  211.0 29.9 %collective-permute-start.2 = (f32[2,81,2048]{2,0,1:T(2,128)}, f32[2,81,2048]{2,0,1:T(2,128)S(1)}, u32[]{:S(2)}, u32[]{:S(2)}) collective-permute-start(f32[2,81,2048]{2,0,1:T(2,128)} %copy.17), channel_id=1, source_target_pairs={{0,2},{1,3},{2,0},{3,1},{4,6},{5,7},{6,4},{7,5},{8,10},{9,11},{10,... | collective-permute-start | bytes 3981320 | tf_op jit(solution)/shard_map/ppermute | solution.py:16
  256.0 3.3 collective-permute-start.3
where the time goes:
time: 336 us; the launch traced here: 330 us
  other arithmetic  92.1 us (27%)
  between operations  91.7 us (27%)
  waiting for transfers between devices  58.7 us (17%)
  blocking collectives  51.1 us (15%)
  local copies, waits for them, and re-layouts  17.6 us (5%)
  matrix products  11.5 us (3%)
  starting transfers between devices  7.13 us (2%)
    ppermute x4, waiting for transfers between devices, partner_2(): return lax.ppermute(value, axis, pairs)  58.7 us
    all_to_all x1, blocking collectives, on_device(): lax.all_to_all(current, 'box', split_axis=2, concat_axis=2, tiled=True)  51.1 us
    div x9, other arithmetic, lagrange_matrix(): factor_product * (targets - node_values[other_node])  46 us
    add x4, other arithmetic, combine(): real_part = cosine * values[0] + sine_part * values[1]  24.9 us
    sub x4, other arithmetic, combine(): cosine * summed[0] - sine_part * summed[1]  11.9 us
    dot_general x8, matrix products, combine(): jnp.einsum('ts,rsb->rtb', child_matrix(which_child, along_first), jnp.sta...  11.5 us
    another operation x4, local copies, waits for them, and re-layouts, combine(): jnp.stack([cosine * summed[0] - sine_part * summed[1], cosine * summed[1]...  7.39 us
    ppermute x4, starting transfers between devices, partner_2(): return lax.ppermute(value, axis, pairs)  7.13 us
  transfers between devices with their start and end apart: 4, of which 3 were waited for; matrix products, arithmetic and copies ran while one was open for 16% of the time, Pallas kernels for 0%

commit v1 on v0

v1 whole, which is shorter than its diff:
```python
import math

import numpy as np

import jax
import jax.numpy as jnp
from jax import lax
from jax.experimental import pallas as pl
from jax.experimental.pallas import tpu as pltpu
from jax.sharding import PartitionSpec as P

CHEB = 9
POINTS = CHEB * CHEB
KINDS = 4
LEVELS = 4
SLOTS = 1 << LEVELS
LANES = 128
WEIGHT_ROWS = 2 * POINTS
PHASE_ROWS = 4 * LEVELS
USED_ROWS = WEIGHT_ROWS + PHASE_ROWS
ROWS = (USED_ROWS + 7) // 8 * 8

NODES = np.cos(math.pi * (2.0 * np.arange(CHEB) + 1.0) / (2.0 * CHEB))
NODES[CHEB // 2] = 0.0


def interpolation_halves():
    targets = (NODES - 1.0) / 2.0
    matrix = np.ones((CHEB, CHEB))
    for t in range(CHEB):
        for m in range(CHEB):
            if m != t:
                matrix[t] *= (targets - NODES[m]) / (NODES[t] - NODES[m])
    return (matrix + matrix[::-1]) / 2.0, (matrix - matrix[::-1]) / 2.0


EVEN_HALF, ODD_HALF = interpolation_halves()

SIN_COEFS = (3.1415926401839673, -5.167710090328242, 2.5500776596583643, -0.5982921590176602, 0.0776594073245765)
COS_COEFS = (0.999999953466542, -4.934792858659144, 4.05841191384421, -1.3318801591805476, 0.219696794464285)


def cos_sin_turns(turns):
    rest = turns - jnp.round(turns)
    square = rest * rest
    sine = jnp.float32(SIN_COEFS[-1])
    cosine = jnp.float32(COS_COEFS[-1])
    for s, c in zip(SIN_COEFS[-2::-1], COS_COEFS[-2::-1]):
        sine = sine * square + s
        cosine = cosine * square + c
    sine = sine * rest
    twice = sine + sine
    return 1.0 - twice * sine, twice * cosine


def phase_rows(wave, center, kind, coef_ref):
    a = b = e = jnp.zeros(kind.shape, jnp.float32)
    for index in range(KINDS):
        chosen = kind == index
        a = jnp.where(chosen, coef_ref[index, 0], a)
        b = jnp.where(chosen, coef_ref[index, 1], b)
        e = jnp.where(chosen, coef_ref[index, 2], e)
    k1, k2 = wave
    x1, x2 = center
    level = lax.broadcasted_iota(jnp.int32, k1.shape, 0)
    half = jnp.full(k1.shape, 2.0**-LEVELS, jnp.float32)
    for index in range(1, LEVELS):
        half = jnp.where(level == index, 2.0 ** (index - LEVELS), half)
    scaled = b * k1
    root = a * jnp.sqrt(scaled * scaled + k2 * k2 + 1.0)
    bent = root * e
    constant = x1 * k1 + x2 * k2 + root + bent * x1 * x1
    constant = constant - jnp.round(constant)
    return constant, half * (k1 + 2.0 * bent * x1), half * half * bent, half * k2


def pack_kernel(me_ref, coef_ref, weights_ref, wave_ref, center_ref, kind_ref, *refs):
    outs, phases_ref = refs[:-1], refs[-1]
    rows = phase_rows(
        (wave_ref[:, 0, :], wave_ref[:, 1, :]), (center_ref[:, 0, :], center_ref[:, 1, :]), kind_ref[...], coef_ref
    )
    for index, values in enumerate(rows):
        phases_ref[index * LEVELS : (index + 1) * LEVELS, :] = values
    width = outs[0].shape[-1]
    for step, out in enumerate(outs):
        columns = pl.ds(pl.multiple_of((me_ref[0] ^ step) * width, width), width)
        out[:POINTS, :] = weights_ref[0, :, columns]
        out[POINTS:WEIGHT_ROWS, :] = weights_ref[1, :, columns]
        out[WEIGHT_ROWS:USED_ROWS, :] = phases_ref[:, columns]
        out[USED_ROWS:, :] = jnp.zeros((ROWS - USED_ROWS, width), jnp.float32)


def pack(me, phase_coef, weights, wave, center, kind):
    block = jax.ShapeDtypeStruct((ROWS, LANES), jnp.float32)
    vmem = pl.BlockSpec(memory_space=pltpu.VMEM)
    smem = pl.BlockSpec(memory_space=pltpu.SMEM)
    return pl.pallas_call(
        pack_kernel,
        out_shape=[block] * SLOTS,
        in_specs=[smem, smem, vmem, vmem, vmem, vmem],
        out_specs=[vmem] * SLOTS,
        scratch_shapes=[pltpu.VMEM((PHASE_ROWS, weights.shape[-1]), jnp.float32)],
        compiler_params=pltpu.CompilerParams(vmem_limit_bytes=32 * 2**20),
        name="pack",
    )(me, phase_coef, weights, wave, center, kind)


def level_factors(level, tile, phase_of, parent_ref, child_ref, common_ref):
    constant, linear, quadratic, other = (phase_of(level, part, tile) for part in range(4))
    if level % 2 == 0:
        split = lambda x: constant + x * (linear + x * quadratic)
        common = lambda x: x * other
    else:
        split = lambda x: constant + x * other
        common = lambda x: x * (linear + x * quadratic)
    for t in range(CHEB):
        node = float(NODES[t])
        parent_ref[tile, t, 0], parent_ref[tile, t, 1] = cos_sin_turns(split(node))
        for child in range(2):
            shifted = (node + 2.0 * child - 1.0) / 2.0
            child_ref[tile, child, t, 0], child_ref[tile, child, t, 1] = cos_sin_turns(split(shifted))
        cosine, sine = cos_sin_turns(common(node))
        common_ref[tile, t] = cosine * cosine + sine * sine


def level_column(tile, column, children, parent_ref, child_ref, common_ref, store):
    scaled = []
    for child in range(2):
        line = []
        for s in range(CHEB):
            real, imag = children[child][s]
            cosine, sine = child_ref[tile, child, s, 0], child_ref[tile, child, s, 1]
            line.append((cosine * real + sine * imag, cosine * imag - sine * real))
        scaled.append(line)
    halves = []
    for part in range(2):
        plus = [scaled[0][s][part] + scaled[1][CHEB - 1 - s][part] for s in range(CHEB)]
        minus = [scaled[0][s][part] - scaled[1][CHEB - 1 - s][part] for s in range(CHEB)]
        halves.append((plus, minus))
    common = common_ref[tile, column]
    mid = CHEB // 2
    for t in range(mid + 1):
        sums = []
        for part in range(2):
            plus, minus = halves[part]
            even = plus[0] * float(EVEN_HALF[t, 0])
            for s in range(1, CHEB):
                even = even + plus[s] * float(EVEN_HALF[t, s])
            if t == mid:
                sums.append((even,))
                continue
            odd = minus[0] * float(ODD_HALF[t, 0])
            for s in range(1, CHEB):
                odd = odd + minus[s] * float(ODD_HALF[t, s])
            sums.append((even + odd, even - odd))
        for which, row in enumerate((t,) if t == mid else (t, CHEB - 1 - t)):
            real, imag = sums[0][which] * common, sums[1][which] * common
            cosine, sine = parent_ref[tile, row, 0], parent_ref[tile, row, 1]
            store(row, cosine * real - sine * imag, cosine * imag + sine * real)


def combine_kernel(me_ref, *refs):
    blocks = refs[:SLOTS]
    out_ref, held, work, parent_ref, child_ref, common_ref, sems = refs[SLOTS:]
    me = me_ref[0]
    copies = []
    for step in range(SLOTS):
        spot = pl.ds(pl.multiple_of((me ^ step) * ROWS, 8), ROWS)
        copies.append(pltpu.make_async_copy(blocks[step], held.at[spot, :], sems.at[step]))
        copies[-1].start()
    for copy in copies:
        copy.wait()

    def received(row, tile):
        return held[pl.ds(tile * 8 * ROWS + row, 8, stride=ROWS), :]

    def phase_of(level, part, tile):
        return received(WEIGHT_ROWS + part * LEVELS + level, tile)

    for level in range(LEVELS):
        for tile in range(2):
            level_factors(level, tile, phase_of, parent_ref, child_ref, common_ref)
        bit = 1 << (LEVELS - 1 - level)
        along_first = level % 2 == 0

        def row_of(split, column, part, along_first=along_first):
            return part * POINTS + (split * CHEB + column if along_first else column * CHEB + split)

        def column_step(column, _, level=level, bit=bit, row_of=row_of):
            if level == 0:
                children = [
                    [tuple(received(row_of(s, column, part), child) for part in range(2)) for s in range(CHEB)]
                    for child in range(2)
                ]
            for tile in range(2):
                if level > 0:
                    upper = (lax.broadcasted_iota(jnp.int32, (8, LANES), 0) & bit) != 0
                    children = [[], []]
                    for s in range(CHEB):
                        pairs = [[], []]
                        for part in range(2):
                            value = work[row_of(s, column, part), tile]
                            down = pltpu.roll(value, bit, 0)
                            up = down if bit == 4 else pltpu.roll(value, 8 - bit, 0)
                            pairs[0].append(jnp.where(upper, down, value))
                            pairs[1].append(jnp.where(upper, value, up))
                        children[0].append(tuple(pairs[0]))
                        children[1].append(tuple(pairs[1]))

                def store(row, real, imag, tile=tile):
                    work[row_of(row, column, 0), tile] = real
                    work[row_of(row, column, 1), tile] = imag

                level_column(tile, column, children, parent_ref, child_ref, common_ref, store)
            return 0

        lax.fori_loop(0, CHEB, column_step, 0)

    for box in range(SLOTS):
        for part in range(2):
            out_ref[part, :, box * LANES : (box + 1) * LANES] = work[
                part * POINTS : (part + 1) * POINTS, box // 8, box % 8, :
            ]


def combine(me, blocks):
    hbm = pl.BlockSpec(memory_space=pl.ANY)
    vmem = pl.BlockSpec(memory_space=pltpu.VMEM)
    smem = pl.BlockSpec(memory_space=pltpu.SMEM)
    return pl.pallas_call(
        combine_kernel,
        out_shape=jax.ShapeDtypeStruct((2, POINTS, SLOTS * LANES), jnp.float32),
        in_specs=[smem] + [hbm] * SLOTS,
        out_specs=vmem,
        scratch_shapes=[
            pltpu.VMEM((SLOTS * ROWS, LANES), jnp.float32),
            pltpu.VMEM((WEIGHT_ROWS, 2, 8, LANES), jnp.float32),
            pltpu.VMEM((2, CHEB, 2, 8, LANES), jnp.float32),
            pltpu.VMEM((2, 2, CHEB, 2, 8, LANES), jnp.float32),
            pltpu.VMEM((2, CHEB, 8, LANES), jnp.float32),
            pltpu.SemaphoreType.DMA((SLOTS,)),
        ],
        compiler_params=pltpu.CompilerParams(vmem_limit_bytes=32 * 2**20),
        name="combine",
    )(me, *blocks)


def on_device(source_weights, wave_vectors, source_centers, phase_coef, phase_kind):
    devices = lax.axis_size("box")
    me = lax.axis_index("box").astype(jnp.int32)[None]
    kind = phase_kind[None, :]
    if devices == SLOTS:
        blocks = pack(me, phase_coef, source_weights, wave_vectors, source_centers, kind)
        moved = [blocks[0]] + [None] * (SLOTS - 1)
        for step in range(SLOTS - 1, 0, -1):
            moved[step] = lax.ppermute(blocks[step], "box", [(s, s ^ step) for s in range(SLOTS)])
        return combine(me, moved)
    zero = jnp.zeros_like(me)
    blocks = pack(zero, phase_coef, source_weights, wave_vectors, source_centers, kind)
    whole = jnp.concatenate(blocks, axis=1)
    whole = lax.all_to_all(whole, "box", split_axis=1, concat_axis=1, tiled=True)
    return combine(zero, [whole[:, s * LANES : (s + 1) * LANES] for s in range(SLOTS)])


def solution(mesh):
    in_specs = (
        P(None, None, ("groups", "box")),
        P(None, None, ("groups", "box")),
        P(None, None, ("groups", "box")),
        P(),
        P(("groups", "box")),
    )
    out_specs = P(None, None, ("groups", "box"))
    return jax.shard_map(on_device, mesh=mesh, in_specs=in_specs, out_specs=out_specs, check_vma=False)
```

time: 336 us -> 59.7 us (0.18)
  the two profiles are of different devices: /device:TPU:0 before, /device:TPU:17 now
where the time goes in v1:
time: 59.7 us; the launch traced here: 59.6 us
  starting transfers between devices  28.6 us (48%)
  waiting for transfers between devices  15.6 us (26%)
  Pallas kernels  11 us (18%)
  local copies, waits for them, and re-layouts  4.25 us (7%)
    ppermute x15, starting transfers between devices, on_device(): lax.ppermute(blocks[step], 'box', [(s, s ^ step) for s in range(SLOTS)])  28.6 us
    ppermute x15, waiting for transfers between devices, on_device(): lax.ppermute(blocks[step], 'box', [(s, s ^ step) for s in range(SLOTS)])  15.6 us
    pallas_call x1, Pallas kernels, combine(): pl.pallas_call(combine_kernel, out_shape=jax.ShapeDtypeStruct((2, POINTS,...  10.2 us
    unnamed x9, local copies, waits for them, and re-layouts  2.17 us
    pallas_call x1, local copies, waits for them, and re-layouts, combine(): pl.pallas_call(combine_kernel, out_shape=jax.ShapeDtypeStruct((2, POINTS,...  2.09 us
  transfers between devices with their start and end apart: 15, of which 5 were waited for; matrix products, arithmetic and copies ran while one was open for 0% of the time, Pallas kernels for 0%

profile of v1, /device:TPU:17, one launch (start us, length us, event | category | flops | bytes accessed | tf_op | source)
XLA Modules:
  0.0 59.6 jit_solution(5835299426553548939)
XLA Ops:
  0.0 2.2 %copy.6.weights_ref = f32[2,81,2048]{2,1,0:T(8,128)S(1)} copy(f32[2,81,2048]{2,0,1:T(2,128)} %param.5) | data formatting | bytes 2654208 | tf_op args[0]
  2.2 0.8 %pack.1 = (f32[184,128]{1,0:T(8,128)S(1)}, f32[184,128]{1,0:T(8,128)S(1)}, f32[184,128]{1,0:T(8,128)S(1)}, f32[184,128]{1,0:T(8,128)S(1)}, f32[184,128]{1,0:T(8,...) custom-call(s32[1]{0:T(128)} %bitcast.me_ref, ...), custom_call_target="tpu_custom_call" | custom-call | tf_op jit(solution)/shard_map/pack/pallas_call | solution.py:97
  3.1 0.7 %collective-permute-start = (f32[184,128]{1,0:T(8,128)S(1)}, f32[184,128]{1,0:T(8,128)S(1)}, u32[]{:S(2)}, u32[]{:S(2)}) collective-permute-start(f32[184,128]{1,0:T(8,128)S(1)} %get-tuple-element.22), channel_id=1, source_target_pairs={{0,1},{1,0},{2,3},{3,2},{4,5},{5,4},{6,7},{7,6},{8,9},{9,8},{10,11... | collective-permute-start | bytes 282632 | tf_op jit(solution)/shard_map/ppermute | solution.py:256
  3.8 1.3 %collective-permute-start.1 = (f32[184,128]{1,0:T(8,128)S(1)}, f32[184,128]{1,0:T(8,128)S(1)}, u32[]{:S(2)}, u32[]{:S(2)}) collective-permute-start(f32[184,128]{1,0:T(8,128)S(1)} %get-tuple-element.23), channel_id=1, source_target_pairs={{0,2},{1,3},{2,0},{3,1},{4,6},{5,7},{6,4},{7,5},{8,10},{9,11},{10,... | collective-permute-start | bytes 282632 | tf_op jit(solution)/shard_map/ppermute | solution.py:256
  5.1 0.4 collective-permute-start.2
  5.5 1.3 %collective-permute-start.3 = (f32[184,128]{1,0:T(8,128)S(1)}, f32[184,128]{1,0:T(8,128)S(1)}, u32[]{:S(2)}, u32[]{:S(2)}) collective-permute-start(f32[184,128]{1,0:T(8,128)S(1)} %get-tuple-element.25), channel_id=1, source_target_pairs={{0,4},{1,5},{2,6},{3,7},{4,0},{5,1},{6,2},{7,3},{8,12},{9,13},{10,... | collective-permute-start | bytes 282632 | tf_op jit(solution)/shard_map/ppermute | solution.py:256
  6.8 0.5 collective-permute-start.4
  7.3 0.0 collective-permute-done.refs_1_
  7.3 2.3 %collective-permute-start.5 = (f32[184,128]{1,0:T(8,128)S(1)}, f32[184,128]{1,0:T(8,128)S(1)}, u32[]{:S(2)}, u32[]{:S(2)}) collective-permute-start(f32[184,128]{1,0:T(8,128)S(1)} %get-tuple-element.27), channel_id=1, source_target_pairs={{0,6},{1,7},{2,4},{3,5},{4,2},{5,3},{6,0},{7,1},{8,14},{9,15},{10,... | collective-permute-start | bytes 282632 | tf_op jit(solution)/shard_map/ppermute | solution.py:256
  9.6 0.0 collective-permute-done.1.refs_2_
  9.6 2.0 %collective-permute-start.6 = (f32[184,128]{1,0:T(8,128)S(1)}, f32[184,128]{1,0:T(8,128)S(1)}, u32[]{:S(2)}, u32[]{:S(2)}) collective-permute-start(f32[184,128]{1,0:T(8,128)S(1)} %get-tuple-element.28), channel_id=1, source_target_pairs={{0,7},{1,6},{2,5},{3,4},{4,3},{5,2},{6,1},{7,0},{8,15},{9,14},{10,... | collective-permute-start | bytes 282632 | tf_op jit(solution)/shard_map/ppermute | solution.py:256
  11.5 0.0 collective-permute-done.2.refs_3_
  11.5 0.1 collective-permute-start.7
  11.6 0.0 collective-permute-done.3.refs_4_
  11.6 1.7 %collective-permute-start.8 = (f32[184,128]{1,0:T(8,128)S(1)}, f32[184,128]{1,0:T(8,128)S(1)}, u32[]{:S(2)}, u32[]{:S(2)}) collective-permute-start(f32[184,128]{1,0:T(8,128)S(1)} %get-tuple-element.30), channel_id=1, source_target_pairs={{0,9},{1,8},{2,11},{3,10},{4,13},{5,12},{6,15},{7,14},{8,1},{9,0},... | collective-permute-start | bytes 282632 | tf_op jit(solution)/shard_map/ppermute | solution.py:256
  13.3 0.0 collective-permute-done.4.refs_5_
  13.3 1.0 %collective-permute-start.9 = (f32[184,128]{1,0:T(8,128)S(1)}, f32[184,128]{1,0:T(8,128)S(1)}, u32[]{:S(2)}, u32[]{:S(2)}) collective-permute-start(f32[184,128]{1,0:T(8,128)S(1)} %get-tuple-element.31), channel_id=1, source_target_pairs={{0,10},{1,11},{2,8},{3,9},{4,14},{5,15},{6,12},{7,13},{8,2},{9,3},... | collective-permute-start | bytes 282632 | tf_op jit(solution)/shard_map/ppermute | solution.py:256
  14.3 0.6 collective-permute-done.5.refs_6_
  14.8 2.9 %collective-permute-start.10 = (f32[184,128]{1,0:T(8,128)S(1)}, f32[184,128]{1,0:T(8,128)S(1)}, u32[]{:S(2)}, u32[]{:S(2)}) collective-permute-start(f32[184,128]{1,0:T(8,128)S(1)} %get-tuple-element.32), channel_id=1, source_target_pairs={{0,11},{1,10},{2,9},{3,8},{4,15},{5,14},{6,13},{7,12},{8,3},{9,2},... | collective-permute-start | bytes 282632 | tf_op jit(solution)/shard_map/ppermute | solution.py:256
  17.7 0.0 collective-permute-done.6.refs_7_
  17.7 2.7 %collective-permute-start.11 = (f32[184,128]{1,0:T(8,128)S(1)}, f32[184,128]{1,0:T(8,128)S(1)}, u32[]{:S(2)}, u32[]{:S(2)}) collective-permute-start(f32[184,128]{1,0:T(8,128)S(1)} %get-tuple-element.33), channel_id=1, source_target_pairs={{0,12},{1,13},{2,14},{3,15},{4,8},{5,9},{6,10},{7,11},{8,4},{9,5},... | collective-permute-start | bytes 282632 | tf_op jit(solution)/shard_map/ppermute | solution.py:256
  20.5 0.0 collective-permute-done.7.refs_8_
  20.5 6.7 %collective-permute-start.12 = (f32[184,128]{1,0:T(8,128)S(1)}, f32[184,128]{1,0:T(8,128)S(1)}, u32[]{:S(2)}, u32[]{:S(2)}) collective-permute-start(f32[184,128]{1,0:T(8,128)S(1)} %get-tuple-element.34), channel_id=1, source_target_pairs={{0,13},{1,12},{2,15},{3,14},{4,9},{5,8},{6,11},{7,10},{8,5},{9,4},... | collective-permute-start | bytes 282632 | tf_op jit(solution)/shard_map/ppermute | solution.py:256
  27.2 0.0 collective-permute-done.8.refs_9_
  27.2 2.2 %collective-permute-start.13 = (f32[184,128]{1,0:T(8,128)S(1)}, f32[184,128]{1,0:T(8,128)S(1)}, u32[]{:S(2)}, u32[]{:S(2)}) collective-permute-start(f32[184,128]{1,0:T(8,128)S(1)} %get-tuple-element.35), channel_id=1, source_target_pairs={{0,14},{1,15},{2,12},{3,13},{4,10},{5,11},{6,8},{7,9},{8,6},{9,7},... | collective-permute-start | bytes 282632 | tf_op jit(solution)/shard_map/ppermute | solution.py:256
  29.4 2.9 %collective-permute-start.14 = (f32[184,128]{1,0:T(8,128)S(1)}, f32[184,128]{1,0:T(8,128)S(1)}, u32[]{:S(2)}, u32[]{:S(2)}) collective-permute-start(f32[184,128]{1,0:T(8,128)S(1)} %get-tuple-element.36), channel_id=1, source_target_pairs={{0,15},{1,14},{2,13},{3,12},{4,11},{5,10},{6,9},{7,8},{8,7},{9,6},... | collective-permute-start | bytes 282632 | tf_op jit(solution)/shard_map/ppermute | solution.py:256
  32.3 8.0 %collective-permute-done.11.refs_12_ = f32[184,128]{1,0:T(8,128)S(1)} collective-permute-done((f32[184,128]{1,0:T(8,128)S(1)}, f32[184,128]{1,0:T(8,128)S(1)}, u32[]{:S(2)}, u32[]{:S(2)}) %collective-permute-start.11) | collective-permute-done | bytes 94240 | tf_op jit(solution)/shard_map/ppermute | solution.py:256
  40.3 2.3 %collective-permute-done.12.refs_13_ = f32[184,128]{1,0:T(8,128)S(1)} collective-permute-done((f32[184,128]{1,0:T(8,128)S(1)}, f32[184,128]{1,0:T(8,128)S(1)}, u32[]{:S(2)}, u32[]{:S(2)}) %collective-permute-start.12) | collective-permute-done | bytes 94240 | tf_op jit(solution)/shard_map/ppermute | solution.py:256
  42.6 2.7 %collective-permute-done.13.refs_14_ = f32[184,128]{1,0:T(8,128)S(1)} collective-permute-done((f32[184,128]{1,0:T(8,128)S(1)}, f32[184,128]{1,0:T(8,128)S(1)}, u32[]{:S(2)}, u32[]{:S(2)}) %collective-permute-start.13) | collective-permute-done | bytes 94240 | tf_op jit(solution)/shard_map/ppermute | solution.py:256
  45.3 2.0 %collective-permute-done.14.refs_15_ = f32[184,128]{1,0:T(8,128)S(1)} collective-permute-done((f32[184,128]{1,0:T(8,128)S(1)}, f32[184,128]{1,0:T(8,128)S(1)}, u32[]{:S(2)}, u32[]{:S(2)}) %collective-permute-start.14) | collective-permute-done | bytes 94240 | tf_op jit(solution)/shard_map/ppermute | solution.py:256
  47.3 10.2 %combine.1 = f32[2,81,2048]{2,1,0:T(8,128)S(1)} custom-call(s32[1]{0:T(128)} %bitcast.me_ref, f32[184,128]{1,0:T(8,128)S(1)} %get-tuple-element.21.refs_0_, f32[184,128]{1,0:T(8,128)S(1)} %collective-permute-done.refs_1_, f32[184,128]{1,0:T(8,128)S(1)} %collective-permute-done.1.refs_2_, f32[184,128]{1,0:T(8,128)S(1)} %collective-permute-done.2.refs_3_, ...), custom_call_target="tpu_custom_call" | custom-call | tf_op jit(solution)/shard_map/combine/pallas_call | solution.py:230
  57.5 2.1 %copy.7 = f32[2,81,2048]{2,0,1:T(2,128)} copy(f32[2,81,2048]{2,1,0:T(8,128)S(1)} %combine.1) | data formatting | bytes 2654208 | tf_op jit(solution)/shard_map/combine/pallas_call | solution.py:230
  (10 shorter events, 0.0 us)
Async XLA Ops:
  0.0 2.2 %copy-start.2 = (s32[2048]{0:T(1024)S(1)}, s32[2048]{0:T(1024)}, u32[]{:S(2)}) copy-start(s32[2048]{0:T(1024)} %param.9) | copy-start | bytes 24580
  0.0 2.2 %copy-start.3 = (f32[4,3]{1,0:T(4,128)S(1)}, f32[4,3]{1,0:T(4,128)}, u32[]{:S(2)}) copy-start(f32[4,3]{1,0:T(4,128)} %coef_ref.1) | copy-start | bytes 148
  0.0 2.2 %copy-start.1 = (f32[4,2,2048]{2,1,0:T(2,128)S(1)}, f32[4,2,2048]{2,1,0:T(2,128)}, u32[]{:S(2)}) copy-start(f32[4,2,2048]{2,1,0:T(2,128)} %center_ref.1) | copy-start | bytes 196612
  0.0 2.2 %copy-start = (f32[4,2,2048]{2,1,0:T(2,128)S(1)}, f32[4,2,2048]{2,1,0:T(2,128)}, u32[]{:S(2)}) copy-start(f32[4,2,2048]{2,1,0:T(2,128)} %wave_ref.1) | copy-start | bytes 196612
  3.1 4.3 %collective-permute-start = (f32[184,128]{1,0:T(8,128)S(1)}, f32[184,128]{1,0:T(8,128)S(1)}, u32[]{:S(2)}, u32[]{:S(2)}) collective-permute-start(f32[184,128]{1,0:T(8,128)S(1)} %get-tuple-element.22), channel_id=1, source_target_pairs={{0,1},{1,0},{2,3},{3,2},{4,5},{5,4},{6,7},{7,6},{8,9},{9,8},{10,11... | collective-permute-start | bytes 282632 | tf_op jit(solution)/shard_map/ppermute | solution.py:256
  3.8 5.8 %collective-permute-start.1 = (f32[184,128]{1,0:T(8,128)S(1)}, f32[184,128]{1,0:T(8,128)S(1)}, u32[]{:S(2)}, u32[]{:S(2)}) collective-permute-start(f32[184,128]{1,0:T(8,128)S(1)} %get-tuple-element.23), channel_id=1, source_target_pairs={{0,2},{1,3},{2,0},{3,1},{4,6},{5,7},{6,4},{7,5},{8,10},{9,11},{10,... | collective-permute-start | bytes 282632 | tf_op jit(solution)/shard_map/ppermute | solution.py:256
  5.1 6.5 %collective-permute-start.2 = (f32[184,128]{1,0:T(8,128)S(1)}, f32[184,128]{1,0:T(8,128)S(1)}, u32[]{:S(2)}, u32[]{:S(2)}) collective-permute-start(f32[184,128]{1,0:T(8,128)S(1)} %get-tuple-element.24), channel_id=1, source_target_pairs={{0,3},{1,2},{2,1},{3,0},{4,7},{5,6},{6,5},{7,4},{8,11},{9,10},{10,... | collective-permute-start | bytes 282632 | tf_op jit(solution)/shard_map/ppermute | solution.py:256
  5.5 6.1 %collective-permute-start.3 = (f32[184,128]{1,0:T(8,128)S(1)}, f32[184,128]{1,0:T(8,128)S(1)}, u32[]{:S(2)}, u32[]{:S(2)}) collective-permute-start(f32[184,128]{1,0:T(8,128)S(1)} %get-tuple-element.25), channel_id=1, source_target_pairs={{0,4},{1,5},{2,6},{3,7},{4,0},{5,1},{6,2},{7,3},{8,12},{9,13},{10,... | collective-permute-start | bytes 282632 | tf_op jit(solution)/shard_map/ppermute | solution.py:256
  6.8 6.5 %collective-permute-start.4 = (f32[184,128]{1,0:T(8,128)S(1)}, f32[184,128]{1,0:T(8,128)S(1)}, u32[]{:S(2)}, u32[]{:S(2)}) collective-permute-start(f32[184,128]{1,0:T(8,128)S(1)} %get-tuple-element.26), channel_id=1, source_target_pairs={{0,5},{1,4},{2,7},{3,6},{4,1},{5,0},{6,3},{7,2},{8,13},{9,12},{10,... | collective-permute-start | bytes 282632 | tf_op jit(solution)/shard_map/ppermute | solution.py:256
  7.3 7.5 %collective-permute-start.5 = (f32[184,128]{1,0:T(8,128)S(1)}, f32[184,128]{1,0:T(8,128)S(1)}, u32[]{:S(2)}, u32[]{:S(2)}) collective-permute-start(f32[184,128]{1,0:T(8,128)S(1)} %get-tuple-element.27), channel_id=1, source_target_pairs={{0,6},{1,7},{2,4},{3,5},{4,2},{5,3},{6,0},{7,1},{8,14},{9,15},{10,... | collective-permute-start | bytes 282632 | tf_op jit(solution)/shard_map/ppermute | solution.py:256
  9.6 8.2 %collective-permute-start.6 = (f32[184,128]{1,0:T(8,128)S(1)}, f32[184,128]{1,0:T(8,128)S(1)}, u32[]{:S(2)}, u32[]{:S(2)}) collective-permute-start(f32[184,128]{1,0:T(8,128)S(1)} %get-tuple-element.28), channel_id=1, source_target_pairs={{0,7},{1,6},{2,5},{3,4},{4,3},{5,2},{6,1},{7,0},{8,15},{9,14},{10,... | collective-permute-start | bytes 282632 | tf_op jit(solution)/shard_map/ppermute | solution.py:256
  11.5 8.9 %collective-permute-start.7 = (f32[184,128]{1,0:T(8,128)S(1)}, f32[184,128]{1,0:T(8,128)S(1)}, u32[]{:S(2)}, u32[]{:S(2)}) collective-permute-start(f32[184,128]{1,0:T(8,128)S(1)} %get-tuple-element.29), channel_id=1, source_target_pairs={{0,8},{1,9},{2,10},{3,11},{4,12},{5,13},{6,14},{7,15},{8,0},{9,1},... | collective-permute-start | bytes 282632 | tf_op jit(solution)/shard_map/ppermute | solution.py:256
  11.6 15.6 %collective-permute-start.8 = (f32[184,128]{1,0:T(8,128)S(1)}, f32[184,128]{1,0:T(8,128)S(1)}, u32[]{:S(2)}, u32[]{:S(2)}) collective-permute-start(f32[184,128]{1,0:T(8,128)S(1)} %get-tuple-element.30), channel_id=1, source_target_pairs={{0,9},{1,8},{2,11},{3,10},{4,13},{5,12},{6,15},{7,14},{8,1},{9,0},... | collective-permute-start | bytes 282632 | tf_op jit(solution)/shard_map/ppermute | solution.py:256
  13.3 16.1 %collective-permute-start.9 = (f32[184,128]{1,0:T(8,128)S(1)}, f32[184,128]{1,0:T(8,128)S(1)}, u32[]{:S(2)}, u32[]{:S(2)}) collective-permute-start(f32[184,128]{1,0:T(8,128)S(1)} %get-tuple-element.31), channel_id=1, source_target_pairs={{0,10},{1,11},{2,8},{3,9},{4,14},{5,15},{6,12},{7,13},{8,2},{9,3},... | collective-permute-start | bytes 282632 | tf_op jit(solution)/shard_map/ppermute | solution.py:256
  14.8 17.5 %collective-permute-start.10 = (f32[184,128]{1,0:T(8,128)S(1)}, f32[184,128]{1,0:T(8,128)S(1)}, u32[]{:S(2)}, u32[]{:S(2)}) collective-permute-start(f32[184,128]{1,0:T(8,128)S(1)} %get-tuple-element.32), channel_id=1, source_target_pairs={{0,11},{1,10},{2,9},{3,8},{4,15},{5,14},{6,13},{7,12},{8,3},{9,2},... | collective-permute-start | bytes 282632 | tf_op jit(solution)/shard_map/ppermute | solution.py:256
  17.7 22.5 %collective-permute-start.11 = (f32[184,128]{1,0:T(8,128)S(1)}, f32[184,128]{1,0:T(8,128)S(1)}, u32[]{:S(2)}, u32[]{:S(2)}) collective-permute-start(f32[184,128]{1,0:T(8,128)S(1)} %get-tuple-element.33), channel_id=1, source_target_pairs={{0,12},{1,13},{2,14},{3,15},{4,8},{5,9},{6,10},{7,11},{8,4},{9,5},... | collective-permute-start | bytes 282632 | tf_op jit(solution)/shard_map/ppermute | solution.py:256
  20.5 22.1 %collective-permute-start.12 = (f32[184,128]{1,0:T(8,128)S(1)}, f32[184,128]{1,0:T(8,128)S(1)}, u32[]{:S(2)}, u32[]{:S(2)}) collective-permute-start(f32[184,128]{1,0:T(8,128)S(1)} %get-tuple-element.34), channel_id=1, source_target_pairs={{0,13},{1,12},{2,15},{3,14},{4,9},{5,8},{6,11},{7,10},{8,5},{9,4},... | collective-permute-start | bytes 282632 | tf_op jit(solution)/shard_map/ppermute | solution.py:256
  27.2 18.1 %collective-permute-start.13 = (f32[184,128]{1,0:T(8,128)S(1)}, f32[184,128]{1,0:T(8,128)S(1)}, u32[]{:S(2)}, u32[]{:S(2)}) collective-permute-start(f32[184,128]{1,0:T(8,128)S(1)} %get-tuple-element.35), channel_id=1, source_target_pairs={{0,14},{1,15},{2,12},{3,13},{4,10},{5,11},{6,8},{7,9},{8,6},{9,7},... | collective-permute-start | bytes 282632 | tf_op jit(solution)/shard_map/ppermute | solution.py:256
  29.4 17.9 %collective-permute-start.14 = (f32[184,128]{1,0:T(8,128)S(1)}, f32[184,128]{1,0:T(8,128)S(1)}, u32[]{:S(2)}, u32[]{:S(2)}) collective-permute-start(f32[184,128]{1,0:T(8,128)S(1)} %get-tuple-element.36), channel_id=1, source_target_pairs={{0,15},{1,14},{2,13},{3,12},{4,11},{5,10},{6,9},{7,8},{8,7},{9,6},... | collective-permute-start | bytes 282632 | tf_op jit(solution)/shard_map/ppermute | solution.py:256

commit v2 on v1

--- a/solution.py
+++ b/solution.py
@@ -19,6 +19,7 @@
 PHASE_ROWS = 4 * LEVELS
 USED_ROWS = WEIGHT_ROWS + PHASE_ROWS
 ROWS = (USED_ROWS + 7) // 8 * 8
+ORDER = (8, 1, 9, 2, 10, 3, 11, 4, 12, 5, 13, 6, 14, 7, 15, 0)
 
 NODES = np.cos(math.pi * (2.0 * np.arange(CHEB) + 1.0) / (2.0 * CHEB))
 NODES[CHEB // 2] = 0.0
@@ -82,10 +83,13 @@
     for index, values in enumerate(rows):
         phases_ref[index * LEVELS : (index + 1) * LEVELS, :] = values
     width = outs[0].shape[-1]
-    for step, out in enumerate(outs):
-        columns = pl.ds(pl.multiple_of((me_ref[0] ^ step) * width, width), width)
-        out[:POINTS, :] = weights_ref[0, :, columns]
-        out[POINTS:WEIGHT_ROWS, :] = weights_ref[1, :, columns]
+    for step, out in zip(ORDER, outs):
+        slot = me_ref[0] ^ step
+        columns = pl.ds(pl.multiple_of(slot * width, width), width)
+        for part in range(2):
+            out[part * POINTS : (part + 1) * POINTS, :] = weights_ref[
+                pl.ds(2 * slot + part, POINTS, stride=2 * SLOTS), :
+            ]
         out[WEIGHT_ROWS:USED_ROWS, :] = phases_ref[:, columns]
         out[USED_ROWS:, :] = jnp.zeros((ROWS - USED_ROWS, width), jnp.float32)
 
@@ -99,7 +103,7 @@
         out_shape=[block] * SLOTS,
         in_specs=[smem, smem, vmem, vmem, vmem, vmem],
         out_specs=[vmem] * SLOTS,
-        scratch_shapes=[pltpu.VMEM((PHASE_ROWS, weights.shape[-1]), jnp.float32)],
+        scratch_shapes=[pltpu.VMEM((PHASE_ROWS, kind.shape[-1]), jnp.float32)],
         compiler_params=pltpu.CompilerParams(vmem_limit_bytes=32 * 2**20),
         name="pack",
     )(me, phase_coef, weights, wave, center, kind)
@@ -164,9 +168,9 @@
     out_ref, held, work, parent_ref, child_ref, common_ref, sems = refs[SLOTS:]
     me = me_ref[0]
     copies = []
-    for step in range(SLOTS):
+    for index, step in enumerate(ORDER):
         spot = pl.ds(pl.multiple_of((me ^ step) * ROWS, 8), ROWS)
-        copies.append(pltpu.make_async_copy(blocks[step], held.at[spot, :], sems.at[step]))
+        copies.append(pltpu.make_async_copy(blocks[index], held.at[spot, :], sems.at[index]))
         copies[-1].start()
     for copy in copies:
         copy.wait()
@@ -208,19 +212,18 @@
                         children[1].append(tuple(pairs[1]))
 
                 def store(row, real, imag, tile=tile):
-                    work[row_of(row, column, 0), tile] = real
-                    work[row_of(row, column, 1), tile] = imag
+                    for part, value in enumerate((real, imag)):
+                        index = row_of(row, column, part)
+                        if level < LEVELS - 1:
+                            work[index, tile] = value
+                        else:
+                            start = (index - part * POINTS) * 2 * SLOTS + tile * 16 + part
+                            out_ref[pl.ds(start, 8, stride=2), :] = value
 
                 level_column(tile, column, children, parent_ref, child_ref, common_ref, store)
             return 0
 
         lax.fori_loop(0, CHEB, column_step, 0)
-
-    for box in range(SLOTS):
-        for part in range(2):
-            out_ref[part, :, box * LANES : (box + 1) * LANES] = work[
-                part * POINTS : (part + 1) * POINTS, box // 8, box % 8, :
-            ]
 
 
 def combine(me, blocks):
@@ -229,7 +232,7 @@
     smem = pl.BlockSpec(memory_space=pltpu.SMEM)
     return pl.pallas_call(
         combine_kernel,
-        out_shape=jax.ShapeDtypeStruct((2, POINTS, SLOTS * LANES), jnp.float32),
+        out_shape=jax.ShapeDtypeStruct((WEIGHT_ROWS * SLOTS, LANES), jnp.float32),
         in_specs=[smem] + [hbm] * SLOTS,
         out_specs=vmem,
         scratch_shapes=[
@@ -245,21 +248,33 @@
     )(me, *blocks)
 
 
+def to_rows(weights):
+    return weights.reshape(2, POINTS, SLOTS, LANES).transpose(1, 2, 0, 3).reshape(WEIGHT_ROWS * SLOTS, LANES)
+
+
+def from_rows(rows):
+    return rows.reshape(POINTS, SLOTS, 2, LANES).transpose(2, 0, 1, 3).reshape(2, POINTS, SLOTS * LANES)
+
+
 def on_device(source_weights, wave_vectors, source_centers, phase_coef, phase_kind):
     devices = lax.axis_size("box")
     me = lax.axis_index("box").astype(jnp.int32)[None]
-    kind = phase_kind[None, :]
-    if devices == SLOTS:
-        blocks = pack(me, phase_coef, source_weights, wave_vectors, source_centers, kind)
-        moved = [blocks[0]] + [None] * (SLOTS - 1)
-        for step in range(SLOTS - 1, 0, -1):
-            moved[step] = lax.ppermute(blocks[step], "box", [(s, s ^ step) for s in range(SLOTS)])
-        return combine(me, moved)
-    zero = jnp.zeros_like(me)
-    blocks = pack(zero, phase_coef, source_weights, wave_vectors, source_centers, kind)
-    whole = jnp.concatenate(blocks, axis=1)
-    whole = lax.all_to_all(whole, "box", split_axis=1, concat_axis=1, tiled=True)
-    return combine(zero, [whole[:, s * LANES : (s + 1) * LANES] for s in range(SLOTS)])
+    direct = devices == SLOTS
+    if not direct:
+        me = jnp.zeros_like(me)
+    blocks = pack(
+        me, phase_coef, to_rows(source_weights), wave_vectors, source_centers, phase_kind[None, :]
+    )
+    if direct:
+        blocks = [
+            lax.ppermute(block, "box", [(s, s ^ step) for s in range(SLOTS)]) if step else block
+            for step, block in zip(ORDER, blocks)
+        ]
+    else:
+        whole = jnp.concatenate([blocks[ORDER.index(s)] for s in range(SLOTS)], axis=1)
+        whole = lax.all_to_all(whole, "box", split_axis=1, concat_axis=1, tiled=True)
+        blocks = [whole[:, s * LANES : (s + 1) * LANES] for s in ORDER]
+    return from_rows(combine(me, blocks))
 
 
 def solution(mesh):

time: 59.7 us -> 55.1 us (0.923)
  the two profiles are of different devices: /device:TPU:17 before, /device:TPU:0 now
where the time goes in v2:
time: 55.1 us; the launch traced here: 54.8 us
  starting transfers between devices  28.1 us (51%)
  Pallas kernels  12.1 us (22%)
  waiting for transfers between devices  10.1 us (18%)
  local copies, waits for them, and re-layouts  4.38 us (8%)
    ppermute x15, starting transfers between devices, on_device(): lax.ppermute(block, 'box', [(s, s ^ step) for s in range(SLOTS)])  28.1 us
    pallas_call x1, Pallas kernels, combine(): pl.pallas_call(combine_kernel, out_shape=jax.ShapeDtypeStruct((WEIGHT_ROW...  10.5 us
    ppermute x15, waiting for transfers between devices, on_device(): lax.ppermute(block, 'box', [(s, s ^ step) for s in range(SLOTS)])  10.1 us
    unnamed x10, local copies, waits for them, and re-layouts  4.38 us
    pallas_call x1, Pallas kernels, pack(): pl.pallas_call(pack_kernel, out_shape=[block] * SLOTS, in_specs=[smem, sm...  1.6 us
  transfers between devices with their start and end apart: 15, of which 3 were waited for; matrix products, arithmetic and copies ran while one was open for 0% of the time, Pallas kernels for 0%

profile of v2, /device:TPU:0, one launch (start us, length us, event | category | flops | bytes accessed | tf_op | source)
XLA Modules:
  0.0 54.8 jit_solution(13836407697088309426)
XLA Ops:
  0.0 1.3 %copy-done = f32[2,81,2048]{2,0,1:T(2,128)S(1)} copy-done((f32[2,81,2048]{2,0,1:T(2,128)S(1)}, f32[2,81,2048]{2,0,1:T(2,128)}, u32[]{:S(2)}) %copy-start) | copy-done | bytes 1327128
  1.3 0.8 %copy-done.1 = f32[4,2,2048]{2,1,0:T(2,128)S(1)} copy-done((f32[4,2,2048]{2,1,0:T(2,128)S(1)}, f32[4,2,2048]{2,1,0:T(2,128)}, u32[]{:S(2)}) %copy-start.1) | copy-done | bytes 65560
  2.2 0.8 %copy-done.2 = f32[4,2,2048]{2,1,0:T(2,128)S(1)} copy-done((f32[4,2,2048]{2,1,0:T(2,128)S(1)}, f32[4,2,2048]{2,1,0:T(2,128)}, u32[]{:S(2)}) %copy-start.2) | copy-done | bytes 65560
  3.0 0.7 %copy-done.3 = s32[2048]{0:T(1024)S(1)} copy-done((s32[2048]{0:T(1024)S(1)}, s32[2048]{0:T(1024)}, u32[]{:S(2)}) %copy-start.3) | copy-done | bytes 8216
  3.7 0.7 %copy-done.4 = f32[4,3]{1,0:T(4,128)S(1)} copy-done((f32[4,3]{1,0:T(4,128)S(1)}, f32[4,3]{1,0:T(4,128)}, u32[]{:S(2)}) %copy-start.4) | copy-done | bytes 72
  4.4 1.6 %pack.1 = (f32[184,128]{1,0:T(8,128)S(1)}, f32[184,128]{1,0:T(8,128)S(1)}, f32[184,128]{1,0:T(8,128)S(1)}, f32[184,128]{1,0:T(8,128)S(1)}, f32[184,128]{1,0:T(8,...) custom-call(s32[1]{0:T(128)} %bitcast.me_ref, ...), custom_call_target="tpu_custom_call" | custom-call | tf_op jit(solution)/shard_map/pack/pallas_call | solution.py:101
  6.0 4.1 %collective-permute-start = (f32[184,128]{1,0:T(8,128)S(1)}, f32[184,128]{1,0:T(8,128)S(1)}, u32[]{:S(2)}, u32[]{:S(2)}) collective-permute-start(f32[184,128]{1,0:T(8,128)S(1)} %get-tuple-element.21), channel_id=1, source_target_pairs={{0,8},{1,9},{2,10},{3,11},{4,12},{5,13},{6,14},{7,15},{8,0},{9,1},... | collective-permute-start | bytes 282632 | tf_op jit(solution)/shard_map/ppermute | solution.py:270
  10.1 0.0 collective-permute-start.1
  10.1 0.2 collective-permute-start.2
  10.3 1.8 %collective-permute-start.3 = (f32[184,128]{1,0:T(8,128)S(1)}, f32[184,128]{1,0:T(8,128)S(1)}, u32[]{:S(2)}, u32[]{:S(2)}) collective-permute-start(f32[184,128]{1,0:T(8,128)S(1)} %get-tuple-element.24), channel_id=1, source_target_pairs={{0,2},{1,3},{2,0},{3,1},{4,6},{5,7},{6,4},{7,5},{8,10},{9,11},{10,... | collective-permute-start | bytes 282632 | tf_op jit(solution)/shard_map/ppermute | solution.py:270
  12.1 2.5 %collective-permute-start.4 = (f32[184,128]{1,0:T(8,128)S(1)}, f32[184,128]{1,0:T(8,128)S(1)}, u32[]{:S(2)}, u32[]{:S(2)}) collective-permute-start(f32[184,128]{1,0:T(8,128)S(1)} %get-tuple-element.25), channel_id=1, source_target_pairs={{0,10},{1,11},{2,8},{3,9},{4,14},{5,15},{6,12},{7,13},{8,2},{9,3},... | collective-permute-start | bytes 282632 | tf_op jit(solution)/shard_map/ppermute | solution.py:270
  14.6 5.1 %collective-permute-done.refs_0_ = f32[184,128]{1,0:T(8,128)S(1)} collective-permute-done((f32[184,128]{1,0:T(8,128)S(1)}, f32[184,128]{1,0:T(8,128)S(1)}, u32[]{:S(2)}, u32[]{:S(2)}) %collective-permute-start) | collective-permute-done | bytes 94240 | tf_op jit(solution)/shard_map/ppermute | solution.py:270
  19.7 0.0 collective-permute-start.5
  19.7 0.0 collective-permute-done.1.refs_1_
  19.7 0.6 %collective-permute-start.6 = (f32[184,128]{1,0:T(8,128)S(1)}, f32[184,128]{1,0:T(8,128)S(1)}, u32[]{:S(2)}, u32[]{:S(2)}) collective-permute-start(f32[184,128]{1,0:T(8,128)S(1)} %get-tuple-element.27), channel_id=1, source_target_pairs={{0,11},{1,10},{2,9},{3,8},{4,15},{5,14},{6,13},{7,12},{8,3},{9,2},... | collective-permute-start | bytes 282632 | tf_op jit(solution)/shard_map/ppermute | solution.py:270
  20.3 0.0 collective-permute-done.2.refs_2_
  20.3 4.0 %collective-permute-start.7 = (f32[184,128]{1,0:T(8,128)S(1)}, f32[184,128]{1,0:T(8,128)S(1)}, u32[]{:S(2)}, u32[]{:S(2)}) collective-permute-start(f32[184,128]{1,0:T(8,128)S(1)} %get-tuple-element.28), channel_id=1, source_target_pairs={{0,4},{1,5},{2,6},{3,7},{4,0},{5,1},{6,2},{7,3},{8,12},{9,13},{10,... | collective-permute-start | bytes 282632 | tf_op jit(solution)/shard_map/ppermute | solution.py:270
  24.2 0.0 collective-permute-done.3.refs_3_
  24.2 1.0 %collective-permute-start.8 = (f32[184,128]{1,0:T(8,128)S(1)}, f32[184,128]{1,0:T(8,128)S(1)}, u32[]{:S(2)}, u32[]{:S(2)}) collective-permute-start(f32[184,128]{1,0:T(8,128)S(1)} %get-tuple-element.29), channel_id=1, source_target_pairs={{0,12},{1,13},{2,14},{3,15},{4,8},{5,9},{6,10},{7,11},{8,4},{9,5},... | collective-permute-start | bytes 282632 | tf_op jit(solution)/shard_map/ppermute | solution.py:270
  25.3 0.0 collective-permute-done.4.refs_4_
  25.3 1.0 %collective-permute-done.5.refs_5_ = f32[184,128]{1,0:T(8,128)S(1)} collective-permute-done((f32[184,128]{1,0:T(8,128)S(1)}, f32[184,128]{1,0:T(8,128)S(1)}, u32[]{:S(2)}, u32[]{:S(2)}) %collective-permute-start.5) | collective-permute-done | bytes 94240 | tf_op jit(solution)/shard_map/ppermute | solution.py:270
  26.3 2.7 %collective-permute-start.10 = (f32[184,128]{1,0:T(8,128)S(1)}, f32[184,128]{1,0:T(8,128)S(1)}, u32[]{:S(2)}, u32[]{:S(2)}) collective-permute-start(f32[184,128]{1,0:T(8,128)S(1)} %get-tuple-element.31), channel_id=1, source_target_pairs={{0,13},{1,12},{2,15},{3,14},{4,9},{5,8},{6,11},{7,10},{8,5},{9,4},... | collective-permute-start | bytes 282632 | tf_op jit(solution)/shard_map/ppermute | solution.py:270
  29.0 1.4 %collective-permute-start.11 = (f32[184,128]{1,0:T(8,128)S(1)}, f32[184,128]{1,0:T(8,128)S(1)}, u32[]{:S(2)}, u32[]{:S(2)}) collective-permute-start(f32[184,128]{1,0:T(8,128)S(1)} %get-tuple-element.32), channel_id=1, source_target_pairs={{0,6},{1,7},{2,4},{3,5},{4,2},{5,3},{6,0},{7,1},{8,14},{9,15},{10,... | collective-permute-start | bytes 282632 | tf_op jit(solution)/shard_map/ppermute | solution.py:270
  30.4 0.0 collective-permute-done.7.refs_7_
  30.4 6.1 %collective-permute-start.12 = (f32[184,128]{1,0:T(8,128)S(1)}, f32[184,128]{1,0:T(8,128)S(1)}, u32[]{:S(2)}, u32[]{:S(2)}) collective-permute-start(f32[184,128]{1,0:T(8,128)S(1)} %get-tuple-element.33), channel_id=1, source_target_pairs={{0,14},{1,15},{2,12},{3,13},{4,10},{5,11},{6,8},{7,9},{8,6},{9,7},... | collective-permute-start | bytes 282632 | tf_op jit(solution)/shard_map/ppermute | solution.py:270
  36.5 0.0 collective-permute-done.8.refs_8_
  36.5 0.0 collective-permute-start.13
  36.5 0.0 collective-permute-done.9.refs_9_
  36.5 3.7 %collective-permute-start.14 = (f32[184,128]{1,0:T(8,128)S(1)}, f32[184,128]{1,0:T(8,128)S(1)}, u32[]{:S(2)}, u32[]{:S(2)}) collective-permute-start(f32[184,128]{1,0:T(8,128)S(1)} %get-tuple-element.35), channel_id=1, source_target_pairs={{0,15},{1,14},{2,13},{3,12},{4,11},{5,10},{6,9},{7,8},{8,7},{9,6},... | collective-permute-start | bytes 282632 | tf_op jit(solution)/shard_map/ppermute | solution.py:270
  40.3 3.9 %collective-permute-done.13.refs_13_ = f32[184,128]{1,0:T(8,128)S(1)} collective-permute-done((f32[184,128]{1,0:T(8,128)S(1)}, f32[184,128]{1,0:T(8,128)S(1)}, u32[]{:S(2)}, u32[]{:S(2)}) %collective-permute-start.13) | collective-permute-done | bytes 94240 | tf_op jit(solution)/shard_map/ppermute | solution.py:270
  44.2 0.0 collective-permute-done.14.refs_14_
  44.2 10.5 %combine.1 = f32[2592,128]{1,0:T(8,128)} custom-call(s32[1]{0:T(128)} %bitcast.me_ref, f32[184,128]{1,0:T(8,128)S(1)} %collective-permute-done.refs_0_, f32[184,128]{1,0:T(8,128)S(1)} %collective-permute-done.1.refs_1_, f32[184,128]{1,0:T(8,128)S(1)} %collective-permute-done.2.refs_2_, f32[184,128]{1,0:T(8,128)S(1)} %collective-permute-done.3.refs_3_, ...), custom_call_target="tpu_custom_call" | custom-call | tf_op jit(solution)/shard_map/combine/pallas_call | solution.py:233
  (10 shorter events, 0.0 us)
Async XLA Ops:
  0.0 1.3 %copy-start = (f32[2,81,2048]{2,0,1:T(2,128)S(1)}, f32[2,81,2048]{2,0,1:T(2,128)}, u32[]{:S(2)}) copy-start(f32[2,81,2048]{2,0,1:T(2,128)} %param.5) | copy-start | bytes 3981316
  1.3 0.8 %copy-start.1 = (f32[4,2,2048]{2,1,0:T(2,128)S(1)}, f32[4,2,2048]{2,1,0:T(2,128)}, u32[]{:S(2)}) copy-start(f32[4,2,2048]{2,1,0:T(2,128)} %wave_ref.1) | copy-start | bytes 196612
  2.2 0.8 %copy-start.2 = (f32[4,2,2048]{2,1,0:T(2,128)S(1)}, f32[4,2,2048]{2,1,0:T(2,128)}, u32[]{:S(2)}) copy-start(f32[4,2,2048]{2,1,0:T(2,128)} %center_ref.1) | copy-start | bytes 196612
  3.0 0.7 %copy-start.3 = (s32[2048]{0:T(1024)S(1)}, s32[2048]{0:T(1024)}, u32[]{:S(2)}) copy-start(s32[2048]{0:T(1024)} %param.9) | copy-start | bytes 24580
  3.7 0.7 %copy-start.4 = (f32[4,3]{1,0:T(4,128)S(1)}, f32[4,3]{1,0:T(4,128)}, u32[]{:S(2)}) copy-start(f32[4,3]{1,0:T(4,128)} %coef_ref.1) | copy-start | bytes 148
  6.0 13.7 %collective-permute-start = (f32[184,128]{1,0:T(8,128)S(1)}, f32[184,128]{1,0:T(8,128)S(1)}, u32[]{:S(2)}, u32[]{:S(2)}) collective-permute-start(f32[184,128]{1,0:T(8,128)S(1)} %get-tuple-element.21), channel_id=1, source_target_pairs={{0,8},{1,9},{2,10},{3,11},{4,12},{5,13},{6,14},{7,15},{8,0},{9,1},... | collective-permute-start | bytes 282632 | tf_op jit(solution)/shard_map/ppermute | solution.py:270
  10.1 9.6 %collective-permute-start.1 = (f32[184,128]{1,0:T(8,128)S(1)}, f32[184,128]{1,0:T(8,128)S(1)}, u32[]{:S(2)}, u32[]{:S(2)}) collective-permute-start(f32[184,128]{1,0:T(8,128)S(1)} %get-tuple-element.22), channel_id=1, source_target_pairs={{0,1},{1,0},{2,3},{3,2},{4,5},{5,4},{6,7},{7,6},{8,9},{9,8},{10,11... | collective-permute-start | bytes 282632 | tf_op jit(solution)/shard_map/ppermute | solution.py:270
  10.1 10.2 %collective-permute-start.2 = (f32[184,128]{1,0:T(8,128)S(1)}, f32[184,128]{1,0:T(8,128)S(1)}, u32[]{:S(2)}, u32[]{:S(2)}) collective-permute-start(f32[184,128]{1,0:T(8,128)S(1)} %get-tuple-element.23), channel_id=1, source_target_pairs={{0,9},{1,8},{2,11},{3,10},{4,13},{5,12},{6,15},{7,14},{8,1},{9,0},... | collective-permute-start | bytes 282632 | tf_op jit(solution)/shard_map/ppermute | solution.py:270
  10.3 13.9 %collective-permute-start.3 = (f32[184,128]{1,0:T(8,128)S(1)}, f32[184,128]{1,0:T(8,128)S(1)}, u32[]{:S(2)}, u32[]{:S(2)}) collective-permute-start(f32[184,128]{1,0:T(8,128)S(1)} %get-tuple-element.24), channel_id=1, source_target_pairs={{0,2},{1,3},{2,0},{3,1},{4,6},{5,7},{6,4},{7,5},{8,10},{9,11},{10,... | collective-permute-start | bytes 282632 | tf_op jit(solution)/shard_map/ppermute | solution.py:270
  12.1 13.2 %collective-permute-start.4 = (f32[184,128]{1,0:T(8,128)S(1)}, f32[184,128]{1,0:T(8,128)S(1)}, u32[]{:S(2)}, u32[]{:S(2)}) collective-permute-start(f32[184,128]{1,0:T(8,128)S(1)} %get-tuple-element.25), channel_id=1, source_target_pairs={{0,10},{1,11},{2,8},{3,9},{4,14},{5,15},{6,12},{7,13},{8,2},{9,3},... | collective-permute-start | bytes 282632 | tf_op jit(solution)/shard_map/ppermute | solution.py:270
  19.7 6.6 %collective-permute-start.5 = (f32[184,128]{1,0:T(8,128)S(1)}, f32[184,128]{1,0:T(8,128)S(1)}, u32[]{:S(2)}, u32[]{:S(2)}) collective-permute-start(f32[184,128]{1,0:T(8,128)S(1)} %get-tuple-element.26), channel_id=1, source_target_pairs={{0,3},{1,2},{2,1},{3,0},{4,7},{5,6},{6,5},{7,4},{8,11},{9,10},{10,... | collective-permute-start | bytes 282632 | tf_op jit(solution)/shard_map/ppermute | solution.py:270
  19.7 9.3 %collective-permute-start.6 = (f32[184,128]{1,0:T(8,128)S(1)}, f32[184,128]{1,0:T(8,128)S(1)}, u32[]{:S(2)}, u32[]{:S(2)}) collective-permute-start(f32[184,128]{1,0:T(8,128)S(1)} %get-tuple-element.27), channel_id=1, source_target_pairs={{0,11},{1,10},{2,9},{3,8},{4,15},{5,14},{6,13},{7,12},{8,3},{9,2},... | collective-permute-start | bytes 282632 | tf_op jit(solution)/shard_map/ppermute | solution.py:270
  20.3 10.1 %collective-permute-start.7 = (f32[184,128]{1,0:T(8,128)S(1)}, f32[184,128]{1,0:T(8,128)S(1)}, u32[]{:S(2)}, u32[]{:S(2)}) collective-permute-start(f32[184,128]{1,0:T(8,128)S(1)} %get-tuple-element.28), channel_id=1, source_target_pairs={{0,4},{1,5},{2,6},{3,7},{4,0},{5,1},{6,2},{7,3},{8,12},{9,13},{10,... | collective-permute-start | bytes 282632 | tf_op jit(solution)/shard_map/ppermute | solution.py:270
  24.2 12.3 %collective-permute-start.8 = (f32[184,128]{1,0:T(8,128)S(1)}, f32[184,128]{1,0:T(8,128)S(1)}, u32[]{:S(2)}, u32[]{:S(2)}) collective-permute-start(f32[184,128]{1,0:T(8,128)S(1)} %get-tuple-element.29), channel_id=1, source_target_pairs={{0,12},{1,13},{2,14},{3,15},{4,8},{5,9},{6,10},{7,11},{8,4},{9,5},... | collective-permute-start | bytes 282632 | tf_op jit(solution)/shard_map/ppermute | solution.py:270
  25.3 11.3 %collective-permute-start.9 = (f32[184,128]{1,0:T(8,128)S(1)}, f32[184,128]{1,0:T(8,128)S(1)}, u32[]{:S(2)}, u32[]{:S(2)}) collective-permute-start(f32[184,128]{1,0:T(8,128)S(1)} %get-tuple-element.30), channel_id=1, source_target_pairs={{0,5},{1,4},{2,7},{3,6},{4,1},{5,0},{6,3},{7,2},{8,13},{9,12},{10,... | collective-permute-start | bytes 282632 | tf_op jit(solution)/shard_map/ppermute | solution.py:270
  26.3 14.0 %collective-permute-start.10 = (f32[184,128]{1,0:T(8,128)S(1)}, f32[184,128]{1,0:T(8,128)S(1)}, u32[]{:S(2)}, u32[]{:S(2)}) collective-permute-start(f32[184,128]{1,0:T(8,128)S(1)} %get-tuple-element.31), channel_id=1, source_target_pairs={{0,13},{1,12},{2,15},{3,14},{4,9},{5,8},{6,11},{7,10},{8,5},{9,4},... | collective-permute-start | bytes 282632 | tf_op jit(solution)/shard_map/ppermute | solution.py:270
  29.0 11.2 %collective-permute-start.11 = (f32[184,128]{1,0:T(8,128)S(1)}, f32[184,128]{1,0:T(8,128)S(1)}, u32[]{:S(2)}, u32[]{:S(2)}) collective-permute-start(f32[184,128]{1,0:T(8,128)S(1)} %get-tuple-element.32), channel_id=1, source_target_pairs={{0,6},{1,7},{2,4},{3,5},{4,2},{5,3},{6,0},{7,1},{8,14},{9,15},{10,... | collective-permute-start | bytes 282632 | tf_op jit(solution)/shard_map/ppermute | solution.py:270
  30.4 9.9 %collective-permute-start.12 = (f32[184,128]{1,0:T(8,128)S(1)}, f32[184,128]{1,0:T(8,128)S(1)}, u32[]{:S(2)}, u32[]{:S(2)}) collective-permute-start(f32[184,128]{1,0:T(8,128)S(1)} %get-tuple-element.33), channel_id=1, source_target_pairs={{0,14},{1,15},{2,12},{3,13},{4,10},{5,11},{6,8},{7,9},{8,6},{9,7},... | collective-permute-start | bytes 282632 | tf_op jit(solution)/shard_map/ppermute | solution.py:270
  36.5 7.7 %collective-permute-start.13 = (f32[184,128]{1,0:T(8,128)S(1)}, f32[184,128]{1,0:T(8,128)S(1)}, u32[]{:S(2)}, u32[]{:S(2)}) collective-permute-start(f32[184,128]{1,0:T(8,128)S(1)} %get-tuple-element.34), channel_id=1, source_target_pairs={{0,7},{1,6},{2,5},{3,4},{4,3},{5,2},{6,1},{7,0},{8,15},{9,14},{10,... | collective-permute-start | bytes 282632 | tf_op jit(solution)/shard_map/ppermute | solution.py:270
  36.5 7.7 %collective-permute-start.14 = (f32[184,128]{1,0:T(8,128)S(1)}, f32[184,128]{1,0:T(8,128)S(1)}, u32[]{:S(2)}, u32[]{:S(2)}) collective-permute-start(f32[184,128]{1,0:T(8,128)S(1)} %get-tuple-element.35), channel_id=1, source_target_pairs={{0,15},{1,14},{2,13},{3,12},{4,11},{5,10},{6,9},{7,8},{8,7},{9,6},... | collective-permute-start | bytes 282632 | tf_op jit(solution)/shard_map/ppermute | solution.py:270

commit v3 on v2

v3 whole, which is shorter than its diff:
```python
import functools
import math

import numpy as np

import jax
import jax.numpy as jnp
from jax import lax
from jax.experimental import pallas as pl
from jax.experimental.pallas import tpu as pltpu
from jax.sharding import PartitionSpec as P

CHEB = 9
POINTS = CHEB * CHEB
KINDS = 4
LEVELS = 4
SLOTS = 1 << LEVELS
LANES = 128
WEIGHT_ROWS = 2 * POINTS
PHASE_ROWS = 4 * LEVELS
USED_ROWS = WEIGHT_ROWS + PHASE_ROWS
ROWS = (USED_ROWS + 7) // 8 * 8
OCT = SLOTS // 2
EVEN_ORDER = (8, 10, 2, 12, 4, 14, 6, 0)
ODD_ORDER = (9, 11, 3, 13, 5, 15, 7, 1)

NODES = np.cos(math.pi * (2.0 * np.arange(CHEB) + 1.0) / (2.0 * CHEB))
NODES[CHEB // 2] = 0.0


def interpolation_halves():
    targets = (NODES - 1.0) / 2.0
    matrix = np.ones((CHEB, CHEB))
    for t in range(CHEB):
        for m in range(CHEB):
            if m != t:
                matrix[t] *= (targets - NODES[m]) / (NODES[t] - NODES[m])
    return (matrix + matrix[::-1]) / 2.0, (matrix - matrix[::-1]) / 2.0


EVEN_HALF, ODD_HALF = interpolation_halves()

SIN_COEFS = (3.1415926401839673, -5.167710090328242, 2.5500776596583643, -0.5982921590176602, 0.0776594073245765)
COS_COEFS = (0.999999953466542, -4.934792858659144, 4.05841191384421, -1.3318801591805476, 0.219696794464285)


def cos_sin_turns(turns):
    rest = turns - jnp.round(turns)
    square = rest * rest
    sine = jnp.float32(SIN_COEFS[-1])
    cosine = jnp.float32(COS_COEFS[-1])
    for s, c in zip(SIN_COEFS[-2::-1], COS_COEFS[-2::-1]):
        sine = sine * square + s
        cosine = cosine * square + c
    sine = sine * rest
    twice = sine + sine
    return 1.0 - twice * sine, twice * cosine


def phase_rows(wave, center, kind, coef_ref):
    a = b = e = jnp.zeros(kind.shape, jnp.float32)
    for index in range(KINDS):
        chosen = kind == index
        a = jnp.where(chosen, coef_ref[index, 0], a)
        b = jnp.where(chosen, coef_ref[index, 1], b)
        e = jnp.where(chosen, coef_ref[index, 2], e)
    k1, k2 = wave
    x1, x2 = center
    level = lax.broadcasted_iota(jnp.int32, k1.shape, 0)
    half = jnp.full(k1.shape, 2.0**-LEVELS, jnp.float32)
    for index in range(1, LEVELS):
        half = jnp.where(level == index, 2.0 ** (index - LEVELS), half)
    scaled = b * k1
    root = a * jnp.sqrt(scaled * scaled + k2 * k2 + 1.0)
    bent = root * e
    constant = x1 * k1 + x2 * k2 + root + bent * x1 * x1
    constant = constant - jnp.round(constant)
    return constant, half * (k1 + 2.0 * bent * x1), half * half * bent, half * k2


def pack_kernel(far, me_ref, coef_hbm, weights_hbm, wave_hbm, center_hbm, kind_hbm, *refs):
    outs = refs[:OCT]
    coef_ref, wave_ref, center_ref, kind_ref, phases_ref, sems, block_sems = refs[OCT:]
    me = me_ref[0]
    first = ((me // OCT) ^ far) * OCT
    columns = pl.ds(pl.multiple_of(first * LANES, OCT * LANES), OCT * LANES)
    small = [
        pltpu.make_async_copy(coef_hbm, coef_ref, sems.at[0]),
        pltpu.make_async_copy(wave_hbm.at[:, :, columns], wave_ref, sems.at[1]),
        pltpu.make_async_copy(center_hbm.at[:, :, columns], center_ref, sems.at[2]),
        pltpu.make_async_copy(kind_hbm.at[:, columns], kind_ref, sems.at[3]),
    ]
    large = [
        pltpu.make_async_copy(
            weights_hbm.at[:, first + ((me % OCT) ^ step)], outs[step].at[pl.ds(0, POINTS)], block_sems.at[step]
        )
        for step in range(OCT)
    ]
    for copy in small + large:
        copy.start()
    for copy in small:
        copy.wait()
    rows = phase_rows(
        (wave_ref[:, 0, :], wave_ref[:, 1, :]), (center_ref[:, 0, :], center_ref[:, 1, :]), kind_ref[...], coef_ref
    )
    for index, values in enumerate(rows):
        for level in range(LEVELS):
            row = index * LEVELS + level
            phases_ref[row // 2, row % 2, :] = values[level]
    for step, out in enumerate(outs):
        mine = pl.ds(pl.multiple_of(((me % OCT) ^ step) * LANES, LANES), LANES)
        out[POINTS : USED_ROWS // 2] = phases_ref[:, :, mine]
        out[USED_ROWS // 2 :] = jnp.zeros(((ROWS - USED_ROWS) // 2, 2, LANES), jnp.float32)
    for copy in large:
        copy.wait()


def pack(far, me, phase_coef, weights, wave, center, kind):
    block = jax.ShapeDtypeStruct((ROWS // 2, 2, LANES), jnp.float32)
    vmem = pl.BlockSpec(memory_space=pltpu.VMEM)
    hbm = pl.BlockSpec(memory_space=pltpu.HBM)
    blocks = pl.pallas_call(
        functools.partial(pack_kernel, far),
        out_shape=[block] * OCT,
        in_specs=[pl.BlockSpec(memory_space=pltpu.SMEM)] + [hbm] * 5,
        out_specs=[vmem] * OCT,
        scratch_shapes=[
            pltpu.SMEM(phase_coef.shape, jnp.float32),
            pltpu.VMEM((LEVELS, 2, OCT * LANES), jnp.float32),
            pltpu.VMEM((LEVELS, 2, OCT * LANES), jnp.float32),
            pltpu.VMEM((1, OCT * LANES), jnp.int32),
            pltpu.VMEM((PHASE_ROWS // 2, 2, OCT * LANES), jnp.float32),
            pltpu.SemaphoreType.DMA((4,)),
            pltpu.SemaphoreType.DMA((OCT,)),
        ],
        compiler_params=pltpu.CompilerParams(vmem_limit_bytes=16 * 2**20),
        cost_estimate=pl.CostEstimate(flops=2**20, bytes_accessed=2 * 2**20, transcendentals=0),
        name="pack_far" if far else "pack_near",
    )(me, phase_coef, weights, wave, center, kind)
    return [block.reshape(ROWS, LANES) for block in blocks]


def level_factors(level, phases, parent_ref, child_ref, common_ref):
    constant, linear, quadratic, other = phases
    if level % 2 == 0:
        split = lambda x: constant + x * (linear + x * quadratic)
        common = lambda x: x * other
    else:
        split = lambda x: constant + x * other
        common = lambda x: x * (linear + x * quadratic)
    for t in range(CHEB):
        node = float(NODES[t])
        parent_ref[t, 0], parent_ref[t, 1] = cos_sin_turns(split(node))
        for child in range(2):
            shifted = (node + 2.0 * child - 1.0) / 2.0
            child_ref[child, t, 0], child_ref[child, t, 1] = cos_sin_turns(split(shifted))
        cosine, sine = cos_sin_turns(common(node))
        common_ref[t] = cosine * cosine + sine * sine


def level_column(column, children, parent_ref, child_ref, common_ref, store):
    scaled = []
    for child in range(2):
        line = []
        for s in range(CHEB):
            real, imag = children[child][s]
            cosine, sine = child_ref[child, s, 0], child_ref[child, s, 1]
            line.append((cosine * real + sine * imag, cosine * imag - sine * real))
        scaled.append(line)
    halves = []
    for part in range(2):
        plus = [scaled[0][s][part] + scaled[1][CHEB - 1 - s][part] for s in range(CHEB)]
        minus = [scaled[0][s][part] - scaled[1][CHEB - 1 - s][part] for s in range(CHEB)]
        halves.append((plus, minus))
    common = common_ref[column]
    mid = CHEB // 2
    for t in range(mid + 1):
        sums = []
        for part in range(2):
            plus, minus = halves[part]
            even = plus[0] * float(EVEN_HALF[t, 0])
            for s in range(1, CHEB):
                even = even + plus[s] * float(EVEN_HALF[t, s])
            if t == mid:
                sums.append((even,))
                continue
            odd = minus[0] * float(ODD_HALF[t, 0])
            for s in range(1, CHEB):
                odd = odd + minus[s] * float(ODD_HALF[t, s])
            sums.append((even + odd, even - odd))
        for which, row in enumerate((t,) if t == mid else (t, CHEB - 1 - t)):
            real, imag = sums[0][which] * common, sums[1][which] * common
            cosine, sine = parent_ref[row, 0], parent_ref[row, 1]
            store(row, cosine * real - sine * imag, cosine * imag + sine * real)


def row_of(level, split, column, part):
    return part + 2 * (split * CHEB + column if level % 2 == 0 else column * CHEB + split)


def join_chips(me, blocks, order, held, sems, work, last_phases, factors):
    copies = []
    for index, step in enumerate(order):
        spot = pl.ds(pl.multiple_of(((me ^ step) // 2) * ROWS, 8), ROWS)
        copies.append(pltpu.make_async_copy(blocks[index], held.at[spot, :], sems.at[index]))
        copies[-1].start()
    for copy in copies:
        copy.wait()

    def received(row):
        return held[pl.ds(row, OCT, stride=ROWS), :]

    for part in range(4):
        last_phases[part] = received(WEIGHT_ROWS + part * LEVELS + LEVELS - 1)
    for level in range(LEVELS - 1):
        level_factors(level, [received(WEIGHT_ROWS + part * LEVELS + level) for part in range(4)], *factors)
        bit = OCT >> (level + 1)

        def column_step(column, _, level=level, bit=bit):
            upper = (lax.broadcasted_iota(jnp.int32, (OCT, LANES), 0) & bit) != 0
            children = [[], []]
            for s in range(CHEB):
                pairs = [[], []]
                for part in range(2):
                    row = row_of(level, s, column, part)
                    value = received(row) if level == 0 else work[row]
                    down = pltpu.roll(value, bit, 0)
                    up = down if 2 * bit == OCT else pltpu.roll(value, OCT - bit, 0)
                    pairs[0].append(jnp.where(upper, down, value))
                    pairs[1].append(jnp.where(upper, value, up))
                children[0].append(tuple(pairs[0]))
                children[1].append(tuple(pairs[1]))

            def store(row, real, imag):
                work[row_of(level, row, column, 0)] = real
                work[row_of(level, row, column, 1)] = imag

            level_column(column, children, *factors, store)
            return 0

        lax.fori_loop(0, CHEB, column_step, 0)


def even_kernel(me_ref, *refs):
    blocks = refs[:OCT]
    work, last_phases, held, parent_ref, child_ref, common_ref, sems = refs[OCT:]
    factors = (parent_ref, child_ref, common_ref)
    join_chips(me_ref[0], blocks, EVEN_ORDER, held, sems, work, last_phases, factors)


def odd_kernel(me_ref, even_work, even_phases, *refs):
    blocks = refs[:OCT]
    out_hbm, work, last_phases, held, out_ref, parent_ref, child_ref, common_ref, sems, out_sems = refs[OCT:]
    me = me_ref[0]
    own = me % 2
    early = [
        pltpu.make_async_copy(even_work, work.at[own], out_sems.at[0]),
        pltpu.make_async_copy(even_phases, last_phases.at[own], out_sems.at[1]),
    ]
    for copy in early:
        copy.start()
    factors = [ref.at[0] for ref in (parent_ref, child_ref, common_ref)]
    join_chips(me, blocks, ODD_ORDER, held, sems, work.at[1 - own], last_phases.at[1 - own], factors)
    for copy in early:
        copy.wait()

    level = LEVELS - 1
    for parity in range(2):
        level_factors(
            level,
            [last_phases[parity, part] for part in range(4)],
            parent_ref.at[parity],
            child_ref.at[parity],
            common_ref.at[parity],
        )
    chunk = out_ref.shape[0] // CHEB

    def leave(column):
        rows = pl.ds(pl.multiple_of(column * chunk, 8), chunk)
        return pltpu.make_async_copy(out_ref.at[rows, :], out_hbm.at[rows, :], out_sems.at[column])

    def column_step(column, _):
        children = [
            [tuple(work[child, row_of(level, s, column, part)] for part in range(2)) for s in range(CHEB)]
            for child in range(2)
        ]
        for parity in range(2):

            def store(row, real, imag, parity=parity):
                start = row_of(level, row, column, 0) * SLOTS + 2 * parity
                out_ref[pl.ds(start, OCT, stride=4), :] = real
                out_ref[pl.ds(start + 1, OCT, stride=4), :] = imag

            level_column(
                column, children, parent_ref.at[parity], child_ref.at[parity], common_ref.at[parity], store
            )
        leave(column).start()
        return 0

    lax.fori_loop(0, CHEB, column_step, 0)
    for column in range(CHEB):
        leave(column).wait()


def factor_scratch(count):
    return [
        pltpu.VMEM(count + (CHEB, 2, OCT, LANES), jnp.float32),
        pltpu.VMEM(count + (2, CHEB, 2, OCT, LANES), jnp.float32),
        pltpu.VMEM(count + (CHEB, OCT, LANES), jnp.float32),
    ]


def combine_even(me, blocks):
    vmem = pl.BlockSpec(memory_space=pltpu.VMEM)
    return pl.pallas_call(
        even_kernel,
        out_shape=[
            jax.ShapeDtypeStruct((WEIGHT_ROWS, OCT, LANES), jnp.float32),
            jax.ShapeDtypeStruct((4, OCT, LANES), jnp.float32),
        ],
        in_specs=[pl.BlockSpec(memory_space=pltpu.SMEM)] + [pl.BlockSpec(memory_space=pl.ANY)] * OCT,
        out_specs=[vmem, vmem],
        scratch_shapes=[
            pltpu.VMEM((OCT * ROWS, LANES), jnp.float32),
            *factor_scratch(()),
            pltpu.SemaphoreType.DMA((OCT,)),
        ],
        compiler_params=pltpu.CompilerParams(vmem_limit_bytes=16 * 2**20),
        cost_estimate=pl.CostEstimate(flops=40 * 2**20, bytes_accessed=12 * 2**20, transcendentals=0),
        name="combine_even",
    )(me, *blocks)


def combine_odd(me, even, blocks):
    hbm = pl.BlockSpec(memory_space=pltpu.HBM)
    anywhere = pl.BlockSpec(memory_space=pl.ANY)
    return pl.pallas_call(
        odd_kernel,
        out_shape=jax.ShapeDtypeStruct((WEIGHT_ROWS * SLOTS, LANES), jnp.float32),
        in_specs=[pl.BlockSpec(memory_space=pltpu.SMEM)] + [anywhere] * (2 + OCT),
        out_specs=hbm,
        scratch_shapes=[
            pltpu.VMEM((2, WEIGHT_ROWS, OCT, LANES), jnp.float32),
            pltpu.VMEM((2, 4, OCT, LANES), jnp.float32),
            pltpu.VMEM((OCT * ROWS, LANES), jnp.float32),
            pltpu.VMEM((WEIGHT_ROWS * SLOTS, LANES), jnp.float32),
            *factor_scratch((2,)),
            pltpu.SemaphoreType.DMA((OCT,)),
            pltpu.SemaphoreType.DMA((CHEB,)),
        ],
        compiler_params=pltpu.CompilerParams(vmem_limit_bytes=16 * 2**20),
        cost_estimate=pl.CostEstimate(flops=80 * 2**20, bytes_accessed=20 * 2**20, transcendentals=0),
        name="combine_odd",
    )(me, *even, *blocks)


def on_device(source_weights, wave_vectors, source_centers, phase_coef, phase_kind):
    devices = lax.axis_size("box")
    me = lax.axis_index("box").astype(jnp.int32)[None]
    direct = devices == SLOTS
    if not direct:
        me = jnp.zeros_like(me)
    weights = source_weights.reshape(2, POINTS, SLOTS, LANES).transpose(1, 2, 0, 3)
    operands = [phase_coef, weights, wave_vectors, source_centers, phase_kind[None, :]]
    operands = [me] + [pltpu.with_memory_space_constraint(operand, pltpu.HBM) for operand in operands]
    far_blocks = pack(1, *operands)
    operands[0], far_blocks[0] = lax.optimization_barrier((me, far_blocks[0]))
    near_blocks = pack(0, *operands)
    blocks = near_blocks + far_blocks
    if direct:
        for step in EVEN_ORDER + ODD_ORDER:
            if step:
                blocks[step] = lax.ppermute(blocks[step], "box", [(s, s ^ step) for s in range(SLOTS)])
    else:
        whole = jnp.concatenate(blocks, axis=1)
        whole = lax.all_to_all(whole, "box", split_axis=1, concat_axis=1, tiled=True)
        blocks = [whole[:, s * LANES : (s + 1) * LANES] for s in range(SLOTS)]
    even = combine_even(me, [blocks[step] for step in EVEN_ORDER])
    rows = combine_odd(me, even, [blocks[step] for step in ODD_ORDER])
    return rows.reshape(POINTS, SLOTS, 2, LANES).transpose(2, 0, 1, 3).reshape(2, POINTS, SLOTS * LANES)


def solution(mesh):
    in_specs = (
        P(None, None, ("groups", "box")),
        P(None, None, ("groups", "box")),
        P(None, None, ("groups", "box")),
        P(),
        P(("groups", "box")),
    )
    out_specs = P(None, None, ("groups", "box"))
    return jax.shard_map(on_device, mesh=mesh, in_specs=in_specs, out_specs=out_specs, check_vma=False)
```

time: 55.1 us -> 51.9 us (0.942)
  local copies, waits for them, and re-layouts: 4.38 us -> 0 us
  waiting for transfers between devices: 10.1 us -> 13.1 us
  starting transfers between devices: 28.1 us -> 25.3 us
  Pallas kernels: 12.1 us -> 13.2 us
    unnamed x10 -> x0, local copies, waits for them, and re-layouts: 4.38 us -> none
    ppermute x15, waiting for transfers between devices: 10.1 us -> 13.1 us  [on_device(): lax.ppermute(blocks[step], 'box', [(s, s ^ step) for s in range(SLOTS)])]
    ppermute x15, starting transfers between devices: 28.1 us -> 25.3 us  [on_device(): lax.ppermute(blocks[step], 'box', [(s, s ^ step) for s in range(SLOTS)])]
    pallas_call x2 -> x4, Pallas kernels: 12.1 us -> 13.2 us  [the longest x1 6.64 us: combine_odd(): pl.pallas_call(odd_kernel, out_shape=jax.ShapeDtypeStruct((WEIGHT_ROWS *...]
  transfers between devices with their start and end apart: 15 -> 15, of which waited for: 3 -> 5; matrix products, arithmetic and copies ran while one was open for 0% -> 0% of each run, Pallas kernels for 0% -> 10%
where the time goes in v3:
time: 51.9 us; the launch traced here: 51.7 us
  starting transfers between devices  25.3 us (49%)
  Pallas kernels  13.2 us (25%)
  waiting for transfers between devices  13.1 us (25%)
    ppermute x15, starting transfers between devices, on_device(): lax.ppermute(blocks[step], 'box', [(s, s ^ step) for s in range(SLOTS)])  25.3 us
    ppermute x15, waiting for transfers between devices, on_device(): lax.ppermute(blocks[step], 'box', [(s, s ^ step) for s in range(SLOTS)])  13.1 us
    pallas_call x1, Pallas kernels, combine_odd(): pl.pallas_call(odd_kernel, out_shape=jax.ShapeDtypeStruct((WEIGHT_ROWS *...  6.64 us
    pallas_call x1, Pallas kernels, combine_even(): pl.pallas_call(even_kernel, out_shape=[jax.ShapeDtypeStruct((WEIGHT_ROWS,...  3.93 us
    pallas_call x2, Pallas kernels, pack(): pl.pallas_call(functools.partial(pack_kernel, far), out_shape=[block] * O...  2.66 us
  transfers between devices with their start and end apart: 15, of which 5 were waited for; matrix products, arithmetic and copies ran while one was open for 0% of the time, Pallas kernels for 10%

profile of v3, /device:TPU:0, one launch (start us, length us, event | category | flops | bytes accessed | tf_op | source)
XLA Modules:
  0.0 51.7 jit_solution(9991304337594306796)
XLA Ops:
  0.0 1.3 %pack_far.1 = (f32[92,2,128]{2,1,0:T(2,128)S(1)}, f32[92,2,128]{2,1,0:T(2,128)S(1)}, f32[92,2,128]{2,1,0:T(2,128)S(1)}, f32[92,2,128]{2,1,0:T(2,128)S(1)}, f32[9...) custom-call(s32[1]{0:T(128)} %bitcast.me_ref, ...), custom_call_target="tpu_custom_call" | custom-call | flops 1048576 | bytes 2097152 | tf_op jit(solution)/shard_map/pack_far/pallas_call | solution.py:122
  1.3 4.1 %collective-permute-start = (f32[184,128]{1,0:T(8,128)S(1)}, f32[184,128]{1,0:T(8,128)S(1)}, u32[]{:S(2)}, u32[]{:S(2)}) collective-permute-start(f32[184,128]{1,0:T(8,128)S(1)} %bitcast.41), channel_id=1, source_target_pairs={{0,8},{1,9},{2,10},{3,11},{4,12},{5,13},{6,14},{7,15},{8,0},{9,1},... | collective-permute-start | bytes 282632 | tf_op jit(solution)/shard_map/ppermute | solution.py:373
  5.4 1.3 %collective-permute-start.1 = (f32[184,128]{1,0:T(8,128)S(1)}, f32[184,128]{1,0:T(8,128)S(1)}, u32[]{:S(2)}, u32[]{:S(2)}) collective-permute-start(f32[184,128]{1,0:T(8,128)S(1)} %bitcast.40), channel_id=1, source_target_pairs={{0,10},{1,11},{2,8},{3,9},{4,14},{5,15},{6,12},{7,13},{8,2},{9,3},... | collective-permute-start | bytes 282632 | tf_op jit(solution)/shard_map/ppermute | solution.py:373
  6.7 3.6 %collective-permute-start.3 = (f32[184,128]{1,0:T(8,128)S(1)}, f32[184,128]{1,0:T(8,128)S(1)}, u32[]{:S(2)}, u32[]{:S(2)}) collective-permute-start(f32[184,128]{1,0:T(8,128)S(1)} %bitcast.39), channel_id=1, source_target_pairs={{0,12},{1,13},{2,14},{3,15},{4,8},{5,9},{6,10},{7,11},{8,4},{9,5},... | collective-permute-start | bytes 282632 | tf_op jit(solution)/shard_map/ppermute | solution.py:373
  10.3 0.0 collective-permute-start.5
  10.3 0.0 collective-permute-start.7
  10.3 1.3 %pack_near.1 = (f32[92,2,128]{2,1,0:T(2,128)S(1)}, f32[92,2,128]{2,1,0:T(2,128)S(1)}, f32[92,2,128]{2,1,0:T(2,128)S(1)}, f32[92,2,128]{2,1,0:T(2,128)S(1)}, f32[...) custom-call(s32[1]{0:T(128)} %bitcast.me_ref, ...), custom_call_target="tpu_custom_call" | custom-call | flops 1048576 | bytes 2097152 | tf_op jit(solution)/shard_map/pack_near/pallas_call | solution.py:122
  11.7 7.3 %collective-permute-done.refs_0_ = f32[184,128]{1,0:T(8,128)S(1)} collective-permute-done((f32[184,128]{1,0:T(8,128)S(1)}, f32[184,128]{1,0:T(8,128)S(1)}, u32[]{:S(2)}, u32[]{:S(2)}) %collective-permute-start) | collective-permute-done | bytes 94240 | tf_op jit(solution)/shard_map/ppermute | solution.py:373
  19.0 0.0 collective-permute-start.8
  19.0 3.2 %collective-permute-done.1.refs_1_ = f32[184,128]{1,0:T(8,128)S(1)} collective-permute-done((f32[184,128]{1,0:T(8,128)S(1)}, f32[184,128]{1,0:T(8,128)S(1)}, u32[]{:S(2)}, u32[]{:S(2)}) %collective-permute-start.1) | collective-permute-done | bytes 94240 | tf_op jit(solution)/shard_map/ppermute | solution.py:373
  22.2 4.2 %collective-permute-start.10 = (f32[184,128]{1,0:T(8,128)S(1)}, f32[184,128]{1,0:T(8,128)S(1)}, u32[]{:S(2)}, u32[]{:S(2)}) collective-permute-start(f32[184,128]{1,0:T(8,128)S(1)} %bitcast.32), channel_id=1, source_target_pairs={{0,13},{1,12},{2,15},{3,14},{4,9},{5,8},{6,11},{7,10},{8,5},{9,4},... | collective-permute-start | bytes 282632 | tf_op jit(solution)/shard_map/ppermute | solution.py:373
  26.4 0.0 collective-permute-done.3.refs_3_
  26.4 0.0 collective-permute-start.4
  26.4 0.0 collective-permute-done.5.refs_5_
  26.4 0.2 collective-permute-start.2
  26.6 1.0 %collective-permute-done.7.refs_0_ = f32[184,128]{1,0:T(8,128)S(1)} collective-permute-done((f32[184,128]{1,0:T(8,128)S(1)}, f32[184,128]{1,0:T(8,128)S(1)}, u32[]{:S(2)}, u32[]{:S(2)}) %collective-permute-start.7) | collective-permute-done | bytes 94240 | tf_op jit(solution)/shard_map/ppermute | solution.py:373
  27.6 4.6 %collective-permute-start.6 = (f32[184,128]{1,0:T(8,128)S(1)}, f32[184,128]{1,0:T(8,128)S(1)}, u32[]{:S(2)}, u32[]{:S(2)}) collective-permute-start(f32[184,128]{1,0:T(8,128)S(1)} %bitcast.33), channel_id=1, source_target_pairs={{0,6},{1,7},{2,4},{3,5},{4,2},{5,3},{6,0},{7,1},{8,14},{9,15},{10,... | collective-permute-start | bytes 282632 | tf_op jit(solution)/shard_map/ppermute | solution.py:373
  32.3 0.4 collective-permute-done.8.refs_1_
  32.6 3.8 %collective-permute-start.12 = (f32[184,128]{1,0:T(8,128)S(1)}, f32[184,128]{1,0:T(8,128)S(1)}, u32[]{:S(2)}, u32[]{:S(2)}) collective-permute-start(f32[184,128]{1,0:T(8,128)S(1)} %bitcast.27), channel_id=1, source_target_pairs={{0,15},{1,14},{2,13},{3,12},{4,11},{5,10},{6,9},{7,8},{8,7},{9,6},... | collective-permute-start | bytes 282632 | tf_op jit(solution)/shard_map/ppermute | solution.py:373
  36.5 0.0 collective-permute-done.10.refs_3_
  36.5 1.6 %collective-permute-start.9 = (f32[184,128]{1,0:T(8,128)S(1)}, f32[184,128]{1,0:T(8,128)S(1)}, u32[]{:S(2)}, u32[]{:S(2)}) collective-permute-start(f32[184,128]{1,0:T(8,128)S(1)} %bitcast.31), channel_id=1, source_target_pairs={{0,3},{1,2},{2,1},{3,0},{4,7},{5,6},{6,5},{7,4},{8,11},{9,10},{10,... | collective-permute-start | bytes 282632 | tf_op jit(solution)/shard_map/ppermute | solution.py:373
  38.1 0.0 collective-permute-done.4.refs_4_
  38.1 0.0 collective-permute-start.11
  38.1 0.0 collective-permute-done.2.refs_2_
  38.1 1.7 %collective-permute-start.13 = (f32[184,128]{1,0:T(8,128)S(1)}, f32[184,128]{1,0:T(8,128)S(1)}, u32[]{:S(2)}, u32[]{:S(2)}) collective-permute-start(f32[184,128]{1,0:T(8,128)S(1)} %bitcast.29), channel_id=1, source_target_pairs={{0,7},{1,6},{2,5},{3,4},{4,3},{5,2},{6,1},{7,0},{8,15},{9,14},{10,... | collective-permute-start | bytes 282632 | tf_op jit(solution)/shard_map/ppermute | solution.py:373
  39.8 0.0 collective-permute-done.6.refs_6_
  39.8 0.1 collective-permute-start.14
  39.8 3.9 %combine_even.1 = (f32[162,8,128]{2,1,0:T(8,128)S(1)}, f32[4,8,128]{2,1,0:T(8,128)S(1)}) custom-call(s32[1]{0:T(128)} %bitcast.me_ref, f32[184,128]{1,0:T(8,128)S(1)} %collective-permute-done.refs_0_, f32[184,128]{1,0:T(8,128)S(1)} %collective-permute-done.1.refs_1_, f32[184,128]{1,0:T(8,128)S(1)} %collective-permute-done.2.refs_2_, ...), custom_call_target="tpu_custom_call" | custom-call | flops 41943040 | bytes 12582912 | tf_op jit(solution)/shard_map/combine_even/pallas_call | solution.py:315
  43.8 0.0 collective-permute-done.9.refs_2_
  43.8 0.0 collective-permute-done.11.refs_4_
  43.8 1.3 %collective-permute-done.13.refs_6_ = f32[184,128]{1,0:T(8,128)S(1)} collective-permute-done((f32[184,128]{1,0:T(8,128)S(1)}, f32[184,128]{1,0:T(8,128)S(1)}, u32[]{:S(2)}, u32[]{:S(2)}) %collective-permute-start.13) | collective-permute-done | bytes 94240 | tf_op jit(solution)/shard_map/ppermute | solution.py:373
  45.1 6.6 %combine_odd.1 = f32[2592,128]{1,0:T(8,128)} custom-call(s32[1]{0:T(128)} %bitcast.me_ref, f32[162,8,128]{2,1,0:T(8,128)S(1)} %get-tuple-element.35.even_work, f32[4,8,128]{2,1,0:T(8,128)S(1)} %get-tuple-element.36.even_phases, f32[184,128]{1,0:T(8,128)S(1)} %collective-permute-done.7.refs_0_, f32[184,128]{1,0:T(8,128)S(1)} %collective-permute-done.8.refs_1_, ...), custom_call_target="tpu_custom_call" | custom-call | flops 83886080 | bytes 20971520 | tf_op jit(solution)/shard_map/combine_odd/pallas_call | solution.py:337
  (2 shorter events, 0.0 us)
Async XLA Ops:
  1.3 17.6 %collective-permute-start = (f32[184,128]{1,0:T(8,128)S(1)}, f32[184,128]{1,0:T(8,128)S(1)}, u32[]{:S(2)}, u32[]{:S(2)}) collective-permute-start(f32[184,128]{1,0:T(8,128)S(1)} %bitcast.41), channel_id=1, source_target_pairs={{0,8},{1,9},{2,10},{3,11},{4,12},{5,13},{6,14},{7,15},{8,0},{9,1},... | collective-permute-start | bytes 282632 | tf_op jit(solution)/shard_map/ppermute | solution.py:373
  5.4 16.7 %collective-permute-start.1 = (f32[184,128]{1,0:T(8,128)S(1)}, f32[184,128]{1,0:T(8,128)S(1)}, u32[]{:S(2)}, u32[]{:S(2)}) collective-permute-start(f32[184,128]{1,0:T(8,128)S(1)} %bitcast.40), channel_id=1, source_target_pairs={{0,10},{1,11},{2,8},{3,9},{4,14},{5,15},{6,12},{7,13},{8,2},{9,3},... | collective-permute-start | bytes 282632 | tf_op jit(solution)/shard_map/ppermute | solution.py:373
  6.7 19.7 %collective-permute-start.3 = (f32[184,128]{1,0:T(8,128)S(1)}, f32[184,128]{1,0:T(8,128)S(1)}, u32[]{:S(2)}, u32[]{:S(2)}) collective-permute-start(f32[184,128]{1,0:T(8,128)S(1)} %bitcast.39), channel_id=1, source_target_pairs={{0,12},{1,13},{2,14},{3,15},{4,8},{5,9},{6,10},{7,11},{8,4},{9,5},... | collective-permute-start | bytes 282632 | tf_op jit(solution)/shard_map/ppermute | solution.py:373
  10.3 16.1 %collective-permute-start.5 = (f32[184,128]{1,0:T(8,128)S(1)}, f32[184,128]{1,0:T(8,128)S(1)}, u32[]{:S(2)}, u32[]{:S(2)}) collective-permute-start(f32[184,128]{1,0:T(8,128)S(1)} %bitcast.38), channel_id=1, source_target_pairs={{0,14},{1,15},{2,12},{3,13},{4,10},{5,11},{6,8},{7,9},{8,6},{9,7},... | collective-permute-start | bytes 282632 | tf_op jit(solution)/shard_map/ppermute | solution.py:373
  10.3 17.3 %collective-permute-start.7 = (f32[184,128]{1,0:T(8,128)S(1)}, f32[184,128]{1,0:T(8,128)S(1)}, u32[]{:S(2)}, u32[]{:S(2)}) collective-permute-start(f32[184,128]{1,0:T(8,128)S(1)} %bitcast.36), channel_id=1, source_target_pairs={{0,9},{1,8},{2,11},{3,10},{4,13},{5,12},{6,15},{7,14},{8,1},{9,0},... | collective-permute-start | bytes 282632 | tf_op jit(solution)/shard_map/ppermute | solution.py:373
  19.0 13.7 %collective-permute-start.8 = (f32[184,128]{1,0:T(8,128)S(1)}, f32[184,128]{1,0:T(8,128)S(1)}, u32[]{:S(2)}, u32[]{:S(2)}) collective-permute-start(f32[184,128]{1,0:T(8,128)S(1)} %bitcast.34), channel_id=1, source_target_pairs={{0,11},{1,10},{2,9},{3,8},{4,15},{5,14},{6,13},{7,12},{8,3},{9,2},... | collective-permute-start | bytes 282632 | tf_op jit(solution)/shard_map/ppermute | solution.py:373
  22.2 14.3 %collective-permute-start.10 = (f32[184,128]{1,0:T(8,128)S(1)}, f32[184,128]{1,0:T(8,128)S(1)}, u32[]{:S(2)}, u32[]{:S(2)}) collective-permute-start(f32[184,128]{1,0:T(8,128)S(1)} %bitcast.32), channel_id=1, source_target_pairs={{0,13},{1,12},{2,15},{3,14},{4,9},{5,8},{6,11},{7,10},{8,5},{9,4},... | collective-permute-start | bytes 282632 | tf_op jit(solution)/shard_map/ppermute | solution.py:373
  26.4 11.7 %collective-permute-start.4 = (f32[184,128]{1,0:T(8,128)S(1)}, f32[184,128]{1,0:T(8,128)S(1)}, u32[]{:S(2)}, u32[]{:S(2)}) collective-permute-start(f32[184,128]{1,0:T(8,128)S(1)} %bitcast.37), channel_id=1, source_target_pairs={{0,4},{1,5},{2,6},{3,7},{4,0},{5,1},{6,2},{7,3},{8,12},{9,13},{10,... | collective-permute-start | bytes 282632 | tf_op jit(solution)/shard_map/ppermute | solution.py:373
  26.4 11.7 %collective-permute-start.2 = (f32[184,128]{1,0:T(8,128)S(1)}, f32[184,128]{1,0:T(8,128)S(1)}, u32[]{:S(2)}, u32[]{:S(2)}) collective-permute-start(f32[184,128]{1,0:T(8,128)S(1)} %bitcast.35), channel_id=1, source_target_pairs={{0,2},{1,3},{2,0},{3,1},{4,6},{5,7},{6,4},{7,5},{8,10},{9,11},{10,... | collective-permute-start | bytes 282632 | tf_op jit(solution)/shard_map/ppermute | solution.py:373
  27.6 12.1 %collective-permute-start.6 = (f32[184,128]{1,0:T(8,128)S(1)}, f32[184,128]{1,0:T(8,128)S(1)}, u32[]{:S(2)}, u32[]{:S(2)}) collective-permute-start(f32[184,128]{1,0:T(8,128)S(1)} %bitcast.33), channel_id=1, source_target_pairs={{0,6},{1,7},{2,4},{3,5},{4,2},{5,3},{6,0},{7,1},{8,14},{9,15},{10,... | collective-permute-start | bytes 282632 | tf_op jit(solution)/shard_map/ppermute | solution.py:373
  32.6 11.1 %collective-permute-start.12 = (f32[184,128]{1,0:T(8,128)S(1)}, f32[184,128]{1,0:T(8,128)S(1)}, u32[]{:S(2)}, u32[]{:S(2)}) collective-permute-start(f32[184,128]{1,0:T(8,128)S(1)} %bitcast.27), channel_id=1, source_target_pairs={{0,15},{1,14},{2,13},{3,12},{4,11},{5,10},{6,9},{7,8},{8,7},{9,6},... | collective-permute-start | bytes 282632 | tf_op jit(solution)/shard_map/ppermute | solution.py:373
  36.5 7.3 %collective-permute-start.9 = (f32[184,128]{1,0:T(8,128)S(1)}, f32[184,128]{1,0:T(8,128)S(1)}, u32[]{:S(2)}, u32[]{:S(2)}) collective-permute-start(f32[184,128]{1,0:T(8,128)S(1)} %bitcast.31), channel_id=1, source_target_pairs={{0,3},{1,2},{2,1},{3,0},{4,7},{5,6},{6,5},{7,4},{8,11},{9,10},{10,... | collective-permute-start | bytes 282632 | tf_op jit(solution)/shard_map/ppermute | solution.py:373
  38.1 5.7 %collective-permute-start.11 = (f32[184,128]{1,0:T(8,128)S(1)}, f32[184,128]{1,0:T(8,128)S(1)}, u32[]{:S(2)}, u32[]{:S(2)}) collective-permute-start(f32[184,128]{1,0:T(8,128)S(1)} %bitcast.30), channel_id=1, source_target_pairs={{0,5},{1,4},{2,7},{3,6},{4,1},{5,0},{6,3},{7,2},{8,13},{9,12},{10,... | collective-permute-start | bytes 282632 | tf_op jit(solution)/shard_map/ppermute | solution.py:373
  38.1 7.0 %collective-permute-start.13 = (f32[184,128]{1,0:T(8,128)S(1)}, f32[184,128]{1,0:T(8,128)S(1)}, u32[]{:S(2)}, u32[]{:S(2)}) collective-permute-start(f32[184,128]{1,0:T(8,128)S(1)} %bitcast.29), channel_id=1, source_target_pairs={{0,7},{1,6},{2,5},{3,4},{4,3},{5,2},{6,1},{7,0},{8,15},{9,14},{10,... | collective-permute-start | bytes 282632 | tf_op jit(solution)/shard_map/ppermute | solution.py:373
  39.8 5.3 %collective-permute-start.14 = (f32[184,128]{1,0:T(8,128)S(1)}, f32[184,128]{1,0:T(8,128)S(1)}, u32[]{:S(2)}, u32[]{:S(2)}) collective-permute-start(f32[184,128]{1,0:T(8,128)S(1)} %bitcast.28), channel_id=1, source_target_pairs={{0,1},{1,0},{2,3},{3,2},{4,5},{5,4},{6,7},{7,6},{8,9},{9,8},{10,11... | collective-permute-start | bytes 282632 | tf_op jit(solution)/shard_map/ppermute | solution.py:373

commit v4 on v3

--- a/solution.py
+++ b/solution.py
@@ -21,8 +21,9 @@
 USED_ROWS = WEIGHT_ROWS + PHASE_ROWS
 ROWS = (USED_ROWS + 7) // 8 * 8
 OCT = SLOTS // 2
-EVEN_ORDER = (8, 10, 2, 12, 4, 14, 6, 0)
-ODD_ORDER = (9, 11, 3, 13, 5, 15, 7, 1)
+FAR = ((8, 9), (10, 11), (12,), (14,), (13,), (15,))
+NEAR = ((2, 3), (4, 5), (6, 7), (1,), (0,))
+SENDS = ((8, None), (10, None), (2, None), (4, None), (6, None), (12, 2), (14, 4), (13, 12), (15, 14))
 
 NODES = np.cos(math.pi * (2.0 * np.arange(CHEB) + 1.0) / (2.0 * CHEB))
 NODES[CHEB // 2] = 0.0
@@ -78,9 +79,12 @@
     return constant, half * (k1 + 2.0 * bent * x1), half * half * bent, half * k2
 
 
-def pack_kernel(far, me_ref, coef_hbm, weights_hbm, wave_hbm, center_hbm, kind_hbm, *refs):
-    outs = refs[:OCT]
-    coef_ref, wave_ref, center_ref, kind_ref, phases_ref, sems, block_sems = refs[OCT:]
+def pack_kernel(far, messages, me_ref, coef_hbm, weights_hbm, wave_hbm, center_hbm, kind_hbm, *refs):
+    coef_ref, wave_ref, center_ref, kind_ref, phases_ref, sems, block_sems = refs[len(messages) :]
+    outs = [None] * OCT
+    for message, ref in zip(messages, refs):
+        for index, step in enumerate(message):
+            outs[step % OCT] = ref.at[pl.ds(index * (ROWS // 2), ROWS // 2)]
     me = me_ref[0]
     first = ((me // OCT) ^ far) * OCT
     columns = pl.ds(pl.multiple_of(first * LANES, OCT * LANES), OCT * LANES)
@@ -116,14 +120,14 @@
 
 
 def pack(far, me, phase_coef, weights, wave, center, kind):
-    block = jax.ShapeDtypeStruct((ROWS // 2, 2, LANES), jnp.float32)
+    messages = FAR if far else NEAR
     vmem = pl.BlockSpec(memory_space=pltpu.VMEM)
     hbm = pl.BlockSpec(memory_space=pltpu.HBM)
-    blocks = pl.pallas_call(
-        functools.partial(pack_kernel, far),
-        out_shape=[block] * OCT,
+    arrays = pl.pallas_call(
+        functools.partial(pack_kernel, far, messages),
+        out_shape=[jax.ShapeDtypeStruct((len(m) * ROWS // 2, 2, LANES), jnp.float32) for m in messages],
         in_specs=[pl.BlockSpec(memory_space=pltpu.SMEM)] + [hbm] * 5,
-        out_specs=[vmem] * OCT,
+        out_specs=[vmem] * len(messages),
         scratch_shapes=[
             pltpu.SMEM(phase_coef.shape, jnp.float32),
             pltpu.VMEM((LEVELS, 2, OCT * LANES), jnp.float32),
@@ -137,7 +141,7 @@
         cost_estimate=pl.CostEstimate(flops=2**20, bytes_accessed=2 * 2**20, transcendentals=0),
         name="pack_far" if far else "pack_near",
     )(me, phase_coef, weights, wave, center, kind)
-    return [block.reshape(ROWS, LANES) for block in blocks]
+    return {m[0]: array.reshape(-1, LANES) for m, array in zip(messages, arrays)}
 
 
 def level_factors(level, phases, parent_ref, child_ref, common_ref):
@@ -198,11 +202,12 @@
     return part + 2 * (split * CHEB + column if level % 2 == 0 else column * CHEB + split)
 
 
-def join_chips(me, blocks, order, held, sems, work, last_phases, factors):
+def join_chips(me, arrays, pieces, held, sems, work, last_phases, factors):
     copies = []
-    for index, step in enumerate(order):
+    for step, index, block in pieces:
         spot = pl.ds(pl.multiple_of(((me ^ step) // 2) * ROWS, 8), ROWS)
-        copies.append(pltpu.make_async_copy(blocks[index], held.at[spot, :], sems.at[index]))
+        source = arrays[index].at[pl.ds(block * ROWS, ROWS), :]
+        copies.append(pltpu.make_async_copy(source, held.at[spot, :], sems.at[step // 2]))
         copies[-1].start()
     for copy in copies:
         copy.wait()
@@ -241,16 +246,14 @@
         lax.fori_loop(0, CHEB, column_step, 0)
 
 
-def even_kernel(me_ref, *refs):
-    blocks = refs[:OCT]
-    work, last_phases, held, parent_ref, child_ref, common_ref, sems = refs[OCT:]
+def even_kernel(pieces, count, me_ref, *refs):
+    work, last_phases, held, parent_ref, child_ref, common_ref, sems = refs[count:]
     factors = (parent_ref, child_ref, common_ref)
-    join_chips(me_ref[0], blocks, EVEN_ORDER, held, sems, work, last_phases, factors)
-
-
-def odd_kernel(me_ref, even_work, even_phases, *refs):
-    blocks = refs[:OCT]
-    out_hbm, work, last_phases, held, out_ref, parent_ref, child_ref, common_ref, sems, out_sems = refs[OCT:]
+    join_chips(me_ref[0], refs, pieces, held, sems, work, last_phases, factors)
+
+
+def odd_kernel(pieces, count, me_ref, even_work, even_phases, *refs):
+    out_hbm, work, last_phases, held, out_ref, parent_ref, child_ref, common_ref, sems, out_sems = refs[count:]
     me = me_ref[0]
     own = me % 2
     early = [
@@ -260,7 +263,7 @@
     for copy in early:
         copy.start()
     factors = [ref.at[0] for ref in (parent_ref, child_ref, common_ref)]
-    join_chips(me, blocks, ODD_ORDER, held, sems, work.at[1 - own], last_phases.at[1 - own], factors)
+    join_chips(me, refs, pieces, held, sems, work.at[1 - own], last_phases.at[1 - own], factors)
     for copy in early:
         copy.wait()
 
@@ -310,15 +313,15 @@
     ]
 
 
-def combine_even(me, blocks):
+def combine_even(me, arrays, pieces):
     vmem = pl.BlockSpec(memory_space=pltpu.VMEM)
     return pl.pallas_call(
-        even_kernel,
+        functools.partial(even_kernel, pieces, len(arrays)),
         out_shape=[
             jax.ShapeDtypeStruct((WEIGHT_ROWS, OCT, LANES), jnp.float32),
             jax.ShapeDtypeStruct((4, OCT, LANES), jnp.float32),
         ],
-        in_specs=[pl.BlockSpec(memory_space=pltpu.SMEM)] + [pl.BlockSpec(memory_space=pl.ANY)] * OCT,
+        in_specs=[pl.BlockSpec(memory_space=pltpu.SMEM)] + [pl.BlockSpec(memory_space=pl.ANY)] * len(arrays),
         out_specs=[vmem, vmem],
         scratch_shapes=[
             pltpu.VMEM((OCT * ROWS, LANES), jnp.float32),
@@ -328,16 +331,16 @@
         compiler_params=pltpu.CompilerParams(vmem_limit_bytes=16 * 2**20),
         cost_estimate=pl.CostEstimate(flops=40 * 2**20, bytes_accessed=12 * 2**20, transcendentals=0),
         name="combine_even",
-    )(me, *blocks)
-
-
-def combine_odd(me, even, blocks):
+    )(me, *arrays)
+
+
+def combine_odd(me, even, arrays, pieces):
     hbm = pl.BlockSpec(memory_space=pltpu.HBM)
     anywhere = pl.BlockSpec(memory_space=pl.ANY)
     return pl.pallas_call(
-        odd_kernel,
+        functools.partial(odd_kernel, pieces, len(arrays)),
         out_shape=jax.ShapeDtypeStruct((WEIGHT_ROWS * SLOTS, LANES), jnp.float32),
-        in_specs=[pl.BlockSpec(memory_space=pltpu.SMEM)] + [anywhere] * (2 + OCT),
+        in_specs=[pl.BlockSpec(memory_space=pltpu.SMEM)] + [anywhere] * (2 + len(arrays)),
         out_specs=hbm,
         scratch_shapes=[
             pltpu.VMEM((2, WEIGHT_ROWS, OCT, LANES), jnp.float32),
@@ -351,7 +354,7 @@
         compiler_params=pltpu.CompilerParams(vmem_limit_bytes=16 * 2**20),
         cost_estimate=pl.CostEstimate(flops=80 * 2**20, bytes_accessed=20 * 2**20, transcendentals=0),
         name="combine_odd",
-    )(me, *even, *blocks)
+    )(me, *even, *arrays)
 
 
 def on_device(source_weights, wave_vectors, source_centers, phase_coef, phase_kind):
@@ -363,20 +366,36 @@
     weights = source_weights.reshape(2, POINTS, SLOTS, LANES).transpose(1, 2, 0, 3)
     operands = [phase_coef, weights, wave_vectors, source_centers, phase_kind[None, :]]
     operands = [me] + [pltpu.with_memory_space_constraint(operand, pltpu.HBM) for operand in operands]
-    far_blocks = pack(1, *operands)
-    operands[0], far_blocks[0] = lax.optimization_barrier((me, far_blocks[0]))
-    near_blocks = pack(0, *operands)
-    blocks = near_blocks + far_blocks
+    sent = pack(1, *operands)
+    sent.update(pack(0, *operands))
     if direct:
-        for step in EVEN_ORDER + ODD_ORDER:
-            if step:
-                blocks[step] = lax.ppermute(blocks[step], "box", [(s, s ^ step) for s in range(SLOTS)])
+
+        def exchange(array, step):
+            return lax.ppermute(array, "box", [(s, s ^ step) for s in range(SLOTS)])
+
+        for step, earlier in SENDS:
+            if earlier is not None:
+                sent[step], sent[earlier] = lax.optimization_barrier((sent[step], sent[earlier]))
+            sent[step] = exchange(sent[step], step)
+        far_swap = exchange(jnp.concatenate([sent[8][ROWS:], sent[10][ROWS:]]), 1)
+        near_swap = exchange(jnp.concatenate([sent[1], sent[2][ROWS:], sent[4][ROWS:], sent[6][ROWS:]]), 1)
+        even_arrays = [sent[step] for step in range(0, SLOTS, 2)]
+        even_pieces = [(step, step // 2, 0) for step in range(0, SLOTS, 2)]
+        odd_arrays = [near_swap, far_swap, sent[13], sent[15]]
+        odd_pieces = [(1, 0, 0), (3, 0, 1), (5, 0, 2), (7, 0, 3), (9, 1, 0), (11, 1, 1), (13, 2, 0), (15, 3, 0)]
     else:
+        blocks = [None] * SLOTS
+        for message in FAR + NEAR:
+            for index, step in enumerate(message):
+                blocks[step] = sent[message[0]][index * ROWS : (index + 1) * ROWS]
         whole = jnp.concatenate(blocks, axis=1)
         whole = lax.all_to_all(whole, "box", split_axis=1, concat_axis=1, tiled=True)
         blocks = [whole[:, s * LANES : (s + 1) * LANES] for s in range(SLOTS)]
-    even = combine_even(me, [blocks[step] for step in EVEN_ORDER])
-    rows = combine_odd(me, even, [blocks[step] for step in ODD_ORDER])
+        even_arrays, odd_arrays = blocks[0::2], blocks[1::2]
+        even_pieces = [(2 * index, index, 0) for index in range(OCT)]
+        odd_pieces = [(2 * index + 1, index, 0) for index in range(OCT)]
+    even = combine_even(me, even_arrays, even_pieces)
+    rows = combine_odd(me, even, odd_arrays, odd_pieces)
     return rows.reshape(POINTS, SLOTS, 2, LANES).transpose(2, 0, 1, 3).reshape(2, POINTS, SLOTS * LANES)
 
 

time: 51.9 us -> 51.5 us (level)
  starting transfers between devices: 25.3 us -> 19 us
  waiting for transfers between devices: 13.1 us -> 18.8 us
    ppermute x15 -> x11, starting transfers between devices: 25.3 us -> 19 us  [exchange(): return lax.ppermute(array, 'box', [(s, s ^ step) for s in range(SLOTS)])]
    ppermute x15 -> x11, waiting for transfers between devices: 13.1 us -> 18.8 us  [exchange(): return lax.ppermute(array, 'box', [(s, s ^ step) for s in range(SLOTS)])]
  transfers between devices with their start and end apart: 15 -> 11, of which waited for: 5 -> 4; matrix products, arithmetic and copies ran while one was open for 0% -> 0% of each run, Pallas kernels for 10% -> 10%
where the time goes in v4:
time: 51.5 us; the launch traced here: 51.3 us
  starting transfers between devices  19 us (37%)
  waiting for transfers between devices  18.8 us (37%)
  Pallas kernels  13.2 us (26%)
    ppermute x11, starting transfers between devices, exchange(): return lax.ppermute(array, 'box', [(s, s ^ step) for s in range(SLOTS)])  19 us
    ppermute x11, waiting for transfers between devices, exchange(): return lax.ppermute(array, 'box', [(s, s ^ step) for s in range(SLOTS)])  18.8 us
    pallas_call x1, Pallas kernels, combine_odd(): pl.pallas_call(functools.partial(odd_kernel, pieces, len(arrays)), out_sh...  6.65 us
    pallas_call x1, Pallas kernels, combine_even(): pl.pallas_call(functools.partial(even_kernel, pieces, len(arrays)), out_s...  3.93 us
    pallas_call x2, Pallas kernels, pack(): pl.pallas_call(functools.partial(pack_kernel, far, messages), out_shape=[...  2.66 us
  transfers between devices with their start and end apart: 11, of which 4 were waited for; matrix products, arithmetic and copies ran while one was open for 0% of the time, Pallas kernels for 10%

profile of v4, /device:TPU:0, one launch (start us, length us, event | category | flops | bytes accessed | tf_op | source)
XLA Modules:
  0.0 51.3 jit_solution(6744752431763021894)
XLA Ops:
  0.0 1.3 %pack_near.1 = (f32[184,2,128]{2,1,0:T(2,128)S(1)}, f32[184,2,128]{2,1,0:T(2,128)S(1)}, f32[184,2,128]{2,1,0:T(2,128)S(1)}, f32[92,2,128]{2,1,0:T(2,128)S(1)}, f32[92,2,128]{2,1,0:T(2,128)S(1)}) custom-call(s32[1]{0:T(128)} %bitcast.me_ref, f32[4,3]{1,0:T(4,128)} %coef_hbm.3, f32[81,16,2,128]{3,2,1,0:T(2,128)} %bitcast.32, f32[4,2,2048]{2,1,0:T(2,128)} %wave_hbm.3, ...), custom_call_target="tpu_custom_call" | custom-call | flops 1048576 | bytes 2097152 | tf_op jit(solution)/shard_map/pack_near/pallas_call | solution.py:126
  1.3 3.0 %collective-permute-start = (f32[368,128]{1,0:T(8,128)S(1)}, f32[368,128]{1,0:T(8,128)S(1)}, u32[]{:S(2)}, u32[]{:S(2)}) collective-permute-start(f32[368,128]{1,0:T(8,128)S(1)} %bitcast.27), channel_id=1, source_target_pairs={{0,2},{1,3},{2,0},{3,1},{4,6},{5,7},{6,4},{7,5},{8,10},{9,11},{10,... | collective-permute-start | bytes 565256 | tf_op jit(solution)/shard_map/ppermute | solution.py:374
  4.4 1.6 %collective-permute-start.1 = (f32[368,128]{1,0:T(8,128)S(1)}, f32[368,128]{1,0:T(8,128)S(1)}, u32[]{:S(2)}, u32[]{:S(2)}) collective-permute-start(f32[368,128]{1,0:T(8,128)S(1)} %bitcast.26), channel_id=1, source_target_pairs={{0,4},{1,5},{2,6},{3,7},{4,0},{5,1},{6,2},{7,3},{8,12},{9,13},{10,... | collective-permute-start | bytes 565256 | tf_op jit(solution)/shard_map/ppermute | solution.py:374
  5.9 0.0 collective-permute-start.2
  6.0 1.3 %pack_far.1 = (f32[184,2,128]{2,1,0:T(2,128)S(1)}, f32[184,2,128]{2,1,0:T(2,128)S(1)}, f32[92,2,128]{2,1,0:T(2,128)S(1)}, f32[92,2,128]{2,1,0:T(2,128)S(1)}, f32...) custom-call(s32[1]{0:T(128)} %bitcast.me_ref, f32[4,3]{1,0:T(4,128)} %coef_hbm.3, f32[81,16,2,128]{3,2,1,0:T(2,128)} %bitcast.33, ...), custom_call_target="tpu_custom_call" | custom-call | flops 1048576 | bytes 2097152 | tf_op jit(solution)/shard_map/pack_far/pallas_call | solution.py:126
  7.3 3.0 %collective-permute-start.3 = (f32[368,128]{1,0:T(8,128)S(1)}, f32[368,128]{1,0:T(8,128)S(1)}, u32[]{:S(2)}, u32[]{:S(2)}) collective-permute-start(f32[368,128]{1,0:T(8,128)S(1)} %bitcast.24), channel_id=1, source_target_pairs={{0,8},{1,9},{2,10},{3,11},{4,12},{5,13},{6,14},{7,15},{8,0},{9,1},... | collective-permute-start | bytes 565256 | tf_op jit(solution)/shard_map/ppermute | solution.py:374
  10.3 1.3 %collective-permute-start.4 = (f32[368,128]{1,0:T(8,128)S(1)}, f32[368,128]{1,0:T(8,128)S(1)}, u32[]{:S(2)}, u32[]{:S(2)}) collective-permute-start(f32[368,128]{1,0:T(8,128)S(1)} %bitcast.23), channel_id=1, source_target_pairs={{0,10},{1,11},{2,8},{3,9},{4,14},{5,15},{6,12},{7,13},{8,2},{9,3},... | collective-permute-start | bytes 565256 | tf_op jit(solution)/shard_map/ppermute | solution.py:374
  11.6 0.0 collective-permute-done.refs_1_
  11.6 6.9 %collective-permute-done.1.refs_2_ = f32[368,128]{1,0:T(8,128)S(1)} collective-permute-done((f32[368,128]{1,0:T(8,128)S(1)}, f32[368,128]{1,0:T(8,128)S(1)}, u32[]{:S(2)}, u32[]{:S(2)}) %collective-permute-start.1) | collective-permute-done | bytes 188448 | tf_op jit(solution)/shard_map/ppermute | solution.py:374
  18.5 1.3 %collective-permute-done.2.refs_3_ = f32[368,128]{1,0:T(8,128)S(1)} collective-permute-done((f32[368,128]{1,0:T(8,128)S(1)}, f32[368,128]{1,0:T(8,128)S(1)}, u32[]{:S(2)}, u32[]{:S(2)}) %collective-permute-start.2) | collective-permute-done | bytes 188448 | tf_op jit(solution)/shard_map/ppermute | solution.py:374
  19.9 0.1 collective-permute-start.7
  19.9 1.6 %collective-permute-start.5 = (f32[184,128]{1,0:T(8,128)S(1)}, f32[184,128]{1,0:T(8,128)S(1)}, u32[]{:S(2)}, u32[]{:S(2)}) collective-permute-start(f32[184,128]{1,0:T(8,128)S(1)} %bitcast.31), channel_id=1, source_target_pairs={{0,12},{1,13},{2,14},{3,15},{4,8},{5,9},{6,10},{7,11},{8,4},{9,5},... | collective-permute-start | bytes 282632 | tf_op jit(solution)/shard_map/ppermute | solution.py:374
  21.5 4.5 %collective-permute-start.6 = (f32[184,128]{1,0:T(8,128)S(1)}, f32[184,128]{1,0:T(8,128)S(1)}, u32[]{:S(2)}, u32[]{:S(2)}) collective-permute-start(f32[184,128]{1,0:T(8,128)S(1)} %bitcast.30), channel_id=1, source_target_pairs={{0,14},{1,15},{2,12},{3,13},{4,10},{5,11},{6,8},{7,9},{8,6},{9,7},... | collective-permute-start | bytes 282632 | tf_op jit(solution)/shard_map/ppermute | solution.py:374
  26.0 0.0 collective-permute-done.3.refs_4_
  26.0 7.2 %collective-permute-done.4.refs_5_ = f32[368,128]{1,0:T(8,128)S(1)} collective-permute-done((f32[368,128]{1,0:T(8,128)S(1)}, f32[368,128]{1,0:T(8,128)S(1)}, u32[]{:S(2)}, u32[]{:S(2)}) %collective-permute-start.4) | collective-permute-done | bytes 188448 | tf_op jit(solution)/shard_map/ppermute | solution.py:374
  33.3 0.1 collective-permute-start.8
  33.4 0.0 collective-permute-done.5.refs_6_
  33.4 3.7 %collective-permute-start.9 = (f32[184,128]{1,0:T(8,128)S(1)}, f32[184,128]{1,0:T(8,128)S(1)}, u32[]{:S(2)}, u32[]{:S(2)}) collective-permute-start(f32[184,128]{1,0:T(8,128)S(1)} %bitcast.29), channel_id=1, source_target_pairs={{0,13},{1,12},{2,15},{3,14},{4,9},{5,8},{6,11},{7,10},{8,5},{9,4},... | collective-permute-start | bytes 282632 | tf_op jit(solution)/shard_map/ppermute | solution.py:374
  37.1 0.0 collective-permute-done.6.refs_7_
  37.1 0.2 collective-permute-start.10
  37.3 3.9 %combine_even.1 = (f32[162,8,128]{2,1,0:T(8,128)S(1)}, f32[4,8,128]{2,1,0:T(8,128)S(1)}) custom-call(s32[1]{0:T(128)} %bitcast.me_ref, f32[184,128]{1,0:T(8,128)S(1)} %bitcast.21, f32[368,128]{1,0:T(8,128)S(1)} %collective-permute-done.refs_1_, f32[368,128]{1,0:T(8,128)S(1)} %collective-permute-done.1.refs_2_, ...), custom_call_target="tpu_custom_call" | custom-call | flops 41943040 | bytes 12582912 | tf_op jit(solution)/shard_map/combine_even/pallas_call | solution.py:318
  41.2 0.0 collective-permute-done.8.refs_1_
  41.2 0.0 collective-permute-done.9.refs_2_
  41.2 3.4 %collective-permute-done.10.refs_3_ = f32[184,128]{1,0:T(8,128)S(1)} collective-permute-done((f32[184,128]{1,0:T(8,128)S(1)}, f32[184,128]{1,0:T(8,128)S(1)}, u32[]{:S(2)}, u32[]{:S(2)}) %collective-permute-start.10) | collective-permute-done | bytes 94240 | tf_op jit(solution)/shard_map/ppermute | solution.py:374
  44.6 0.0 collective-permute-done.7.refs_0_
  44.7 6.6 %combine_odd.1 = f32[2592,128]{1,0:T(8,128)} custom-call(s32[1]{0:T(128)} %bitcast.me_ref, f32[162,8,128]{2,1,0:T(8,128)S(1)} %get-tuple-element.42.even_work, f32[4,8,128]{2,1,0:T(8,128)S(1)} %get-tuple-element.43.even_phases, f32[736,128]{1,0:T(8,128)S(1)} %collective-permute-done.7.refs_0_, f32[368,128]{1,0:T(8,128)S(1)} %collective-permute-done.8.refs_1_, ...), custom_call_target="tpu_custom_call" | custom-call | flops 83886080 | bytes 20971520 | tf_op jit(solution)/shard_map/combine_odd/pallas_call | solution.py:340
  (7 shorter events, 0.1 us)
Async XLA Ops:
  1.3 10.3 %collective-permute-start = (f32[368,128]{1,0:T(8,128)S(1)}, f32[368,128]{1,0:T(8,128)S(1)}, u32[]{:S(2)}, u32[]{:S(2)}) collective-permute-start(f32[368,128]{1,0:T(8,128)S(1)} %bitcast.27), channel_id=1, source_target_pairs={{0,2},{1,3},{2,0},{3,1},{4,6},{5,7},{6,4},{7,5},{8,10},{9,11},{10,... | collective-permute-start | bytes 565256 | tf_op jit(solution)/shard_map/ppermute | solution.py:374
  4.4 14.1 %collective-permute-start.1 = (f32[368,128]{1,0:T(8,128)S(1)}, f32[368,128]{1,0:T(8,128)S(1)}, u32[]{:S(2)}, u32[]{:S(2)}) collective-permute-start(f32[368,128]{1,0:T(8,128)S(1)} %bitcast.26), channel_id=1, source_target_pairs={{0,4},{1,5},{2,6},{3,7},{4,0},{5,1},{6,2},{7,3},{8,12},{9,13},{10,... | collective-permute-start | bytes 565256 | tf_op jit(solution)/shard_map/ppermute | solution.py:374
  5.9 13.9 %collective-permute-start.2 = (f32[368,128]{1,0:T(8,128)S(1)}, f32[368,128]{1,0:T(8,128)S(1)}, u32[]{:S(2)}, u32[]{:S(2)}) collective-permute-start(f32[368,128]{1,0:T(8,128)S(1)} %bitcast.25), channel_id=1, source_target_pairs={{0,6},{1,7},{2,4},{3,5},{4,2},{5,3},{6,0},{7,1},{8,14},{9,15},{10,... | collective-permute-start | bytes 565256 | tf_op jit(solution)/shard_map/ppermute | solution.py:374
  7.3 18.7 %collective-permute-start.3 = (f32[368,128]{1,0:T(8,128)S(1)}, f32[368,128]{1,0:T(8,128)S(1)}, u32[]{:S(2)}, u32[]{:S(2)}) collective-permute-start(f32[368,128]{1,0:T(8,128)S(1)} %bitcast.24), channel_id=1, source_target_pairs={{0,8},{1,9},{2,10},{3,11},{4,12},{5,13},{6,14},{7,15},{8,0},{9,1},... | collective-permute-start | bytes 565256 | tf_op jit(solution)/shard_map/ppermute | solution.py:374
  10.3 22.9 %collective-permute-start.4 = (f32[368,128]{1,0:T(8,128)S(1)}, f32[368,128]{1,0:T(8,128)S(1)}, u32[]{:S(2)}, u32[]{:S(2)}) collective-permute-start(f32[368,128]{1,0:T(8,128)S(1)} %bitcast.23), channel_id=1, source_target_pairs={{0,10},{1,11},{2,8},{3,9},{4,14},{5,15},{6,12},{7,13},{8,2},{9,3},... | collective-permute-start | bytes 565256 | tf_op jit(solution)/shard_map/ppermute | solution.py:374
  19.9 24.8 %collective-permute-start.7 = (f32[736,128]{1,0:T(8,128)S(1)}, f32[736,128]{1,0:T(8,128)S(1)}, u32[]{:S(2)}, u32[]{:S(2)}) collective-permute-start(f32[736,128]{1,0:T(8,128)S(1)} %pad_maximum_fusion), channel_id=1, source_target_pairs={{0,1},{1,0},{2,3},{3,2},{4,5},{5,4},{6,7},{7,6},{8,9},{9,8},{10,11... | collective-permute-start | bytes 1130504 | tf_op jit(solution)/shard_map/ppermute | solution.py:374
  19.9 13.4 %collective-permute-start.5 = (f32[184,128]{1,0:T(8,128)S(1)}, f32[184,128]{1,0:T(8,128)S(1)}, u32[]{:S(2)}, u32[]{:S(2)}) collective-permute-start(f32[184,128]{1,0:T(8,128)S(1)} %bitcast.31), channel_id=1, source_target_pairs={{0,12},{1,13},{2,14},{3,15},{4,8},{5,9},{6,10},{7,11},{8,4},{9,5},... | collective-permute-start | bytes 282632 | tf_op jit(solution)/shard_map/ppermute | solution.py:374
  21.5 15.6 %collective-permute-start.6 = (f32[184,128]{1,0:T(8,128)S(1)}, f32[184,128]{1,0:T(8,128)S(1)}, u32[]{:S(2)}, u32[]{:S(2)}) collective-permute-start(f32[184,128]{1,0:T(8,128)S(1)} %bitcast.30), channel_id=1, source_target_pairs={{0,14},{1,15},{2,12},{3,13},{4,10},{5,11},{6,8},{7,9},{8,6},{9,7},... | collective-permute-start | bytes 282632 | tf_op jit(solution)/shard_map/ppermute | solution.py:374
  33.3 7.9 %collective-permute-start.8 = (f32[368,128]{1,0:T(8,128)S(1)}, f32[368,128]{1,0:T(8,128)S(1)}, u32[]{:S(2)}, u32[]{:S(2)}) collective-permute-start(f32[368,128]{1,0:T(8,128)S(1)} %pad_maximum_fusion.1), channel_id=1, source_target_pairs={{0,1},{1,0},{2,3},{3,2},{4,5},{5,4},{6,7},{7,6},{8,9},{9,8},{10,11... | collective-permute-start | bytes 565256 | tf_op jit(solution)/shard_map/ppermute | solution.py:374
  33.4 7.8 %collective-permute-start.9 = (f32[184,128]{1,0:T(8,128)S(1)}, f32[184,128]{1,0:T(8,128)S(1)}, u32[]{:S(2)}, u32[]{:S(2)}) collective-permute-start(f32[184,128]{1,0:T(8,128)S(1)} %bitcast.29), channel_id=1, source_target_pairs={{0,13},{1,12},{2,15},{3,14},{4,9},{5,8},{6,11},{7,10},{8,5},{9,4},... | collective-permute-start | bytes 282632 | tf_op jit(solution)/shard_map/ppermute | solution.py:374
  37.1 7.6 %collective-permute-start.10 = (f32[184,128]{1,0:T(8,128)S(1)}, f32[184,128]{1,0:T(8,128)S(1)}, u32[]{:S(2)}, u32[]{:S(2)}) collective-permute-start(f32[184,128]{1,0:T(8,128)S(1)} %bitcast.28), channel_id=1, source_target_pairs={{0,15},{1,14},{2,13},{3,12},{4,11},{5,10},{6,9},{7,8},{8,7},{9,6},... | collective-permute-start | bytes 282632 | tf_op jit(solution)/shard_map/ppermute | solution.py:374

commit v5 on v4

--- a/solution.py
+++ b/solution.py
@@ -21,9 +21,9 @@
 USED_ROWS = WEIGHT_ROWS + PHASE_ROWS
 ROWS = (USED_ROWS + 7) // 8 * 8
 OCT = SLOTS // 2
-FAR = ((8, 9), (10, 11), (12,), (14,), (13,), (15,))
-NEAR = ((2, 3), (4, 5), (6, 7), (1,), (0,))
-SENDS = ((8, None), (10, None), (2, None), (4, None), (6, None), (12, 2), (14, 4), (13, 12), (15, 14))
+PACKS = ((8, 10, 12), (2, 4, 6), (14, 9, 11, 13, 15), (3, 5, 7, 1, 0))
+EVEN_ORDER = (8, 10, 12, 2, 4, 6, 14, 0)
+ODD_ORDER = (9, 11, 13, 15, 3, 5, 7, 1)
 
 NODES = np.cos(math.pi * (2.0 * np.arange(CHEB) + 1.0) / (2.0 * CHEB))
 NODES[CHEB // 2] = 0.0
@@ -79,30 +79,16 @@
     return constant, half * (k1 + 2.0 * bent * x1), half * half * bent, half * k2
 
 
-def pack_kernel(far, messages, me_ref, coef_hbm, weights_hbm, wave_hbm, center_hbm, kind_hbm, *refs):
-    coef_ref, wave_ref, center_ref, kind_ref, phases_ref, sems, block_sems = refs[len(messages) :]
-    outs = [None] * OCT
-    for message, ref in zip(messages, refs):
-        for index, step in enumerate(message):
-            outs[step % OCT] = ref.at[pl.ds(index * (ROWS // 2), ROWS // 2)]
-    me = me_ref[0]
-    first = ((me // OCT) ^ far) * OCT
-    columns = pl.ds(pl.multiple_of(first * LANES, OCT * LANES), OCT * LANES)
-    small = [
-        pltpu.make_async_copy(coef_hbm, coef_ref, sems.at[0]),
-        pltpu.make_async_copy(wave_hbm.at[:, :, columns], wave_ref, sems.at[1]),
-        pltpu.make_async_copy(center_hbm.at[:, :, columns], center_ref, sems.at[2]),
-        pltpu.make_async_copy(kind_hbm.at[:, columns], kind_ref, sems.at[3]),
+def phase_kernel(coef_hbm, wave_hbm, center_hbm, kind_hbm, phases_ref, coef_ref, wave_ref, center_ref, kind_ref, sems):
+    copies = [
+        pltpu.make_async_copy(source, target, sems.at[index])
+        for index, (source, target) in enumerate(
+            ((coef_hbm, coef_ref), (wave_hbm, wave_ref), (center_hbm, center_ref), (kind_hbm, kind_ref))
+        )
     ]
-    large = [
-        pltpu.make_async_copy(
-            weights_hbm.at[:, first + ((me % OCT) ^ step)], outs[step].at[pl.ds(0, POINTS)], block_sems.at[step]
-        )
-        for step in range(OCT)
-    ]
-    for copy in small + large:
+    for copy in copies:
         copy.start()
-    for copy in small:
+    for copy in copies:
         copy.wait()
     rows = phase_rows(
         (wave_ref[:, 0, :], wave_ref[:, 1, :]), (center_ref[:, 0, :], center_ref[:, 1, :]), kind_ref[...], coef_ref
@@ -111,37 +97,59 @@
         for level in range(LEVELS):
             row = index * LEVELS + level
             phases_ref[row // 2, row % 2, :] = values[level]
-    for step, out in enumerate(outs):
-        mine = pl.ds(pl.multiple_of(((me % OCT) ^ step) * LANES, LANES), LANES)
-        out[POINTS : USED_ROWS // 2] = phases_ref[:, :, mine]
+
+
+def pack_kernel(steps, first, me_ref, weights_hbm, *refs):
+    if first:
+        small, refs = refs[:4], refs[4:]
+        outs, refs = refs[: len(steps)], refs[len(steps) :]
+        phases_ref, block_sems, scratch = refs[0], refs[1], refs[2:]
+    else:
+        phases_ref, outs, block_sems = refs[0], refs[1 : 1 + len(steps)], refs[1 + len(steps)]
+    slots = [me_ref[0] ^ step for step in steps]
+    copies = [
+        pltpu.make_async_copy(weights_hbm.at[:, slot], out.at[pl.ds(0, POINTS)], block_sems.at[index])
+        for index, (slot, out) in enumerate(zip(slots, outs))
+    ]
+    for copy in copies:
+        copy.start()
+    if first:
+        phase_kernel(*small, phases_ref, *scratch)
+    for slot, out in zip(slots, outs):
+        out[POINTS : USED_ROWS // 2] = phases_ref[:, :, pl.ds(pl.multiple_of(slot * LANES, LANES), LANES)]
         out[USED_ROWS // 2 :] = jnp.zeros(((ROWS - USED_ROWS) // 2, 2, LANES), jnp.float32)
-    for copy in large:
+    for copy in copies:
         copy.wait()
 
 
-def pack(far, me, phase_coef, weights, wave, center, kind):
-    messages = FAR if far else NEAR
+def pack(steps, me, weights, phases, sources):
+    first = phases is None
     vmem = pl.BlockSpec(memory_space=pltpu.VMEM)
     hbm = pl.BlockSpec(memory_space=pltpu.HBM)
-    arrays = pl.pallas_call(
-        functools.partial(pack_kernel, far, messages),
-        out_shape=[jax.ShapeDtypeStruct((len(m) * ROWS // 2, 2, LANES), jnp.float32) for m in messages],
-        in_specs=[pl.BlockSpec(memory_space=pltpu.SMEM)] + [hbm] * 5,
-        out_specs=[vmem] * len(messages),
-        scratch_shapes=[
-            pltpu.SMEM(phase_coef.shape, jnp.float32),
-            pltpu.VMEM((LEVELS, 2, OCT * LANES), jnp.float32),
-            pltpu.VMEM((LEVELS, 2, OCT * LANES), jnp.float32),
-            pltpu.VMEM((1, OCT * LANES), jnp.int32),
-            pltpu.VMEM((PHASE_ROWS // 2, 2, OCT * LANES), jnp.float32),
-            pltpu.SemaphoreType.DMA((4,)),
-            pltpu.SemaphoreType.DMA((OCT,)),
-        ],
+    out_shape = [jax.ShapeDtypeStruct((ROWS // 2, 2, LANES), jnp.float32) for _ in steps]
+    scratch = [pltpu.SemaphoreType.DMA((len(steps),))]
+    if first:
+        boxes = sources[-1].shape[-1]
+        out_shape.append(jax.ShapeDtypeStruct((PHASE_ROWS // 2, 2, boxes), jnp.float32))
+        scratch += [pltpu.SMEM(sources[0].shape, jnp.float32)]
+        scratch += [pltpu.VMEM(source.shape, source.dtype) for source in sources[1:]]
+        scratch += [pltpu.SemaphoreType.DMA((len(sources),))]
+    operands = sources if first else [phases]
+    *arrays, last = pl.pallas_call(
+        functools.partial(pack_kernel, steps, first),
+        out_shape=out_shape,
+        in_specs=[pl.BlockSpec(memory_space=pltpu.SMEM), hbm] + ([hbm] * len(sources) if first else [vmem]),
+        out_specs=[vmem] * len(out_shape),
+        scratch_shapes=scratch,
         compiler_params=pltpu.CompilerParams(vmem_limit_bytes=16 * 2**20),
-        cost_estimate=pl.CostEstimate(flops=2**20, bytes_accessed=2 * 2**20, transcendentals=0),
-        name="pack_far" if far else "pack_near",
-    )(me, phase_coef, weights, wave, center, kind)
-    return {m[0]: array.reshape(-1, LANES) for m, array in zip(messages, arrays)}
+        cost_estimate=pl.CostEstimate(flops=2**20, bytes_accessed=2**20, transcendentals=0),
+        name="pack",
+    )(me, weights, *operands)
+    if first:
+        phases = last
+    else:
+        arrays.append(last)
+    return dict(zip(steps, arrays)), phases
 
 
 def level_factors(level, phases, parent_ref, child_ref, common_ref):
@@ -364,36 +372,28 @@
     if not direct:
         me = jnp.zeros_like(me)
     weights = source_weights.reshape(2, POINTS, SLOTS, LANES).transpose(1, 2, 0, 3)
-    operands = [phase_coef, weights, wave_vectors, source_centers, phase_kind[None, :]]
-    operands = [me] + [pltpu.with_memory_space_constraint(operand, pltpu.HBM) for operand in operands]
-    sent = pack(1, *operands)
-    sent.update(pack(0, *operands))
+    weights, *sources = [
+        pltpu.with_memory_space_constraint(operand, pltpu.HBM)
+        for operand in (weights, phase_coef, wave_vectors, source_centers, phase_kind[None, :])
+    ]
+    blocks, phases = {}, None
+    for steps in PACKS:
+        if blocks:
+            last = next(reversed(blocks))
+            phases, blocks[last] = lax.optimization_barrier((phases, blocks[last]))
+        packed, phases = pack(steps, me, weights, phases, sources)
+        blocks.update(packed)
+    blocks = {step: block.reshape(ROWS, LANES) for step, block in blocks.items()}
     if direct:
-
-        def exchange(array, step):
-            return lax.ppermute(array, "box", [(s, s ^ step) for s in range(SLOTS)])
-
-        for step, earlier in SENDS:
-            if earlier is not None:
-                sent[step], sent[earlier] = lax.optimization_barrier((sent[step], sent[earlier]))
-            sent[step] = exchange(sent[step], step)
-        far_swap = exchange(jnp.concatenate([sent[8][ROWS:], sent[10][ROWS:]]), 1)
-        near_swap = exchange(jnp.concatenate([sent[1], sent[2][ROWS:], sent[4][ROWS:], sent[6][ROWS:]]), 1)
-        even_arrays = [sent[step] for step in range(0, SLOTS, 2)]
-        even_pieces = [(step, step // 2, 0) for step in range(0, SLOTS, 2)]
-        odd_arrays = [near_swap, far_swap, sent[13], sent[15]]
-        odd_pieces = [(1, 0, 0), (3, 0, 1), (5, 0, 2), (7, 0, 3), (9, 1, 0), (11, 1, 1), (13, 2, 0), (15, 3, 0)]
+        for step in EVEN_ORDER + ODD_ORDER:
+            if step:
+                blocks[step] = lax.ppermute(blocks[step], "box", [(s, s ^ step) for s in range(SLOTS)])
     else:
-        blocks = [None] * SLOTS
-        for message in FAR + NEAR:
-            for index, step in enumerate(message):
-                blocks[step] = sent[message[0]][index * ROWS : (index + 1) * ROWS]
-        whole = jnp.concatenate(blocks, axis=1)
+        whole = jnp.concatenate([blocks[step] for step in range(SLOTS)], axis=1)
         whole = lax.all_to_all(whole, "box", split_axis=1, concat_axis=1, tiled=True)
         blocks = [whole[:, s * LANES : (s + 1) * LANES] for s in range(SLOTS)]
-        even_arrays, odd_arrays = blocks[0::2], blocks[1::2]
-        even_pieces = [(2 * index, index, 0) for index in range(OCT)]
-        odd_pieces = [(2 * index + 1, index, 0) for index in range(OCT)]
+    even_arrays, odd_arrays = ([blocks[step] for step in order] for order in (EVEN_ORDER, ODD_ORDER))
+    even_pieces, odd_pieces = ([(step, index, 0) for index, step in enumerate(o)] for o in (EVEN_ORDER, ODD_ORDER))
     even = combine_even(me, even_arrays, even_pieces)
     rows = combine_odd(me, even, odd_arrays, odd_pieces)
     return rows.reshape(POINTS, SLOTS, 2, LANES).transpose(2, 0, 1, 3).reshape(2, POINTS, SLOTS * LANES)

time: 51.5 us -> 48.9 us (0.950)
  waiting for transfers between devices: 18.8 us -> 12.1 us
  starting transfers between devices: 19 us -> 21.4 us
  Pallas kernels: 13.2 us -> 15 us
    ppermute x11 -> x15, waiting for transfers between devices: 18.8 us -> 12.1 us  [on_device(): lax.ppermute(blocks[step], 'box', [(s, s ^ step) for s in range(SLOTS)])]
    ppermute x11 -> x15, starting transfers between devices: 19 us -> 21.4 us  [on_device(): lax.ppermute(blocks[step], 'box', [(s, s ^ step) for s in range(SLOTS)])]
    pallas_call x2 -> x4, Pallas kernels: 2.66 us -> 4.41 us  [pack(): pl.pallas_call(functools.partial(pack_kernel, steps, first), out_shape=ou...]
  transfers between devices with their start and end apart: 11 -> 15, of which waited for: 4 -> 4; matrix products, arithmetic and copies ran while one was open for 0% -> 0% of each run, Pallas kernels for 10% -> 15%
where the time goes in v5:
time: 48.9 us; the launch traced here: 48.6 us
  starting transfers between devices  21.4 us (44%)
  Pallas kernels  15 us (31%)
  waiting for transfers between devices  12.1 us (25%)
    ppermute x15, starting transfers between devices, on_device(): lax.ppermute(blocks[step], 'box', [(s, s ^ step) for s in range(SLOTS)])  21.4 us
    ppermute x15, waiting for transfers between devices, on_device(): lax.ppermute(blocks[step], 'box', [(s, s ^ step) for s in range(SLOTS)])  12.1 us
    pallas_call x1, Pallas kernels, combine_odd(): pl.pallas_call(functools.partial(odd_kernel, pieces, len(arrays)), out_sh...  6.64 us
    pallas_call x4, Pallas kernels, pack(): pl.pallas_call(functools.partial(pack_kernel, steps, first), out_shape=ou...  4.41 us
    pallas_call x1, Pallas kernels, combine_even(): pl.pallas_call(functools.partial(even_kernel, pieces, len(arrays)), out_s...  3.93 us
  transfers between devices with their start and end apart: 15, of which 4 were waited for; matrix products, arithmetic and copies ran while one was open for 0% of the time, Pallas kernels for 15%

profile of v5, /device:TPU:0, one launch (start us, length us, event | category | flops | bytes accessed | tf_op | source)
XLA Modules:
  0.0 48.6 jit_solution(7446652403394813874)
XLA Ops:
  0.0 1.2 %pack.4 = (f32[92,2,128]{2,1,0:T(2,128)S(1)}, f32[92,2,128]{2,1,0:T(2,128)S(1)}, f32[92,2,128]{2,1,0:T(2,128)S(1)}, f32[8,2,2048]{2,1,0:T(2,128)S(1)}) custom-call(s32[1]{0:T(128)} %bitcast.me_ref, f32[81,16,2,128]{3,2,1,0:T(2,128)} %bitcast.42, f32[4,3]{1,0:T(4,128)} %refs_0_.1, f32[4,2,2048]{2,1,0:T(2,128)} %refs_1_.1, f32[4,2,2048]{2,1,0:T(2,128)} %refs_2_.1, ...), custom_call_target="tpu_custom_call" | custom-call | flops 1048576 | bytes 1048576 | tf_op jit(solution)/shard_map/pack/pallas_call | solution.py:138
  1.2 5.1 %collective-permute-start.2 = (f32[184,128]{1,0:T(8,128)S(1)}, f32[184,128]{1,0:T(8,128)S(1)}, u32[]{:S(2)}, u32[]{:S(2)}) collective-permute-start(f32[184,128]{1,0:T(8,128)S(1)} %bitcast.41), channel_id=1, source_target_pairs={{0,12},{1,13},{2,14},{3,15},{4,8},{5,9},{6,10},{7,11},{8,4},{9,5},... | collective-permute-start | bytes 282632 | tf_op jit(solution)/shard_map/ppermute | solution.py:390
  6.3 0.4 collective-permute-start.1
  6.7 3.5 %collective-permute-start = (f32[184,128]{1,0:T(8,128)S(1)}, f32[184,128]{1,0:T(8,128)S(1)}, u32[]{:S(2)}, u32[]{:S(2)}) collective-permute-start(f32[184,128]{1,0:T(8,128)S(1)} %bitcast.37), channel_id=1, source_target_pairs={{0,8},{1,9},{2,10},{3,11},{4,12},{5,13},{6,14},{7,15},{8,0},{9,1},... | collective-permute-start | bytes 282632 | tf_op jit(solution)/shard_map/ppermute | solution.py:390
  10.2 1.0 %pack.5 = (f32[92,2,128]{2,1,0:T(2,128)S(1)}, f32[92,2,128]{2,1,0:T(2,128)S(1)}, f32[92,2,128]{2,1,0:T(2,128)S(1)}) custom-call(s32[1]{0:T(128)} %bitcast.me_ref, f32[81,16,2,128]{3,2,1,0:T(2,128)} %bitcast.43, f32[8,2,2048]{2,1,0:T(2,128)S(1)} %get-tuple-element.43.refs_0_), custom_call_target="tpu_custom_call" | custom-call | flops 1048576 | bytes 1048576 | tf_op jit(solution)/shard_map/pack/pallas_call | solution.py:138
  11.2 0.1 collective-permute-start.5
  11.3 2.0 %collective-permute-start.4 = (f32[184,128]{1,0:T(8,128)S(1)}, f32[184,128]{1,0:T(8,128)S(1)}, u32[]{:S(2)}, u32[]{:S(2)}) collective-permute-start(f32[184,128]{1,0:T(8,128)S(1)} %bitcast.38), channel_id=1, source_target_pairs={{0,4},{1,5},{2,6},{3,7},{4,0},{5,1},{6,2},{7,3},{8,12},{9,13},{10,... | collective-permute-start | bytes 282632 | tf_op jit(solution)/shard_map/ppermute | solution.py:390
  13.2 1.1 %pack.6 = (f32[92,2,128]{2,1,0:T(2,128)S(1)}, f32[92,2,128]{2,1,0:T(2,128)S(1)}, f32[92,2,128]{2,1,0:T(2,128)S(1)}, f32[92,2,128]{2,1,0:T(2,128)S(1)}, f32[92,2,128]{2,1,0:T(2,128)S(1)}) custom-call(s32[1]{0:T(128)} %bitcast.me_ref, f32[81,16,2,128]{3,2,1,0:T(2,128)} %bitcast.44, f32[8,2,2048]{2,1,0:T(2,128)S(1)} %get-tuple-element.43.refs_0_), custom_call_target="tpu_custom_call" | custom-call | flops 1048576 | bytes 1048576 | tf_op jit(solution)/shard_map/pack/pallas_call | solution.py:138
  14.4 0.0 collective-permute-done.2.refs_2_
  14.4 1.6 %collective-permute-start.3 = (f32[184,128]{1,0:T(8,128)S(1)}, f32[184,128]{1,0:T(8,128)S(1)}, u32[]{:S(2)}, u32[]{:S(2)}) collective-permute-start(f32[184,128]{1,0:T(8,128)S(1)} %bitcast.34), channel_id=1, source_target_pairs={{0,2},{1,3},{2,0},{3,1},{4,6},{5,7},{6,4},{7,5},{8,10},{9,11},{10,... | collective-permute-start | bytes 282632 | tf_op jit(solution)/shard_map/ppermute | solution.py:390
  15.9 2.3 %collective-permute-done.1.refs_1_ = f32[184,128]{1,0:T(8,128)S(1)} collective-permute-done((f32[184,128]{1,0:T(8,128)S(1)}, f32[184,128]{1,0:T(8,128)S(1)}, u32[]{:S(2)}, u32[]{:S(2)}) %collective-permute-start.1) | collective-permute-done | bytes 94240 | tf_op jit(solution)/shard_map/ppermute | solution.py:390
  18.3 1.1 %collective-permute-start.10 = (f32[184,128]{1,0:T(8,128)S(1)}, f32[184,128]{1,0:T(8,128)S(1)}, u32[]{:S(2)}, u32[]{:S(2)}) collective-permute-start(f32[184,128]{1,0:T(8,128)S(1)} %bitcast.35), channel_id=1, source_target_pairs={{0,15},{1,14},{2,13},{3,12},{4,11},{5,10},{6,9},{7,8},{8,7},{9,6},... | collective-permute-start | bytes 282632 | tf_op jit(solution)/shard_map/ppermute | solution.py:390
  19.4 0.0 collective-permute-done.refs_0_
  19.4 2.5 %collective-permute-start.6 = (f32[184,128]{1,0:T(8,128)S(1)}, f32[184,128]{1,0:T(8,128)S(1)}, u32[]{:S(2)}, u32[]{:S(2)}) collective-permute-start(f32[184,128]{1,0:T(8,128)S(1)} %bitcast.31), channel_id=1, source_target_pairs={{0,14},{1,15},{2,12},{3,13},{4,10},{5,11},{6,8},{7,9},{8,6},{9,7},... | collective-permute-start | bytes 282632 | tf_op jit(solution)/shard_map/ppermute | solution.py:390
  21.8 0.0 collective-permute-done.5.refs_5_
  21.8 0.0 collective-permute-start.7
  21.8 0.0 collective-permute-done.4.refs_4_
  21.8 2.7 %collective-permute-start.8 = (f32[184,128]{1,0:T(8,128)S(1)}, f32[184,128]{1,0:T(8,128)S(1)}, u32[]{:S(2)}, u32[]{:S(2)}) collective-permute-start(f32[184,128]{1,0:T(8,128)S(1)} %bitcast.28), channel_id=1, source_target_pairs={{0,11},{1,10},{2,9},{3,8},{4,15},{5,14},{6,13},{7,12},{8,3},{9,2},... | collective-permute-start | bytes 282632 | tf_op jit(solution)/shard_map/ppermute | solution.py:390
  24.5 1.1 %pack.7 = (f32[92,2,128]{2,1,0:T(2,128)S(1)}, f32[92,2,128]{2,1,0:T(2,128)S(1)}, f32[92,2,128]{2,1,0:T(2,128)S(1)}, f32[92,2,128]{2,1,0:T(2,128)S(1)}, f32[92,2,128]{2,1,0:T(2,128)S(1)}) custom-call(s32[1]{0:T(128)} %bitcast.me_ref, f32[81,16,2,128]{3,2,1,0:T(2,128)} %bitcast.45, f32[8,2,2048]{2,1,0:T(2,128)S(1)} %get-tuple-element.43.refs_0_), custom_call_target="tpu_custom_call" | custom-call | flops 1048576 | bytes 1048576 | tf_op jit(solution)/shard_map/pack/pallas_call | solution.py:138
  25.6 0.0 collective-permute-done.3.refs_3_
  25.6 2.4 %collective-permute-start.9 = (f32[184,128]{1,0:T(8,128)S(1)}, f32[184,128]{1,0:T(8,128)S(1)}, u32[]{:S(2)}, u32[]{:S(2)}) collective-permute-start(f32[184,128]{1,0:T(8,128)S(1)} %bitcast.27), channel_id=1, source_target_pairs={{0,13},{1,12},{2,15},{3,14},{4,9},{5,8},{6,11},{7,10},{8,5},{9,4},... | collective-permute-start | bytes 282632 | tf_op jit(solution)/shard_map/ppermute | solution.py:390
  28.0 0.0 collective-permute-done.10.refs_3_
  28.0 0.2 collective-permute-start.11
  28.2 0.0 collective-permute-done.6.refs_6_
  28.2 0.0 collective-permute-start.12
  28.2 8.0 %collective-permute-done.7.refs_0_ = f32[184,128]{1,0:T(8,128)S(1)} collective-permute-done((f32[184,128]{1,0:T(8,128)S(1)}, f32[184,128]{1,0:T(8,128)S(1)}, u32[]{:S(2)}, u32[]{:S(2)}) %collective-permute-start.7) | collective-permute-done | bytes 94240 | tf_op jit(solution)/shard_map/ppermute | solution.py:390
  36.2 1.5 %collective-permute-done.8.refs_1_ = f32[184,128]{1,0:T(8,128)S(1)} collective-permute-done((f32[184,128]{1,0:T(8,128)S(1)}, f32[184,128]{1,0:T(8,128)S(1)}, u32[]{:S(2)}, u32[]{:S(2)}) %collective-permute-start.8) | collective-permute-done | bytes 94240 | tf_op jit(solution)/shard_map/ppermute | solution.py:390
  37.7 0.1 collective-permute-start.14
  37.8 3.9 %combine_even.1 = (f32[162,8,128]{2,1,0:T(8,128)S(1)}, f32[4,8,128]{2,1,0:T(8,128)S(1)}) custom-call(s32[1]{0:T(128)} %bitcast.me_ref, f32[184,128]{1,0:T(8,128)S(1)} %collective-permute-done.refs_0_, f32[184,128]{1,0:T(8,128)S(1)} %collective-permute-done.1.refs_1_, f32[184,128]{1,0:T(8,128)S(1)} %collective-permute-done.2.refs_2_, ...), custom_call_target="tpu_custom_call" | custom-call | flops 41943040 | bytes 12582912 | tf_op jit(solution)/shard_map/combine_even/pallas_call | solution.py:326
  41.7 0.0 collective-permute-done.9.refs_2_
  41.8 0.2 collective-permute-done.13.refs_6_
  41.9 6.6 %combine_odd.1 = f32[2592,128]{1,0:T(8,128)} custom-call(s32[1]{0:T(128)} %bitcast.me_ref, f32[162,8,128]{2,1,0:T(8,128)S(1)} %get-tuple-element.45.even_work, f32[4,8,128]{2,1,0:T(8,128)S(1)} %get-tuple-element.46.even_phases, f32[184,128]{1,0:T(8,128)S(1)} %collective-permute-done.7.refs_0_, f32[184,128]{1,0:T(8,128)S(1)} %collective-permute-done.8.refs_1_, ...), custom_call_target="tpu_custom_call" | custom-call | flops 83886080 | bytes 20971520 | tf_op jit(solution)/shard_map/combine_odd/pallas_call | solution.py:348
  (4 shorter events, 0.0 us)
Async XLA Ops:
  1.2 13.2 %collective-permute-start.2 = (f32[184,128]{1,0:T(8,128)S(1)}, f32[184,128]{1,0:T(8,128)S(1)}, u32[]{:S(2)}, u32[]{:S(2)}) collective-permute-start(f32[184,128]{1,0:T(8,128)S(1)} %bitcast.41), channel_id=1, source_target_pairs={{0,12},{1,13},{2,14},{3,15},{4,8},{5,9},{6,10},{7,11},{8,4},{9,5},... | collective-permute-start | bytes 282632 | tf_op jit(solution)/shard_map/ppermute | solution.py:390
  6.3 12.0 %collective-permute-start.1 = (f32[184,128]{1,0:T(8,128)S(1)}, f32[184,128]{1,0:T(8,128)S(1)}, u32[]{:S(2)}, u32[]{:S(2)}) collective-permute-start(f32[184,128]{1,0:T(8,128)S(1)} %bitcast.39), channel_id=1, source_target_pairs={{0,10},{1,11},{2,8},{3,9},{4,14},{5,15},{6,12},{7,13},{8,2},{9,3},... | collective-permute-start | bytes 282632 | tf_op jit(solution)/shard_map/ppermute | solution.py:390
  6.7 12.7 %collective-permute-start = (f32[184,128]{1,0:T(8,128)S(1)}, f32[184,128]{1,0:T(8,128)S(1)}, u32[]{:S(2)}, u32[]{:S(2)}) collective-permute-start(f32[184,128]{1,0:T(8,128)S(1)} %bitcast.37), channel_id=1, source_target_pairs={{0,8},{1,9},{2,10},{3,11},{4,12},{5,13},{6,14},{7,15},{8,0},{9,1},... | collective-permute-start | bytes 282632 | tf_op jit(solution)/shard_map/ppermute | solution.py:390
  11.2 10.6 %collective-permute-start.5 = (f32[184,128]{1,0:T(8,128)S(1)}, f32[184,128]{1,0:T(8,128)S(1)}, u32[]{:S(2)}, u32[]{:S(2)}) collective-permute-start(f32[184,128]{1,0:T(8,128)S(1)} %bitcast.40), channel_id=1, source_target_pairs={{0,6},{1,7},{2,4},{3,5},{4,2},{5,3},{6,0},{7,1},{8,14},{9,15},{10,... | collective-permute-start | bytes 282632 | tf_op jit(solution)/shard_map/ppermute | solution.py:390
  11.3 10.6 %collective-permute-start.4 = (f32[184,128]{1,0:T(8,128)S(1)}, f32[184,128]{1,0:T(8,128)S(1)}, u32[]{:S(2)}, u32[]{:S(2)}) collective-permute-start(f32[184,128]{1,0:T(8,128)S(1)} %bitcast.38), channel_id=1, source_target_pairs={{0,4},{1,5},{2,6},{3,7},{4,0},{5,1},{6,2},{7,3},{8,12},{9,13},{10,... | collective-permute-start | bytes 282632 | tf_op jit(solution)/shard_map/ppermute | solution.py:390
  14.4 11.3 %collective-permute-start.3 = (f32[184,128]{1,0:T(8,128)S(1)}, f32[184,128]{1,0:T(8,128)S(1)}, u32[]{:S(2)}, u32[]{:S(2)}) collective-permute-start(f32[184,128]{1,0:T(8,128)S(1)} %bitcast.34), channel_id=1, source_target_pairs={{0,2},{1,3},{2,0},{3,1},{4,6},{5,7},{6,4},{7,5},{8,10},{9,11},{10,... | collective-permute-start | bytes 282632 | tf_op jit(solution)/shard_map/ppermute | solution.py:390
  18.3 9.8 %collective-permute-start.10 = (f32[184,128]{1,0:T(8,128)S(1)}, f32[184,128]{1,0:T(8,128)S(1)}, u32[]{:S(2)}, u32[]{:S(2)}) collective-permute-start(f32[184,128]{1,0:T(8,128)S(1)} %bitcast.35), channel_id=1, source_target_pairs={{0,15},{1,14},{2,13},{3,12},{4,11},{5,10},{6,9},{7,8},{8,7},{9,6},... | collective-permute-start | bytes 282632 | tf_op jit(solution)/shard_map/ppermute | solution.py:390
  19.4 8.8 %collective-permute-start.6 = (f32[184,128]{1,0:T(8,128)S(1)}, f32[184,128]{1,0:T(8,128)S(1)}, u32[]{:S(2)}, u32[]{:S(2)}) collective-permute-start(f32[184,128]{1,0:T(8,128)S(1)} %bitcast.31), channel_id=1, source_target_pairs={{0,14},{1,15},{2,12},{3,13},{4,10},{5,11},{6,8},{7,9},{8,6},{9,7},... | collective-permute-start | bytes 282632 | tf_op jit(solution)/shard_map/ppermute | solution.py:390
  21.8 14.4 %collective-permute-start.7 = (f32[184,128]{1,0:T(8,128)S(1)}, f32[184,128]{1,0:T(8,128)S(1)}, u32[]{:S(2)}, u32[]{:S(2)}) collective-permute-start(f32[184,128]{1,0:T(8,128)S(1)} %bitcast.29), channel_id=1, source_target_pairs={{0,9},{1,8},{2,11},{3,10},{4,13},{5,12},{6,15},{7,14},{8,1},{9,0},... | collective-permute-start | bytes 282632 | tf_op jit(solution)/shard_map/ppermute | solution.py:390
  21.8 15.9 %collective-permute-start.8 = (f32[184,128]{1,0:T(8,128)S(1)}, f32[184,128]{1,0:T(8,128)S(1)}, u32[]{:S(2)}, u32[]{:S(2)}) collective-permute-start(f32[184,128]{1,0:T(8,128)S(1)} %bitcast.28), channel_id=1, source_target_pairs={{0,11},{1,10},{2,9},{3,8},{4,15},{5,14},{6,13},{7,12},{8,3},{9,2},... | collective-permute-start | bytes 282632 | tf_op jit(solution)/shard_map/ppermute | solution.py:390
  25.6 16.1 %collective-permute-start.9 = (f32[184,128]{1,0:T(8,128)S(1)}, f32[184,128]{1,0:T(8,128)S(1)}, u32[]{:S(2)}, u32[]{:S(2)}) collective-permute-start(f32[184,128]{1,0:T(8,128)S(1)} %bitcast.27), channel_id=1, source_target_pairs={{0,13},{1,12},{2,15},{3,14},{4,9},{5,8},{6,11},{7,10},{8,5},{9,4},... | collective-permute-start | bytes 282632 | tf_op jit(solution)/shard_map/ppermute | solution.py:390
  28.0 13.7 %collective-permute-start.11 = (f32[184,128]{1,0:T(8,128)S(1)}, f32[184,128]{1,0:T(8,128)S(1)}, u32[]{:S(2)}, u32[]{:S(2)}) collective-permute-start(f32[184,128]{1,0:T(8,128)S(1)} %bitcast.36), channel_id=1, source_target_pairs={{0,3},{1,2},{2,1},{3,0},{4,7},{5,6},{6,5},{7,4},{8,11},{9,10},{10,... | collective-permute-start | bytes 282632 | tf_op jit(solution)/shard_map/ppermute | solution.py:390
  28.2 13.6 %collective-permute-start.12 = (f32[184,128]{1,0:T(8,128)S(1)}, f32[184,128]{1,0:T(8,128)S(1)}, u32[]{:S(2)}, u32[]{:S(2)}) collective-permute-start(f32[184,128]{1,0:T(8,128)S(1)} %bitcast.33), channel_id=1, source_target_pairs={{0,5},{1,4},{2,7},{3,6},{4,1},{5,0},{6,3},{7,2},{8,13},{9,12},{10,... | collective-permute-start | bytes 282632 | tf_op jit(solution)/shard_map/ppermute | solution.py:390
  36.2 5.7 %collective-permute-start.13 = (f32[184,128]{1,0:T(8,128)S(1)}, f32[184,128]{1,0:T(8,128)S(1)}, u32[]{:S(2)}, u32[]{:S(2)}) collective-permute-start(f32[184,128]{1,0:T(8,128)S(1)} %bitcast.32), channel_id=1, source_target_pairs={{0,7},{1,6},{2,5},{3,4},{4,3},{5,2},{6,1},{7,0},{8,15},{9,14},{10,... | collective-permute-start | bytes 282632 | tf_op jit(solution)/shard_map/ppermute | solution.py:390
  37.7 4.2 %collective-permute-start.14 = (f32[184,128]{1,0:T(8,128)S(1)}, f32[184,128]{1,0:T(8,128)S(1)}, u32[]{:S(2)}, u32[]{:S(2)}) collective-permute-start(f32[184,128]{1,0:T(8,128)S(1)} %bitcast.30), channel_id=1, source_target_pairs={{0,1},{1,0},{2,3},{3,2},{4,5},{5,4},{6,7},{7,6},{8,9},{9,8},{10,11... | collective-permute-start | bytes 282632 | tf_op jit(solution)/shard_map/ppermute | solution.py:390

commit v6 on v5

--- a/solution.py
+++ b/solution.py
@@ -24,6 +24,7 @@
 PACKS = ((8, 10, 12), (2, 4, 6), (14, 9, 11, 13, 15), (3, 5, 7, 1, 0))
 EVEN_ORDER = (8, 10, 12, 2, 4, 6, 14, 0)
 ODD_ORDER = (9, 11, 13, 15, 3, 5, 7, 1)
+LATE = (7, 1)
 
 NODES = np.cos(math.pi * (2.0 * np.arange(CHEB) + 1.0) / (2.0 * CHEB))
 NODES[CHEB // 2] = 0.0
@@ -210,12 +211,11 @@
     return part + 2 * (split * CHEB + column if level % 2 == 0 else column * CHEB + split)
 
 
-def join_chips(me, arrays, pieces, held, sems, work, last_phases, factors):
+def join_chips(me, blocks, order, held, sems, work, last_phases, factors):
     copies = []
-    for step, index, block in pieces:
+    for index, step in enumerate(order):
         spot = pl.ds(pl.multiple_of(((me ^ step) // 2) * ROWS, 8), ROWS)
-        source = arrays[index].at[pl.ds(block * ROWS, ROWS), :]
-        copies.append(pltpu.make_async_copy(source, held.at[spot, :], sems.at[step // 2]))
+        copies.append(pltpu.make_async_copy(blocks[index], held.at[spot, :], sems.at[index]))
         copies[-1].start()
     for copy in copies:
         copy.wait()
@@ -251,17 +251,17 @@
             level_column(column, children, *factors, store)
             return 0
 
-        lax.fori_loop(0, CHEB, column_step, 0)
-
-
-def even_kernel(pieces, count, me_ref, *refs):
-    work, last_phases, held, parent_ref, child_ref, common_ref, sems = refs[count:]
+        lax.fori_loop(0, CHEB, column_step, 0, unroll=3)
+
+
+def even_kernel(me_ref, *refs):
+    work, last_phases, held, parent_ref, child_ref, common_ref, sems = refs[OCT:]
     factors = (parent_ref, child_ref, common_ref)
-    join_chips(me_ref[0], refs, pieces, held, sems, work, last_phases, factors)
-
-
-def odd_kernel(pieces, count, me_ref, even_work, even_phases, *refs):
-    out_hbm, work, last_phases, held, out_ref, parent_ref, child_ref, common_ref, sems, out_sems = refs[count:]
+    join_chips(me_ref[0], refs, EVEN_ORDER, held, sems, work, last_phases, factors)
+
+
+def odd_kernel(me_ref, even_work, even_phases, *refs):
+    out_hbm, work, last_phases, held, out_ref, parent_ref, child_ref, common_ref, sems, out_sems = refs[OCT:]
     me = me_ref[0]
     own = me % 2
     early = [
@@ -271,7 +271,7 @@
     for copy in early:
         copy.start()
     factors = [ref.at[0] for ref in (parent_ref, child_ref, common_ref)]
-    join_chips(me, refs, pieces, held, sems, work.at[1 - own], last_phases.at[1 - own], factors)
+    join_chips(me, refs, ODD_ORDER, held, sems, work.at[1 - own], last_phases.at[1 - own], factors)
     for copy in early:
         copy.wait()
 
@@ -308,7 +308,7 @@
         leave(column).start()
         return 0
 
-    lax.fori_loop(0, CHEB, column_step, 0)
+    lax.fori_loop(0, CHEB, column_step, 0, unroll=3)
     for column in range(CHEB):
         leave(column).wait()
 
@@ -321,15 +321,15 @@
     ]
 
 
-def combine_even(me, arrays, pieces):
+def combine_even(me, blocks):
     vmem = pl.BlockSpec(memory_space=pltpu.VMEM)
     return pl.pallas_call(
-        functools.partial(even_kernel, pieces, len(arrays)),
+        even_kernel,
         out_shape=[
             jax.ShapeDtypeStruct((WEIGHT_ROWS, OCT, LANES), jnp.float32),
             jax.ShapeDtypeStruct((4, OCT, LANES), jnp.float32),
         ],
-        in_specs=[pl.BlockSpec(memory_space=pltpu.SMEM)] + [pl.BlockSpec(memory_space=pl.ANY)] * len(arrays),
+        in_specs=[pl.BlockSpec(memory_space=pltpu.SMEM)] + [pl.BlockSpec(memory_space=pl.ANY)] * OCT,
         out_specs=[vmem, vmem],
         scratch_shapes=[
             pltpu.VMEM((OCT * ROWS, LANES), jnp.float32),
@@ -339,16 +339,16 @@
         compiler_params=pltpu.CompilerParams(vmem_limit_bytes=16 * 2**20),
         cost_estimate=pl.CostEstimate(flops=40 * 2**20, bytes_accessed=12 * 2**20, transcendentals=0),
         name="combine_even",
-    )(me, *arrays)
-
-
-def combine_odd(me, even, arrays, pieces):
+    )(me, *blocks)
+
+
+def combine_odd(me, even, blocks):
     hbm = pl.BlockSpec(memory_space=pltpu.HBM)
     anywhere = pl.BlockSpec(memory_space=pl.ANY)
     return pl.pallas_call(
-        functools.partial(odd_kernel, pieces, len(arrays)),
+        odd_kernel,
         out_shape=jax.ShapeDtypeStruct((WEIGHT_ROWS * SLOTS, LANES), jnp.float32),
-        in_specs=[pl.BlockSpec(memory_space=pltpu.SMEM)] + [anywhere] * (2 + len(arrays)),
+        in_specs=[pl.BlockSpec(memory_space=pltpu.SMEM)] + [anywhere] * (2 + OCT),
         out_specs=hbm,
         scratch_shapes=[
             pltpu.VMEM((2, WEIGHT_ROWS, OCT, LANES), jnp.float32),
@@ -362,7 +362,7 @@
         compiler_params=pltpu.CompilerParams(vmem_limit_bytes=16 * 2**20),
         cost_estimate=pl.CostEstimate(flops=80 * 2**20, bytes_accessed=20 * 2**20, transcendentals=0),
         name="combine_odd",
-    )(me, *even, *arrays)
+    )(me, *even, *blocks)
 
 
 def on_device(source_weights, wave_vectors, source_centers, phase_coef, phase_kind):
@@ -385,17 +385,23 @@
         blocks.update(packed)
     blocks = {step: block.reshape(ROWS, LANES) for step, block in blocks.items()}
     if direct:
+
+        def send(step):
+            return lax.ppermute(blocks[step], "box", [(s, s ^ step) for s in range(SLOTS)])
+
         for step in EVEN_ORDER + ODD_ORDER:
-            if step:
-                blocks[step] = lax.ppermute(blocks[step], "box", [(s, s ^ step) for s in range(SLOTS)])
+            if step and step not in LATE:
+                blocks[step] = send(step)
     else:
         whole = jnp.concatenate([blocks[step] for step in range(SLOTS)], axis=1)
         whole = lax.all_to_all(whole, "box", split_axis=1, concat_axis=1, tiled=True)
         blocks = [whole[:, s * LANES : (s + 1) * LANES] for s in range(SLOTS)]
-    even_arrays, odd_arrays = ([blocks[step] for step in order] for order in (EVEN_ORDER, ODD_ORDER))
-    even_pieces, odd_pieces = ([(step, index, 0) for index, step in enumerate(o)] for o in (EVEN_ORDER, ODD_ORDER))
-    even = combine_even(me, even_arrays, even_pieces)
-    rows = combine_odd(me, even, odd_arrays, odd_pieces)
+    even = list(combine_even(me, [blocks[step] for step in EVEN_ORDER]))
+    if direct:
+        for step in LATE:
+            even[1], blocks[step] = lax.optimization_barrier((even[1], blocks[step]))
+            blocks[step] = send(step)
+    rows = combine_odd(me, even, [blocks[step] for step in ODD_ORDER])
     return rows.reshape(POINTS, SLOTS, 2, LANES).transpose(2, 0, 1, 3).reshape(2, POINTS, SLOTS * LANES)
 
 

time: 48.9 us -> 49.9 us (1.020)
  starting transfers between devices: 21.4 us -> 24.7 us
  waiting for transfers between devices: 12.1 us -> 10 us
    ppermute x15, starting transfers between devices: 21.4 us -> 24.7 us  [send(): lax.ppermute(blocks[step], 'box', [(s, s ^ step) for s in range(SLOTS)])]
    ppermute x15, waiting for transfers between devices: 12.1 us -> 10 us  [send(): lax.ppermute(blocks[step], 'box', [(s, s ^ step) for s in range(SLOTS)])]
  transfers between devices with their start and end apart: 15 -> 15, of which waited for: 4 -> 6; matrix products, arithmetic and copies ran while one was open for 0% -> 0% of each run, Pallas kernels for 15% -> 14%
where the time goes in v6:
time: 49.9 us; the launch traced here: 49.4 us
  starting transfers between devices  24.7 us (49%)
  Pallas kernels  14.7 us (29%)
  waiting for transfers between devices  10 us (20%)
    ppermute x15, starting transfers between devices, send(): lax.ppermute(blocks[step], 'box', [(s, s ^ step) for s in range(SLOTS)])  24.7 us
    ppermute x15, waiting for transfers between devices, send(): lax.ppermute(blocks[step], 'box', [(s, s ^ step) for s in range(SLOTS)])  10 us
    pallas_call x1, Pallas kernels, combine_odd(): pl.pallas_call(odd_kernel, out_shape=jax.ShapeDtypeStruct((WEIGHT_ROWS *...  6.43 us
    pallas_call x4, Pallas kernels, pack(): pl.pallas_call(functools.partial(pack_kernel, steps, first), out_shape=ou...  4.41 us
    pallas_call x1, Pallas kernels, combine_even(): pl.pallas_call(even_kernel, out_shape=[jax.ShapeDtypeStruct((WEIGHT_ROWS,...  3.82 us
  transfers between devices with their start and end apart: 15, of which 6 were waited for; matrix products, arithmetic and copies ran while one was open for 0% of the time, Pallas kernels for 14%

profile of v6, /device:TPU:0, one launch (start us, length us, event | category | flops | bytes accessed | tf_op | source)
XLA Modules:
  0.0 49.4 jit_solution(1643560151820519953)
XLA Ops:
  0.0 1.2 %pack.4 = (f32[92,2,128]{2,1,0:T(2,128)S(1)}, f32[92,2,128]{2,1,0:T(2,128)S(1)}, f32[92,2,128]{2,1,0:T(2,128)S(1)}, f32[8,2,2048]{2,1,0:T(2,128)S(1)}) custom-call(s32[1]{0:T(128)} %bitcast.me_ref, f32[81,16,2,128]{3,2,1,0:T(2,128)} %bitcast.42, f32[4,3]{1,0:T(4,128)} %refs_0_.1, f32[4,2,2048]{2,1,0:T(2,128)} %refs_1_.1, f32[4,2,2048]{2,1,0:T(2,128)} %refs_2_.1, ...), custom_call_target="tpu_custom_call" | custom-call | flops 1048576 | bytes 1048576 | tf_op jit(solution)/shard_map/pack/pallas_call | solution.py:139
  1.2 5.1 %collective-permute-start.2 = (f32[184,128]{1,0:T(8,128)S(1)}, f32[184,128]{1,0:T(8,128)S(1)}, u32[]{:S(2)}, u32[]{:S(2)}) collective-permute-start(f32[184,128]{1,0:T(8,128)S(1)} %bitcast.41), channel_id=1, source_target_pairs={{0,12},{1,13},{2,14},{3,15},{4,8},{5,9},{6,10},{7,11},{8,4},{9,5},... | collective-permute-start | bytes 282632 | tf_op jit(solution)/shard_map/ppermute | solution.py:390
  6.3 0.4 collective-permute-start.1
  6.7 3.5 %collective-permute-start = (f32[184,128]{1,0:T(8,128)S(1)}, f32[184,128]{1,0:T(8,128)S(1)}, u32[]{:S(2)}, u32[]{:S(2)}) collective-permute-start(f32[184,128]{1,0:T(8,128)S(1)} %bitcast.37), channel_id=1, source_target_pairs={{0,8},{1,9},{2,10},{3,11},{4,12},{5,13},{6,14},{7,15},{8,0},{9,1},... | collective-permute-start | bytes 282632 | tf_op jit(solution)/shard_map/ppermute | solution.py:390
  10.2 1.0 %pack.5 = (f32[92,2,128]{2,1,0:T(2,128)S(1)}, f32[92,2,128]{2,1,0:T(2,128)S(1)}, f32[92,2,128]{2,1,0:T(2,128)S(1)}) custom-call(s32[1]{0:T(128)} %bitcast.me_ref, f32[81,16,2,128]{3,2,1,0:T(2,128)} %bitcast.43, f32[8,2,2048]{2,1,0:T(2,128)S(1)} %get-tuple-element.47.refs_0_), custom_call_target="tpu_custom_call" | custom-call | flops 1048576 | bytes 1048576 | tf_op jit(solution)/shard_map/pack/pallas_call | solution.py:139
  11.2 0.1 collective-permute-start.5
  11.3 2.0 %collective-permute-start.4 = (f32[184,128]{1,0:T(8,128)S(1)}, f32[184,128]{1,0:T(8,128)S(1)}, u32[]{:S(2)}, u32[]{:S(2)}) collective-permute-start(f32[184,128]{1,0:T(8,128)S(1)} %bitcast.38), channel_id=1, source_target_pairs={{0,4},{1,5},{2,6},{3,7},{4,0},{5,1},{6,2},{7,3},{8,12},{9,13},{10,... | collective-permute-start | bytes 282632 | tf_op jit(solution)/shard_map/ppermute | solution.py:390
  13.2 1.1 %pack.6 = (f32[92,2,128]{2,1,0:T(2,128)S(1)}, f32[92,2,128]{2,1,0:T(2,128)S(1)}, f32[92,2,128]{2,1,0:T(2,128)S(1)}, f32[92,2,128]{2,1,0:T(2,128)S(1)}, f32[92,2,128]{2,1,0:T(2,128)S(1)}) custom-call(s32[1]{0:T(128)} %bitcast.me_ref, f32[81,16,2,128]{3,2,1,0:T(2,128)} %bitcast.44, f32[8,2,2048]{2,1,0:T(2,128)S(1)} %get-tuple-element.47.refs_0_), custom_call_target="tpu_custom_call" | custom-call | flops 1048576 | bytes 1048576 | tf_op jit(solution)/shard_map/pack/pallas_call | solution.py:139
  14.4 0.0 collective-permute-done.2.refs_2_
  14.4 1.6 %collective-permute-start.3 = (f32[184,128]{1,0:T(8,128)S(1)}, f32[184,128]{1,0:T(8,128)S(1)}, u32[]{:S(2)}, u32[]{:S(2)}) collective-permute-start(f32[184,128]{1,0:T(8,128)S(1)} %bitcast.34), channel_id=1, source_target_pairs={{0,2},{1,3},{2,0},{3,1},{4,6},{5,7},{6,4},{7,5},{8,10},{9,11},{10,... | collective-permute-start | bytes 282632 | tf_op jit(solution)/shard_map/ppermute | solution.py:390
  15.9 2.3 %collective-permute-done.1.refs_1_ = f32[184,128]{1,0:T(8,128)S(1)} collective-permute-done((f32[184,128]{1,0:T(8,128)S(1)}, f32[184,128]{1,0:T(8,128)S(1)}, u32[]{:S(2)}, u32[]{:S(2)}) %collective-permute-start.1) | collective-permute-done | bytes 94240 | tf_op jit(solution)/shard_map/ppermute | solution.py:390
  18.3 1.7 %collective-permute-start.6 = (f32[184,128]{1,0:T(8,128)S(1)}, f32[184,128]{1,0:T(8,128)S(1)}, u32[]{:S(2)}, u32[]{:S(2)}) collective-permute-start(f32[184,128]{1,0:T(8,128)S(1)} %bitcast.35), channel_id=1, source_target_pairs={{0,14},{1,15},{2,12},{3,13},{4,10},{5,11},{6,8},{7,9},{8,6},{9,7},... | collective-permute-start | bytes 282632 | tf_op jit(solution)/shard_map/ppermute | solution.py:390
  20.0 0.0 collective-permute-done.refs_0_
  20.0 0.4 collective-permute-start.10
  20.4 0.4 collective-permute-done.5.refs_5_
  20.8 0.3 collective-permute-start.7
  21.1 0.0 collective-permute-done.4.refs_4_
  21.1 3.3 %collective-permute-start.8 = (f32[184,128]{1,0:T(8,128)S(1)}, f32[184,128]{1,0:T(8,128)S(1)}, u32[]{:S(2)}, u32[]{:S(2)}) collective-permute-start(f32[184,128]{1,0:T(8,128)S(1)} %bitcast.28), channel_id=1, source_target_pairs={{0,11},{1,10},{2,9},{3,8},{4,15},{5,14},{6,13},{7,12},{8,3},{9,2},... | collective-permute-start | bytes 282632 | tf_op jit(solution)/shard_map/ppermute | solution.py:390
  24.5 1.1 %pack.7 = (f32[92,2,128]{2,1,0:T(2,128)S(1)}, f32[92,2,128]{2,1,0:T(2,128)S(1)}, f32[92,2,128]{2,1,0:T(2,128)S(1)}, f32[92,2,128]{2,1,0:T(2,128)S(1)}, f32[92,2,128]{2,1,0:T(2,128)S(1)}) custom-call(s32[1]{0:T(128)} %bitcast.me_ref, f32[81,16,2,128]{3,2,1,0:T(2,128)} %bitcast.45, f32[8,2,2048]{2,1,0:T(2,128)S(1)} %get-tuple-element.47.refs_0_), custom_call_target="tpu_custom_call" | custom-call | flops 1048576 | bytes 1048576 | tf_op jit(solution)/shard_map/pack/pallas_call | solution.py:139
  25.6 0.0 collective-permute-done.3.refs_3_
  25.6 2.7 %collective-permute-start.9 = (f32[184,128]{1,0:T(8,128)S(1)}, f32[184,128]{1,0:T(8,128)S(1)}, u32[]{:S(2)}, u32[]{:S(2)}) collective-permute-start(f32[184,128]{1,0:T(8,128)S(1)} %bitcast.27), channel_id=1, source_target_pairs={{0,13},{1,12},{2,15},{3,14},{4,9},{5,8},{6,11},{7,10},{8,5},{9,4},... | collective-permute-start | bytes 282632 | tf_op jit(solution)/shard_map/ppermute | solution.py:390
  28.3 0.0 collective-permute-done.6.refs_6_
  28.3 0.0 collective-permute-start.11
  28.3 3.8 %combine_even.1 = (f32[162,8,128]{2,1,0:T(8,128)S(1)}, f32[4,8,128]{2,1,0:T(8,128)S(1)}) custom-call(s32[1]{0:T(128)} %bitcast.me_ref, f32[184,128]{1,0:T(8,128)S(1)} %collective-permute-done.refs_0_, f32[184,128]{1,0:T(8,128)S(1)} %collective-permute-done.1.refs_1_, f32[184,128]{1,0:T(8,128)S(1)} %collective-permute-done.2.refs_2_, ...), custom_call_target="tpu_custom_call" | custom-call | flops 41943040 | bytes 12582912 | tf_op jit(solution)/shard_map/combine_even/pallas_call | solution.py:326
  32.1 2.7 %collective-permute-start.12 = (f32[184,128]{1,0:T(8,128)S(1)}, f32[184,128]{1,0:T(8,128)S(1)}, u32[]{:S(2)}, u32[]{:S(2)}) collective-permute-start(f32[184,128]{1,0:T(8,128)S(1)} %bitcast.33), channel_id=1, source_target_pairs={{0,5},{1,4},{2,7},{3,6},{4,1},{5,0},{6,3},{7,2},{8,13},{9,12},{10,... | collective-permute-start | bytes 282632 | tf_op jit(solution)/shard_map/ppermute | solution.py:390
  34.8 0.7 %collective-permute-done.7.refs_0_ = f32[184,128]{1,0:T(8,128)S(1)} collective-permute-done((f32[184,128]{1,0:T(8,128)S(1)}, f32[184,128]{1,0:T(8,128)S(1)}, u32[]{:S(2)}, u32[]{:S(2)}) %collective-permute-start.7) | collective-permute-done | bytes 94240 | tf_op jit(solution)/shard_map/ppermute | solution.py:390
  35.5 0.9 %collective-permute-start.14 = (f32[184,128]{1,0:T(8,128)S(1)}, f32[184,128]{1,0:T(8,128)S(1)}, u32[]{:S(2)}, u32[]{:S(2)}) collective-permute-start(f32[184,128]{1,0:T(8,128)S(1)} %bitcast.32), channel_id=1, source_target_pairs={{0,1},{1,0},{2,3},{3,2},{4,5},{5,4},{6,7},{7,6},{8,9},{9,8},{10,11... | collective-permute-start | bytes 282632 | tf_op jit(solution)/shard_map/ppermute | solution.py:390
  36.5 1.5 %collective-permute-done.8.refs_1_ = f32[184,128]{1,0:T(8,128)S(1)} collective-permute-done((f32[184,128]{1,0:T(8,128)S(1)}, f32[184,128]{1,0:T(8,128)S(1)}, u32[]{:S(2)}, u32[]{:S(2)}) %collective-permute-start.8) | collective-permute-done | bytes 94240 | tf_op jit(solution)/shard_map/ppermute | solution.py:390
  38.0 0.0 collective-permute-done.11.refs_4_
  38.0 1.9 %collective-permute-done.12.refs_5_ = f32[184,128]{1,0:T(8,128)S(1)} collective-permute-done((f32[184,128]{1,0:T(8,128)S(1)}, f32[184,128]{1,0:T(8,128)S(1)}, u32[]{:S(2)}, u32[]{:S(2)}) %collective-permute-start.12) | collective-permute-done | bytes 94240 | tf_op jit(solution)/shard_map/ppermute | solution.py:390
  39.9 3.1 %collective-permute-done.13.refs_6_ = f32[184,128]{1,0:T(8,128)S(1)} collective-permute-done((f32[184,128]{1,0:T(8,128)S(1)}, f32[184,128]{1,0:T(8,128)S(1)}, u32[]{:S(2)}, u32[]{:S(2)}) %collective-permute-start.13) | collective-permute-done | bytes 94240 | tf_op jit(solution)/shard_map/ppermute | solution.py:390
  43.0 6.4 %combine_odd.1 = f32[2592,128]{1,0:T(8,128)} custom-call(s32[1]{0:T(128)} %bitcast.me_ref, f32[162,8,128]{2,1,0:T(8,128)S(1)} %get-tuple-element.49.even_work, f32[4,8,128]{2,1,0:T(8,128)S(1)} %get-tuple-element.54.even_phases, f32[184,128]{1,0:T(8,128)S(1)} %collective-permute-done.7.refs_0_, f32[184,128]{1,0:T(8,128)S(1)} %collective-permute-done.8.refs_1_, ...), custom_call_target="tpu_custom_call" | custom-call | flops 83886080 | bytes 20971520 | tf_op jit(solution)/shard_map/combine_odd/pallas_call | solution.py:348
  (4 shorter events, 0.0 us)
Async XLA Ops:
  1.2 13.2 %collective-permute-start.2 = (f32[184,128]{1,0:T(8,128)S(1)}, f32[184,128]{1,0:T(8,128)S(1)}, u32[]{:S(2)}, u32[]{:S(2)}) collective-permute-start(f32[184,128]{1,0:T(8,128)S(1)} %bitcast.41), channel_id=1, source_target_pairs={{0,12},{1,13},{2,14},{3,15},{4,8},{5,9},{6,10},{7,11},{8,4},{9,5},... | collective-permute-start | bytes 282632 | tf_op jit(solution)/shard_map/ppermute | solution.py:390
  6.3 12.0 %collective-permute-start.1 = (f32[184,128]{1,0:T(8,128)S(1)}, f32[184,128]{1,0:T(8,128)S(1)}, u32[]{:S(2)}, u32[]{:S(2)}) collective-permute-start(f32[184,128]{1,0:T(8,128)S(1)} %bitcast.39), channel_id=1, source_target_pairs={{0,10},{1,11},{2,8},{3,9},{4,14},{5,15},{6,12},{7,13},{8,2},{9,3},... | collective-permute-start | bytes 282632 | tf_op jit(solution)/shard_map/ppermute | solution.py:390
  6.7 13.3 %collective-permute-start = (f32[184,128]{1,0:T(8,128)S(1)}, f32[184,128]{1,0:T(8,128)S(1)}, u32[]{:S(2)}, u32[]{:S(2)}) collective-permute-start(f32[184,128]{1,0:T(8,128)S(1)} %bitcast.37), channel_id=1, source_target_pairs={{0,8},{1,9},{2,10},{3,11},{4,12},{5,13},{6,14},{7,15},{8,0},{9,1},... | collective-permute-start | bytes 282632 | tf_op jit(solution)/shard_map/ppermute | solution.py:390
  11.2 9.6 %collective-permute-start.5 = (f32[184,128]{1,0:T(8,128)S(1)}, f32[184,128]{1,0:T(8,128)S(1)}, u32[]{:S(2)}, u32[]{:S(2)}) collective-permute-start(f32[184,128]{1,0:T(8,128)S(1)} %bitcast.40), channel_id=1, source_target_pairs={{0,6},{1,7},{2,4},{3,5},{4,2},{5,3},{6,0},{7,1},{8,14},{9,15},{10,... | collective-permute-start | bytes 282632 | tf_op jit(solution)/shard_map/ppermute | solution.py:390
  11.3 9.9 %collective-permute-start.4 = (f32[184,128]{1,0:T(8,128)S(1)}, f32[184,128]{1,0:T(8,128)S(1)}, u32[]{:S(2)}, u32[]{:S(2)}) collective-permute-start(f32[184,128]{1,0:T(8,128)S(1)} %bitcast.38), channel_id=1, source_target_pairs={{0,4},{1,5},{2,6},{3,7},{4,0},{5,1},{6,2},{7,3},{8,12},{9,13},{10,... | collective-permute-start | bytes 282632 | tf_op jit(solution)/shard_map/ppermute | solution.py:390
  14.4 11.2 %collective-permute-start.3 = (f32[184,128]{1,0:T(8,128)S(1)}, f32[184,128]{1,0:T(8,128)S(1)}, u32[]{:S(2)}, u32[]{:S(2)}) collective-permute-start(f32[184,128]{1,0:T(8,128)S(1)} %bitcast.34), channel_id=1, source_target_pairs={{0,2},{1,3},{2,0},{3,1},{4,6},{5,7},{6,4},{7,5},{8,10},{9,11},{10,... | collective-permute-start | bytes 282632 | tf_op jit(solution)/shard_map/ppermute | solution.py:390
  18.3 10.0 %collective-permute-start.6 = (f32[184,128]{1,0:T(8,128)S(1)}, f32[184,128]{1,0:T(8,128)S(1)}, u32[]{:S(2)}, u32[]{:S(2)}) collective-permute-start(f32[184,128]{1,0:T(8,128)S(1)} %bitcast.35), channel_id=1, source_target_pairs={{0,14},{1,15},{2,12},{3,13},{4,10},{5,11},{6,8},{7,9},{8,6},{9,7},... | collective-permute-start | bytes 282632 | tf_op jit(solution)/shard_map/ppermute | solution.py:390
  20.0 12.1 %collective-permute-start.10 = (f32[184,128]{1,0:T(8,128)S(1)}, f32[184,128]{1,0:T(8,128)S(1)}, u32[]{:S(2)}, u32[]{:S(2)}) collective-permute-start(f32[184,128]{1,0:T(8,128)S(1)} %bitcast.30), channel_id=1, source_target_pairs={{0,15},{1,14},{2,13},{3,12},{4,11},{5,10},{6,9},{7,8},{8,7},{9,6},... | collective-permute-start | bytes 282632 | tf_op jit(solution)/shard_map/ppermute | solution.py:390
  20.8 14.7 %collective-permute-start.7 = (f32[184,128]{1,0:T(8,128)S(1)}, f32[184,128]{1,0:T(8,128)S(1)}, u32[]{:S(2)}, u32[]{:S(2)}) collective-permute-start(f32[184,128]{1,0:T(8,128)S(1)} %bitcast.29), channel_id=1, source_target_pairs={{0,9},{1,8},{2,11},{3,10},{4,13},{5,12},{6,15},{7,14},{8,1},{9,0},... | collective-permute-start | bytes 282632 | tf_op jit(solution)/shard_map/ppermute | solution.py:390
  21.1 16.8 %collective-permute-start.8 = (f32[184,128]{1,0:T(8,128)S(1)}, f32[184,128]{1,0:T(8,128)S(1)}, u32[]{:S(2)}, u32[]{:S(2)}) collective-permute-start(f32[184,128]{1,0:T(8,128)S(1)} %bitcast.28), channel_id=1, source_target_pairs={{0,11},{1,10},{2,9},{3,8},{4,15},{5,14},{6,13},{7,12},{8,3},{9,2},... | collective-permute-start | bytes 282632 | tf_op jit(solution)/shard_map/ppermute | solution.py:390
  25.6 12.4 %collective-permute-start.9 = (f32[184,128]{1,0:T(8,128)S(1)}, f32[184,128]{1,0:T(8,128)S(1)}, u32[]{:S(2)}, u32[]{:S(2)}) collective-permute-start(f32[184,128]{1,0:T(8,128)S(1)} %bitcast.27), channel_id=1, source_target_pairs={{0,13},{1,12},{2,15},{3,14},{4,9},{5,8},{6,11},{7,10},{8,5},{9,4},... | collective-permute-start | bytes 282632 | tf_op jit(solution)/shard_map/ppermute | solution.py:390
  28.3 9.7 %collective-permute-start.11 = (f32[184,128]{1,0:T(8,128)S(1)}, f32[184,128]{1,0:T(8,128)S(1)}, u32[]{:S(2)}, u32[]{:S(2)}) collective-permute-start(f32[184,128]{1,0:T(8,128)S(1)} %bitcast.36), channel_id=1, source_target_pairs={{0,3},{1,2},{2,1},{3,0},{4,7},{5,6},{6,5},{7,4},{8,11},{9,10},{10,... | collective-permute-start | bytes 282632 | tf_op jit(solution)/shard_map/ppermute | solution.py:390
  32.1 7.7 %collective-permute-start.12 = (f32[184,128]{1,0:T(8,128)S(1)}, f32[184,128]{1,0:T(8,128)S(1)}, u32[]{:S(2)}, u32[]{:S(2)}) collective-permute-start(f32[184,128]{1,0:T(8,128)S(1)} %bitcast.33), channel_id=1, source_target_pairs={{0,5},{1,4},{2,7},{3,6},{4,1},{5,0},{6,3},{7,2},{8,13},{9,12},{10,... | collective-permute-start | bytes 282632 | tf_op jit(solution)/shard_map/ppermute | solution.py:390
  35.5 4.3 %collective-permute-start.14 = (f32[184,128]{1,0:T(8,128)S(1)}, f32[184,128]{1,0:T(8,128)S(1)}, u32[]{:S(2)}, u32[]{:S(2)}) collective-permute-start(f32[184,128]{1,0:T(8,128)S(1)} %bitcast.32), channel_id=1, source_target_pairs={{0,1},{1,0},{2,3},{3,2},{4,5},{5,4},{6,7},{7,6},{8,9},{9,8},{10,11... | collective-permute-start | bytes 282632 | tf_op jit(solution)/shard_map/ppermute | solution.py:390
  38.0 5.0 %collective-permute-start.13 = (f32[184,128]{1,0:T(8,128)S(1)}, f32[184,128]{1,0:T(8,128)S(1)}, u32[]{:S(2)}, u32[]{:S(2)}) collective-permute-start(f32[184,128]{1,0:T(8,128)S(1)} %bitcast.31), channel_id=1, source_target_pairs={{0,7},{1,6},{2,5},{3,4},{4,3},{5,2},{6,1},{7,0},{8,15},{9,14},{10,... | collective-permute-start | bytes 282632 | tf_op jit(solution)/shard_map/ppermute | solution.py:390

commit v7 on v6

--- a/solution.py
+++ b/solution.py
@@ -21,10 +21,10 @@
 USED_ROWS = WEIGHT_ROWS + PHASE_ROWS
 ROWS = (USED_ROWS + 7) // 8 * 8
 OCT = SLOTS // 2
-PACKS = ((8, 10, 12), (2, 4, 6), (14, 9, 11, 13, 15), (3, 5, 7, 1, 0))
+PACKS = ((8, 10, 12), (2, 4, 6), (14, 9, 15, 3, 5, 7), (11, 13, 1, 0))
 EVEN_ORDER = (8, 10, 12, 2, 4, 6, 14, 0)
-ODD_ORDER = (9, 11, 13, 15, 3, 5, 7, 1)
-LATE = (7, 1)
+ODD_ORDER = (9, 15, 3, 5, 7, 11, 13, 1)
+LATE = (13, 1)
 
 NODES = np.cos(math.pi * (2.0 * np.arange(CHEB) + 1.0) / (2.0 * CHEB))
 NODES[CHEB // 2] = 0.0

time: 49.9 us -> 48.7 us (0.976)
  waiting for transfers between devices: 10 us -> 9.33 us
    ppermute x15, waiting for transfers between devices: 10 us -> 9.33 us  [send(): lax.ppermute(blocks[step], 'box', [(s, s ^ step) for s in range(SLOTS)])]
  transfers between devices with their start and end apart: 15 -> 15, of which waited for: 6 -> 3; matrix products, arithmetic and copies ran while one was open for 0% -> 0% of each run, Pallas kernels for 14% -> 15%
where the time goes in v7:
time: 48.7 us; the launch traced here: 48.4 us
  starting transfers between devices  24.4 us (50%)
  Pallas kernels  14.7 us (30%)
  waiting for transfers between devices  9.33 us (19%)
    ppermute x15, starting transfers between devices, send(): lax.ppermute(blocks[step], 'box', [(s, s ^ step) for s in range(SLOTS)])  24.4 us
    ppermute x15, waiting for transfers between devices, send(): lax.ppermute(blocks[step], 'box', [(s, s ^ step) for s in range(SLOTS)])  9.33 us
    pallas_call x1, Pallas kernels, combine_odd(): pl.pallas_call(odd_kernel, out_shape=jax.ShapeDtypeStruct((WEIGHT_ROWS *...  6.43 us
    pallas_call x4, Pallas kernels, pack(): pl.pallas_call(functools.partial(pack_kernel, steps, first), out_shape=ou...  4.41 us
    pallas_call x1, Pallas kernels, combine_even(): pl.pallas_call(even_kernel, out_shape=[jax.ShapeDtypeStruct((WEIGHT_ROWS,...  3.82 us
  transfers between devices with their start and end apart: 15, of which 3 were waited for; matrix products, arithmetic and copies ran while one was open for 0% of the time, Pallas kernels for 15%

profile of v7, /device:TPU:0, one launch (start us, length us, event | category | flops | bytes accessed | tf_op | source)
XLA Modules:
  0.0 48.4 jit_solution(6316256700559012640)
XLA Ops:
  0.0 1.2 %pack.4 = (f32[92,2,128]{2,1,0:T(2,128)S(1)}, f32[92,2,128]{2,1,0:T(2,128)S(1)}, f32[92,2,128]{2,1,0:T(2,128)S(1)}, f32[8,2,2048]{2,1,0:T(2,128)S(1)}) custom-call(s32[1]{0:T(128)} %bitcast.me_ref, f32[81,16,2,128]{3,2,1,0:T(2,128)} %bitcast.42, f32[4,3]{1,0:T(4,128)} %refs_0_.1, f32[4,2,2048]{2,1,0:T(2,128)} %refs_1_.1, f32[4,2,2048]{2,1,0:T(2,128)} %refs_2_.1, ...), custom_call_target="tpu_custom_call" | custom-call | flops 1048576 | bytes 1048576 | tf_op jit(solution)/shard_map/pack/pallas_call | solution.py:139
  1.2 5.1 %collective-permute-start.2 = (f32[184,128]{1,0:T(8,128)S(1)}, f32[184,128]{1,0:T(8,128)S(1)}, u32[]{:S(2)}, u32[]{:S(2)}) collective-permute-start(f32[184,128]{1,0:T(8,128)S(1)} %bitcast.41), channel_id=1, source_target_pairs={{0,12},{1,13},{2,14},{3,15},{4,8},{5,9},{6,10},{7,11},{8,4},{9,5},... | collective-permute-start | bytes 282632 | tf_op jit(solution)/shard_map/ppermute | solution.py:390
  6.3 0.4 collective-permute-start.1
  6.7 3.5 %collective-permute-start = (f32[184,128]{1,0:T(8,128)S(1)}, f32[184,128]{1,0:T(8,128)S(1)}, u32[]{:S(2)}, u32[]{:S(2)}) collective-permute-start(f32[184,128]{1,0:T(8,128)S(1)} %bitcast.37), channel_id=1, source_target_pairs={{0,8},{1,9},{2,10},{3,11},{4,12},{5,13},{6,14},{7,15},{8,0},{9,1},... | collective-permute-start | bytes 282632 | tf_op jit(solution)/shard_map/ppermute | solution.py:390
  10.2 1.0 %pack.5 = (f32[92,2,128]{2,1,0:T(2,128)S(1)}, f32[92,2,128]{2,1,0:T(2,128)S(1)}, f32[92,2,128]{2,1,0:T(2,128)S(1)}) custom-call(s32[1]{0:T(128)} %bitcast.me_ref, f32[81,16,2,128]{3,2,1,0:T(2,128)} %bitcast.43, f32[8,2,2048]{2,1,0:T(2,128)S(1)} %get-tuple-element.47.refs_0_), custom_call_target="tpu_custom_call" | custom-call | flops 1048576 | bytes 1048576 | tf_op jit(solution)/shard_map/pack/pallas_call | solution.py:139
  11.2 0.1 collective-permute-start.5
  11.3 2.0 %collective-permute-start.4 = (f32[184,128]{1,0:T(8,128)S(1)}, f32[184,128]{1,0:T(8,128)S(1)}, u32[]{:S(2)}, u32[]{:S(2)}) collective-permute-start(f32[184,128]{1,0:T(8,128)S(1)} %bitcast.38), channel_id=1, source_target_pairs={{0,4},{1,5},{2,6},{3,7},{4,0},{5,1},{6,2},{7,3},{8,12},{9,13},{10,... | collective-permute-start | bytes 282632 | tf_op jit(solution)/shard_map/ppermute | solution.py:390
  13.2 1.2 %pack.6 = (f32[92,2,128]{2,1,0:T(2,128)S(1)}, f32[92,2,128]{2,1,0:T(2,128)S(1)}, f32[92,2,128]{2,1,0:T(2,128)S(1)}, f32[92,2,128]{2,1,0:T(2,128)S(1)}, f32[92,2,...) custom-call(s32[1]{0:T(128)} %bitcast.me_ref, f32[81,16,2,128]{3,2,1,0:T(2,128)} %bitcast.44, ...), custom_call_target="tpu_custom_call" | custom-call | flops 1048576 | bytes 1048576 | tf_op jit(solution)/shard_map/pack/pallas_call | solution.py:139
  14.4 0.0 collective-permute-done.2.refs_2_
  14.4 1.6 %collective-permute-start.3 = (f32[184,128]{1,0:T(8,128)S(1)}, f32[184,128]{1,0:T(8,128)S(1)}, u32[]{:S(2)}, u32[]{:S(2)}) collective-permute-start(f32[184,128]{1,0:T(8,128)S(1)} %bitcast.35), channel_id=1, source_target_pairs={{0,2},{1,3},{2,0},{3,1},{4,6},{5,7},{6,4},{7,5},{8,10},{9,11},{10,... | collective-permute-start | bytes 282632 | tf_op jit(solution)/shard_map/ppermute | solution.py:390
  16.0 2.3 %collective-permute-done.1.refs_1_ = f32[184,128]{1,0:T(8,128)S(1)} collective-permute-done((f32[184,128]{1,0:T(8,128)S(1)}, f32[184,128]{1,0:T(8,128)S(1)}, u32[]{:S(2)}, u32[]{:S(2)}) %collective-permute-start.1) | collective-permute-done | bytes 94240 | tf_op jit(solution)/shard_map/ppermute | solution.py:390
  18.3 1.7 %collective-permute-start.6 = (f32[184,128]{1,0:T(8,128)S(1)}, f32[184,128]{1,0:T(8,128)S(1)}, u32[]{:S(2)}, u32[]{:S(2)}) collective-permute-start(f32[184,128]{1,0:T(8,128)S(1)} %bitcast.36), channel_id=1, source_target_pairs={{0,14},{1,15},{2,12},{3,13},{4,10},{5,11},{6,8},{7,9},{8,6},{9,7},... | collective-permute-start | bytes 282632 | tf_op jit(solution)/shard_map/ppermute | solution.py:390
  20.0 0.0 collective-permute-done.refs_0_
  20.0 0.8 %collective-permute-done.5.refs_5_ = f32[184,128]{1,0:T(8,128)S(1)} collective-permute-done((f32[184,128]{1,0:T(8,128)S(1)}, f32[184,128]{1,0:T(8,128)S(1)}, u32[]{:S(2)}, u32[]{:S(2)}) %collective-permute-start.5) | collective-permute-done | bytes 94240 | tf_op jit(solution)/shard_map/ppermute | solution.py:390
  20.8 2.5 %collective-permute-start.7 = (f32[184,128]{1,0:T(8,128)S(1)}, f32[184,128]{1,0:T(8,128)S(1)}, u32[]{:S(2)}, u32[]{:S(2)}) collective-permute-start(f32[184,128]{1,0:T(8,128)S(1)} %bitcast.30), channel_id=1, source_target_pairs={{0,9},{1,8},{2,11},{3,10},{4,13},{5,12},{6,15},{7,14},{8,1},{9,0},... | collective-permute-start | bytes 282632 | tf_op jit(solution)/shard_map/ppermute | solution.py:390
  23.3 0.0 collective-permute-done.4.refs_4_
  23.3 0.8 %collective-permute-start.8 = (f32[184,128]{1,0:T(8,128)S(1)}, f32[184,128]{1,0:T(8,128)S(1)}, u32[]{:S(2)}, u32[]{:S(2)}) collective-permute-start(f32[184,128]{1,0:T(8,128)S(1)} %bitcast.29), channel_id=1, source_target_pairs={{0,15},{1,14},{2,13},{3,12},{4,11},{5,10},{6,9},{7,8},{8,7},{9,6},... | collective-permute-start | bytes 282632 | tf_op jit(solution)/shard_map/ppermute | solution.py:390
  24.1 1.1 %pack.7 = (f32[92,2,128]{2,1,0:T(2,128)S(1)}, f32[92,2,128]{2,1,0:T(2,128)S(1)}, f32[92,2,128]{2,1,0:T(2,128)S(1)}, f32[92,2,128]{2,1,0:T(2,128)S(1)}) custom-call(s32[1]{0:T(128)} %bitcast.me_ref, f32[81,16,2,128]{3,2,1,0:T(2,128)} %bitcast.45, f32[8,2,2048]{2,1,0:T(2,128)S(1)} %get-tuple-element.47.refs_0_), custom_call_target="tpu_custom_call" | custom-call | flops 1048576 | bytes 1048576 | tf_op jit(solution)/shard_map/pack/pallas_call | solution.py:139
  25.2 0.0 collective-permute-done.3.refs_3_
  25.2 3.0 %collective-permute-start.9 = (f32[184,128]{1,0:T(8,128)S(1)}, f32[184,128]{1,0:T(8,128)S(1)}, u32[]{:S(2)}, u32[]{:S(2)}) collective-permute-start(f32[184,128]{1,0:T(8,128)S(1)} %bitcast.28), channel_id=1, source_target_pairs={{0,3},{1,2},{2,1},{3,0},{4,7},{5,6},{6,5},{7,4},{8,11},{9,10},{10,... | collective-permute-start | bytes 282632 | tf_op jit(solution)/shard_map/ppermute | solution.py:390
  28.2 0.0 collective-permute-done.6.refs_6_
  28.2 0.0 collective-permute-start.10
  28.2 3.8 %combine_even.1 = (f32[162,8,128]{2,1,0:T(8,128)S(1)}, f32[4,8,128]{2,1,0:T(8,128)S(1)}) custom-call(s32[1]{0:T(128)} %bitcast.me_ref, f32[184,128]{1,0:T(8,128)S(1)} %collective-permute-done.refs_0_, f32[184,128]{1,0:T(8,128)S(1)} %collective-permute-done.1.refs_1_, f32[184,128]{1,0:T(8,128)S(1)} %collective-permute-done.2.refs_2_, ...), custom_call_target="tpu_custom_call" | custom-call | flops 41943040 | bytes 12582912 | tf_op jit(solution)/shard_map/combine_even/pallas_call | solution.py:326
  32.0 0.0 collective-permute-done.11.refs_4_
  32.0 1.4 %collective-permute-start.12 = (f32[184,128]{1,0:T(8,128)S(1)}, f32[184,128]{1,0:T(8,128)S(1)}, u32[]{:S(2)}, u32[]{:S(2)}) collective-permute-start(f32[184,128]{1,0:T(8,128)S(1)} %bitcast.34), channel_id=1, source_target_pairs={{0,11},{1,10},{2,9},{3,8},{4,15},{5,14},{6,13},{7,12},{8,3},{9,2},... | collective-permute-start | bytes 282632 | tf_op jit(solution)/shard_map/ppermute | solution.py:390
  33.4 0.1 collective-permute-start.14
  33.5 0.0 collective-permute-done.8.refs_1_
  33.5 2.3 %collective-permute-start.13 = (f32[184,128]{1,0:T(8,128)S(1)}, f32[184,128]{1,0:T(8,128)S(1)}, u32[]{:S(2)}, u32[]{:S(2)}) collective-permute-start(f32[184,128]{1,0:T(8,128)S(1)} %bitcast.32), channel_id=1, source_target_pairs={{0,13},{1,12},{2,15},{3,14},{4,9},{5,8},{6,11},{7,10},{8,5},{9,4},... | collective-permute-start | bytes 282632 | tf_op jit(solution)/shard_map/ppermute | solution.py:390
  35.8 0.0 collective-permute-done.9.refs_2_
  35.8 0.0 collective-permute-done.10.refs_3_
  35.8 6.2 %collective-permute-done.12.refs_5_ = f32[184,128]{1,0:T(8,128)S(1)} collective-permute-done((f32[184,128]{1,0:T(8,128)S(1)}, f32[184,128]{1,0:T(8,128)S(1)}, u32[]{:S(2)}, u32[]{:S(2)}) %collective-permute-start.12) | collective-permute-done | bytes 94240 | tf_op jit(solution)/shard_map/ppermute | solution.py:390
  42.0 6.4 %combine_odd.1 = f32[2592,128]{1,0:T(8,128)} custom-call(s32[1]{0:T(128)} %bitcast.me_ref, f32[162,8,128]{2,1,0:T(8,128)S(1)} %get-tuple-element.49.even_work, f32[4,8,128]{2,1,0:T(8,128)S(1)} %get-tuple-element.54.even_phases, f32[184,128]{1,0:T(8,128)S(1)} %collective-permute-done.7.refs_0_, f32[184,128]{1,0:T(8,128)S(1)} %collective-permute-done.8.refs_1_, ...), custom_call_target="tpu_custom_call" | custom-call | flops 83886080 | bytes 20971520 | tf_op jit(solution)/shard_map/combine_odd/pallas_call | solution.py:348
  (4 shorter events, 0.0 us)
Async XLA Ops:
  1.2 13.2 %collective-permute-start.2 = (f32[184,128]{1,0:T(8,128)S(1)}, f32[184,128]{1,0:T(8,128)S(1)}, u32[]{:S(2)}, u32[]{:S(2)}) collective-permute-start(f32[184,128]{1,0:T(8,128)S(1)} %bitcast.41), channel_id=1, source_target_pairs={{0,12},{1,13},{2,14},{3,15},{4,8},{5,9},{6,10},{7,11},{8,4},{9,5},... | collective-permute-start | bytes 282632 | tf_op jit(solution)/shard_map/ppermute | solution.py:390
  6.3 12.0 %collective-permute-start.1 = (f32[184,128]{1,0:T(8,128)S(1)}, f32[184,128]{1,0:T(8,128)S(1)}, u32[]{:S(2)}, u32[]{:S(2)}) collective-permute-start(f32[184,128]{1,0:T(8,128)S(1)} %bitcast.39), channel_id=1, source_target_pairs={{0,10},{1,11},{2,8},{3,9},{4,14},{5,15},{6,12},{7,13},{8,2},{9,3},... | collective-permute-start | bytes 282632 | tf_op jit(solution)/shard_map/ppermute | solution.py:390
  6.7 13.3 %collective-permute-start = (f32[184,128]{1,0:T(8,128)S(1)}, f32[184,128]{1,0:T(8,128)S(1)}, u32[]{:S(2)}, u32[]{:S(2)}) collective-permute-start(f32[184,128]{1,0:T(8,128)S(1)} %bitcast.37), channel_id=1, source_target_pairs={{0,8},{1,9},{2,10},{3,11},{4,12},{5,13},{6,14},{7,15},{8,0},{9,1},... | collective-permute-start | bytes 282632 | tf_op jit(solution)/shard_map/ppermute | solution.py:390
  11.2 9.6 %collective-permute-start.5 = (f32[184,128]{1,0:T(8,128)S(1)}, f32[184,128]{1,0:T(8,128)S(1)}, u32[]{:S(2)}, u32[]{:S(2)}) collective-permute-start(f32[184,128]{1,0:T(8,128)S(1)} %bitcast.40), channel_id=1, source_target_pairs={{0,6},{1,7},{2,4},{3,5},{4,2},{5,3},{6,0},{7,1},{8,14},{9,15},{10,... | collective-permute-start | bytes 282632 | tf_op jit(solution)/shard_map/ppermute | solution.py:390
  11.3 12.0 %collective-permute-start.4 = (f32[184,128]{1,0:T(8,128)S(1)}, f32[184,128]{1,0:T(8,128)S(1)}, u32[]{:S(2)}, u32[]{:S(2)}) collective-permute-start(f32[184,128]{1,0:T(8,128)S(1)} %bitcast.38), channel_id=1, source_target_pairs={{0,4},{1,5},{2,6},{3,7},{4,0},{5,1},{6,2},{7,3},{8,12},{9,13},{10,... | collective-permute-start | bytes 282632 | tf_op jit(solution)/shard_map/ppermute | solution.py:390
  14.4 10.7 %collective-permute-start.3 = (f32[184,128]{1,0:T(8,128)S(1)}, f32[184,128]{1,0:T(8,128)S(1)}, u32[]{:S(2)}, u32[]{:S(2)}) collective-permute-start(f32[184,128]{1,0:T(8,128)S(1)} %bitcast.35), channel_id=1, source_target_pairs={{0,2},{1,3},{2,0},{3,1},{4,6},{5,7},{6,4},{7,5},{8,10},{9,11},{10,... | collective-permute-start | bytes 282632 | tf_op jit(solution)/shard_map/ppermute | solution.py:390
  18.3 9.9 %collective-permute-start.6 = (f32[184,128]{1,0:T(8,128)S(1)}, f32[184,128]{1,0:T(8,128)S(1)}, u32[]{:S(2)}, u32[]{:S(2)}) collective-permute-start(f32[184,128]{1,0:T(8,128)S(1)} %bitcast.36), channel_id=1, source_target_pairs={{0,14},{1,15},{2,12},{3,13},{4,10},{5,11},{6,8},{7,9},{8,6},{9,7},... | collective-permute-start | bytes 282632 | tf_op jit(solution)/shard_map/ppermute | solution.py:390
  20.0 12.0 %collective-permute-start.11 = (f32[184,128]{1,0:T(8,128)S(1)}, f32[184,128]{1,0:T(8,128)S(1)}, u32[]{:S(2)}, u32[]{:S(2)}) collective-permute-start(f32[184,128]{1,0:T(8,128)S(1)} %bitcast.31), channel_id=1, source_target_pairs={{0,7},{1,6},{2,5},{3,4},{4,3},{5,2},{6,1},{7,0},{8,15},{9,14},{10,... | collective-permute-start | bytes 282632 | tf_op jit(solution)/shard_map/ppermute | solution.py:390
  20.8 12.6 %collective-permute-start.7 = (f32[184,128]{1,0:T(8,128)S(1)}, f32[184,128]{1,0:T(8,128)S(1)}, u32[]{:S(2)}, u32[]{:S(2)}) collective-permute-start(f32[184,128]{1,0:T(8,128)S(1)} %bitcast.30), channel_id=1, source_target_pairs={{0,9},{1,8},{2,11},{3,10},{4,13},{5,12},{6,15},{7,14},{8,1},{9,0},... | collective-permute-start | bytes 282632 | tf_op jit(solution)/shard_map/ppermute | solution.py:390
  23.3 10.2 %collective-permute-start.8 = (f32[184,128]{1,0:T(8,128)S(1)}, f32[184,128]{1,0:T(8,128)S(1)}, u32[]{:S(2)}, u32[]{:S(2)}) collective-permute-start(f32[184,128]{1,0:T(8,128)S(1)} %bitcast.29), channel_id=1, source_target_pairs={{0,15},{1,14},{2,13},{3,12},{4,11},{5,10},{6,9},{7,8},{8,7},{9,6},... | collective-permute-start | bytes 282632 | tf_op jit(solution)/shard_map/ppermute | solution.py:390
  25.2 10.6 %collective-permute-start.9 = (f32[184,128]{1,0:T(8,128)S(1)}, f32[184,128]{1,0:T(8,128)S(1)}, u32[]{:S(2)}, u32[]{:S(2)}) collective-permute-start(f32[184,128]{1,0:T(8,128)S(1)} %bitcast.28), channel_id=1, source_target_pairs={{0,3},{1,2},{2,1},{3,0},{4,7},{5,6},{6,5},{7,4},{8,11},{9,10},{10,... | collective-permute-start | bytes 282632 | tf_op jit(solution)/shard_map/ppermute | solution.py:390
  28.2 7.6 %collective-permute-start.10 = (f32[184,128]{1,0:T(8,128)S(1)}, f32[184,128]{1,0:T(8,128)S(1)}, u32[]{:S(2)}, u32[]{:S(2)}) collective-permute-start(f32[184,128]{1,0:T(8,128)S(1)} %bitcast.27), channel_id=1, source_target_pairs={{0,5},{1,4},{2,7},{3,6},{4,1},{5,0},{6,3},{7,2},{8,13},{9,12},{10,... | collective-permute-start | bytes 282632 | tf_op jit(solution)/shard_map/ppermute | solution.py:390
  32.0 10.0 %collective-permute-start.12 = (f32[184,128]{1,0:T(8,128)S(1)}, f32[184,128]{1,0:T(8,128)S(1)}, u32[]{:S(2)}, u32[]{:S(2)}) collective-permute-start(f32[184,128]{1,0:T(8,128)S(1)} %bitcast.34), channel_id=1, source_target_pairs={{0,11},{1,10},{2,9},{3,8},{4,15},{5,14},{6,13},{7,12},{8,3},{9,2},... | collective-permute-start | bytes 282632 | tf_op jit(solution)/shard_map/ppermute | solution.py:390
  33.4 8.6 %collective-permute-start.14 = (f32[184,128]{1,0:T(8,128)S(1)}, f32[184,128]{1,0:T(8,128)S(1)}, u32[]{:S(2)}, u32[]{:S(2)}) collective-permute-start(f32[184,128]{1,0:T(8,128)S(1)} %bitcast.33), channel_id=1, source_target_pairs={{0,1},{1,0},{2,3},{3,2},{4,5},{5,4},{6,7},{7,6},{8,9},{9,8},{10,11... | collective-permute-start | bytes 282632 | tf_op jit(solution)/shard_map/ppermute | solution.py:390
  33.5 8.5 %collective-permute-start.13 = (f32[184,128]{1,0:T(8,128)S(1)}, f32[184,128]{1,0:T(8,128)S(1)}, u32[]{:S(2)}, u32[]{:S(2)}) collective-permute-start(f32[184,128]{1,0:T(8,128)S(1)} %bitcast.32), channel_id=1, source_target_pairs={{0,13},{1,12},{2,15},{3,14},{4,9},{5,8},{6,11},{7,10},{8,5},{9,4},... | collective-permute-start | bytes 282632 | tf_op jit(solution)/shard_map/ppermute | solution.py:390

commit v8 on v7

--- a/solution.py
+++ b/solution.py
@@ -21,10 +21,11 @@
 USED_ROWS = WEIGHT_ROWS + PHASE_ROWS
 ROWS = (USED_ROWS + 7) // 8 * 8
 OCT = SLOTS // 2
-PACKS = ((8, 10, 12), (2, 4, 6), (14, 9, 15, 3, 5, 7), (11, 13, 1, 0))
-EVEN_ORDER = (8, 10, 12, 2, 4, 6, 14, 0)
-ODD_ORDER = (9, 15, 3, 5, 7, 11, 13, 1)
-LATE = (13, 1)
+PACKS = ((12, 4, 6, 10), (2, 14, 9, 15, 3, 11, 8, 7, 13, 5, 1, 0))
+SENDS = (8, 12, 4, 6, 2, 14, 15, 3, 11, 7, 13, 5, 1, 10, 9)
+WAITS = {9: 4, 1: 11}
+EVEN_ORDER = (8, 4, 2, 12, 10, 6, 14, 0)
+ODD_ORDER = (1, 3, 5, 11, 9, 15, 13, 7)
 
 NODES = np.cos(math.pi * (2.0 * np.arange(CHEB) + 1.0) / (2.0 * CHEB))
 NODES[CHEB // 2] = 0.0
@@ -385,22 +386,16 @@
         blocks.update(packed)
     blocks = {step: block.reshape(ROWS, LANES) for step, block in blocks.items()}
     if direct:
-
-        def send(step):
-            return lax.ppermute(blocks[step], "box", [(s, s ^ step) for s in range(SLOTS)])
-
-        for step in EVEN_ORDER + ODD_ORDER:
-            if step and step not in LATE:
-                blocks[step] = send(step)
+        for step in SENDS:
+            if step in WAITS:
+                earlier = WAITS[step]
+                blocks[step], blocks[earlier] = lax.optimization_barrier((blocks[step], blocks[earlier]))
+            blocks[step] = lax.ppermute(blocks[step], "box", [(s, s ^ step) for s in range(SLOTS)])
     else:
         whole = jnp.concatenate([blocks[step] for step in range(SLOTS)], axis=1)
         whole = lax.all_to_all(whole, "box", split_axis=1, concat_axis=1, tiled=True)
         blocks = [whole[:, s * LANES : (s + 1) * LANES] for s in range(SLOTS)]
-    even = list(combine_even(me, [blocks[step] for step in EVEN_ORDER]))
-    if direct:
-        for step in LATE:
-            even[1], blocks[step] = lax.optimization_barrier((even[1], blocks[step]))
-            blocks[step] = send(step)
+    even = combine_even(me, [blocks[step] for step in EVEN_ORDER])
     rows = combine_odd(me, even, [blocks[step] for step in ODD_ORDER])
     return rows.reshape(POINTS, SLOTS, 2, LANES).transpose(2, 0, 1, 3).reshape(2, POINTS, SLOTS * LANES)
 

time: 48.7 us -> 47.1 us (0.967)
  starting transfers between devices: 24.4 us -> 26.6 us
  waiting for transfers between devices: 9.33 us -> 7.32 us
  Pallas kernels: 14.7 us -> 12.9 us
    ppermute x15, starting transfers between devices: 24.4 us -> 26.6 us  [on_device(): lax.ppermute(blocks[step], 'box', [(s, s ^ step) for s in range(SLOTS)])]
    ppermute x15, waiting for transfers between devices: 9.33 us -> 7.32 us  [on_device(): lax.ppermute(blocks[step], 'box', [(s, s ^ step) for s in range(SLOTS)])]
    pallas_call x4 -> x2, Pallas kernels: 4.41 us -> 2.68 us  [pack(): pl.pallas_call(functools.partial(pack_kernel, steps, first), out_shape=ou...]
  transfers between devices with their start and end apart: 15 -> 15, of which waited for: 3 -> 3; matrix products, arithmetic and copies ran while one was open for 0% -> 0% of each run, Pallas kernels for 15% -> 11%
where the time goes in v8:
time: 47.1 us; the launch traced here: 46.9 us
  starting transfers between devices  26.6 us (56%)
  Pallas kernels  12.9 us (27%)
  waiting for transfers between devices  7.32 us (16%)
    ppermute x15, starting transfers between devices, on_device(): lax.ppermute(blocks[step], 'box', [(s, s ^ step) for s in range(SLOTS)])  26.6 us
    ppermute x15, waiting for transfers between devices, on_device(): lax.ppermute(blocks[step], 'box', [(s, s ^ step) for s in range(SLOTS)])  7.32 us
    pallas_call x1, Pallas kernels, combine_odd(): pl.pallas_call(odd_kernel, out_shape=jax.ShapeDtypeStruct((WEIGHT_ROWS *...  6.43 us
    pallas_call x1, Pallas kernels, combine_even(): pl.pallas_call(even_kernel, out_shape=[jax.ShapeDtypeStruct((WEIGHT_ROWS,...  3.82 us
    pallas_call x2, Pallas kernels, pack(): pl.pallas_call(functools.partial(pack_kernel, steps, first), out_shape=ou...  2.68 us
  transfers between devices with their start and end apart: 15, of which 3 were waited for; matrix products, arithmetic and copies ran while one was open for 0% of the time, Pallas kernels for 11%

profile of v8, /device:TPU:0, one launch (start us, length us, event | category | flops | bytes accessed | tf_op | source)
XLA Modules:
  0.0 46.9 jit_solution(10219338093084448166)
XLA Ops:
  0.0 1.2 %pack.2 = (f32[92,2,128]{2,1,0:T(2,128)S(1)}, f32[92,2,128]{2,1,0:T(2,128)S(1)}, f32[92,2,128]{2,1,0:T(2,128)S(1)}, f32[92,2,128]{2,1,0:T(2,128)S(1)}, f32[8,2,2048]{2,1,0:T(2,128)S(1)}) custom-call(s32[1]{0:T(128)} %bitcast.me_ref, f32[81,16,2,128]{3,2,1,0:T(2,128)} %bitcast.42, f32[4,3]{1,0:T(4,128)} %refs_0_.1, f32[4,2,2048]{2,1,0:T(2,128)} %refs_1_.1, ...), custom_call_target="tpu_custom_call" | custom-call | flops 1048576 | bytes 1048576 | tf_op jit(solution)/shard_map/pack/pallas_call | solution.py:140
  1.2 5.1 %collective-permute-start.4 = (f32[184,128]{1,0:T(8,128)S(1)}, f32[184,128]{1,0:T(8,128)S(1)}, u32[]{:S(2)}, u32[]{:S(2)}) collective-permute-start(f32[184,128]{1,0:T(8,128)S(1)} %bitcast.41), channel_id=1, source_target_pairs={{0,10},{1,11},{2,8},{3,9},{4,14},{5,15},{6,12},{7,13},{8,2},{9,3},... | collective-permute-start | bytes 282632 | tf_op jit(solution)/shard_map/ppermute | solution.py:393
  6.3 1.6 %collective-permute-start.1 = (f32[184,128]{1,0:T(8,128)S(1)}, f32[184,128]{1,0:T(8,128)S(1)}, u32[]{:S(2)}, u32[]{:S(2)}) collective-permute-start(f32[184,128]{1,0:T(8,128)S(1)} %bitcast.40), channel_id=1, source_target_pairs={{0,4},{1,5},{2,6},{3,7},{4,0},{5,1},{6,2},{7,3},{8,12},{9,13},{10,... | collective-permute-start | bytes 282632 | tf_op jit(solution)/shard_map/ppermute | solution.py:393
  7.9 0.2 collective-permute-start.3
  8.1 0.6 %collective-permute-start.5 = (f32[184,128]{1,0:T(8,128)S(1)}, f32[184,128]{1,0:T(8,128)S(1)}, u32[]{:S(2)}, u32[]{:S(2)}) collective-permute-start(f32[184,128]{1,0:T(8,128)S(1)} %bitcast.36), channel_id=1, source_target_pairs={{0,6},{1,7},{2,4},{3,5},{4,2},{5,3},{6,0},{7,1},{8,14},{9,15},{10,... | collective-permute-start | bytes 282632 | tf_op jit(solution)/shard_map/ppermute | solution.py:393
  8.7 1.4 %pack.3 = (f32[92,2,128]{2,1,0:T(2,128)S(1)}, f32[92,2,128]{2,1,0:T(2,128)S(1)}, f32[92,2,128]{2,1,0:T(2,128)S(1)}, f32[92,2,128]{2,1,0:T(2,128)S(1)}, f32[92,2,...) custom-call(s32[1]{0:T(128)} %bitcast.me_ref, ...), custom_call_target="tpu_custom_call" | custom-call | flops 1048576 | bytes 1048576 | tf_op jit(solution)/shard_map/pack/pallas_call | solution.py:140
  10.2 2.8 %collective-permute-start.7 = (f32[184,128]{1,0:T(8,128)S(1)}, f32[184,128]{1,0:T(8,128)S(1)}, u32[]{:S(2)}, u32[]{:S(2)}) collective-permute-start(f32[184,128]{1,0:T(8,128)S(1)} %bitcast.39), channel_id=1, source_target_pairs={{0,11},{1,10},{2,9},{3,8},{4,15},{5,14},{6,13},{7,12},{8,3},{9,2},... | collective-permute-start | bytes 282632 | tf_op jit(solution)/shard_map/ppermute | solution.py:393
  13.0 0.0 collective-permute-done.4.refs_4_
  13.0 0.8 %collective-permute-start = (f32[184,128]{1,0:T(8,128)S(1)}, f32[184,128]{1,0:T(8,128)S(1)}, u32[]{:S(2)}, u32[]{:S(2)}) collective-permute-start(f32[184,128]{1,0:T(8,128)S(1)} %bitcast.37), channel_id=1, source_target_pairs={{0,8},{1,9},{2,10},{3,11},{4,12},{5,13},{6,14},{7,15},{8,0},{9,1},... | collective-permute-start | bytes 282632 | tf_op jit(solution)/shard_map/ppermute | solution.py:393
  13.8 0.0 collective-permute-done.1.refs_1_
  13.8 1.5 %collective-permute-start.2 = (f32[184,128]{1,0:T(8,128)S(1)}, f32[184,128]{1,0:T(8,128)S(1)}, u32[]{:S(2)}, u32[]{:S(2)}) collective-permute-start(f32[184,128]{1,0:T(8,128)S(1)} %bitcast.35), channel_id=1, source_target_pairs={{0,2},{1,3},{2,0},{3,1},{4,6},{5,7},{6,4},{7,5},{8,10},{9,11},{10,... | collective-permute-start | bytes 282632 | tf_op jit(solution)/shard_map/ppermute | solution.py:393
  15.3 0.0 collective-permute-done.3.refs_3_
  15.3 2.2 %collective-permute-start.6 = (f32[184,128]{1,0:T(8,128)S(1)}, f32[184,128]{1,0:T(8,128)S(1)}, u32[]{:S(2)}, u32[]{:S(2)}) collective-permute-start(f32[184,128]{1,0:T(8,128)S(1)} %bitcast.34), channel_id=1, source_target_pairs={{0,14},{1,15},{2,12},{3,13},{4,10},{5,11},{6,8},{7,9},{8,6},{9,7},... | collective-permute-start | bytes 282632 | tf_op jit(solution)/shard_map/ppermute | solution.py:393
  17.5 0.0 collective-permute-done.5.refs_5_
  17.5 0.5 collective-permute-start.9
  18.0 2.3 %collective-permute-done.7.refs_3_ = f32[184,128]{1,0:T(8,128)S(1)} collective-permute-done((f32[184,128]{1,0:T(8,128)S(1)}, f32[184,128]{1,0:T(8,128)S(1)}, u32[]{:S(2)}, u32[]{:S(2)}) %collective-permute-start.7) | collective-permute-done | bytes 94240 | tf_op jit(solution)/shard_map/ppermute | solution.py:393
  20.3 3.1 %collective-permute-start.10 = (f32[184,128]{1,0:T(8,128)S(1)}, f32[184,128]{1,0:T(8,128)S(1)}, u32[]{:S(2)}, u32[]{:S(2)}) collective-permute-start(f32[184,128]{1,0:T(8,128)S(1)} %bitcast.32), channel_id=1, source_target_pairs={{0,5},{1,4},{2,7},{3,6},{4,1},{5,0},{6,3},{7,2},{8,13},{9,12},{10,... | collective-permute-start | bytes 282632 | tf_op jit(solution)/shard_map/ppermute | solution.py:393
  23.5 1.9 %collective-permute-done.refs_0_ = f32[184,128]{1,0:T(8,128)S(1)} collective-permute-done((f32[184,128]{1,0:T(8,128)S(1)}, f32[184,128]{1,0:T(8,128)S(1)}, u32[]{:S(2)}, u32[]{:S(2)}) %collective-permute-start) | collective-permute-done | bytes 94240 | tf_op jit(solution)/shard_map/ppermute | solution.py:393
  25.4 2.9 %collective-permute-start.12 = (f32[184,128]{1,0:T(8,128)S(1)}, f32[184,128]{1,0:T(8,128)S(1)}, u32[]{:S(2)}, u32[]{:S(2)}) collective-permute-start(f32[184,128]{1,0:T(8,128)S(1)} %bitcast.31), channel_id=1, source_target_pairs={{0,15},{1,14},{2,13},{3,12},{4,11},{5,10},{6,9},{7,8},{8,7},{9,6},... | collective-permute-start | bytes 282632 | tf_op jit(solution)/shard_map/ppermute | solution.py:393
  28.2 1.4 %collective-permute-start.13 = (f32[184,128]{1,0:T(8,128)S(1)}, f32[184,128]{1,0:T(8,128)S(1)}, u32[]{:S(2)}, u32[]{:S(2)}) collective-permute-start(f32[184,128]{1,0:T(8,128)S(1)} %bitcast.30), channel_id=1, source_target_pairs={{0,13},{1,12},{2,15},{3,14},{4,9},{5,8},{6,11},{7,10},{8,5},{9,4},... | collective-permute-start | bytes 282632 | tf_op jit(solution)/shard_map/ppermute | solution.py:393
  29.6 0.0 collective-permute-done.6.refs_6_
  29.6 0.0 collective-permute-start.14
  29.6 0.0 collective-permute-done.9.refs_1_
  29.6 3.9 %collective-permute-start.11 = (f32[184,128]{1,0:T(8,128)S(1)}, f32[184,128]{1,0:T(8,128)S(1)}, u32[]{:S(2)}, u32[]{:S(2)}) collective-permute-start(f32[184,128]{1,0:T(8,128)S(1)} %bitcast.28), channel_id=1, source_target_pairs={{0,9},{1,8},{2,11},{3,10},{4,13},{5,12},{6,15},{7,14},{8,1},{9,0},... | collective-permute-start | bytes 282632 | tf_op jit(solution)/shard_map/ppermute | solution.py:393
  33.6 0.0 collective-permute-done.10.refs_2_
  33.6 0.0 collective-permute-start.8
  33.6 3.8 %combine_even.1 = (f32[162,8,128]{2,1,0:T(8,128)S(1)}, f32[4,8,128]{2,1,0:T(8,128)S(1)}) custom-call(s32[1]{0:T(128)} %bitcast.me_ref, f32[184,128]{1,0:T(8,128)S(1)} %collective-permute-done.refs_0_, f32[184,128]{1,0:T(8,128)S(1)} %collective-permute-done.1.refs_1_, f32[184,128]{1,0:T(8,128)S(1)} %collective-permute-done.2.refs_2_, ...), custom_call_target="tpu_custom_call" | custom-call | flops 41943040 | bytes 12582912 | tf_op jit(solution)/shard_map/combine_even/pallas_call | solution.py:327
  37.4 0.0 collective-permute-done.12.refs_5_
  37.4 0.0 collective-permute-done.14.refs_7_
  37.4 3.0 %collective-permute-done.11.refs_4_ = f32[184,128]{1,0:T(8,128)S(1)} collective-permute-done((f32[184,128]{1,0:T(8,128)S(1)}, f32[184,128]{1,0:T(8,128)S(1)}, u32[]{:S(2)}, u32[]{:S(2)}) %collective-permute-start.11) | collective-permute-done | bytes 94240 | tf_op jit(solution)/shard_map/ppermute | solution.py:393
  40.5 0.0 collective-permute-done.8.refs_0_
  40.5 6.4 %combine_odd.1 = f32[2592,128]{1,0:T(8,128)} custom-call(s32[1]{0:T(128)} %bitcast.me_ref, f32[162,8,128]{2,1,0:T(8,128)S(1)} %get-tuple-element.43.even_work, f32[4,8,128]{2,1,0:T(8,128)S(1)} %get-tuple-element.44.even_phases, f32[184,128]{1,0:T(8,128)S(1)} %collective-permute-done.8.refs_0_, f32[184,128]{1,0:T(8,128)S(1)} %collective-permute-done.9.refs_1_, ...), custom_call_target="tpu_custom_call" | custom-call | flops 83886080 | bytes 20971520 | tf_op jit(solution)/shard_map/combine_odd/pallas_call | solution.py:349
  (2 shorter events, 0.0 us)
Async XLA Ops:
  1.2 11.8 %collective-permute-start.4 = (f32[184,128]{1,0:T(8,128)S(1)}, f32[184,128]{1,0:T(8,128)S(1)}, u32[]{:S(2)}, u32[]{:S(2)}) collective-permute-start(f32[184,128]{1,0:T(8,128)S(1)} %bitcast.41), channel_id=1, source_target_pairs={{0,10},{1,11},{2,8},{3,9},{4,14},{5,15},{6,12},{7,13},{8,2},{9,3},... | collective-permute-start | bytes 282632 | tf_op jit(solution)/shard_map/ppermute | solution.py:393
  6.3 7.5 %collective-permute-start.1 = (f32[184,128]{1,0:T(8,128)S(1)}, f32[184,128]{1,0:T(8,128)S(1)}, u32[]{:S(2)}, u32[]{:S(2)}) collective-permute-start(f32[184,128]{1,0:T(8,128)S(1)} %bitcast.40), channel_id=1, source_target_pairs={{0,4},{1,5},{2,6},{3,7},{4,0},{5,1},{6,2},{7,3},{8,12},{9,13},{10,... | collective-permute-start | bytes 282632 | tf_op jit(solution)/shard_map/ppermute | solution.py:393
  7.9 7.5 %collective-permute-start.3 = (f32[184,128]{1,0:T(8,128)S(1)}, f32[184,128]{1,0:T(8,128)S(1)}, u32[]{:S(2)}, u32[]{:S(2)}) collective-permute-start(f32[184,128]{1,0:T(8,128)S(1)} %bitcast.38), channel_id=1, source_target_pairs={{0,12},{1,13},{2,14},{3,15},{4,8},{5,9},{6,10},{7,11},{8,4},{9,5},... | collective-permute-start | bytes 282632 | tf_op jit(solution)/shard_map/ppermute | solution.py:393
  8.1 9.4 %collective-permute-start.5 = (f32[184,128]{1,0:T(8,128)S(1)}, f32[184,128]{1,0:T(8,128)S(1)}, u32[]{:S(2)}, u32[]{:S(2)}) collective-permute-start(f32[184,128]{1,0:T(8,128)S(1)} %bitcast.36), channel_id=1, source_target_pairs={{0,6},{1,7},{2,4},{3,5},{4,2},{5,3},{6,0},{7,1},{8,14},{9,15},{10,... | collective-permute-start | bytes 282632 | tf_op jit(solution)/shard_map/ppermute | solution.py:393
  10.2 10.1 %collective-permute-start.7 = (f32[184,128]{1,0:T(8,128)S(1)}, f32[184,128]{1,0:T(8,128)S(1)}, u32[]{:S(2)}, u32[]{:S(2)}) collective-permute-start(f32[184,128]{1,0:T(8,128)S(1)} %bitcast.39), channel_id=1, source_target_pairs={{0,11},{1,10},{2,9},{3,8},{4,15},{5,14},{6,13},{7,12},{8,3},{9,2},... | collective-permute-start | bytes 282632 | tf_op jit(solution)/shard_map/ppermute | solution.py:393
  13.0 12.4 %collective-permute-start = (f32[184,128]{1,0:T(8,128)S(1)}, f32[184,128]{1,0:T(8,128)S(1)}, u32[]{:S(2)}, u32[]{:S(2)}) collective-permute-start(f32[184,128]{1,0:T(8,128)S(1)} %bitcast.37), channel_id=1, source_target_pairs={{0,8},{1,9},{2,10},{3,11},{4,12},{5,13},{6,14},{7,15},{8,0},{9,1},... | collective-permute-start | bytes 282632 | tf_op jit(solution)/shard_map/ppermute | solution.py:393
  13.8 14.4 %collective-permute-start.2 = (f32[184,128]{1,0:T(8,128)S(1)}, f32[184,128]{1,0:T(8,128)S(1)}, u32[]{:S(2)}, u32[]{:S(2)}) collective-permute-start(f32[184,128]{1,0:T(8,128)S(1)} %bitcast.35), channel_id=1, source_target_pairs={{0,2},{1,3},{2,0},{3,1},{4,6},{5,7},{6,4},{7,5},{8,10},{9,11},{10,... | collective-permute-start | bytes 282632 | tf_op jit(solution)/shard_map/ppermute | solution.py:393
  15.3 14.3 %collective-permute-start.6 = (f32[184,128]{1,0:T(8,128)S(1)}, f32[184,128]{1,0:T(8,128)S(1)}, u32[]{:S(2)}, u32[]{:S(2)}) collective-permute-start(f32[184,128]{1,0:T(8,128)S(1)} %bitcast.34), channel_id=1, source_target_pairs={{0,14},{1,15},{2,12},{3,13},{4,10},{5,11},{6,8},{7,9},{8,6},{9,7},... | collective-permute-start | bytes 282632 | tf_op jit(solution)/shard_map/ppermute | solution.py:393
  17.5 12.1 %collective-permute-start.9 = (f32[184,128]{1,0:T(8,128)S(1)}, f32[184,128]{1,0:T(8,128)S(1)}, u32[]{:S(2)}, u32[]{:S(2)}) collective-permute-start(f32[184,128]{1,0:T(8,128)S(1)} %bitcast.33), channel_id=1, source_target_pairs={{0,3},{1,2},{2,1},{3,0},{4,7},{5,6},{6,5},{7,4},{8,11},{9,10},{10,... | collective-permute-start | bytes 282632 | tf_op jit(solution)/shard_map/ppermute | solution.py:393
  20.3 13.3 %collective-permute-start.10 = (f32[184,128]{1,0:T(8,128)S(1)}, f32[184,128]{1,0:T(8,128)S(1)}, u32[]{:S(2)}, u32[]{:S(2)}) collective-permute-start(f32[184,128]{1,0:T(8,128)S(1)} %bitcast.32), channel_id=1, source_target_pairs={{0,5},{1,4},{2,7},{3,6},{4,1},{5,0},{6,3},{7,2},{8,13},{9,12},{10,... | collective-permute-start | bytes 282632 | tf_op jit(solution)/shard_map/ppermute | solution.py:393
  25.4 12.0 %collective-permute-start.12 = (f32[184,128]{1,0:T(8,128)S(1)}, f32[184,128]{1,0:T(8,128)S(1)}, u32[]{:S(2)}, u32[]{:S(2)}) collective-permute-start(f32[184,128]{1,0:T(8,128)S(1)} %bitcast.31), channel_id=1, source_target_pairs={{0,15},{1,14},{2,13},{3,12},{4,11},{5,10},{6,9},{7,8},{8,7},{9,6},... | collective-permute-start | bytes 282632 | tf_op jit(solution)/shard_map/ppermute | solution.py:393
  28.2 9.2 %collective-permute-start.13 = (f32[184,128]{1,0:T(8,128)S(1)}, f32[184,128]{1,0:T(8,128)S(1)}, u32[]{:S(2)}, u32[]{:S(2)}) collective-permute-start(f32[184,128]{1,0:T(8,128)S(1)} %bitcast.30), channel_id=1, source_target_pairs={{0,13},{1,12},{2,15},{3,14},{4,9},{5,8},{6,11},{7,10},{8,5},{9,4},... | collective-permute-start | bytes 282632 | tf_op jit(solution)/shard_map/ppermute | solution.py:393
  29.6 7.8 %collective-permute-start.14 = (f32[184,128]{1,0:T(8,128)S(1)}, f32[184,128]{1,0:T(8,128)S(1)}, u32[]{:S(2)}, u32[]{:S(2)}) collective-permute-start(f32[184,128]{1,0:T(8,128)S(1)} %bitcast.29), channel_id=1, source_target_pairs={{0,7},{1,6},{2,5},{3,4},{4,3},{5,2},{6,1},{7,0},{8,15},{9,14},{10,... | collective-permute-start | bytes 282632 | tf_op jit(solution)/shard_map/ppermute | solution.py:393
  29.6 10.8 %collective-permute-start.11 = (f32[184,128]{1,0:T(8,128)S(1)}, f32[184,128]{1,0:T(8,128)S(1)}, u32[]{:S(2)}, u32[]{:S(2)}) collective-permute-start(f32[184,128]{1,0:T(8,128)S(1)} %bitcast.28), channel_id=1, source_target_pairs={{0,9},{1,8},{2,11},{3,10},{4,13},{5,12},{6,15},{7,14},{8,1},{9,0},... | collective-permute-start | bytes 282632 | tf_op jit(solution)/shard_map/ppermute | solution.py:393
  33.6 6.9 %collective-permute-start.8 = (f32[184,128]{1,0:T(8,128)S(1)}, f32[184,128]{1,0:T(8,128)S(1)}, u32[]{:S(2)}, u32[]{:S(2)}) collective-permute-start(f32[184,128]{1,0:T(8,128)S(1)} %bitcast.27), channel_id=1, source_target_pairs={{0,1},{1,0},{2,3},{3,2},{4,5},{5,4},{6,7},{7,6},{8,9},{9,8},{10,11... | collective-permute-start | bytes 282632 | tf_op jit(solution)/shard_map/ppermute | solution.py:393

commit v9 on v8

--- a/solution.py
+++ b/solution.py
@@ -18,8 +18,7 @@
 LANES = 128
 WEIGHT_ROWS = 2 * POINTS
 PHASE_ROWS = 4 * LEVELS
-USED_ROWS = WEIGHT_ROWS + PHASE_ROWS
-ROWS = (USED_ROWS + 7) // 8 * 8
+ROWS = WEIGHT_ROWS + PHASE_ROWS
 OCT = SLOTS // 2
 PACKS = ((12, 4, 6, 10), (2, 14, 9, 15, 3, 11, 8, 7, 13, 5, 1, 0))
 SENDS = (8, 12, 4, 6, 2, 14, 15, 3, 11, 7, 13, 5, 1, 10, 9)
@@ -118,8 +117,7 @@
     if first:
         phase_kernel(*small, phases_ref, *scratch)
     for slot, out in zip(slots, outs):
-        out[POINTS : USED_ROWS // 2] = phases_ref[:, :, pl.ds(pl.multiple_of(slot * LANES, LANES), LANES)]
-        out[USED_ROWS // 2 :] = jnp.zeros(((ROWS - USED_ROWS) // 2, 2, LANES), jnp.float32)
+        out[POINTS:] = phases_ref[:, :, pl.ds(pl.multiple_of(slot * LANES, LANES), LANES)]
     for copy in copies:
         copy.wait()
 
@@ -154,22 +152,56 @@
     return dict(zip(steps, arrays)), phases
 
 
+def turn_both_ways(base, step):
+    cc, ss = base[0] * step[0], base[1] * step[1]
+    sc, cs = base[1] * step[0], base[0] * step[1]
+    return (cc - ss, sc + cs), (cc + ss, sc - cs)
+
+
 def level_factors(level, phases, parent_ref, child_ref, common_ref):
     constant, linear, quadratic, other = phases
+    mid = CHEB // 2
+
+    def put(ref, index, pair):
+        ref[index + (0,)], ref[index + (1,)] = pair
+
+    def norm(turns):
+        cosine, sine = cos_sin_turns(turns)
+        return cosine * cosine + sine * sine
+
+    common_ref[mid] = jnp.ones_like(constant)
+    for t in range(mid):
+        node = float(NODES[t])
+        if level % 2 == 0:
+            common_ref[t] = common_ref[CHEB - 1 - t] = norm(node * other)
+        else:
+            common_ref[t] = norm(node * (linear + node * quadratic))
+            common_ref[CHEB - 1 - t] = norm(node * (node * quadratic - linear))
     if level % 2 == 0:
-        split = lambda x: constant + x * (linear + x * quadratic)
-        common = lambda x: x * other
-    else:
-        split = lambda x: constant + x * other
-        common = lambda x: x * (linear + x * quadratic)
-    for t in range(CHEB):
-        node = float(NODES[t])
-        parent_ref[t, 0], parent_ref[t, 1] = cos_sin_turns(split(node))
+        for t in range(CHEB):
+            node = float(NODES[t])
+            put(parent_ref, (t,), cos_sin_turns(constant + node * (linear + node * quadratic)))
+            for child in range(2):
+                shifted = (node + 2.0 * child - 1.0) / 2.0
+                pair = cos_sin_turns(constant + shifted * (linear + shifted * quadratic))
+                put(child_ref, (child, t), pair)
+        return
+    center = cos_sin_turns(constant)
+    centers = [cos_sin_turns(constant + (child - 0.5) * other) for child in range(2)]
+    put(parent_ref, (mid,), center)
+    for child in range(2):
+        put(child_ref, (child, mid), centers[child])
+    for t in range(mid):
+        half_step = cos_sin_turns((0.5 * float(NODES[t])) * other)
         for child in range(2):
-            shifted = (node + 2.0 * child - 1.0) / 2.0
-            child_ref[child, t, 0], child_ref[child, t, 1] = cos_sin_turns(split(shifted))
-        cosine, sine = cos_sin_turns(common(node))
-        common_ref[t] = cosine * cosine + sine * sine
+            forth, back = turn_both_ways(centers[child], half_step)
+            put(child_ref, (child, t), forth)
+            put(child_ref, (child, CHEB - 1 - t), back)
+        twice = half_step[1] + half_step[1]
+        full_step = (1.0 - twice * half_step[1], twice * half_step[0])
+        forth, back = turn_both_ways(center, full_step)
+        put(parent_ref, (t,), forth)
+        put(parent_ref, (CHEB - 1 - t,), back)
 
 
 def level_column(column, children, parent_ref, child_ref, common_ref, store):
@@ -215,14 +247,15 @@
 def join_chips(me, blocks, order, held, sems, work, last_phases, factors):
     copies = []
     for index, step in enumerate(order):
-        spot = pl.ds(pl.multiple_of(((me ^ step) // 2) * ROWS, 8), ROWS)
-        copies.append(pltpu.make_async_copy(blocks[index], held.at[spot, :], sems.at[index]))
+        spot = pl.ds(((me ^ step) // 2) * (ROWS // 2), ROWS // 2)
+        copies.append(pltpu.make_async_copy(blocks[index], held.at[spot], sems.at[index]))
         copies[-1].start()
     for copy in copies:
         copy.wait()
+    rows = held.reshape(OCT * ROWS, LANES)
 
     def received(row):
-        return held[pl.ds(row, OCT, stride=ROWS), :]
+        return rows[pl.ds(row, OCT, stride=ROWS), :]
 
     for part in range(4):
         last_phases[part] = received(WEIGHT_ROWS + part * LEVELS + LEVELS - 1)
@@ -333,7 +366,7 @@
         in_specs=[pl.BlockSpec(memory_space=pltpu.SMEM)] + [pl.BlockSpec(memory_space=pl.ANY)] * OCT,
         out_specs=[vmem, vmem],
         scratch_shapes=[
-            pltpu.VMEM((OCT * ROWS, LANES), jnp.float32),
+            pltpu.VMEM((OCT * ROWS // 2, 2, LANES), jnp.float32),
             *factor_scratch(()),
             pltpu.SemaphoreType.DMA((OCT,)),
         ],
@@ -354,7 +387,7 @@
         scratch_shapes=[
             pltpu.VMEM((2, WEIGHT_ROWS, OCT, LANES), jnp.float32),
             pltpu.VMEM((2, 4, OCT, LANES), jnp.float32),
-            pltpu.VMEM((OCT * ROWS, LANES), jnp.float32),
+            pltpu.VMEM((OCT * ROWS // 2, 2, LANES), jnp.float32),
             pltpu.VMEM((WEIGHT_ROWS * SLOTS, LANES), jnp.float32),
             *factor_scratch((2,)),
             pltpu.SemaphoreType.DMA((OCT,)),
@@ -384,7 +417,6 @@
             phases, blocks[last] = lax.optimization_barrier((phases, blocks[last]))
         packed, phases = pack(steps, me, weights, phases, sources)
         blocks.update(packed)
-    blocks = {step: block.reshape(ROWS, LANES) for step, block in blocks.items()}
     if direct:
         for step in SENDS:
             if step in WAITS:
@@ -392,9 +424,9 @@
                 blocks[step], blocks[earlier] = lax.optimization_barrier((blocks[step], blocks[earlier]))
             blocks[step] = lax.ppermute(blocks[step], "box", [(s, s ^ step) for s in range(SLOTS)])
     else:
-        whole = jnp.concatenate([blocks[step] for step in range(SLOTS)], axis=1)
-        whole = lax.all_to_all(whole, "box", split_axis=1, concat_axis=1, tiled=True)
-        blocks = [whole[:, s * LANES : (s + 1) * LANES] for s in range(SLOTS)]
+        whole = jnp.concatenate([blocks[step] for step in range(SLOTS)], axis=2)
+        whole = lax.all_to_all(whole, "box", split_axis=2, concat_axis=2, tiled=True)
+        blocks = [whole[:, :, s * LANES : (s + 1) * LANES] for s in range(SLOTS)]
     even = combine_even(me, [blocks[step] for step in EVEN_ORDER])
     rows = combine_odd(me, even, [blocks[step] for step in ODD_ORDER])
     return rows.reshape(POINTS, SLOTS, 2, LANES).transpose(2, 0, 1, 3).reshape(2, POINTS, SLOTS * LANES)

time: 47.1 us -> 46 us (0.977)
  waiting for transfers between devices: 7.32 us -> 5.11 us
  starting transfers between devices: 26.6 us -> 28.1 us
  Pallas kernels: 12.9 us -> 12.4 us
    ppermute x15, waiting for transfers between devices: 7.32 us -> 5.11 us  [on_device(): lax.ppermute(blocks[step], 'box', [(s, s ^ step) for s in range(SLOTS)])]
    ppermute x15, starting transfers between devices: 26.6 us -> 28.1 us  [on_device(): lax.ppermute(blocks[step], 'box', [(s, s ^ step) for s in range(SLOTS)])]
  transfers between devices with their start and end apart: 15 -> 15, of which waited for: 3 -> 2; matrix products, arithmetic and copies ran while one was open for 0% -> 0% of each run, Pallas kernels for 11% -> 11%
where the time goes in v9:
time: 46 us; the launch traced here: 45.7 us
  starting transfers between devices  28.1 us (61%)
  Pallas kernels  12.4 us (27%)
  waiting for transfers between devices  5.11 us (11%)
    ppermute x15, starting transfers between devices, on_device(): lax.ppermute(blocks[step], 'box', [(s, s ^ step) for s in range(SLOTS)])  28.1 us
    pallas_call x1, Pallas kernels, combine_odd(): pl.pallas_call(odd_kernel, out_shape=jax.ShapeDtypeStruct((WEIGHT_ROWS *...  6.13 us
    ppermute x15, waiting for transfers between devices, on_device(): lax.ppermute(blocks[step], 'box', [(s, s ^ step) for s in range(SLOTS)])  5.11 us
    pallas_call x1, Pallas kernels, combine_even(): pl.pallas_call(even_kernel, out_shape=[jax.ShapeDtypeStruct((WEIGHT_ROWS,...  3.64 us
    pallas_call x2, Pallas kernels, pack(): pl.pallas_call(functools.partial(pack_kernel, steps, first), out_shape=ou...  2.68 us
  transfers between devices with their start and end apart: 15, of which 2 were waited for; matrix products, arithmetic and copies ran while one was open for 0% of the time, Pallas kernels for 11%

profile of v9, /device:TPU:0, one launch (start us, length us, event | category | flops | bytes accessed | tf_op | source)
XLA Modules:
  0.0 45.7 jit_solution(3779855550476201657)
XLA Ops:
  0.0 1.2 %pack.2 = (f32[89,2,128]{2,1,0:T(2,128)S(1)}, f32[89,2,128]{2,1,0:T(2,128)S(1)}, f32[89,2,128]{2,1,0:T(2,128)S(1)}, f32[89,2,128]{2,1,0:T(2,128)S(1)}, f32[8,2,2048]{2,1,0:T(2,128)S(1)}) custom-call(s32[1]{0:T(128)} %bitcast.me_ref, f32[81,16,2,128]{3,2,1,0:T(2,128)} %bitcast.10, f32[4,3]{1,0:T(4,128)} %refs_0_.1, f32[4,2,2048]{2,1,0:T(2,128)} %refs_1_.1, ...), custom_call_target="tpu_custom_call" | custom-call | flops 1048576 | bytes 1048576 | tf_op jit(solution)/shard_map/pack/pallas_call | solution.py:138
  1.2 5.1 %collective-permute-start.4 = (f32[89,2,128]{2,1,0:T(2,128)S(1)}, f32[89,2,128]{2,1,0:T(2,128)S(1)}, u32[]{:S(2)}, u32[]{:S(2)}) collective-permute-start(f32[89,2,128]{2,1,0:T(2,128)S(1)} %get-tuple-element.39), channel_id=1, source_target_pairs={{0,10},{1,11},{2,8},{3,9},{4,14},{5,15},{6,12},{7,13},{8,2},{9,3},... | collective-permute-start | bytes 273416 | tf_op jit(solution)/shard_map/ppermute | solution.py:425
  6.3 1.6 %collective-permute-start.1 = (f32[89,2,128]{2,1,0:T(2,128)S(1)}, f32[89,2,128]{2,1,0:T(2,128)S(1)}, u32[]{:S(2)}, u32[]{:S(2)}) collective-permute-start(f32[89,2,128]{2,1,0:T(2,128)S(1)} %get-tuple-element.35), channel_id=1, source_target_pairs={{0,4},{1,5},{2,6},{3,7},{4,0},{5,1},{6,2},{7,3},{8,12},{9,13},{10,... | collective-permute-start | bytes 273416 | tf_op jit(solution)/shard_map/ppermute | solution.py:425
  7.9 0.2 collective-permute-start.3
  8.1 0.6 %collective-permute-start.5 = (f32[89,2,128]{2,1,0:T(2,128)S(1)}, f32[89,2,128]{2,1,0:T(2,128)S(1)}, u32[]{:S(2)}, u32[]{:S(2)}) collective-permute-start(f32[89,2,128]{2,1,0:T(2,128)S(1)} %get-tuple-element.40), channel_id=1, source_target_pairs={{0,6},{1,7},{2,4},{3,5},{4,2},{5,3},{6,0},{7,1},{8,14},{9,15},{10,... | collective-permute-start | bytes 273416 | tf_op jit(solution)/shard_map/ppermute | solution.py:425
  8.7 1.4 %pack.3 = (f32[89,2,128]{2,1,0:T(2,128)S(1)}, f32[89,2,128]{2,1,0:T(2,128)S(1)}, f32[89,2,128]{2,1,0:T(2,128)S(1)}, f32[89,2,128]{2,1,0:T(2,128)S(1)}, f32[89,2,...) custom-call(s32[1]{0:T(128)} %bitcast.me_ref, ...), custom_call_target="tpu_custom_call" | custom-call | flops 1048576 | bytes 1048576 | tf_op jit(solution)/shard_map/pack/pallas_call | solution.py:138
  10.2 2.8 %collective-permute-start.7 = (f32[89,2,128]{2,1,0:T(2,128)S(1)}, f32[89,2,128]{2,1,0:T(2,128)S(1)}, u32[]{:S(2)}, u32[]{:S(2)}) collective-permute-start(f32[89,2,128]{2,1,0:T(2,128)S(1)} %get-tuple-element.46), channel_id=1, source_target_pairs={{0,11},{1,10},{2,9},{3,8},{4,15},{5,14},{6,13},{7,12},{8,3},{9,2},... | collective-permute-start | bytes 273416 | tf_op jit(solution)/shard_map/ppermute | solution.py:425
  13.0 0.0 collective-permute-done.4.refs_4_
  13.0 0.8 %collective-permute-start = (f32[89,2,128]{2,1,0:T(2,128)S(1)}, f32[89,2,128]{2,1,0:T(2,128)S(1)}, u32[]{:S(2)}, u32[]{:S(2)}) collective-permute-start(f32[89,2,128]{2,1,0:T(2,128)S(1)} %get-tuple-element.33), channel_id=1, source_target_pairs={{0,8},{1,9},{2,10},{3,11},{4,12},{5,13},{6,14},{7,15},{8,0},{9,1},... | collective-permute-start | bytes 273416 | tf_op jit(solution)/shard_map/ppermute | solution.py:425
  13.8 0.0 collective-permute-done.1.refs_1_
  13.8 1.5 %collective-permute-start.2 = (f32[89,2,128]{2,1,0:T(2,128)S(1)}, f32[89,2,128]{2,1,0:T(2,128)S(1)}, u32[]{:S(2)}, u32[]{:S(2)}) collective-permute-start(f32[89,2,128]{2,1,0:T(2,128)S(1)} %get-tuple-element.37), channel_id=1, source_target_pairs={{0,2},{1,3},{2,0},{3,1},{4,6},{5,7},{6,4},{7,5},{8,10},{9,11},{10,... | collective-permute-start | bytes 273416 | tf_op jit(solution)/shard_map/ppermute | solution.py:425
  15.3 0.0 collective-permute-done.3.refs_3_
  15.3 2.0 %collective-permute-start.6 = (f32[89,2,128]{2,1,0:T(2,128)S(1)}, f32[89,2,128]{2,1,0:T(2,128)S(1)}, u32[]{:S(2)}, u32[]{:S(2)}) collective-permute-start(f32[89,2,128]{2,1,0:T(2,128)S(1)} %get-tuple-element.41), channel_id=1, source_target_pairs={{0,14},{1,15},{2,12},{3,13},{4,10},{5,11},{6,8},{7,9},{8,6},{9,7},... | collective-permute-start | bytes 273416 | tf_op jit(solution)/shard_map/ppermute | solution.py:425
  17.3 0.0 collective-permute-done.5.refs_5_
  17.3 0.7 %collective-permute-start.9 = (f32[89,2,128]{2,1,0:T(2,128)S(1)}, f32[89,2,128]{2,1,0:T(2,128)S(1)}, u32[]{:S(2)}, u32[]{:S(2)}) collective-permute-start(f32[89,2,128]{2,1,0:T(2,128)S(1)} %get-tuple-element.48), channel_id=1, source_target_pairs={{0,3},{1,2},{2,1},{3,0},{4,7},{5,6},{6,5},{7,4},{8,11},{9,10},{10,... | collective-permute-start | bytes 273416 | tf_op jit(solution)/shard_map/ppermute | solution.py:425
  18.0 0.0 collective-permute-done.7.refs_3_
  18.0 4.9 %collective-permute-start.10 = (f32[89,2,128]{2,1,0:T(2,128)S(1)}, f32[89,2,128]{2,1,0:T(2,128)S(1)}, u32[]{:S(2)}, u32[]{:S(2)}) collective-permute-start(f32[89,2,128]{2,1,0:T(2,128)S(1)} %get-tuple-element.49), channel_id=1, source_target_pairs={{0,5},{1,4},{2,7},{3,6},{4,1},{5,0},{6,3},{7,2},{8,13},{9,12},{10,... | collective-permute-start | bytes 273416 | tf_op jit(solution)/shard_map/ppermute | solution.py:425
  22.9 2.1 %collective-permute-done.refs_0_ = f32[89,2,128]{2,1,0:T(2,128)S(1)} collective-permute-done((f32[89,2,128]{2,1,0:T(2,128)S(1)}, f32[89,2,128]{2,1,0:T(2,128)S(1)}, u32[]{:S(2)}, u32[]{:S(2)}) %collective-permute-start) | collective-permute-done | bytes 91168 | tf_op jit(solution)/shard_map/ppermute | solution.py:425
  25.0 2.6 %collective-permute-start.12 = (f32[89,2,128]{2,1,0:T(2,128)S(1)}, f32[89,2,128]{2,1,0:T(2,128)S(1)}, u32[]{:S(2)}, u32[]{:S(2)}) collective-permute-start(f32[89,2,128]{2,1,0:T(2,128)S(1)} %get-tuple-element.52), channel_id=1, source_target_pairs={{0,15},{1,14},{2,13},{3,12},{4,11},{5,10},{6,9},{7,8},{8,7},{9,6},... | collective-permute-start | bytes 273416 | tf_op jit(solution)/shard_map/ppermute | solution.py:425
  27.6 0.0 collective-permute-done.2.refs_2_
  27.6 1.7 %collective-permute-start.13 = (f32[89,2,128]{2,1,0:T(2,128)S(1)}, f32[89,2,128]{2,1,0:T(2,128)S(1)}, u32[]{:S(2)}, u32[]{:S(2)}) collective-permute-start(f32[89,2,128]{2,1,0:T(2,128)S(1)} %get-tuple-element.53), channel_id=1, source_target_pairs={{0,13},{1,12},{2,15},{3,14},{4,9},{5,8},{6,11},{7,10},{8,5},{9,4},... | collective-permute-start | bytes 273416 | tf_op jit(solution)/shard_map/ppermute | solution.py:425
  29.3 0.0 collective-permute-done.6.refs_6_
  29.3 0.0 collective-permute-start.14
  29.3 0.0 collective-permute-done.9.refs_1_
  29.3 3.7 %collective-permute-start.11 = (f32[89,2,128]{2,1,0:T(2,128)S(1)}, f32[89,2,128]{2,1,0:T(2,128)S(1)}, u32[]{:S(2)}, u32[]{:S(2)}) collective-permute-start(f32[89,2,128]{2,1,0:T(2,128)S(1)} %get-tuple-element.51), channel_id=1, source_target_pairs={{0,9},{1,8},{2,11},{3,10},{4,13},{5,12},{6,15},{7,14},{8,1},{9,0},... | collective-permute-start | bytes 273416 | tf_op jit(solution)/shard_map/ppermute | solution.py:425
  33.0 0.0 collective-permute-done.10.refs_2_
  33.0 0.0 collective-permute-start.8
  33.0 3.6 %combine_even.1 = (f32[162,8,128]{2,1,0:T(8,128)S(1)}, f32[4,8,128]{2,1,0:T(8,128)S(1)}) custom-call(s32[1]{0:T(128)} %bitcast.me_ref, f32[89,2,128]{2,1,0:T(2,128)S(1)} %collective-permute-done.refs_0_, f32[89,2,128]{2,1,0:T(2,128)S(1)} %collective-permute-done.1.refs_1_, f32[89,2,128]{2,1,0:T(2,128)S(1)} %collective-permute-done.2.refs_2_, ...), custom_call_target="tpu_custom_call" | custom-call | flops 41943040 | bytes 12582912 | tf_op jit(solution)/shard_map/combine_even/pallas_call | solution.py:360
  36.7 0.0 collective-permute-done.13.refs_6_
  36.7 0.0 collective-permute-done.14.refs_7_
  36.7 2.9 %collective-permute-done.11.refs_4_ = f32[89,2,128]{2,1,0:T(2,128)S(1)} collective-permute-done((f32[89,2,128]{2,1,0:T(2,128)S(1)}, f32[89,2,128]{2,1,0:T(2,128)S(1)}, u32[]{:S(2)}, u32[]{:S(2)}) %collective-permute-start.11) | collective-permute-done | bytes 91168 | tf_op jit(solution)/shard_map/ppermute | solution.py:425
  39.6 6.1 %combine_odd.1 = f32[2592,128]{1,0:T(8,128)} custom-call(s32[1]{0:T(128)} %bitcast.me_ref, f32[162,8,128]{2,1,0:T(8,128)S(1)} %get-tuple-element.43.even_work, f32[4,8,128]{2,1,0:T(8,128)S(1)} %get-tuple-element.44.even_phases, f32[89,2,128]{2,1,0:T(2,128)S(1)} %collective-permute-done.8.refs_0_, f32[89,2,128]{2,1,0:T(2,128)S(1)} %collective-permute-done.9.refs_1_, ...), custom_call_target="tpu_custom_call" | custom-call | flops 83886080 | bytes 20971520 | tf_op jit(solution)/shard_map/combine_odd/pallas_call | solution.py:382
  (2 shorter events, 0.0 us)
Async XLA Ops:
  1.2 11.8 %collective-permute-start.4 = (f32[89,2,128]{2,1,0:T(2,128)S(1)}, f32[89,2,128]{2,1,0:T(2,128)S(1)}, u32[]{:S(2)}, u32[]{:S(2)}) collective-permute-start(f32[89,2,128]{2,1,0:T(2,128)S(1)} %get-tuple-element.39), channel_id=1, source_target_pairs={{0,10},{1,11},{2,8},{3,9},{4,14},{5,15},{6,12},{7,13},{8,2},{9,3},... | collective-permute-start | bytes 273416 | tf_op jit(solution)/shard_map/ppermute | solution.py:425
  6.3 7.5 %collective-permute-start.1 = (f32[89,2,128]{2,1,0:T(2,128)S(1)}, f32[89,2,128]{2,1,0:T(2,128)S(1)}, u32[]{:S(2)}, u32[]{:S(2)}) collective-permute-start(f32[89,2,128]{2,1,0:T(2,128)S(1)} %get-tuple-element.35), channel_id=1, source_target_pairs={{0,4},{1,5},{2,6},{3,7},{4,0},{5,1},{6,2},{7,3},{8,12},{9,13},{10,... | collective-permute-start | bytes 273416 | tf_op jit(solution)/shard_map/ppermute | solution.py:425
  7.9 7.5 %collective-permute-start.3 = (f32[89,2,128]{2,1,0:T(2,128)S(1)}, f32[89,2,128]{2,1,0:T(2,128)S(1)}, u32[]{:S(2)}, u32[]{:S(2)}) collective-permute-start(f32[89,2,128]{2,1,0:T(2,128)S(1)} %get-tuple-element.38), channel_id=1, source_target_pairs={{0,12},{1,13},{2,14},{3,15},{4,8},{5,9},{6,10},{7,11},{8,4},{9,5},... | collective-permute-start | bytes 273416 | tf_op jit(solution)/shard_map/ppermute | solution.py:425
  8.1 9.2 %collective-permute-start.5 = (f32[89,2,128]{2,1,0:T(2,128)S(1)}, f32[89,2,128]{2,1,0:T(2,128)S(1)}, u32[]{:S(2)}, u32[]{:S(2)}) collective-permute-start(f32[89,2,128]{2,1,0:T(2,128)S(1)} %get-tuple-element.40), channel_id=1, source_target_pairs={{0,6},{1,7},{2,4},{3,5},{4,2},{5,3},{6,0},{7,1},{8,14},{9,15},{10,... | collective-permute-start | bytes 273416 | tf_op jit(solution)/shard_map/ppermute | solution.py:425
  10.2 7.8 %collective-permute-start.7 = (f32[89,2,128]{2,1,0:T(2,128)S(1)}, f32[89,2,128]{2,1,0:T(2,128)S(1)}, u32[]{:S(2)}, u32[]{:S(2)}) collective-permute-start(f32[89,2,128]{2,1,0:T(2,128)S(1)} %get-tuple-element.46), channel_id=1, source_target_pairs={{0,11},{1,10},{2,9},{3,8},{4,15},{5,14},{6,13},{7,12},{8,3},{9,2},... | collective-permute-start | bytes 273416 | tf_op jit(solution)/shard_map/ppermute | solution.py:425
  13.0 12.0 %collective-permute-start = (f32[89,2,128]{2,1,0:T(2,128)S(1)}, f32[89,2,128]{2,1,0:T(2,128)S(1)}, u32[]{:S(2)}, u32[]{:S(2)}) collective-permute-start(f32[89,2,128]{2,1,0:T(2,128)S(1)} %get-tuple-element.33), channel_id=1, source_target_pairs={{0,8},{1,9},{2,10},{3,11},{4,12},{5,13},{6,14},{7,15},{8,0},{9,1},... | collective-permute-start | bytes 273416 | tf_op jit(solution)/shard_map/ppermute | solution.py:425
  13.8 13.8 %collective-permute-start.2 = (f32[89,2,128]{2,1,0:T(2,128)S(1)}, f32[89,2,128]{2,1,0:T(2,128)S(1)}, u32[]{:S(2)}, u32[]{:S(2)}) collective-permute-start(f32[89,2,128]{2,1,0:T(2,128)S(1)} %get-tuple-element.37), channel_id=1, source_target_pairs={{0,2},{1,3},{2,0},{3,1},{4,6},{5,7},{6,4},{7,5},{8,10},{9,11},{10,... | collective-permute-start | bytes 273416 | tf_op jit(solution)/shard_map/ppermute | solution.py:425
  15.3 13.9 %collective-permute-start.6 = (f32[89,2,128]{2,1,0:T(2,128)S(1)}, f32[89,2,128]{2,1,0:T(2,128)S(1)}, u32[]{:S(2)}, u32[]{:S(2)}) collective-permute-start(f32[89,2,128]{2,1,0:T(2,128)S(1)} %get-tuple-element.41), channel_id=1, source_target_pairs={{0,14},{1,15},{2,12},{3,13},{4,10},{5,11},{6,8},{7,9},{8,6},{9,7},... | collective-permute-start | bytes 273416 | tf_op jit(solution)/shard_map/ppermute | solution.py:425
  17.3 12.0 %collective-permute-start.9 = (f32[89,2,128]{2,1,0:T(2,128)S(1)}, f32[89,2,128]{2,1,0:T(2,128)S(1)}, u32[]{:S(2)}, u32[]{:S(2)}) collective-permute-start(f32[89,2,128]{2,1,0:T(2,128)S(1)} %get-tuple-element.48), channel_id=1, source_target_pairs={{0,3},{1,2},{2,1},{3,0},{4,7},{5,6},{6,5},{7,4},{8,11},{9,10},{10,... | collective-permute-start | bytes 273416 | tf_op jit(solution)/shard_map/ppermute | solution.py:425
  18.0 15.0 %collective-permute-start.10 = (f32[89,2,128]{2,1,0:T(2,128)S(1)}, f32[89,2,128]{2,1,0:T(2,128)S(1)}, u32[]{:S(2)}, u32[]{:S(2)}) collective-permute-start(f32[89,2,128]{2,1,0:T(2,128)S(1)} %get-tuple-element.49), channel_id=1, source_target_pairs={{0,5},{1,4},{2,7},{3,6},{4,1},{5,0},{6,3},{7,2},{8,13},{9,12},{10,... | collective-permute-start | bytes 273416 | tf_op jit(solution)/shard_map/ppermute | solution.py:425
  25.0 11.6 %collective-permute-start.12 = (f32[89,2,128]{2,1,0:T(2,128)S(1)}, f32[89,2,128]{2,1,0:T(2,128)S(1)}, u32[]{:S(2)}, u32[]{:S(2)}) collective-permute-start(f32[89,2,128]{2,1,0:T(2,128)S(1)} %get-tuple-element.52), channel_id=1, source_target_pairs={{0,15},{1,14},{2,13},{3,12},{4,11},{5,10},{6,9},{7,8},{8,7},{9,6},... | collective-permute-start | bytes 273416 | tf_op jit(solution)/shard_map/ppermute | solution.py:425
  27.6 9.0 %collective-permute-start.13 = (f32[89,2,128]{2,1,0:T(2,128)S(1)}, f32[89,2,128]{2,1,0:T(2,128)S(1)}, u32[]{:S(2)}, u32[]{:S(2)}) collective-permute-start(f32[89,2,128]{2,1,0:T(2,128)S(1)} %get-tuple-element.53), channel_id=1, source_target_pairs={{0,13},{1,12},{2,15},{3,14},{4,9},{5,8},{6,11},{7,10},{8,5},{9,4},... | collective-permute-start | bytes 273416 | tf_op jit(solution)/shard_map/ppermute | solution.py:425
  29.3 7.4 %collective-permute-start.14 = (f32[89,2,128]{2,1,0:T(2,128)S(1)}, f32[89,2,128]{2,1,0:T(2,128)S(1)}, u32[]{:S(2)}, u32[]{:S(2)}) collective-permute-start(f32[89,2,128]{2,1,0:T(2,128)S(1)} %get-tuple-element.54), channel_id=1, source_target_pairs={{0,7},{1,6},{2,5},{3,4},{4,3},{5,2},{6,1},{7,0},{8,15},{9,14},{10,... | collective-permute-start | bytes 273416 | tf_op jit(solution)/shard_map/ppermute | solution.py:425
  29.3 10.3 %collective-permute-start.11 = (f32[89,2,128]{2,1,0:T(2,128)S(1)}, f32[89,2,128]{2,1,0:T(2,128)S(1)}, u32[]{:S(2)}, u32[]{:S(2)}) collective-permute-start(f32[89,2,128]{2,1,0:T(2,128)S(1)} %get-tuple-element.51), channel_id=1, source_target_pairs={{0,9},{1,8},{2,11},{3,10},{4,13},{5,12},{6,15},{7,14},{8,1},{9,0},... | collective-permute-start | bytes 273416 | tf_op jit(solution)/shard_map/ppermute | solution.py:425
  33.0 6.6 %collective-permute-start.8 = (f32[89,2,128]{2,1,0:T(2,128)S(1)}, f32[89,2,128]{2,1,0:T(2,128)S(1)}, u32[]{:S(2)}, u32[]{:S(2)}) collective-permute-start(f32[89,2,128]{2,1,0:T(2,128)S(1)} %get-tuple-element.47), channel_id=1, source_target_pairs={{0,1},{1,0},{2,3},{3,2},{4,5},{5,4},{6,7},{7,6},{8,9},{9,8},{10,11... | collective-permute-start | bytes 273416 | tf_op jit(solution)/shard_map/ppermute | solution.py:425

commit v10 on v9

--- a/solution.py
+++ b/solution.py
@@ -20,11 +20,12 @@
 PHASE_ROWS = 4 * LEVELS
 ROWS = WEIGHT_ROWS + PHASE_ROWS
 OCT = SLOTS // 2
-PACKS = ((12, 4, 6, 10), (2, 14, 9, 15, 3, 11, 8, 7, 13, 5, 1, 0))
-SENDS = (8, 12, 4, 6, 2, 14, 15, 3, 11, 7, 13, 5, 1, 10, 9)
-WAITS = {9: 4, 1: 11}
-EVEN_ORDER = (8, 4, 2, 12, 10, 6, 14, 0)
-ODD_ORDER = (1, 3, 5, 11, 9, 15, 13, 7)
+PACKS = ((14, 8, 1), (6, 12, 2, 4, 10, 15, 7), (9, 11, 13), (5, 3, 0))
+SENDS = (14, 8, 6, 12, 2, 4, 10, 15, 7, 9, 11, 13, 5, 3, 1)
+WAITS = {2: 14, 1: 9}
+SEEN = (15,)
+EVEN_ORDER = (14, 8, 6, 12, 2, 4, 10, 0)
+ODD_ORDER = (9, 7, 3, 15, 1, 13, 11, 5)
 
 NODES = np.cos(math.pi * (2.0 * np.arange(CHEB) + 1.0) / (2.0 * CHEB))
 NODES[CHEB // 2] = 0.0
@@ -423,11 +424,15 @@
                 earlier = WAITS[step]
                 blocks[step], blocks[earlier] = lax.optimization_barrier((blocks[step], blocks[earlier]))
             blocks[step] = lax.ppermute(blocks[step], "box", [(s, s ^ step) for s in range(SLOTS)])
+        own = me
+        for step in SEEN:
+            own, blocks[step] = lax.optimization_barrier((own, blocks[step]))
     else:
+        own = me
         whole = jnp.concatenate([blocks[step] for step in range(SLOTS)], axis=2)
         whole = lax.all_to_all(whole, "box", split_axis=2, concat_axis=2, tiled=True)
         blocks = [whole[:, :, s * LANES : (s + 1) * LANES] for s in range(SLOTS)]
-    even = combine_even(me, [blocks[step] for step in EVEN_ORDER])
+    even = combine_even(own, [blocks[step] for step in EVEN_ORDER])
     rows = combine_odd(me, even, [blocks[step] for step in ODD_ORDER])
     return rows.reshape(POINTS, SLOTS, 2, LANES).transpose(2, 0, 1, 3).reshape(2, POINTS, SLOTS * LANES)
 

time: 46 us -> 45.3 us (0.985)
  Pallas kernels: 12.4 us -> 14.2 us
  starting transfers between devices: 28.1 us -> 26.4 us
  waiting for transfers between devices: 5.11 us -> 4.39 us
    ppermute x15, starting transfers between devices: 28.1 us -> 26.4 us  [on_device(): lax.ppermute(blocks[step], 'box', [(s, s ^ step) for s in range(SLOTS)])]
    pallas_call x2 -> x4, Pallas kernels: 2.68 us -> 4.41 us  [pack(): pl.pallas_call(functools.partial(pack_kernel, steps, first), out_shape=ou...]
    ppermute x15, waiting for transfers between devices: 5.11 us -> 4.39 us  [on_device(): lax.ppermute(blocks[step], 'box', [(s, s ^ step) for s in range(SLOTS)])]
  transfers between devices with their start and end apart: 15 -> 15, of which waited for: 2 -> 1; matrix products, arithmetic and copies ran while one was open for 0% -> 0% of each run, Pallas kernels for 11% -> 15%
where the time goes in v10:
time: 45.3 us; the launch traced here: 45 us
  starting transfers between devices  26.4 us (58%)
  Pallas kernels  14.2 us (31%)
  waiting for transfers between devices  4.39 us (10%)
    ppermute x15, starting transfers between devices, on_device(): lax.ppermute(blocks[step], 'box', [(s, s ^ step) for s in range(SLOTS)])  26.4 us
    pallas_call x1, Pallas kernels, combine_odd(): pl.pallas_call(odd_kernel, out_shape=jax.ShapeDtypeStruct((WEIGHT_ROWS *...  6.15 us
    pallas_call x4, Pallas kernels, pack(): pl.pallas_call(functools.partial(pack_kernel, steps, first), out_shape=ou...  4.41 us
    ppermute x15, waiting for transfers between devices, on_device(): lax.ppermute(blocks[step], 'box', [(s, s ^ step) for s in range(SLOTS)])  4.39 us
    pallas_call x1, Pallas kernels, combine_even(): pl.pallas_call(even_kernel, out_shape=[jax.ShapeDtypeStruct((WEIGHT_ROWS,...  3.61 us
  transfers between devices with their start and end apart: 15, of which 1 were waited for; matrix products, arithmetic and copies ran while one was open for 0% of the time, Pallas kernels for 15%

profile of v10, /device:TPU:0, one launch (start us, length us, event | category | flops | bytes accessed | tf_op | source)
XLA Modules:
  0.0 45.0 jit_solution(16986412014374459107)
XLA Ops:
  0.0 1.2 %pack.4 = (f32[89,2,128]{2,1,0:T(2,128)S(1)}, f32[89,2,128]{2,1,0:T(2,128)S(1)}, f32[89,2,128]{2,1,0:T(2,128)S(1)}, f32[8,2,2048]{2,1,0:T(2,128)S(1)}) custom-call(s32[1]{0:T(128)} %bitcast.me_ref, f32[81,16,2,128]{3,2,1,0:T(2,128)} %bitcast.10, f32[4,3]{1,0:T(4,128)} %refs_0_.1, f32[4,2,2048]{2,1,0:T(2,128)} %refs_1_.1, f32[4,2,2048]{2,1,0:T(2,128)} %refs_2_.1, ...), custom_call_target="tpu_custom_call" | custom-call | flops 1048576 | bytes 1048576 | tf_op jit(solution)/shard_map/pack/pallas_call | solution.py:139
  1.2 6.1 %collective-permute-start.1 = (f32[89,2,128]{2,1,0:T(2,128)S(1)}, f32[89,2,128]{2,1,0:T(2,128)S(1)}, u32[]{:S(2)}, u32[]{:S(2)}) collective-permute-start(f32[89,2,128]{2,1,0:T(2,128)S(1)} %get-tuple-element.42), channel_id=1, source_target_pairs={{0,14},{1,15},{2,12},{3,13},{4,10},{5,11},{6,8},{7,9},{8,6},{9,7},... | collective-permute-start | bytes 273416 | tf_op jit(solution)/shard_map/ppermute | solution.py:426
  7.3 0.0 collective-permute-start.2
  7.3 1.2 %pack.5 = (f32[89,2,128]{2,1,0:T(2,128)S(1)}, f32[89,2,128]{2,1,0:T(2,128)S(1)}, f32[89,2,128]{2,1,0:T(2,128)S(1)}, f32[89,2,128]{2,1,0:T(2,128)S(1)}, f32[89,2,...) custom-call(s32[1]{0:T(128)} %bitcast.me_ref, f32[81,16,2,128]{3,2,1,0:T(2,128)} %bitcast.11, ...), custom_call_target="tpu_custom_call" | custom-call | flops 1048576 | bytes 1048576 | tf_op jit(solution)/shard_map/pack/pallas_call | solution.py:139
  8.5 0.1 collective-permute-start.9
  8.6 5.0 %collective-permute-start = (f32[89,2,128]{2,1,0:T(2,128)S(1)}, f32[89,2,128]{2,1,0:T(2,128)S(1)}, u32[]{:S(2)}, u32[]{:S(2)}) collective-permute-start(f32[89,2,128]{2,1,0:T(2,128)S(1)} %get-tuple-element.39), channel_id=1, source_target_pairs={{0,15},{1,14},{2,13},{3,12},{4,11},{5,10},{6,9},{7,8},{8,7},{9,6},... | collective-permute-start | bytes 273416 | tf_op jit(solution)/shard_map/ppermute | solution.py:426
  13.6 1.0 %pack.6 = (f32[89,2,128]{2,1,0:T(2,128)S(1)}, f32[89,2,128]{2,1,0:T(2,128)S(1)}, f32[89,2,128]{2,1,0:T(2,128)S(1)}) custom-call(s32[1]{0:T(128)} %bitcast.me_ref, f32[81,16,2,128]{3,2,1,0:T(2,128)} %bitcast.12, f32[8,2,2048]{2,1,0:T(2,128)S(1)} %get-tuple-element.53.refs_0_), custom_call_target="tpu_custom_call" | custom-call | flops 1048576 | bytes 1048576 | tf_op jit(solution)/shard_map/pack/pallas_call | solution.py:139
  14.6 0.1 collective-permute-start.8
  14.6 0.0 collective-permute-done.1.refs_0_
  14.7 0.7 %collective-permute-start.3 = (f32[89,2,128]{2,1,0:T(2,128)S(1)}, f32[89,2,128]{2,1,0:T(2,128)S(1)}, u32[]{:S(2)}, u32[]{:S(2)}) collective-permute-start(f32[89,2,128]{2,1,0:T(2,128)S(1)} %get-tuple-element.45), channel_id=1, source_target_pairs={{0,6},{1,7},{2,4},{3,5},{4,2},{5,3},{6,0},{7,1},{8,14},{9,15},{10,... | collective-permute-start | bytes 273416 | tf_op jit(solution)/shard_map/ppermute | solution.py:426
  15.4 4.4 %collective-permute-done.2.refs_1_ = f32[89,2,128]{2,1,0:T(2,128)S(1)} collective-permute-done((f32[89,2,128]{2,1,0:T(2,128)S(1)}, f32[89,2,128]{2,1,0:T(2,128)S(1)}, u32[]{:S(2)}, u32[]{:S(2)}) %collective-permute-start.2) | collective-permute-done | bytes 91168 | tf_op jit(solution)/shard_map/ppermute | solution.py:426
  19.7 2.3 %collective-permute-start.4 = (f32[89,2,128]{2,1,0:T(2,128)S(1)}, f32[89,2,128]{2,1,0:T(2,128)S(1)}, u32[]{:S(2)}, u32[]{:S(2)}) collective-permute-start(f32[89,2,128]{2,1,0:T(2,128)S(1)} %get-tuple-element.46), channel_id=1, source_target_pairs={{0,12},{1,13},{2,14},{3,15},{4,8},{5,9},{6,10},{7,11},{8,4},{9,5},... | collective-permute-start | bytes 273416 | tf_op jit(solution)/shard_map/ppermute | solution.py:426
  22.0 0.0 collective-permute-done.9.refs_1_
  22.0 0.0 collective-permute-start.6
  22.0 0.0 collective-permute-done.refs_3_
  22.1 0.9 %collective-permute-start.7 = (f32[89,2,128]{2,1,0:T(2,128)S(1)}, f32[89,2,128]{2,1,0:T(2,128)S(1)}, u32[]{:S(2)}, u32[]{:S(2)}) collective-permute-start(f32[89,2,128]{2,1,0:T(2,128)S(1)} %get-tuple-element.49), channel_id=1, source_target_pairs={{0,10},{1,11},{2,8},{3,9},{4,14},{5,15},{6,12},{7,13},{8,2},{9,3},... | collective-permute-start | bytes 273416 | tf_op jit(solution)/shard_map/ppermute | solution.py:426
  22.9 0.0 collective-permute-done.8.refs_0_
  22.9 2.6 %collective-permute-start.5 = (f32[89,2,128]{2,1,0:T(2,128)S(1)}, f32[89,2,128]{2,1,0:T(2,128)S(1)}, u32[]{:S(2)}, u32[]{:S(2)}) collective-permute-start(f32[89,2,128]{2,1,0:T(2,128)S(1)} %get-tuple-element.47), channel_id=1, source_target_pairs={{0,2},{1,3},{2,0},{3,1},{4,6},{5,7},{6,4},{7,5},{8,10},{9,11},{10,... | collective-permute-start | bytes 273416 | tf_op jit(solution)/shard_map/ppermute | solution.py:426
  25.6 1.0 %pack.7 = (f32[89,2,128]{2,1,0:T(2,128)S(1)}, f32[89,2,128]{2,1,0:T(2,128)S(1)}, f32[89,2,128]{2,1,0:T(2,128)S(1)}) custom-call(s32[1]{0:T(128)} %bitcast.me_ref, f32[81,16,2,128]{3,2,1,0:T(2,128)} %bitcast.13, f32[8,2,2048]{2,1,0:T(2,128)S(1)} %get-tuple-element.53.refs_0_), custom_call_target="tpu_custom_call" | custom-call | flops 1048576 | bytes 1048576 | tf_op jit(solution)/shard_map/pack/pallas_call | solution.py:139
  26.6 0.0 collective-permute-done.3.refs_2_
  26.6 1.4 %collective-permute-start.12 = (f32[89,2,128]{2,1,0:T(2,128)S(1)}, f32[89,2,128]{2,1,0:T(2,128)S(1)}, u32[]{:S(2)}, u32[]{:S(2)}) collective-permute-start(f32[89,2,128]{2,1,0:T(2,128)S(1)} %get-tuple-element.64), channel_id=1, source_target_pairs={{0,13},{1,12},{2,15},{3,14},{4,9},{5,8},{6,11},{7,10},{8,5},{9,4},... | collective-permute-start | bytes 273416 | tf_op jit(solution)/shard_map/ppermute | solution.py:426
  28.0 0.0 collective-permute-done.4.refs_3_
  28.0 0.2 collective-permute-start.13
  28.2 0.0 collective-permute-done.6.refs_5_
  28.2 4.2 %collective-permute-start.10 = (f32[89,2,128]{2,1,0:T(2,128)S(1)}, f32[89,2,128]{2,1,0:T(2,128)S(1)}, u32[]{:S(2)}, u32[]{:S(2)}) collective-permute-start(f32[89,2,128]{2,1,0:T(2,128)S(1)} %get-tuple-element.61), channel_id=1, source_target_pairs={{0,3},{1,2},{2,1},{3,0},{4,7},{5,6},{6,5},{7,4},{8,11},{9,10},{10,... | collective-permute-start | bytes 273416 | tf_op jit(solution)/shard_map/ppermute | solution.py:426
  32.5 0.0 collective-permute-done.7.refs_6_
  32.5 2.7 %collective-permute-start.11 = (f32[89,2,128]{2,1,0:T(2,128)S(1)}, f32[89,2,128]{2,1,0:T(2,128)S(1)}, u32[]{:S(2)}, u32[]{:S(2)}) collective-permute-start(f32[89,2,128]{2,1,0:T(2,128)S(1)} %get-tuple-element.63), channel_id=1, source_target_pairs={{0,1},{1,0},{2,3},{3,2},{4,5},{5,4},{6,7},{7,6},{8,9},{9,8},{10,11... | collective-permute-start | bytes 273416 | tf_op jit(solution)/shard_map/ppermute | solution.py:426
  35.2 3.6 %combine_even.1 = (f32[162,8,128]{2,1,0:T(8,128)S(1)}, f32[4,8,128]{2,1,0:T(8,128)S(1)}) custom-call(s32[1]{0:T(128)} %bitcast.me_ref, f32[89,2,128]{2,1,0:T(2,128)S(1)} %collective-permute-done.1.refs_0_, f32[89,2,128]{2,1,0:T(2,128)S(1)} %collective-permute-done.2.refs_1_, f32[89,2,128]{2,1,0:T(2,128)S(1)} %collective-permute-done.3.refs_2_, ...), custom_call_target="tpu_custom_call" | custom-call | flops 41943040 | bytes 12582912 | tf_op jit(solution)/shard_map/combine_even/pallas_call | solution.py:361
  38.8 0.0 collective-permute-done.12.refs_5_
  38.9 0.0 collective-permute-done.10.refs_2_
  38.9 0.0 collective-permute-done.14.refs_7_
  38.9 6.1 %combine_odd.1 = f32[2592,128]{1,0:T(8,128)} custom-call(s32[1]{0:T(128)} %bitcast.me_ref, f32[162,8,128]{2,1,0:T(8,128)S(1)} %get-tuple-element.55.even_work, f32[4,8,128]{2,1,0:T(8,128)S(1)} %get-tuple-element.56.even_phases, f32[89,2,128]{2,1,0:T(2,128)S(1)} %collective-permute-done.8.refs_0_, f32[89,2,128]{2,1,0:T(2,128)S(1)} %collective-permute-done.9.refs_1_, ...), custom_call_target="tpu_custom_call" | custom-call | flops 83886080 | bytes 20971520 | tf_op jit(solution)/shard_map/combine_odd/pallas_call | solution.py:383
  (4 shorter events, 0.0 us)
Async XLA Ops:
  1.2 13.5 %collective-permute-start.1 = (f32[89,2,128]{2,1,0:T(2,128)S(1)}, f32[89,2,128]{2,1,0:T(2,128)S(1)}, u32[]{:S(2)}, u32[]{:S(2)}) collective-permute-start(f32[89,2,128]{2,1,0:T(2,128)S(1)} %get-tuple-element.42), channel_id=1, source_target_pairs={{0,14},{1,15},{2,12},{3,13},{4,10},{5,11},{6,8},{7,9},{8,6},{9,7},... | collective-permute-start | bytes 273416 | tf_op jit(solution)/shard_map/ppermute | solution.py:426
  7.3 12.5 %collective-permute-start.2 = (f32[89,2,128]{2,1,0:T(2,128)S(1)}, f32[89,2,128]{2,1,0:T(2,128)S(1)}, u32[]{:S(2)}, u32[]{:S(2)}) collective-permute-start(f32[89,2,128]{2,1,0:T(2,128)S(1)} %get-tuple-element.44), channel_id=1, source_target_pairs={{0,8},{1,9},{2,10},{3,11},{4,12},{5,13},{6,14},{7,15},{8,0},{9,1},... | collective-permute-start | bytes 273416 | tf_op jit(solution)/shard_map/ppermute | solution.py:426
  8.5 13.6 %collective-permute-start.9 = (f32[89,2,128]{2,1,0:T(2,128)S(1)}, f32[89,2,128]{2,1,0:T(2,128)S(1)}, u32[]{:S(2)}, u32[]{:S(2)}) collective-permute-start(f32[89,2,128]{2,1,0:T(2,128)S(1)} %get-tuple-element.60), channel_id=1, source_target_pairs={{0,7},{1,6},{2,5},{3,4},{4,3},{5,2},{6,1},{7,0},{8,15},{9,14},{10,... | collective-permute-start | bytes 273416 | tf_op jit(solution)/shard_map/ppermute | solution.py:426
  8.6 13.5 %collective-permute-start = (f32[89,2,128]{2,1,0:T(2,128)S(1)}, f32[89,2,128]{2,1,0:T(2,128)S(1)}, u32[]{:S(2)}, u32[]{:S(2)}) collective-permute-start(f32[89,2,128]{2,1,0:T(2,128)S(1)} %get-tuple-element.39), channel_id=1, source_target_pairs={{0,15},{1,14},{2,13},{3,12},{4,11},{5,10},{6,9},{7,8},{8,7},{9,6},... | collective-permute-start | bytes 273416 | tf_op jit(solution)/shard_map/ppermute | solution.py:426
  14.6 8.4 %collective-permute-start.8 = (f32[89,2,128]{2,1,0:T(2,128)S(1)}, f32[89,2,128]{2,1,0:T(2,128)S(1)}, u32[]{:S(2)}, u32[]{:S(2)}) collective-permute-start(f32[89,2,128]{2,1,0:T(2,128)S(1)} %get-tuple-element.58), channel_id=1, source_target_pairs={{0,9},{1,8},{2,11},{3,10},{4,13},{5,12},{6,15},{7,14},{8,1},{9,0},... | collective-permute-start | bytes 273416 | tf_op jit(solution)/shard_map/ppermute | solution.py:426
  14.7 11.9 %collective-permute-start.3 = (f32[89,2,128]{2,1,0:T(2,128)S(1)}, f32[89,2,128]{2,1,0:T(2,128)S(1)}, u32[]{:S(2)}, u32[]{:S(2)}) collective-permute-start(f32[89,2,128]{2,1,0:T(2,128)S(1)} %get-tuple-element.45), channel_id=1, source_target_pairs={{0,6},{1,7},{2,4},{3,5},{4,2},{5,3},{6,0},{7,1},{8,14},{9,15},{10,... | collective-permute-start | bytes 273416 | tf_op jit(solution)/shard_map/ppermute | solution.py:426
  19.7 8.3 %collective-permute-start.4 = (f32[89,2,128]{2,1,0:T(2,128)S(1)}, f32[89,2,128]{2,1,0:T(2,128)S(1)}, u32[]{:S(2)}, u32[]{:S(2)}) collective-permute-start(f32[89,2,128]{2,1,0:T(2,128)S(1)} %get-tuple-element.46), channel_id=1, source_target_pairs={{0,12},{1,13},{2,14},{3,15},{4,8},{5,9},{6,10},{7,11},{8,4},{9,5},... | collective-permute-start | bytes 273416 | tf_op jit(solution)/shard_map/ppermute | solution.py:426
  22.0 6.2 %collective-permute-start.6 = (f32[89,2,128]{2,1,0:T(2,128)S(1)}, f32[89,2,128]{2,1,0:T(2,128)S(1)}, u32[]{:S(2)}, u32[]{:S(2)}) collective-permute-start(f32[89,2,128]{2,1,0:T(2,128)S(1)} %get-tuple-element.48), channel_id=1, source_target_pairs={{0,4},{1,5},{2,6},{3,7},{4,0},{5,1},{6,2},{7,3},{8,12},{9,13},{10,... | collective-permute-start | bytes 273416 | tf_op jit(solution)/shard_map/ppermute | solution.py:426
  22.1 10.4 %collective-permute-start.7 = (f32[89,2,128]{2,1,0:T(2,128)S(1)}, f32[89,2,128]{2,1,0:T(2,128)S(1)}, u32[]{:S(2)}, u32[]{:S(2)}) collective-permute-start(f32[89,2,128]{2,1,0:T(2,128)S(1)} %get-tuple-element.49), channel_id=1, source_target_pairs={{0,10},{1,11},{2,8},{3,9},{4,14},{5,15},{6,12},{7,13},{8,2},{9,3},... | collective-permute-start | bytes 273416 | tf_op jit(solution)/shard_map/ppermute | solution.py:426
  22.9 9.6 %collective-permute-start.5 = (f32[89,2,128]{2,1,0:T(2,128)S(1)}, f32[89,2,128]{2,1,0:T(2,128)S(1)}, u32[]{:S(2)}, u32[]{:S(2)}) collective-permute-start(f32[89,2,128]{2,1,0:T(2,128)S(1)} %get-tuple-element.47), channel_id=1, source_target_pairs={{0,2},{1,3},{2,0},{3,1},{4,6},{5,7},{6,4},{7,5},{8,10},{9,11},{10,... | collective-permute-start | bytes 273416 | tf_op jit(solution)/shard_map/ppermute | solution.py:426
  26.6 12.2 %collective-permute-start.12 = (f32[89,2,128]{2,1,0:T(2,128)S(1)}, f32[89,2,128]{2,1,0:T(2,128)S(1)}, u32[]{:S(2)}, u32[]{:S(2)}) collective-permute-start(f32[89,2,128]{2,1,0:T(2,128)S(1)} %get-tuple-element.64), channel_id=1, source_target_pairs={{0,13},{1,12},{2,15},{3,14},{4,9},{5,8},{6,11},{7,10},{8,5},{9,4},... | collective-permute-start | bytes 273416 | tf_op jit(solution)/shard_map/ppermute | solution.py:426
  28.0 10.8 %collective-permute-start.13 = (f32[89,2,128]{2,1,0:T(2,128)S(1)}, f32[89,2,128]{2,1,0:T(2,128)S(1)}, u32[]{:S(2)}, u32[]{:S(2)}) collective-permute-start(f32[89,2,128]{2,1,0:T(2,128)S(1)} %get-tuple-element.65), channel_id=1, source_target_pairs={{0,11},{1,10},{2,9},{3,8},{4,15},{5,14},{6,13},{7,12},{8,3},{9,2},... | collective-permute-start | bytes 273416 | tf_op jit(solution)/shard_map/ppermute | solution.py:426
  28.2 10.6 %collective-permute-start.10 = (f32[89,2,128]{2,1,0:T(2,128)S(1)}, f32[89,2,128]{2,1,0:T(2,128)S(1)}, u32[]{:S(2)}, u32[]{:S(2)}) collective-permute-start(f32[89,2,128]{2,1,0:T(2,128)S(1)} %get-tuple-element.61), channel_id=1, source_target_pairs={{0,3},{1,2},{2,1},{3,0},{4,7},{5,6},{6,5},{7,4},{8,11},{9,10},{10,... | collective-permute-start | bytes 273416 | tf_op jit(solution)/shard_map/ppermute | solution.py:426
  32.5 6.4 %collective-permute-start.14 = (f32[89,2,128]{2,1,0:T(2,128)S(1)}, f32[89,2,128]{2,1,0:T(2,128)S(1)}, u32[]{:S(2)}, u32[]{:S(2)}) collective-permute-start(f32[89,2,128]{2,1,0:T(2,128)S(1)} %get-tuple-element.66), channel_id=1, source_target_pairs={{0,5},{1,4},{2,7},{3,6},{4,1},{5,0},{6,3},{7,2},{8,13},{9,12},{10,... | collective-permute-start | bytes 273416 | tf_op jit(solution)/shard_map/ppermute | solution.py:426
  32.5 6.4 %collective-permute-start.11 = (f32[89,2,128]{2,1,0:T(2,128)S(1)}, f32[89,2,128]{2,1,0:T(2,128)S(1)}, u32[]{:S(2)}, u32[]{:S(2)}) collective-permute-start(f32[89,2,128]{2,1,0:T(2,128)S(1)} %get-tuple-element.63), channel_id=1, source_target_pairs={{0,1},{1,0},{2,3},{3,2},{4,5},{5,4},{6,7},{7,6},{8,9},{9,8},{10,11... | collective-permute-start | bytes 273416 | tf_op jit(solution)/shard_map/ppermute | solution.py:426

commit v11 on v9

--- a/solution.py
+++ b/solution.py
@@ -19,12 +19,15 @@
 WEIGHT_ROWS = 2 * POINTS
 PHASE_ROWS = 4 * LEVELS
 ROWS = WEIGHT_ROWS + PHASE_ROWS
+PAIRS = ROWS // 2
+ACROSS_Y = 2
 OCT = SLOTS // 2
-PACKS = ((12, 4, 6, 10), (2, 14, 9, 15, 3, 11, 8, 7, 13, 5, 1, 0))
-SENDS = (8, 12, 4, 6, 2, 14, 15, 3, 11, 7, 13, 5, 1, 10, 9)
-WAITS = {9: 4, 1: 11}
-EVEN_ORDER = (8, 4, 2, 12, 10, 6, 14, 0)
-ODD_ORDER = (1, 3, 5, 11, 9, 15, 13, 7)
+PACKS = (((8, 10), (4, 6), (2,), (1, 3)), ((12,), (5,), (7,), (14,), (9, 11), (15,), (13,), (0,)))
+ONWARD = {"even": (2, 8, 4), "odd": (9, 1)}
+SENDS = (8, 4, 1, 12, 5, 7, 14, 9, 15, 13, "even", "odd")
+WAITS = {14: 1, 15: 5, 12: 8, 7: 5, 5: 8}
+EVEN_ORDER = (8, 12, 14, 4, "even", 0)
+ODD_ORDER = (1, 13, 15, 7, 5, "odd", 9)
 
 NODES = np.cos(math.pi * (2.0 * np.arange(CHEB) + 1.0) / (2.0 * CHEB))
 NODES[CHEB // 2] = 0.0
@@ -100,14 +103,19 @@
             phases_ref[row // 2, row % 2, :] = values[level]
 
 
-def pack_kernel(steps, first, me_ref, weights_hbm, *refs):
+def pack_kernel(messages, first, me_ref, weights_hbm, *refs):
+    count = len(messages)
     if first:
         small, refs = refs[:4], refs[4:]
-        outs, refs = refs[: len(steps)], refs[len(steps) :]
-        phases_ref, block_sems, scratch = refs[0], refs[1], refs[2:]
+        arrays, phases_ref, block_sems, scratch = refs[:count], refs[count], refs[count + 1], refs[count + 2 :]
     else:
-        phases_ref, outs, block_sems = refs[0], refs[1 : 1 + len(steps)], refs[1 + len(steps)]
-    slots = [me_ref[0] ^ step for step in steps]
+        phases_ref, arrays, block_sems = refs[0], refs[1 : 1 + count], refs[1 + count]
+    slots = [me_ref[0] ^ step for message in messages for step in message]
+    outs = [
+        array.at[pl.ds(index * PAIRS, PAIRS)]
+        for message, array in zip(messages, arrays)
+        for index in range(len(message))
+    ]
     copies = [
         pltpu.make_async_copy(weights_hbm.at[:, slot], out.at[pl.ds(0, POINTS)], block_sems.at[index])
         for index, (slot, out) in enumerate(zip(slots, outs))
@@ -122,12 +130,12 @@
         copy.wait()
 
 
-def pack(steps, me, weights, phases, sources):
+def pack(messages, me, weights, phases, sources):
     first = phases is None
     vmem = pl.BlockSpec(memory_space=pltpu.VMEM)
     hbm = pl.BlockSpec(memory_space=pltpu.HBM)
-    out_shape = [jax.ShapeDtypeStruct((ROWS // 2, 2, LANES), jnp.float32) for _ in steps]
-    scratch = [pltpu.SemaphoreType.DMA((len(steps),))]
+    out_shape = [jax.ShapeDtypeStruct((len(m) * PAIRS, 2, LANES), jnp.float32) for m in messages]
+    scratch = [pltpu.SemaphoreType.DMA((sum(map(len, messages)),))]
     if first:
         boxes = sources[-1].shape[-1]
         out_shape.append(jax.ShapeDtypeStruct((PHASE_ROWS // 2, 2, boxes), jnp.float32))
@@ -136,7 +144,7 @@
         scratch += [pltpu.SemaphoreType.DMA((len(sources),))]
     operands = sources if first else [phases]
     *arrays, last = pl.pallas_call(
-        functools.partial(pack_kernel, steps, first),
+        functools.partial(pack_kernel, messages, first),
         out_shape=out_shape,
         in_specs=[pl.BlockSpec(memory_space=pltpu.SMEM), hbm] + ([hbm] * len(sources) if first else [vmem]),
         out_specs=[vmem] * len(out_shape),
@@ -149,7 +157,7 @@
         phases = last
     else:
         arrays.append(last)
-    return dict(zip(steps, arrays)), phases
+    return {m[0]: array for m, array in zip(messages, arrays)}, phases
 
 
 def turn_both_ways(base, step):
@@ -244,11 +252,12 @@
     return part + 2 * (split * CHEB + column if level % 2 == 0 else column * CHEB + split)
 
 
-def join_chips(me, blocks, order, held, sems, work, last_phases, factors):
+def join_chips(me, arrays, pieces, held, sems, work, last_phases, factors):
     copies = []
-    for index, step in enumerate(order):
-        spot = pl.ds(((me ^ step) // 2) * (ROWS // 2), ROWS // 2)
-        copies.append(pltpu.make_async_copy(blocks[index], held.at[spot], sems.at[index]))
+    for step, (index, part) in pieces.items():
+        spot = pl.ds(((me ^ step) // 2) * PAIRS, PAIRS)
+        source = arrays[index].at[pl.ds(part * PAIRS, PAIRS)]
+        copies.append(pltpu.make_async_copy(source, held.at[spot], sems.at[step // 2]))
         copies[-1].start()
     for copy in copies:
         copy.wait()
@@ -288,14 +297,14 @@
         lax.fori_loop(0, CHEB, column_step, 0, unroll=3)
 
 
-def even_kernel(me_ref, *refs):
-    work, last_phases, held, parent_ref, child_ref, common_ref, sems = refs[OCT:]
+def even_kernel(pieces, count, me_ref, *refs):
+    work, last_phases, held, parent_ref, child_ref, common_ref, sems = refs[count:]
     factors = (parent_ref, child_ref, common_ref)
-    join_chips(me_ref[0], refs, EVEN_ORDER, held, sems, work, last_phases, factors)
-
-
-def odd_kernel(me_ref, even_work, even_phases, *refs):
-    out_hbm, work, last_phases, held, out_ref, parent_ref, child_ref, common_ref, sems, out_sems = refs[OCT:]
+    join_chips(me_ref[0], refs, pieces, held, sems, work, last_phases, factors)
+
+
+def odd_kernel(pieces, count, me_ref, even_work, even_phases, *refs):
+    out_hbm, work, last_phases, held, out_ref, parent_ref, child_ref, common_ref, sems, out_sems = refs[count:]
     me = me_ref[0]
     own = me % 2
     early = [
@@ -305,7 +314,7 @@
     for copy in early:
         copy.start()
     factors = [ref.at[0] for ref in (parent_ref, child_ref, common_ref)]
-    join_chips(me, refs, ODD_ORDER, held, sems, work.at[1 - own], last_phases.at[1 - own], factors)
+    join_chips(me, refs, pieces, held, sems, work.at[1 - own], last_phases.at[1 - own], factors)
     for copy in early:
         copy.wait()
 
@@ -355,39 +364,39 @@
     ]
 
 
-def combine_even(me, blocks):
+def combine_even(me, arrays, pieces):
     vmem = pl.BlockSpec(memory_space=pltpu.VMEM)
     return pl.pallas_call(
-        even_kernel,
+        functools.partial(even_kernel, pieces, len(arrays)),
         out_shape=[
             jax.ShapeDtypeStruct((WEIGHT_ROWS, OCT, LANES), jnp.float32),
             jax.ShapeDtypeStruct((4, OCT, LANES), jnp.float32),
         ],
-        in_specs=[pl.BlockSpec(memory_space=pltpu.SMEM)] + [pl.BlockSpec(memory_space=pl.ANY)] * OCT,
+        in_specs=[pl.BlockSpec(memory_space=pltpu.SMEM)] + [pl.BlockSpec(memory_space=pl.ANY)] * len(arrays),
         out_specs=[vmem, vmem],
         scratch_shapes=[
-            pltpu.VMEM((OCT * ROWS // 2, 2, LANES), jnp.float32),
+            pltpu.VMEM((OCT * PAIRS, 2, LANES), jnp.float32),
             *factor_scratch(()),
             pltpu.SemaphoreType.DMA((OCT,)),
         ],
         compiler_params=pltpu.CompilerParams(vmem_limit_bytes=16 * 2**20),
         cost_estimate=pl.CostEstimate(flops=40 * 2**20, bytes_accessed=12 * 2**20, transcendentals=0),
         name="combine_even",
-    )(me, *blocks)
-
-
-def combine_odd(me, even, blocks):
+    )(me, *arrays)
+
+
+def combine_odd(me, even, arrays, pieces):
     hbm = pl.BlockSpec(memory_space=pltpu.HBM)
     anywhere = pl.BlockSpec(memory_space=pl.ANY)
     return pl.pallas_call(
-        odd_kernel,
+        functools.partial(odd_kernel, pieces, len(arrays)),
         out_shape=jax.ShapeDtypeStruct((WEIGHT_ROWS * SLOTS, LANES), jnp.float32),
-        in_specs=[pl.BlockSpec(memory_space=pltpu.SMEM)] + [anywhere] * (2 + OCT),
+        in_specs=[pl.BlockSpec(memory_space=pltpu.SMEM)] + [anywhere] * (2 + len(arrays)),
         out_specs=hbm,
         scratch_shapes=[
             pltpu.VMEM((2, WEIGHT_ROWS, OCT, LANES), jnp.float32),
             pltpu.VMEM((2, 4, OCT, LANES), jnp.float32),
-            pltpu.VMEM((OCT * ROWS // 2, 2, LANES), jnp.float32),
+            pltpu.VMEM((OCT * PAIRS, 2, LANES), jnp.float32),
             pltpu.VMEM((WEIGHT_ROWS * SLOTS, LANES), jnp.float32),
             *factor_scratch((2,)),
             pltpu.SemaphoreType.DMA((OCT,)),
@@ -396,7 +405,7 @@
         compiler_params=pltpu.CompilerParams(vmem_limit_bytes=16 * 2**20),
         cost_estimate=pl.CostEstimate(flops=80 * 2**20, bytes_accessed=20 * 2**20, transcendentals=0),
         name="combine_odd",
-    )(me, *even, *blocks)
+    )(me, *even, *arrays)
 
 
 def on_device(source_weights, wave_vectors, source_centers, phase_coef, phase_kind):
@@ -411,24 +420,42 @@
         for operand in (weights, phase_coef, wave_vectors, source_centers, phase_kind[None, :])
     ]
     blocks, phases = {}, None
-    for steps in PACKS:
+    for messages in PACKS:
         if blocks:
             last = next(reversed(blocks))
             phases, blocks[last] = lax.optimization_barrier((phases, blocks[last]))
-        packed, phases = pack(steps, me, weights, phases, sources)
+        packed, phases = pack(messages, me, weights, phases, sources)
         blocks.update(packed)
+    inside = {m[0]: m for messages in PACKS for m in messages}
     if direct:
-        for step in SENDS:
-            if step in WAITS:
-                earlier = WAITS[step]
-                blocks[step], blocks[earlier] = lax.optimization_barrier((blocks[step], blocks[earlier]))
-            blocks[step] = lax.ppermute(blocks[step], "box", [(s, s ^ step) for s in range(SLOTS)])
+        pairs = {step for step, message in inside.items() if len(message) > 1}
+        for name in SENDS:
+            step = name
+            if name in ONWARD:
+                step = ACROSS_Y
+                parts = [blocks[part][PAIRS:] if part in pairs else blocks[part] for part in ONWARD[name]]
+                blocks[name] = jnp.concatenate(parts)
+                inside[name] = tuple(part ^ ACROSS_Y if part in pairs else part for part in ONWARD[name])
+            if name in WAITS:
+                earlier = WAITS[name]
+                blocks[name], blocks[earlier] = lax.optimization_barrier((blocks[name], blocks[earlier]))
+            blocks[name] = lax.ppermute(blocks[name], "box", [(s, s ^ step) for s in range(SLOTS)])
+            inside[step] = inside[step] if name in ONWARD else inside[step][:1]
+        orders = EVEN_ORDER, ODD_ORDER
     else:
-        whole = jnp.concatenate([blocks[step] for step in range(SLOTS)], axis=2)
+        parts = {step: blocks[m[0]][i * PAIRS : (i + 1) * PAIRS] for m in inside.values() for i, step in enumerate(m)}
+        whole = jnp.concatenate([parts[step] for step in range(SLOTS)], axis=2)
         whole = lax.all_to_all(whole, "box", split_axis=2, concat_axis=2, tiled=True)
-        blocks = [whole[:, :, s * LANES : (s + 1) * LANES] for s in range(SLOTS)]
-    even = combine_even(me, [blocks[step] for step in EVEN_ORDER])
-    rows = combine_odd(me, even, [blocks[step] for step in ODD_ORDER])
+        blocks = {s: whole[:, :, s * LANES : (s + 1) * LANES] for s in range(SLOTS)}
+        inside = {s: (s,) for s in range(SLOTS)}
+        orders = range(0, SLOTS, 2), range(1, SLOTS, 2)
+    arrays = [[blocks[name] for name in order] for order in orders]
+    pieces = [
+        {step: (index, part) for index, name in enumerate(order) for part, step in enumerate(inside[name])}
+        for order in orders
+    ]
+    even = combine_even(me, arrays[0], pieces[0])
+    rows = combine_odd(me, even, arrays[1], pieces[1])
     return rows.reshape(POINTS, SLOTS, 2, LANES).transpose(2, 0, 1, 3).reshape(2, POINTS, SLOTS * LANES)
 
 

time: 46 us -> 46.2 us (level)
  starting transfers between devices: 28.1 us -> 21.9 us
  waiting for transfers between devices: 5.11 us -> 11.2 us
    ppermute x15 -> x12, starting transfers between devices: 28.1 us -> 21.9 us  [on_device(): lax.ppermute(blocks[name], 'box', [(s, s ^ step) for s in range(SLOTS)])]
    ppermute x15 -> x12, waiting for transfers between devices: 5.11 us -> 11.2 us  [on_device(): lax.ppermute(blocks[name], 'box', [(s, s ^ step) for s in range(SLOTS)])]
  transfers between devices with their start and end apart: 15 -> 12, of which waited for: 2 -> 4; matrix products, arithmetic and copies ran while one was open for 0% -> 1% of each run, Pallas kernels for 11% -> 11%
where the time goes in v11:
time: 46.2 us; the launch traced here: 46 us
  starting transfers between devices  21.9 us (47%)
  Pallas kernels  12.5 us (27%)
  waiting for transfers between devices  11.2 us (24%)
    ppermute x12, starting transfers between devices, on_device(): lax.ppermute(blocks[name], 'box', [(s, s ^ step) for s in range(SLOTS)])  21.9 us
    ppermute x12, waiting for transfers between devices, on_device(): lax.ppermute(blocks[name], 'box', [(s, s ^ step) for s in range(SLOTS)])  11.2 us
    pallas_call x1, Pallas kernels, combine_odd(): pl.pallas_call(functools.partial(odd_kernel, pieces, len(arrays)), out_sh...  6.13 us
    pallas_call x1, Pallas kernels, combine_even(): pl.pallas_call(functools.partial(even_kernel, pieces, len(arrays)), out_s...  3.62 us
    pallas_call x2, Pallas kernels, pack(): pl.pallas_call(functools.partial(pack_kernel, messages, first), out_shape...  2.74 us
  transfers between devices with their start and end apart: 12, of which 4 were waited for; matrix products, arithmetic and copies ran while one was open for 1% of the time, Pallas kernels for 11%

profile of v11, /device:TPU:0, one launch (start us, length us, event | category | flops | bytes accessed | tf_op | source)
XLA Modules:
  0.0 46.0 jit_solution(12810864122856432989)
XLA Ops:
  0.0 1.4 %pack.2 = (f32[178,2,128]{2,1,0:T(2,128)S(1)}, f32[178,2,128]{2,1,0:T(2,128)S(1)}, f32[89,2,128]{2,1,0:T(2,128)S(1)}, f32[178,2,128]{2,1,0:T(2,128)S(1)}, f32[8,2,2048]{2,1,0:T(2,128)S(1)}) custom-call(s32[1]{0:T(128)} %bitcast.me_ref, f32[81,16,2,128]{3,2,1,0:T(2,128)} %bitcast.10, f32[4,3]{1,0:T(4,128)} %refs_0_.1, f32[4,2,2048]{2,1,0:T(2,128)} %refs_1_.1, ...), custom_call_target="tpu_custom_call" | custom-call | flops 1048576 | bytes 1048576 | tf_op jit(solution)/shard_map/pack/pallas_call | solution.py:146
  1.4 4.1 %collective-permute-start = (f32[178,2,128]{2,1,0:T(2,128)S(1)}, f32[178,2,128]{2,1,0:T(2,128)S(1)}, u32[]{:S(2)}, u32[]{:S(2)}) collective-permute-start(f32[178,2,128]{2,1,0:T(2,128)S(1)} %get-tuple-element.37), channel_id=1, source_target_pairs={{0,8},{1,9},{2,10},{3,11},{4,12},{5,13},{6,14},{7,15},{8,0},{9,1},... | collective-permute-start | bytes 546824 | tf_op jit(solution)/shard_map/ppermute | solution.py:442
  5.5 0.0 collective-permute-start.2
  5.5 1.6 %collective-permute-start.4 = (f32[178,2,128]{2,1,0:T(2,128)S(1)}, f32[178,2,128]{2,1,0:T(2,128)S(1)}, u32[]{:S(2)}, u32[]{:S(2)}) collective-permute-start(f32[178,2,128]{2,1,0:T(2,128)S(1)} %get-tuple-element.44), channel_id=1, source_target_pairs={{0,4},{1,5},{2,6},{3,7},{4,0},{5,1},{6,2},{7,3},{8,12},{9,13},{10,... | collective-permute-start | bytes 546824 | tf_op jit(solution)/shard_map/ppermute | solution.py:442
  7.1 1.3 %pack.3 = (f32[89,2,128]{2,1,0:T(2,128)S(1)}, f32[89,2,128]{2,1,0:T(2,128)S(1)}, f32[89,2,128]{2,1,0:T(2,128)S(1)}, f32[89,2,128]{2,1,0:T(2,128)S(1)}, f32[178,2...) custom-call(s32[1]{0:T(128)} %bitcast.me_ref, ...), custom_call_target="tpu_custom_call" | custom-call | flops 1048576 | bytes 1048576 | tf_op jit(solution)/shard_map/pack/pallas_call | solution.py:146
  8.4 0.2 collective-permute-start.10
  8.7 7.1 %collective-permute-done.refs_0_ = f32[178,2,128]{2,1,0:T(2,128)S(1)} collective-permute-done((f32[178,2,128]{2,1,0:T(2,128)S(1)}, f32[178,2,128]{2,1,0:T(2,128)S(1)}, u32[]{:S(2)}, u32[]{:S(2)}) %collective-permute-start) | collective-permute-done | bytes 182304 | tf_op jit(solution)/shard_map/ppermute | solution.py:442
  15.8 0.0 collective-permute-done.2.refs_0_
  15.8 4.1 %collective-permute-start.3 = (f32[89,2,128]{2,1,0:T(2,128)S(1)}, f32[89,2,128]{2,1,0:T(2,128)S(1)}, u32[]{:S(2)}, u32[]{:S(2)}) collective-permute-start(f32[89,2,128]{2,1,0:T(2,128)S(1)} %get-tuple-element.43), channel_id=1, source_target_pairs={{0,14},{1,15},{2,12},{3,13},{4,10},{5,11},{6,8},{7,9},{8,6},{9,7},... | collective-permute-start | bytes 273416 | tf_op jit(solution)/shard_map/ppermute | solution.py:442
  19.9 0.0 collective-permute-start.7
  19.9 4.1 %collective-permute-start.1 = (f32[89,2,128]{2,1,0:T(2,128)S(1)}, f32[89,2,128]{2,1,0:T(2,128)S(1)}, u32[]{:S(2)}, u32[]{:S(2)}) collective-permute-start(f32[89,2,128]{2,1,0:T(2,128)S(1)} %get-tuple-element.40), channel_id=1, source_target_pairs={{0,12},{1,13},{2,14},{3,15},{4,8},{5,9},{6,10},{7,11},{8,4},{9,5},... | collective-permute-start | bytes 273416 | tf_op jit(solution)/shard_map/ppermute | solution.py:442
  24.0 0.0 collective-permute-done.4.refs_3_
  24.0 0.1 pad_maximum_fusion
  24.2 0.1 collective-permute-start.5
  24.3 0.0 collective-permute-done.10.refs_6_
  24.3 0.1 pad_maximum_fusion.1
  24.4 2.1 %collective-permute-start.11 = (f32[178,2,128]{2,1,0:T(2,128)S(1)}, f32[178,2,128]{2,1,0:T(2,128)S(1)}, u32[]{:S(2)}, u32[]{:S(2)}) collective-permute-start(f32[178,2,128]{2,1,0:T(2,128)S(1)} %pad_maximum_fusion.1), channel_id=1, source_target_pairs={{0,2},{1,3},{2,0},{3,1},{4,6},{5,7},{6,4},{7,5},{8,10},{9,11},{10,... | collective-permute-start | bytes 546824 | tf_op jit(solution)/shard_map/ppermute | solution.py:442
  26.4 0.6 %collective-permute-done.7.refs_4_ = f32[89,2,128]{2,1,0:T(2,128)S(1)} collective-permute-done((f32[89,2,128]{2,1,0:T(2,128)S(1)}, f32[89,2,128]{2,1,0:T(2,128)S(1)}, u32[]{:S(2)}, u32[]{:S(2)}) %collective-permute-start.7) | collective-permute-done | bytes 91168 | tf_op jit(solution)/shard_map/ppermute | solution.py:442
  27.1 3.8 %collective-permute-start.6 = (f32[89,2,128]{2,1,0:T(2,128)S(1)}, f32[89,2,128]{2,1,0:T(2,128)S(1)}, u32[]{:S(2)}, u32[]{:S(2)}) collective-permute-start(f32[89,2,128]{2,1,0:T(2,128)S(1)} %get-tuple-element.50), channel_id=1, source_target_pairs={{0,13},{1,12},{2,15},{3,14},{4,9},{5,8},{6,11},{7,10},{8,5},{9,4},... | collective-permute-start | bytes 273416 | tf_op jit(solution)/shard_map/ppermute | solution.py:442
  30.9 0.0 collective-permute-done.3.refs_2_
  30.9 1.4 %collective-permute-start.8 = (f32[89,2,128]{2,1,0:T(2,128)S(1)}, f32[89,2,128]{2,1,0:T(2,128)S(1)}, u32[]{:S(2)}, u32[]{:S(2)}) collective-permute-start(f32[89,2,128]{2,1,0:T(2,128)S(1)} %get-tuple-element.55), channel_id=1, source_target_pairs={{0,15},{1,14},{2,13},{3,12},{4,11},{5,10},{6,9},{7,8},{8,7},{9,6},... | collective-permute-start | bytes 273416 | tf_op jit(solution)/shard_map/ppermute | solution.py:442
  32.3 0.0 collective-permute-done.1.refs_1_
  32.3 0.4 collective-permute-start.9
  32.7 0.0 collective-permute-done.5.refs_4_
  32.7 3.6 %combine_even.1 = (f32[162,8,128]{2,1,0:T(8,128)S(1)}, f32[4,8,128]{2,1,0:T(8,128)S(1)}) custom-call(s32[1]{0:T(128)} %bitcast.me_ref, f32[178,2,128]{2,1,0:T(2,128)S(1)} %collective-permute-done.refs_0_, f32[89,2,128]{2,1,0:T(2,128)S(1)} %collective-permute-done.1.refs_1_, f32[89,2,128]{2,1,0:T(2,128)S(1)} %collective-permute-done.3.refs_2_, ...), custom_call_target="tpu_custom_call" | custom-call | flops 41943040 | bytes 12582912 | tf_op jit(solution)/shard_map/combine_even/pallas_call | solution.py:369
  36.3 0.0 collective-permute-done.6.refs_1_
  36.4 1.7 %collective-permute-done.8.refs_2_ = f32[89,2,128]{2,1,0:T(2,128)S(1)} collective-permute-done((f32[89,2,128]{2,1,0:T(2,128)S(1)}, f32[89,2,128]{2,1,0:T(2,128)S(1)}, u32[]{:S(2)}, u32[]{:S(2)}) %collective-permute-start.8) | collective-permute-done | bytes 91168 | tf_op jit(solution)/shard_map/ppermute | solution.py:442
  38.0 1.8 %collective-permute-done.9.refs_3_ = f32[89,2,128]{2,1,0:T(2,128)S(1)} collective-permute-done((f32[89,2,128]{2,1,0:T(2,128)S(1)}, f32[89,2,128]{2,1,0:T(2,128)S(1)}, u32[]{:S(2)}, u32[]{:S(2)}) %collective-permute-start.9) | collective-permute-done | bytes 91168 | tf_op jit(solution)/shard_map/ppermute | solution.py:442
  39.9 0.0 collective-permute-done.11.refs_5_
  39.9 6.1 %combine_odd.1 = f32[2592,128]{1,0:T(8,128)} custom-call(s32[1]{0:T(128)} %bitcast.me_ref, f32[162,8,128]{2,1,0:T(8,128)S(1)} %get-tuple-element.47.even_work, f32[4,8,128]{2,1,0:T(8,128)S(1)} %get-tuple-element.48.even_phases, f32[178,2,128]{2,1,0:T(2,128)S(1)} %collective-permute-done.2.refs_0_, f32[89,2,128]{2,1,0:T(2,128)S(1)} %collective-permute-done.6.refs_1_, ...), custom_call_target="tpu_custom_call" | custom-call | flops 83886080 | bytes 20971520 | tf_op jit(solution)/shard_map/combine_odd/pallas_call | solution.py:391
  (4 shorter events, 0.0 us)
Async XLA Ops:
  1.4 14.3 %collective-permute-start = (f32[178,2,128]{2,1,0:T(2,128)S(1)}, f32[178,2,128]{2,1,0:T(2,128)S(1)}, u32[]{:S(2)}, u32[]{:S(2)}) collective-permute-start(f32[178,2,128]{2,1,0:T(2,128)S(1)} %get-tuple-element.37), channel_id=1, source_target_pairs={{0,8},{1,9},{2,10},{3,11},{4,12},{5,13},{6,14},{7,15},{8,0},{9,1},... | collective-permute-start | bytes 546824 | tf_op jit(solution)/shard_map/ppermute | solution.py:442
  5.5 10.2 %collective-permute-start.2 = (f32[178,2,128]{2,1,0:T(2,128)S(1)}, f32[178,2,128]{2,1,0:T(2,128)S(1)}, u32[]{:S(2)}, u32[]{:S(2)}) collective-permute-start(f32[178,2,128]{2,1,0:T(2,128)S(1)} %get-tuple-element.42), channel_id=1, source_target_pairs={{0,1},{1,0},{2,3},{3,2},{4,5},{5,4},{6,7},{7,6},{8,9},{9,8},{10,11... | collective-permute-start | bytes 546824 | tf_op jit(solution)/shard_map/ppermute | solution.py:442
  5.5 18.5 %collective-permute-start.4 = (f32[178,2,128]{2,1,0:T(2,128)S(1)}, f32[178,2,128]{2,1,0:T(2,128)S(1)}, u32[]{:S(2)}, u32[]{:S(2)}) collective-permute-start(f32[178,2,128]{2,1,0:T(2,128)S(1)} %get-tuple-element.44), channel_id=1, source_target_pairs={{0,4},{1,5},{2,6},{3,7},{4,0},{5,1},{6,2},{7,3},{8,12},{9,13},{10,... | collective-permute-start | bytes 546824 | tf_op jit(solution)/shard_map/ppermute | solution.py:442
  8.4 15.8 %collective-permute-start.10 = (f32[178,2,128]{2,1,0:T(2,128)S(1)}, f32[178,2,128]{2,1,0:T(2,128)S(1)}, u32[]{:S(2)}, u32[]{:S(2)}) collective-permute-start(f32[178,2,128]{2,1,0:T(2,128)S(1)} %get-tuple-element.58), channel_id=1, source_target_pairs={{0,9},{1,8},{2,11},{3,10},{4,13},{5,12},{6,15},{7,14},{8,1},{9,0},... | collective-permute-start | bytes 546824 | tf_op jit(solution)/shard_map/ppermute | solution.py:442
  15.8 15.1 %collective-permute-start.3 = (f32[89,2,128]{2,1,0:T(2,128)S(1)}, f32[89,2,128]{2,1,0:T(2,128)S(1)}, u32[]{:S(2)}, u32[]{:S(2)}) collective-permute-start(f32[89,2,128]{2,1,0:T(2,128)S(1)} %get-tuple-element.43), channel_id=1, source_target_pairs={{0,14},{1,15},{2,12},{3,13},{4,10},{5,11},{6,8},{7,9},{8,6},{9,7},... | collective-permute-start | bytes 273416 | tf_op jit(solution)/shard_map/ppermute | solution.py:442
  19.9 7.1 %collective-permute-start.7 = (f32[89,2,128]{2,1,0:T(2,128)S(1)}, f32[89,2,128]{2,1,0:T(2,128)S(1)}, u32[]{:S(2)}, u32[]{:S(2)}) collective-permute-start(f32[89,2,128]{2,1,0:T(2,128)S(1)} %get-tuple-element.53), channel_id=1, source_target_pairs={{0,5},{1,4},{2,7},{3,6},{4,1},{5,0},{6,3},{7,2},{8,13},{9,12},{10,... | collective-permute-start | bytes 273416 | tf_op jit(solution)/shard_map/ppermute | solution.py:442
  19.9 12.4 %collective-permute-start.1 = (f32[89,2,128]{2,1,0:T(2,128)S(1)}, f32[89,2,128]{2,1,0:T(2,128)S(1)}, u32[]{:S(2)}, u32[]{:S(2)}) collective-permute-start(f32[89,2,128]{2,1,0:T(2,128)S(1)} %get-tuple-element.40), channel_id=1, source_target_pairs={{0,12},{1,13},{2,14},{3,15},{4,8},{5,9},{6,10},{7,11},{8,4},{9,5},... | collective-permute-start | bytes 273416 | tf_op jit(solution)/shard_map/ppermute | solution.py:442
  24.2 8.5 %collective-permute-start.5 = (f32[267,2,128]{2,1,0:T(2,128)S(1)}, f32[267,2,128]{2,1,0:T(2,128)S(1)}, u32[]{:S(2)}, u32[]{:S(2)}) collective-permute-start(f32[267,2,128]{2,1,0:T(2,128)S(1)} %pad_maximum_fusion), channel_id=1, source_target_pairs={{0,2},{1,3},{2,0},{3,1},{4,6},{5,7},{6,4},{7,5},{8,10},{9,11},{10,... | collective-permute-start | bytes 820232 | tf_op jit(solution)/shard_map/ppermute | solution.py:442
  24.4 15.5 %collective-permute-start.11 = (f32[178,2,128]{2,1,0:T(2,128)S(1)}, f32[178,2,128]{2,1,0:T(2,128)S(1)}, u32[]{:S(2)}, u32[]{:S(2)}) collective-permute-start(f32[178,2,128]{2,1,0:T(2,128)S(1)} %pad_maximum_fusion.1), channel_id=1, source_target_pairs={{0,2},{1,3},{2,0},{3,1},{4,6},{5,7},{6,4},{7,5},{8,10},{9,11},{10,... | collective-permute-start | bytes 546824 | tf_op jit(solution)/shard_map/ppermute | solution.py:442
  27.1 9.3 %collective-permute-start.6 = (f32[89,2,128]{2,1,0:T(2,128)S(1)}, f32[89,2,128]{2,1,0:T(2,128)S(1)}, u32[]{:S(2)}, u32[]{:S(2)}) collective-permute-start(f32[89,2,128]{2,1,0:T(2,128)S(1)} %get-tuple-element.50), channel_id=1, source_target_pairs={{0,13},{1,12},{2,15},{3,14},{4,9},{5,8},{6,11},{7,10},{8,5},{9,4},... | collective-permute-start | bytes 273416 | tf_op jit(solution)/shard_map/ppermute | solution.py:442
  30.9 7.1 %collective-permute-start.8 = (f32[89,2,128]{2,1,0:T(2,128)S(1)}, f32[89,2,128]{2,1,0:T(2,128)S(1)}, u32[]{:S(2)}, u32[]{:S(2)}) collective-permute-start(f32[89,2,128]{2,1,0:T(2,128)S(1)} %get-tuple-element.55), channel_id=1, source_target_pairs={{0,15},{1,14},{2,13},{3,12},{4,11},{5,10},{6,9},{7,8},{8,7},{9,6},... | collective-permute-start | bytes 273416 | tf_op jit(solution)/shard_map/ppermute | solution.py:442
  32.3 7.6 %collective-permute-start.9 = (f32[89,2,128]{2,1,0:T(2,128)S(1)}, f32[89,2,128]{2,1,0:T(2,128)S(1)}, u32[]{:S(2)}, u32[]{:S(2)}) collective-permute-start(f32[89,2,128]{2,1,0:T(2,128)S(1)} %get-tuple-element.56), channel_id=1, source_target_pairs={{0,7},{1,6},{2,5},{3,4},{4,3},{5,2},{6,1},{7,0},{8,15},{9,14},{10,... | collective-permute-start | bytes 273416 | tf_op jit(solution)/shard_map/ppermute | solution.py:442

commit v12 on v9

--- a/solution.py
+++ b/solution.py
@@ -20,11 +20,11 @@
 PHASE_ROWS = 4 * LEVELS
 ROWS = WEIGHT_ROWS + PHASE_ROWS
 OCT = SLOTS // 2
-PACKS = ((12, 4, 6, 10), (2, 14, 9, 15, 3, 11, 8, 7, 13, 5, 1, 0))
-SENDS = (8, 12, 4, 6, 2, 14, 15, 3, 11, 7, 13, 5, 1, 10, 9)
+PACKS = ((12, 4, 6, 10), (2, 14, 9, 15, 3, 11, 8), (7, 13, 5, 1, 0))
+SENDS = (12, 4, 8, 6, 2, 14, 15, 3, 10, 11, 7, 13, 5, 1, 9)
 WAITS = {9: 4, 1: 11}
-EVEN_ORDER = (8, 4, 2, 12, 10, 6, 14, 0)
-ODD_ORDER = (1, 3, 5, 11, 9, 15, 13, 7)
+EVEN_ORDER = (10, 6, 12, 14, 4, 2, 8, 0)
+ODD_ORDER = (3, 11, 15, 9, 13, 1, 7, 5)
 
 NODES = np.cos(math.pi * (2.0 * np.arange(CHEB) + 1.0) / (2.0 * CHEB))
 NODES[CHEB // 2] = 0.0

time: 46 us -> 45.7 us (level)
  starting transfers between devices: 28.1 us -> 23.3 us
  waiting for transfers between devices: 5.11 us -> 8.77 us
  Pallas kernels: 12.4 us -> 13.3 us
    ppermute x15, starting transfers between devices: 28.1 us -> 23.3 us  [on_device(): lax.ppermute(blocks[step], 'box', [(s, s ^ step) for s in range(SLOTS)])]
    ppermute x15, waiting for transfers between devices: 5.11 us -> 8.77 us  [on_device(): lax.ppermute(blocks[step], 'box', [(s, s ^ step) for s in range(SLOTS)])]
    pallas_call x2 -> x3, Pallas kernels: 2.68 us -> 3.57 us  [pack(): pl.pallas_call(functools.partial(pack_kernel, steps, first), out_shape=ou...]
  transfers between devices with their start and end apart: 15 -> 15, of which waited for: 2 -> 3; matrix products, arithmetic and copies ran while one was open for 0% -> 0% of each run, Pallas kernels for 11% -> 13%
where the time goes in v12:
time: 45.7 us; the launch traced here: 45.4 us
  starting transfers between devices  23.3 us (51%)
  Pallas kernels  13.3 us (29%)
  waiting for transfers between devices  8.77 us (19%)
    ppermute x15, starting transfers between devices, on_device(): lax.ppermute(blocks[step], 'box', [(s, s ^ step) for s in range(SLOTS)])  23.3 us
    ppermute x15, waiting for transfers between devices, on_device(): lax.ppermute(blocks[step], 'box', [(s, s ^ step) for s in range(SLOTS)])  8.77 us
    pallas_call x1, Pallas kernels, combine_odd(): pl.pallas_call(odd_kernel, out_shape=jax.ShapeDtypeStruct((WEIGHT_ROWS *...  6.13 us
    pallas_call x1, Pallas kernels, combine_even(): pl.pallas_call(even_kernel, out_shape=[jax.ShapeDtypeStruct((WEIGHT_ROWS,...  3.61 us
    pallas_call x3, Pallas kernels, pack(): pl.pallas_call(functools.partial(pack_kernel, steps, first), out_shape=ou...  3.57 us
  transfers between devices with their start and end apart: 15, of which 3 were waited for; matrix products, arithmetic and copies ran while one was open for 0% of the time, Pallas kernels for 13%

profile of v12, /device:TPU:0, one launch (start us, length us, event | category | flops | bytes accessed | tf_op | source)
XLA Modules:
  0.0 45.4 jit_solution(3384193383210698933)
XLA Ops:
  0.0 1.2 %pack.3 = (f32[89,2,128]{2,1,0:T(2,128)S(1)}, f32[89,2,128]{2,1,0:T(2,128)S(1)}, f32[89,2,128]{2,1,0:T(2,128)S(1)}, f32[89,2,128]{2,1,0:T(2,128)S(1)}, f32[8,2,2048]{2,1,0:T(2,128)S(1)}) custom-call(s32[1]{0:T(128)} %bitcast.me_ref, f32[81,16,2,128]{3,2,1,0:T(2,128)} %bitcast.10, f32[4,3]{1,0:T(4,128)} %refs_0_.1, f32[4,2,2048]{2,1,0:T(2,128)} %refs_1_.1, ...), custom_call_target="tpu_custom_call" | custom-call | flops 1048576 | bytes 1048576 | tf_op jit(solution)/shard_map/pack/pallas_call | solution.py:138
  1.2 5.1 %collective-permute-start = (f32[89,2,128]{2,1,0:T(2,128)S(1)}, f32[89,2,128]{2,1,0:T(2,128)S(1)}, u32[]{:S(2)}, u32[]{:S(2)}) collective-permute-start(f32[89,2,128]{2,1,0:T(2,128)S(1)} %get-tuple-element.34), channel_id=1, source_target_pairs={{0,10},{1,11},{2,8},{3,9},{4,14},{5,15},{6,12},{7,13},{8,2},{9,3},... | collective-permute-start | bytes 273416 | tf_op jit(solution)/shard_map/ppermute | solution.py:425
  6.3 1.5 %collective-permute-start.1 = (f32[89,2,128]{2,1,0:T(2,128)S(1)}, f32[89,2,128]{2,1,0:T(2,128)S(1)}, u32[]{:S(2)}, u32[]{:S(2)}) collective-permute-start(f32[89,2,128]{2,1,0:T(2,128)S(1)} %get-tuple-element.35), channel_id=1, source_target_pairs={{0,6},{1,7},{2,4},{3,5},{4,2},{5,3},{6,0},{7,1},{8,14},{9,15},{10,... | collective-permute-start | bytes 273416 | tf_op jit(solution)/shard_map/ppermute | solution.py:425
  7.8 0.0 collective-permute-start.2
  7.8 0.9 %collective-permute-start.4 = (f32[89,2,128]{2,1,0:T(2,128)S(1)}, f32[89,2,128]{2,1,0:T(2,128)S(1)}, u32[]{:S(2)}, u32[]{:S(2)}) collective-permute-start(f32[89,2,128]{2,1,0:T(2,128)S(1)} %get-tuple-element.40), channel_id=1, source_target_pairs={{0,4},{1,5},{2,6},{3,7},{4,0},{5,1},{6,2},{7,3},{8,12},{9,13},{10,... | collective-permute-start | bytes 273416 | tf_op jit(solution)/shard_map/ppermute | solution.py:425
  8.7 1.2 %pack.4 = (f32[89,2,128]{2,1,0:T(2,128)S(1)}, f32[89,2,128]{2,1,0:T(2,128)S(1)}, f32[89,2,128]{2,1,0:T(2,128)S(1)}, f32[89,2,128]{2,1,0:T(2,128)S(1)}, f32[89,2,...) custom-call(s32[1]{0:T(128)} %bitcast.me_ref, f32[81,16,2,128]{3,2,1,0:T(2,128)} %bitcast.11, ...), custom_call_target="tpu_custom_call" | custom-call | flops 1048576 | bytes 1048576 | tf_op jit(solution)/shard_map/pack/pallas_call | solution.py:138
  10.0 2.8 %collective-permute-start.8 = (f32[89,2,128]{2,1,0:T(2,128)S(1)}, f32[89,2,128]{2,1,0:T(2,128)S(1)}, u32[]{:S(2)}, u32[]{:S(2)}) collective-permute-start(f32[89,2,128]{2,1,0:T(2,128)S(1)} %get-tuple-element.51), channel_id=1, source_target_pairs={{0,11},{1,10},{2,9},{3,8},{4,15},{5,14},{6,13},{7,12},{8,3},{9,2},... | collective-permute-start | bytes 273416 | tf_op jit(solution)/shard_map/ppermute | solution.py:425
  12.8 0.0 collective-permute-done.refs_0_
  12.8 0.8 %collective-permute-start.6 = (f32[89,2,128]{2,1,0:T(2,128)S(1)}, f32[89,2,128]{2,1,0:T(2,128)S(1)}, u32[]{:S(2)}, u32[]{:S(2)}) collective-permute-start(f32[89,2,128]{2,1,0:T(2,128)S(1)} %get-tuple-element.44), channel_id=1, source_target_pairs={{0,8},{1,9},{2,10},{3,11},{4,12},{5,13},{6,14},{7,15},{8,0},{9,1},... | collective-permute-start | bytes 273416 | tf_op jit(solution)/shard_map/ppermute | solution.py:425
  13.6 0.0 collective-permute-done.1.refs_1_
  13.6 2.8 %collective-permute-start.3 = (f32[89,2,128]{2,1,0:T(2,128)S(1)}, f32[89,2,128]{2,1,0:T(2,128)S(1)}, u32[]{:S(2)}, u32[]{:S(2)}) collective-permute-start(f32[89,2,128]{2,1,0:T(2,128)S(1)} %get-tuple-element.38), channel_id=1, source_target_pairs={{0,14},{1,15},{2,12},{3,13},{4,10},{5,11},{6,8},{7,9},{8,6},{9,7},... | collective-permute-start | bytes 273416 | tf_op jit(solution)/shard_map/ppermute | solution.py:425
  16.4 0.0 collective-permute-done.2.refs_2_
  16.4 1.5 %collective-permute-start.5 = (f32[89,2,128]{2,1,0:T(2,128)S(1)}, f32[89,2,128]{2,1,0:T(2,128)S(1)}, u32[]{:S(2)}, u32[]{:S(2)}) collective-permute-start(f32[89,2,128]{2,1,0:T(2,128)S(1)} %get-tuple-element.42), channel_id=1, source_target_pairs={{0,2},{1,3},{2,0},{3,1},{4,6},{5,7},{6,4},{7,5},{8,10},{9,11},{10,... | collective-permute-start | bytes 273416 | tf_op jit(solution)/shard_map/ppermute | solution.py:425
  17.9 0.0 collective-permute-done.4.refs_4_
  17.9 0.0 collective-permute-start.7
  17.9 5.3 %collective-permute-done.8.refs_1_ = f32[89,2,128]{2,1,0:T(2,128)S(1)} collective-permute-done((f32[89,2,128]{2,1,0:T(2,128)S(1)}, f32[89,2,128]{2,1,0:T(2,128)S(1)}, u32[]{:S(2)}, u32[]{:S(2)}) %collective-permute-start.8) | collective-permute-done | bytes 91168 | tf_op jit(solution)/shard_map/ppermute | solution.py:425
  23.2 3.5 %collective-permute-start.9 = (f32[89,2,128]{2,1,0:T(2,128)S(1)}, f32[89,2,128]{2,1,0:T(2,128)S(1)}, u32[]{:S(2)}, u32[]{:S(2)}) collective-permute-start(f32[89,2,128]{2,1,0:T(2,128)S(1)} %get-tuple-element.53), channel_id=1, source_target_pairs={{0,15},{1,14},{2,13},{3,12},{4,11},{5,10},{6,9},{7,8},{8,7},{9,6},... | collective-permute-start | bytes 273416 | tf_op jit(solution)/shard_map/ppermute | solution.py:425
  26.7 1.1 %pack.5 = (f32[89,2,128]{2,1,0:T(2,128)S(1)}, f32[89,2,128]{2,1,0:T(2,128)S(1)}, f32[89,2,128]{2,1,0:T(2,128)S(1)}, f32[89,2,128]{2,1,0:T(2,128)S(1)}, f32[89,2,128]{2,1,0:T(2,128)S(1)}) custom-call(s32[1]{0:T(128)} %bitcast.me_ref, f32[81,16,2,128]{3,2,1,0:T(2,128)} %bitcast.12, f32[8,2,2048]{2,1,0:T(2,128)S(1)} %get-tuple-element.45.refs_0_), custom_call_target="tpu_custom_call" | custom-call | flops 1048576 | bytes 1048576 | tf_op jit(solution)/shard_map/pack/pallas_call | solution.py:138
  27.8 0.0 collective-permute-done.6.refs_6_
  27.8 0.5 %collective-permute-start.11 = (f32[89,2,128]{2,1,0:T(2,128)S(1)}, f32[89,2,128]{2,1,0:T(2,128)S(1)}, u32[]{:S(2)}, u32[]{:S(2)}) collective-permute-start(f32[89,2,128]{2,1,0:T(2,128)S(1)} %get-tuple-element.55), channel_id=1, source_target_pairs={{0,13},{1,12},{2,15},{3,14},{4,9},{5,8},{6,11},{7,10},{8,5},{9,4},... | collective-permute-start | bytes 273416 | tf_op jit(solution)/shard_map/ppermute | solution.py:425
  28.3 0.0 collective-permute-done.3.refs_3_
  28.3 0.0 collective-permute-start.13
  28.3 0.0 collective-permute-done.5.refs_5_
  28.3 2.2 %collective-permute-start.14 = (f32[89,2,128]{2,1,0:T(2,128)S(1)}, f32[89,2,128]{2,1,0:T(2,128)S(1)}, u32[]{:S(2)}, u32[]{:S(2)}) collective-permute-start(f32[89,2,128]{2,1,0:T(2,128)S(1)} %get-tuple-element.58), channel_id=1, source_target_pairs={{0,5},{1,4},{2,7},{3,6},{4,1},{5,0},{6,3},{7,2},{8,13},{9,12},{10,... | collective-permute-start | bytes 273416 | tf_op jit(solution)/shard_map/ppermute | solution.py:425
  30.6 0.0 collective-permute-done.7.refs_0_
  30.6 1.5 %collective-permute-start.10 = (f32[89,2,128]{2,1,0:T(2,128)S(1)}, f32[89,2,128]{2,1,0:T(2,128)S(1)}, u32[]{:S(2)}, u32[]{:S(2)}) collective-permute-start(f32[89,2,128]{2,1,0:T(2,128)S(1)} %get-tuple-element.54), channel_id=1, source_target_pairs={{0,9},{1,8},{2,11},{3,10},{4,13},{5,12},{6,15},{7,14},{8,1},{9,0},... | collective-permute-start | bytes 273416 | tf_op jit(solution)/shard_map/ppermute | solution.py:425
  32.1 0.1 collective-permute-start.12
  32.2 3.6 %combine_even.1 = (f32[162,8,128]{2,1,0:T(8,128)S(1)}, f32[4,8,128]{2,1,0:T(8,128)S(1)}) custom-call(s32[1]{0:T(128)} %bitcast.me_ref, f32[89,2,128]{2,1,0:T(2,128)S(1)} %collective-permute-done.refs_0_, f32[89,2,128]{2,1,0:T(2,128)S(1)} %collective-permute-done.1.refs_1_, f32[89,2,128]{2,1,0:T(2,128)S(1)} %collective-permute-done.2.refs_2_, ...), custom_call_target="tpu_custom_call" | custom-call | flops 41943040 | bytes 12582912 | tf_op jit(solution)/shard_map/combine_even/pallas_call | solution.py:360
  35.8 0.0 collective-permute-done.11.refs_4_
  35.8 2.0 %collective-permute-done.13.refs_6_ = f32[89,2,128]{2,1,0:T(2,128)S(1)} collective-permute-done((f32[89,2,128]{2,1,0:T(2,128)S(1)}, f32[89,2,128]{2,1,0:T(2,128)S(1)}, u32[]{:S(2)}, u32[]{:S(2)}) %collective-permute-start.13) | collective-permute-done | bytes 91168 | tf_op jit(solution)/shard_map/ppermute | solution.py:425
  37.8 1.5 %collective-permute-done.14.refs_7_ = f32[89,2,128]{2,1,0:T(2,128)S(1)} collective-permute-done((f32[89,2,128]{2,1,0:T(2,128)S(1)}, f32[89,2,128]{2,1,0:T(2,128)S(1)}, u32[]{:S(2)}, u32[]{:S(2)}) %collective-permute-start.14) | collective-permute-done | bytes 91168 | tf_op jit(solution)/shard_map/ppermute | solution.py:425
  39.3 6.1 %combine_odd.1 = f32[2592,128]{1,0:T(8,128)} custom-call(s32[1]{0:T(128)} %bitcast.me_ref, f32[162,8,128]{2,1,0:T(8,128)S(1)} %get-tuple-element.47.even_work, f32[4,8,128]{2,1,0:T(8,128)S(1)} %get-tuple-element.48.even_phases, f32[89,2,128]{2,1,0:T(2,128)S(1)} %collective-permute-done.7.refs_0_, f32[89,2,128]{2,1,0:T(2,128)S(1)} %collective-permute-done.8.refs_1_, ...), custom_call_target="tpu_custom_call" | custom-call | flops 83886080 | bytes 20971520 | tf_op jit(solution)/shard_map/combine_odd/pallas_call | solution.py:382
  (3 shorter events, 0.0 us)
Async XLA Ops:
  1.2 11.5 %collective-permute-start = (f32[89,2,128]{2,1,0:T(2,128)S(1)}, f32[89,2,128]{2,1,0:T(2,128)S(1)}, u32[]{:S(2)}, u32[]{:S(2)}) collective-permute-start(f32[89,2,128]{2,1,0:T(2,128)S(1)} %get-tuple-element.34), channel_id=1, source_target_pairs={{0,10},{1,11},{2,8},{3,9},{4,14},{5,15},{6,12},{7,13},{8,2},{9,3},... | collective-permute-start | bytes 273416 | tf_op jit(solution)/shard_map/ppermute | solution.py:425
  6.3 7.3 %collective-permute-start.1 = (f32[89,2,128]{2,1,0:T(2,128)S(1)}, f32[89,2,128]{2,1,0:T(2,128)S(1)}, u32[]{:S(2)}, u32[]{:S(2)}) collective-permute-start(f32[89,2,128]{2,1,0:T(2,128)S(1)} %get-tuple-element.35), channel_id=1, source_target_pairs={{0,6},{1,7},{2,4},{3,5},{4,2},{5,3},{6,0},{7,1},{8,14},{9,15},{10,... | collective-permute-start | bytes 273416 | tf_op jit(solution)/shard_map/ppermute | solution.py:425
  7.8 8.5 %collective-permute-start.2 = (f32[89,2,128]{2,1,0:T(2,128)S(1)}, f32[89,2,128]{2,1,0:T(2,128)S(1)}, u32[]{:S(2)}, u32[]{:S(2)}) collective-permute-start(f32[89,2,128]{2,1,0:T(2,128)S(1)} %get-tuple-element.36), channel_id=1, source_target_pairs={{0,12},{1,13},{2,14},{3,15},{4,8},{5,9},{6,10},{7,11},{8,4},{9,5},... | collective-permute-start | bytes 273416 | tf_op jit(solution)/shard_map/ppermute | solution.py:425
  7.8 10.1 %collective-permute-start.4 = (f32[89,2,128]{2,1,0:T(2,128)S(1)}, f32[89,2,128]{2,1,0:T(2,128)S(1)}, u32[]{:S(2)}, u32[]{:S(2)}) collective-permute-start(f32[89,2,128]{2,1,0:T(2,128)S(1)} %get-tuple-element.40), channel_id=1, source_target_pairs={{0,4},{1,5},{2,6},{3,7},{4,0},{5,1},{6,2},{7,3},{8,12},{9,13},{10,... | collective-permute-start | bytes 273416 | tf_op jit(solution)/shard_map/ppermute | solution.py:425
  10.0 13.2 %collective-permute-start.8 = (f32[89,2,128]{2,1,0:T(2,128)S(1)}, f32[89,2,128]{2,1,0:T(2,128)S(1)}, u32[]{:S(2)}, u32[]{:S(2)}) collective-permute-start(f32[89,2,128]{2,1,0:T(2,128)S(1)} %get-tuple-element.51), channel_id=1, source_target_pairs={{0,11},{1,10},{2,9},{3,8},{4,15},{5,14},{6,13},{7,12},{8,3},{9,2},... | collective-permute-start | bytes 273416 | tf_op jit(solution)/shard_map/ppermute | solution.py:425
  12.8 15.0 %collective-permute-start.6 = (f32[89,2,128]{2,1,0:T(2,128)S(1)}, f32[89,2,128]{2,1,0:T(2,128)S(1)}, u32[]{:S(2)}, u32[]{:S(2)}) collective-permute-start(f32[89,2,128]{2,1,0:T(2,128)S(1)} %get-tuple-element.44), channel_id=1, source_target_pairs={{0,8},{1,9},{2,10},{3,11},{4,12},{5,13},{6,14},{7,15},{8,0},{9,1},... | collective-permute-start | bytes 273416 | tf_op jit(solution)/shard_map/ppermute | solution.py:425
  13.6 14.7 %collective-permute-start.3 = (f32[89,2,128]{2,1,0:T(2,128)S(1)}, f32[89,2,128]{2,1,0:T(2,128)S(1)}, u32[]{:S(2)}, u32[]{:S(2)}) collective-permute-start(f32[89,2,128]{2,1,0:T(2,128)S(1)} %get-tuple-element.38), channel_id=1, source_target_pairs={{0,14},{1,15},{2,12},{3,13},{4,10},{5,11},{6,8},{7,9},{8,6},{9,7},... | collective-permute-start | bytes 273416 | tf_op jit(solution)/shard_map/ppermute | solution.py:425
  16.4 11.9 %collective-permute-start.5 = (f32[89,2,128]{2,1,0:T(2,128)S(1)}, f32[89,2,128]{2,1,0:T(2,128)S(1)}, u32[]{:S(2)}, u32[]{:S(2)}) collective-permute-start(f32[89,2,128]{2,1,0:T(2,128)S(1)} %get-tuple-element.42), channel_id=1, source_target_pairs={{0,2},{1,3},{2,0},{3,1},{4,6},{5,7},{6,4},{7,5},{8,10},{9,11},{10,... | collective-permute-start | bytes 273416 | tf_op jit(solution)/shard_map/ppermute | solution.py:425
  17.9 12.7 %collective-permute-start.7 = (f32[89,2,128]{2,1,0:T(2,128)S(1)}, f32[89,2,128]{2,1,0:T(2,128)S(1)}, u32[]{:S(2)}, u32[]{:S(2)}) collective-permute-start(f32[89,2,128]{2,1,0:T(2,128)S(1)} %get-tuple-element.49), channel_id=1, source_target_pairs={{0,3},{1,2},{2,1},{3,0},{4,7},{5,6},{6,5},{7,4},{8,11},{9,10},{10,... | collective-permute-start | bytes 273416 | tf_op jit(solution)/shard_map/ppermute | solution.py:425
  23.2 8.9 %collective-permute-start.9 = (f32[89,2,128]{2,1,0:T(2,128)S(1)}, f32[89,2,128]{2,1,0:T(2,128)S(1)}, u32[]{:S(2)}, u32[]{:S(2)}) collective-permute-start(f32[89,2,128]{2,1,0:T(2,128)S(1)} %get-tuple-element.53), channel_id=1, source_target_pairs={{0,15},{1,14},{2,13},{3,12},{4,11},{5,10},{6,9},{7,8},{8,7},{9,6},... | collective-permute-start | bytes 273416 | tf_op jit(solution)/shard_map/ppermute | solution.py:425
  27.8 8.0 %collective-permute-start.11 = (f32[89,2,128]{2,1,0:T(2,128)S(1)}, f32[89,2,128]{2,1,0:T(2,128)S(1)}, u32[]{:S(2)}, u32[]{:S(2)}) collective-permute-start(f32[89,2,128]{2,1,0:T(2,128)S(1)} %get-tuple-element.55), channel_id=1, source_target_pairs={{0,13},{1,12},{2,15},{3,14},{4,9},{5,8},{6,11},{7,10},{8,5},{9,4},... | collective-permute-start | bytes 273416 | tf_op jit(solution)/shard_map/ppermute | solution.py:425
  28.3 9.5 %collective-permute-start.13 = (f32[89,2,128]{2,1,0:T(2,128)S(1)}, f32[89,2,128]{2,1,0:T(2,128)S(1)}, u32[]{:S(2)}, u32[]{:S(2)}) collective-permute-start(f32[89,2,128]{2,1,0:T(2,128)S(1)} %get-tuple-element.57), channel_id=1, source_target_pairs={{0,7},{1,6},{2,5},{3,4},{4,3},{5,2},{6,1},{7,0},{8,15},{9,14},{10,... | collective-permute-start | bytes 273416 | tf_op jit(solution)/shard_map/ppermute | solution.py:425
  28.3 11.0 %collective-permute-start.14 = (f32[89,2,128]{2,1,0:T(2,128)S(1)}, f32[89,2,128]{2,1,0:T(2,128)S(1)}, u32[]{:S(2)}, u32[]{:S(2)}) collective-permute-start(f32[89,2,128]{2,1,0:T(2,128)S(1)} %get-tuple-element.58), channel_id=1, source_target_pairs={{0,5},{1,4},{2,7},{3,6},{4,1},{5,0},{6,3},{7,2},{8,13},{9,12},{10,... | collective-permute-start | bytes 273416 | tf_op jit(solution)/shard_map/ppermute | solution.py:425
  30.6 8.7 %collective-permute-start.10 = (f32[89,2,128]{2,1,0:T(2,128)S(1)}, f32[89,2,128]{2,1,0:T(2,128)S(1)}, u32[]{:S(2)}, u32[]{:S(2)}) collective-permute-start(f32[89,2,128]{2,1,0:T(2,128)S(1)} %get-tuple-element.54), channel_id=1, source_target_pairs={{0,9},{1,8},{2,11},{3,10},{4,13},{5,12},{6,15},{7,14},{8,1},{9,0},... | collective-permute-start | bytes 273416 | tf_op jit(solution)/shard_map/ppermute | solution.py:425
  32.1 7.2 %collective-permute-start.12 = (f32[89,2,128]{2,1,0:T(2,128)S(1)}, f32[89,2,128]{2,1,0:T(2,128)S(1)}, u32[]{:S(2)}, u32[]{:S(2)}) collective-permute-start(f32[89,2,128]{2,1,0:T(2,128)S(1)} %get-tuple-element.56), channel_id=1, source_target_pairs={{0,1},{1,0},{2,3},{3,2},{4,5},{5,4},{6,7},{7,6},{8,9},{9,8},{10,11... | collective-permute-start | bytes 273416 | tf_op jit(solution)/shard_map/ppermute | solution.py:425

commit v13 on v12

--- a/solution.py
+++ b/solution.py
@@ -244,23 +244,31 @@
     return part + 2 * (split * CHEB + column if level % 2 == 0 else column * CHEB + split)
 
 
-def join_chips(me, blocks, order, held, sems, work, last_phases, factors):
+def join_chips(me, blocks, order, held, sems, work, last_phases, factors, unroll, meanwhile=None):
     copies = []
-    for index, step in enumerate(order):
-        spot = pl.ds(((me ^ step) // 2) * (ROWS // 2), ROWS // 2)
-        copies.append(pltpu.make_async_copy(blocks[index], held.at[spot], sems.at[index]))
-        copies[-1].start()
-    for copy in copies:
-        copy.wait()
+    for kind, (first, size) in enumerate(((POINTS, ROWS // 2 - POINTS), (0, POINTS))):
+        for index, step in enumerate(order):
+            spot = ((me ^ step) // 2) * (ROWS // 2) + first
+            source = blocks[index].at[pl.ds(first, size)]
+            copies.append(pltpu.make_async_copy(source, held.at[pl.ds(spot, size)], sems.at[kind, index]))
+            copies[-1].start()
     rows = held.reshape(OCT * ROWS, LANES)
 
     def received(row):
         return rows[pl.ds(row, OCT, stride=ROWS), :]
 
+    for copy in copies[:OCT]:
+        copy.wait()
     for part in range(4):
         last_phases[part] = received(WEIGHT_ROWS + part * LEVELS + LEVELS - 1)
     for level in range(LEVELS - 1):
-        level_factors(level, [received(WEIGHT_ROWS + part * LEVELS + level) for part in range(4)], *factors)
+        phases = [received(WEIGHT_ROWS + part * LEVELS + level) for part in range(4)]
+        level_factors(level, phases, *factors[level])
+    if meanwhile is not None:
+        meanwhile()
+    for copy in copies[OCT:]:
+        copy.wait()
+    for level in range(LEVELS - 1):
         bit = OCT >> (level + 1)
 
         def column_step(column, _, level=level, bit=bit):
@@ -282,42 +290,41 @@
                 work[row_of(level, row, column, 0)] = real
                 work[row_of(level, row, column, 1)] = imag
 
-            level_column(column, children, *factors, store)
+            level_column(column, children, *factors[level], store)
             return 0
 
-        lax.fori_loop(0, CHEB, column_step, 0, unroll=3)
+        lax.fori_loop(0, CHEB, column_step, 0, unroll=unroll)
 
 
 def even_kernel(me_ref, *refs):
-    work, last_phases, held, parent_ref, child_ref, common_ref, sems = refs[OCT:]
-    factors = (parent_ref, child_ref, common_ref)
-    join_chips(me_ref[0], refs, EVEN_ORDER, held, sems, work, last_phases, factors)
+    work, last_phases, held, *factor_refs, sems = refs[OCT:]
+    factors = [[ref.at[level] for ref in factor_refs] for level in range(LEVELS - 1)]
+    join_chips(me_ref[0], refs, EVEN_ORDER, held, sems, work, last_phases, factors, CHEB)
 
 
 def odd_kernel(me_ref, even_work, even_phases, *refs):
-    out_hbm, work, last_phases, held, out_ref, parent_ref, child_ref, common_ref, sems, out_sems = refs[OCT:]
+    out_hbm, work, last_phases, held, out_ref, *factor_refs, sems, out_sems = refs[OCT:]
     me = me_ref[0]
     own = me % 2
     early = [
+        pltpu.make_async_copy(even_phases, last_phases.at[own], out_sems.at[1]),
         pltpu.make_async_copy(even_work, work.at[own], out_sems.at[0]),
-        pltpu.make_async_copy(even_phases, last_phases.at[own], out_sems.at[1]),
     ]
     for copy in early:
         copy.start()
-    factors = [ref.at[0] for ref in (parent_ref, child_ref, common_ref)]
-    join_chips(me, refs, ODD_ORDER, held, sems, work.at[1 - own], last_phases.at[1 - own], factors)
-    for copy in early:
-        copy.wait()
-
+    factors = [[ref.at[index] for ref in factor_refs] for index in range(LEVELS + 1)]
     level = LEVELS - 1
-    for parity in range(2):
-        level_factors(
-            level,
-            [last_phases[parity, part] for part in range(4)],
-            parent_ref.at[parity],
-            child_ref.at[parity],
-            common_ref.at[parity],
-        )
+
+    def last_factors():
+        early[0].wait()
+        for parity in range(2):
+            level_factors(level, [last_phases[parity, part] for part in range(4)], *factors[level + parity])
+
+    join_chips(
+        me, refs, ODD_ORDER, held, sems, work.at[1 - own], last_phases.at[1 - own], factors, 3, last_factors
+    )
+    early[1].wait()
+
     chunk = out_ref.shape[0] // CHEB
 
     def leave(column):
@@ -336,9 +343,7 @@
                 out_ref[pl.ds(start, OCT, stride=4), :] = real
                 out_ref[pl.ds(start + 1, OCT, stride=4), :] = imag
 
-            level_column(
-                column, children, parent_ref.at[parity], child_ref.at[parity], common_ref.at[parity], store
-            )
+            level_column(column, children, *factors[level + parity], store)
         leave(column).start()
         return 0
 
@@ -367,8 +372,8 @@
         out_specs=[vmem, vmem],
         scratch_shapes=[
             pltpu.VMEM((OCT * ROWS // 2, 2, LANES), jnp.float32),
-            *factor_scratch(()),
-            pltpu.SemaphoreType.DMA((OCT,)),
+            *factor_scratch((LEVELS - 1,)),
+            pltpu.SemaphoreType.DMA((2, OCT)),
         ],
         compiler_params=pltpu.CompilerParams(vmem_limit_bytes=16 * 2**20),
         cost_estimate=pl.CostEstimate(flops=40 * 2**20, bytes_accessed=12 * 2**20, transcendentals=0),
@@ -389,8 +394,8 @@
             pltpu.VMEM((2, 4, OCT, LANES), jnp.float32),
             pltpu.VMEM((OCT * ROWS // 2, 2, LANES), jnp.float32),
             pltpu.VMEM((WEIGHT_ROWS * SLOTS, LANES), jnp.float32),
-            *factor_scratch((2,)),
-            pltpu.SemaphoreType.DMA((OCT,)),
+            *factor_scratch((LEVELS + 1,)),
+            pltpu.SemaphoreType.DMA((2, OCT)),
             pltpu.SemaphoreType.DMA((CHEB,)),
         ],
         compiler_params=pltpu.CompilerParams(vmem_limit_bytes=16 * 2**20),

time: 45.7 us -> 45.8 us (level)
  no operation moved by 1% of the time
where the time goes in v13:
time: 45.8 us; the launch traced here: 45.5 us
  starting transfers between devices  23.3 us (51%)
  Pallas kernels  13.4 us (29%)
  waiting for transfers between devices  8.77 us (19%)
    ppermute x15, starting transfers between devices, on_device(): lax.ppermute(blocks[step], 'box', [(s, s ^ step) for s in range(SLOTS)])  23.3 us
    ppermute x15, waiting for transfers between devices, on_device(): lax.ppermute(blocks[step], 'box', [(s, s ^ step) for s in range(SLOTS)])  8.77 us
    pallas_call x1, Pallas kernels, combine_odd(): pl.pallas_call(odd_kernel, out_shape=jax.ShapeDtypeStruct((WEIGHT_ROWS *...  6.21 us
    pallas_call x1, Pallas kernels, combine_even(): pl.pallas_call(even_kernel, out_shape=[jax.ShapeDtypeStruct((WEIGHT_ROWS,...  3.61 us
    pallas_call x3, Pallas kernels, pack(): pl.pallas_call(functools.partial(pack_kernel, steps, first), out_shape=ou...  3.57 us
  transfers between devices with their start and end apart: 15, of which 3 were waited for; matrix products, arithmetic and copies ran while one was open for 0% of the time, Pallas kernels for 13%

profile of v13, /device:TPU:0, one launch (start us, length us, event | category | flops | bytes accessed | tf_op | source)
XLA Modules:
  0.0 45.5 jit_solution(2609433922801068400)
XLA Ops:
  0.0 1.2 %pack.3 = (f32[89,2,128]{2,1,0:T(2,128)S(1)}, f32[89,2,128]{2,1,0:T(2,128)S(1)}, f32[89,2,128]{2,1,0:T(2,128)S(1)}, f32[89,2,128]{2,1,0:T(2,128)S(1)}, f32[8,2,2048]{2,1,0:T(2,128)S(1)}) custom-call(s32[1]{0:T(128)} %bitcast.me_ref, f32[81,16,2,128]{3,2,1,0:T(2,128)} %bitcast.10, f32[4,3]{1,0:T(4,128)} %refs_0_.1, f32[4,2,2048]{2,1,0:T(2,128)} %refs_1_.1, ...), custom_call_target="tpu_custom_call" | custom-call | flops 1048576 | bytes 1048576 | tf_op jit(solution)/shard_map/pack/pallas_call | solution.py:138
  1.2 5.1 %collective-permute-start = (f32[89,2,128]{2,1,0:T(2,128)S(1)}, f32[89,2,128]{2,1,0:T(2,128)S(1)}, u32[]{:S(2)}, u32[]{:S(2)}) collective-permute-start(f32[89,2,128]{2,1,0:T(2,128)S(1)} %get-tuple-element.34), channel_id=1, source_target_pairs={{0,10},{1,11},{2,8},{3,9},{4,14},{5,15},{6,12},{7,13},{8,2},{9,3},... | collective-permute-start | bytes 273416 | tf_op jit(solution)/shard_map/ppermute | solution.py:430
  6.3 1.5 %collective-permute-start.1 = (f32[89,2,128]{2,1,0:T(2,128)S(1)}, f32[89,2,128]{2,1,0:T(2,128)S(1)}, u32[]{:S(2)}, u32[]{:S(2)}) collective-permute-start(f32[89,2,128]{2,1,0:T(2,128)S(1)} %get-tuple-element.35), channel_id=1, source_target_pairs={{0,6},{1,7},{2,4},{3,5},{4,2},{5,3},{6,0},{7,1},{8,14},{9,15},{10,... | collective-permute-start | bytes 273416 | tf_op jit(solution)/shard_map/ppermute | solution.py:430
  7.8 0.0 collective-permute-start.2
  7.8 0.9 %collective-permute-start.4 = (f32[89,2,128]{2,1,0:T(2,128)S(1)}, f32[89,2,128]{2,1,0:T(2,128)S(1)}, u32[]{:S(2)}, u32[]{:S(2)}) collective-permute-start(f32[89,2,128]{2,1,0:T(2,128)S(1)} %get-tuple-element.40), channel_id=1, source_target_pairs={{0,4},{1,5},{2,6},{3,7},{4,0},{5,1},{6,2},{7,3},{8,12},{9,13},{10,... | collective-permute-start | bytes 273416 | tf_op jit(solution)/shard_map/ppermute | solution.py:430
  8.7 1.2 %pack.4 = (f32[89,2,128]{2,1,0:T(2,128)S(1)}, f32[89,2,128]{2,1,0:T(2,128)S(1)}, f32[89,2,128]{2,1,0:T(2,128)S(1)}, f32[89,2,128]{2,1,0:T(2,128)S(1)}, f32[89,2,...) custom-call(s32[1]{0:T(128)} %bitcast.me_ref, f32[81,16,2,128]{3,2,1,0:T(2,128)} %bitcast.11, ...), custom_call_target="tpu_custom_call" | custom-call | flops 1048576 | bytes 1048576 | tf_op jit(solution)/shard_map/pack/pallas_call | solution.py:138
  10.0 2.8 %collective-permute-start.8 = (f32[89,2,128]{2,1,0:T(2,128)S(1)}, f32[89,2,128]{2,1,0:T(2,128)S(1)}, u32[]{:S(2)}, u32[]{:S(2)}) collective-permute-start(f32[89,2,128]{2,1,0:T(2,128)S(1)} %get-tuple-element.51), channel_id=1, source_target_pairs={{0,11},{1,10},{2,9},{3,8},{4,15},{5,14},{6,13},{7,12},{8,3},{9,2},... | collective-permute-start | bytes 273416 | tf_op jit(solution)/shard_map/ppermute | solution.py:430
  12.8 0.0 collective-permute-done.refs_0_
  12.8 0.8 %collective-permute-start.6 = (f32[89,2,128]{2,1,0:T(2,128)S(1)}, f32[89,2,128]{2,1,0:T(2,128)S(1)}, u32[]{:S(2)}, u32[]{:S(2)}) collective-permute-start(f32[89,2,128]{2,1,0:T(2,128)S(1)} %get-tuple-element.44), channel_id=1, source_target_pairs={{0,8},{1,9},{2,10},{3,11},{4,12},{5,13},{6,14},{7,15},{8,0},{9,1},... | collective-permute-start | bytes 273416 | tf_op jit(solution)/shard_map/ppermute | solution.py:430
  13.6 0.0 collective-permute-done.1.refs_1_
  13.6 2.8 %collective-permute-start.3 = (f32[89,2,128]{2,1,0:T(2,128)S(1)}, f32[89,2,128]{2,1,0:T(2,128)S(1)}, u32[]{:S(2)}, u32[]{:S(2)}) collective-permute-start(f32[89,2,128]{2,1,0:T(2,128)S(1)} %get-tuple-element.38), channel_id=1, source_target_pairs={{0,14},{1,15},{2,12},{3,13},{4,10},{5,11},{6,8},{7,9},{8,6},{9,7},... | collective-permute-start | bytes 273416 | tf_op jit(solution)/shard_map/ppermute | solution.py:430
  16.4 0.0 collective-permute-done.2.refs_2_
  16.4 1.5 %collective-permute-start.5 = (f32[89,2,128]{2,1,0:T(2,128)S(1)}, f32[89,2,128]{2,1,0:T(2,128)S(1)}, u32[]{:S(2)}, u32[]{:S(2)}) collective-permute-start(f32[89,2,128]{2,1,0:T(2,128)S(1)} %get-tuple-element.42), channel_id=1, source_target_pairs={{0,2},{1,3},{2,0},{3,1},{4,6},{5,7},{6,4},{7,5},{8,10},{9,11},{10,... | collective-permute-start | bytes 273416 | tf_op jit(solution)/shard_map/ppermute | solution.py:430
  17.9 0.0 collective-permute-done.4.refs_4_
  17.9 0.0 collective-permute-start.7
  17.9 5.3 %collective-permute-done.8.refs_1_ = f32[89,2,128]{2,1,0:T(2,128)S(1)} collective-permute-done((f32[89,2,128]{2,1,0:T(2,128)S(1)}, f32[89,2,128]{2,1,0:T(2,128)S(1)}, u32[]{:S(2)}, u32[]{:S(2)}) %collective-permute-start.8) | collective-permute-done | bytes 91168 | tf_op jit(solution)/shard_map/ppermute | solution.py:430
  23.2 3.5 %collective-permute-start.9 = (f32[89,2,128]{2,1,0:T(2,128)S(1)}, f32[89,2,128]{2,1,0:T(2,128)S(1)}, u32[]{:S(2)}, u32[]{:S(2)}) collective-permute-start(f32[89,2,128]{2,1,0:T(2,128)S(1)} %get-tuple-element.53), channel_id=1, source_target_pairs={{0,15},{1,14},{2,13},{3,12},{4,11},{5,10},{6,9},{7,8},{8,7},{9,6},... | collective-permute-start | bytes 273416 | tf_op jit(solution)/shard_map/ppermute | solution.py:430
  26.7 1.1 %pack.5 = (f32[89,2,128]{2,1,0:T(2,128)S(1)}, f32[89,2,128]{2,1,0:T(2,128)S(1)}, f32[89,2,128]{2,1,0:T(2,128)S(1)}, f32[89,2,128]{2,1,0:T(2,128)S(1)}, f32[89,2,128]{2,1,0:T(2,128)S(1)}) custom-call(s32[1]{0:T(128)} %bitcast.me_ref, f32[81,16,2,128]{3,2,1,0:T(2,128)} %bitcast.12, f32[8,2,2048]{2,1,0:T(2,128)S(1)} %get-tuple-element.45.refs_0_), custom_call_target="tpu_custom_call" | custom-call | flops 1048576 | bytes 1048576 | tf_op jit(solution)/shard_map/pack/pallas_call | solution.py:138
  27.8 0.0 collective-permute-done.6.refs_6_
  27.8 0.5 %collective-permute-start.11 = (f32[89,2,128]{2,1,0:T(2,128)S(1)}, f32[89,2,128]{2,1,0:T(2,128)S(1)}, u32[]{:S(2)}, u32[]{:S(2)}) collective-permute-start(f32[89,2,128]{2,1,0:T(2,128)S(1)} %get-tuple-element.55), channel_id=1, source_target_pairs={{0,13},{1,12},{2,15},{3,14},{4,9},{5,8},{6,11},{7,10},{8,5},{9,4},... | collective-permute-start | bytes 273416 | tf_op jit(solution)/shard_map/ppermute | solution.py:430
  28.3 0.0 collective-permute-done.3.refs_3_
  28.3 0.0 collective-permute-start.13
  28.3 0.0 collective-permute-done.5.refs_5_
  28.3 2.2 %collective-permute-start.14 = (f32[89,2,128]{2,1,0:T(2,128)S(1)}, f32[89,2,128]{2,1,0:T(2,128)S(1)}, u32[]{:S(2)}, u32[]{:S(2)}) collective-permute-start(f32[89,2,128]{2,1,0:T(2,128)S(1)} %get-tuple-element.58), channel_id=1, source_target_pairs={{0,5},{1,4},{2,7},{3,6},{4,1},{5,0},{6,3},{7,2},{8,13},{9,12},{10,... | collective-permute-start | bytes 273416 | tf_op jit(solution)/shard_map/ppermute | solution.py:430
  30.6 0.0 collective-permute-done.7.refs_0_
  30.6 1.5 %collective-permute-start.10 = (f32[89,2,128]{2,1,0:T(2,128)S(1)}, f32[89,2,128]{2,1,0:T(2,128)S(1)}, u32[]{:S(2)}, u32[]{:S(2)}) collective-permute-start(f32[89,2,128]{2,1,0:T(2,128)S(1)} %get-tuple-element.54), channel_id=1, source_target_pairs={{0,9},{1,8},{2,11},{3,10},{4,13},{5,12},{6,15},{7,14},{8,1},{9,0},... | collective-permute-start | bytes 273416 | tf_op jit(solution)/shard_map/ppermute | solution.py:430
  32.1 0.0 collective-permute-done.9.refs_2_
  32.1 0.1 collective-permute-start.12
  32.2 3.6 %combine_even.1 = (f32[162,8,128]{2,1,0:T(8,128)S(1)}, f32[4,8,128]{2,1,0:T(8,128)S(1)}) custom-call(s32[1]{0:T(128)} %bitcast.me_ref, f32[89,2,128]{2,1,0:T(2,128)S(1)} %collective-permute-done.refs_0_, f32[89,2,128]{2,1,0:T(2,128)S(1)} %collective-permute-done.1.refs_1_, f32[89,2,128]{2,1,0:T(2,128)S(1)} %collective-permute-done.2.refs_2_, ...), custom_call_target="tpu_custom_call" | custom-call | flops 41943040 | bytes 12582912 | tf_op jit(solution)/shard_map/combine_even/pallas_call | solution.py:365
  35.8 2.0 %collective-permute-done.13.refs_6_ = f32[89,2,128]{2,1,0:T(2,128)S(1)} collective-permute-done((f32[89,2,128]{2,1,0:T(2,128)S(1)}, f32[89,2,128]{2,1,0:T(2,128)S(1)}, u32[]{:S(2)}, u32[]{:S(2)}) %collective-permute-start.13) | collective-permute-done | bytes 91168 | tf_op jit(solution)/shard_map/ppermute | solution.py:430
  37.8 1.5 %collective-permute-done.14.refs_7_ = f32[89,2,128]{2,1,0:T(2,128)S(1)} collective-permute-done((f32[89,2,128]{2,1,0:T(2,128)S(1)}, f32[89,2,128]{2,1,0:T(2,128)S(1)}, u32[]{:S(2)}, u32[]{:S(2)}) %collective-permute-start.14) | collective-permute-done | bytes 91168 | tf_op jit(solution)/shard_map/ppermute | solution.py:430
  39.3 6.2 %combine_odd.1 = f32[2592,128]{1,0:T(8,128)} custom-call(s32[1]{0:T(128)} %bitcast.me_ref, f32[162,8,128]{2,1,0:T(8,128)S(1)} %get-tuple-element.47.even_work, f32[4,8,128]{2,1,0:T(8,128)S(1)} %get-tuple-element.48.even_phases, f32[89,2,128]{2,1,0:T(2,128)S(1)} %collective-permute-done.7.refs_0_, f32[89,2,128]{2,1,0:T(2,128)S(1)} %collective-permute-done.8.refs_1_, ...), custom_call_target="tpu_custom_call" | custom-call | flops 83886080 | bytes 20971520 | tf_op jit(solution)/shard_map/combine_odd/pallas_call | solution.py:387
  (3 shorter events, 0.0 us)
Async XLA Ops:
  1.2 11.5 %collective-permute-start = (f32[89,2,128]{2,1,0:T(2,128)S(1)}, f32[89,2,128]{2,1,0:T(2,128)S(1)}, u32[]{:S(2)}, u32[]{:S(2)}) collective-permute-start(f32[89,2,128]{2,1,0:T(2,128)S(1)} %get-tuple-element.34), channel_id=1, source_target_pairs={{0,10},{1,11},{2,8},{3,9},{4,14},{5,15},{6,12},{7,13},{8,2},{9,3},... | collective-permute-start | bytes 273416 | tf_op jit(solution)/shard_map/ppermute | solution.py:430
  6.3 7.3 %collective-permute-start.1 = (f32[89,2,128]{2,1,0:T(2,128)S(1)}, f32[89,2,128]{2,1,0:T(2,128)S(1)}, u32[]{:S(2)}, u32[]{:S(2)}) collective-permute-start(f32[89,2,128]{2,1,0:T(2,128)S(1)} %get-tuple-element.35), channel_id=1, source_target_pairs={{0,6},{1,7},{2,4},{3,5},{4,2},{5,3},{6,0},{7,1},{8,14},{9,15},{10,... | collective-permute-start | bytes 273416 | tf_op jit(solution)/shard_map/ppermute | solution.py:430
  7.8 8.5 %collective-permute-start.2 = (f32[89,2,128]{2,1,0:T(2,128)S(1)}, f32[89,2,128]{2,1,0:T(2,128)S(1)}, u32[]{:S(2)}, u32[]{:S(2)}) collective-permute-start(f32[89,2,128]{2,1,0:T(2,128)S(1)} %get-tuple-element.36), channel_id=1, source_target_pairs={{0,12},{1,13},{2,14},{3,15},{4,8},{5,9},{6,10},{7,11},{8,4},{9,5},... | collective-permute-start | bytes 273416 | tf_op jit(solution)/shard_map/ppermute | solution.py:430
  7.8 10.1 %collective-permute-start.4 = (f32[89,2,128]{2,1,0:T(2,128)S(1)}, f32[89,2,128]{2,1,0:T(2,128)S(1)}, u32[]{:S(2)}, u32[]{:S(2)}) collective-permute-start(f32[89,2,128]{2,1,0:T(2,128)S(1)} %get-tuple-element.40), channel_id=1, source_target_pairs={{0,4},{1,5},{2,6},{3,7},{4,0},{5,1},{6,2},{7,3},{8,12},{9,13},{10,... | collective-permute-start | bytes 273416 | tf_op jit(solution)/shard_map/ppermute | solution.py:430
  10.0 13.2 %collective-permute-start.8 = (f32[89,2,128]{2,1,0:T(2,128)S(1)}, f32[89,2,128]{2,1,0:T(2,128)S(1)}, u32[]{:S(2)}, u32[]{:S(2)}) collective-permute-start(f32[89,2,128]{2,1,0:T(2,128)S(1)} %get-tuple-element.51), channel_id=1, source_target_pairs={{0,11},{1,10},{2,9},{3,8},{4,15},{5,14},{6,13},{7,12},{8,3},{9,2},... | collective-permute-start | bytes 273416 | tf_op jit(solution)/shard_map/ppermute | solution.py:430
  12.8 15.0 %collective-permute-start.6 = (f32[89,2,128]{2,1,0:T(2,128)S(1)}, f32[89,2,128]{2,1,0:T(2,128)S(1)}, u32[]{:S(2)}, u32[]{:S(2)}) collective-permute-start(f32[89,2,128]{2,1,0:T(2,128)S(1)} %get-tuple-element.44), channel_id=1, source_target_pairs={{0,8},{1,9},{2,10},{3,11},{4,12},{5,13},{6,14},{7,15},{8,0},{9,1},... | collective-permute-start | bytes 273416 | tf_op jit(solution)/shard_map/ppermute | solution.py:430
  13.6 14.7 %collective-permute-start.3 = (f32[89,2,128]{2,1,0:T(2,128)S(1)}, f32[89,2,128]{2,1,0:T(2,128)S(1)}, u32[]{:S(2)}, u32[]{:S(2)}) collective-permute-start(f32[89,2,128]{2,1,0:T(2,128)S(1)} %get-tuple-element.38), channel_id=1, source_target_pairs={{0,14},{1,15},{2,12},{3,13},{4,10},{5,11},{6,8},{7,9},{8,6},{9,7},... | collective-permute-start | bytes 273416 | tf_op jit(solution)/shard_map/ppermute | solution.py:430
  16.4 11.9 %collective-permute-start.5 = (f32[89,2,128]{2,1,0:T(2,128)S(1)}, f32[89,2,128]{2,1,0:T(2,128)S(1)}, u32[]{:S(2)}, u32[]{:S(2)}) collective-permute-start(f32[89,2,128]{2,1,0:T(2,128)S(1)} %get-tuple-element.42), channel_id=1, source_target_pairs={{0,2},{1,3},{2,0},{3,1},{4,6},{5,7},{6,4},{7,5},{8,10},{9,11},{10,... | collective-permute-start | bytes 273416 | tf_op jit(solution)/shard_map/ppermute | solution.py:430
  17.9 12.7 %collective-permute-start.7 = (f32[89,2,128]{2,1,0:T(2,128)S(1)}, f32[89,2,128]{2,1,0:T(2,128)S(1)}, u32[]{:S(2)}, u32[]{:S(2)}) collective-permute-start(f32[89,2,128]{2,1,0:T(2,128)S(1)} %get-tuple-element.49), channel_id=1, source_target_pairs={{0,3},{1,2},{2,1},{3,0},{4,7},{5,6},{6,5},{7,4},{8,11},{9,10},{10,... | collective-permute-start | bytes 273416 | tf_op jit(solution)/shard_map/ppermute | solution.py:430
  23.2 8.9 %collective-permute-start.9 = (f32[89,2,128]{2,1,0:T(2,128)S(1)}, f32[89,2,128]{2,1,0:T(2,128)S(1)}, u32[]{:S(2)}, u32[]{:S(2)}) collective-permute-start(f32[89,2,128]{2,1,0:T(2,128)S(1)} %get-tuple-element.53), channel_id=1, source_target_pairs={{0,15},{1,14},{2,13},{3,12},{4,11},{5,10},{6,9},{7,8},{8,7},{9,6},... | collective-permute-start | bytes 273416 | tf_op jit(solution)/shard_map/ppermute | solution.py:430
  27.8 8.0 %collective-permute-start.11 = (f32[89,2,128]{2,1,0:T(2,128)S(1)}, f32[89,2,128]{2,1,0:T(2,128)S(1)}, u32[]{:S(2)}, u32[]{:S(2)}) collective-permute-start(f32[89,2,128]{2,1,0:T(2,128)S(1)} %get-tuple-element.55), channel_id=1, source_target_pairs={{0,13},{1,12},{2,15},{3,14},{4,9},{5,8},{6,11},{7,10},{8,5},{9,4},... | collective-permute-start | bytes 273416 | tf_op jit(solution)/shard_map/ppermute | solution.py:430
  28.3 9.5 %collective-permute-start.13 = (f32[89,2,128]{2,1,0:T(2,128)S(1)}, f32[89,2,128]{2,1,0:T(2,128)S(1)}, u32[]{:S(2)}, u32[]{:S(2)}) collective-permute-start(f32[89,2,128]{2,1,0:T(2,128)S(1)} %get-tuple-element.57), channel_id=1, source_target_pairs={{0,7},{1,6},{2,5},{3,4},{4,3},{5,2},{6,1},{7,0},{8,15},{9,14},{10,... | collective-permute-start | bytes 273416 | tf_op jit(solution)/shard_map/ppermute | solution.py:430
  28.3 11.0 %collective-permute-start.14 = (f32[89,2,128]{2,1,0:T(2,128)S(1)}, f32[89,2,128]{2,1,0:T(2,128)S(1)}, u32[]{:S(2)}, u32[]{:S(2)}) collective-permute-start(f32[89,2,128]{2,1,0:T(2,128)S(1)} %get-tuple-element.58), channel_id=1, source_target_pairs={{0,5},{1,4},{2,7},{3,6},{4,1},{5,0},{6,3},{7,2},{8,13},{9,12},{10,... | collective-permute-start | bytes 273416 | tf_op jit(solution)/shard_map/ppermute | solution.py:430
  30.6 8.7 %collective-permute-start.10 = (f32[89,2,128]{2,1,0:T(2,128)S(1)}, f32[89,2,128]{2,1,0:T(2,128)S(1)}, u32[]{:S(2)}, u32[]{:S(2)}) collective-permute-start(f32[89,2,128]{2,1,0:T(2,128)S(1)} %get-tuple-element.54), channel_id=1, source_target_pairs={{0,9},{1,8},{2,11},{3,10},{4,13},{5,12},{6,15},{7,14},{8,1},{9,0},... | collective-permute-start | bytes 273416 | tf_op jit(solution)/shard_map/ppermute | solution.py:430
  32.1 7.2 %collective-permute-start.12 = (f32[89,2,128]{2,1,0:T(2,128)S(1)}, f32[89,2,128]{2,1,0:T(2,128)S(1)}, u32[]{:S(2)}, u32[]{:S(2)}) collective-permute-start(f32[89,2,128]{2,1,0:T(2,128)S(1)} %get-tuple-element.56), channel_id=1, source_target_pairs={{0,1},{1,0},{2,3},{3,2},{4,5},{5,4},{6,7},{7,6},{8,9},{9,8},{10,11... | collective-permute-start | bytes 273416 | tf_op jit(solution)/shard_map/ppermute | solution.py:430

commit v14 on v13

--- a/solution.py
+++ b/solution.py
@@ -41,6 +41,10 @@
 
 
 EVEN_HALF, ODD_HALF = interpolation_halves()
+ONES = (CHEB // 2, CHEB - 2)
+ROW_SCALE = EVEN_HALF[:, ONES[1]].copy()
+COLUMN_SCALE = EVEN_HALF[ONES[0]] / ROW_SCALE[ONES[0]]
+EVEN_HALF, ODD_HALF = (half / ROW_SCALE[:, None] / COLUMN_SCALE for half in (EVEN_HALF, ODD_HALF))
 
 SIN_COEFS = (3.1415926401839673, -5.167710090328242, 2.5500776596583643, -0.5982921590176602, 0.0776594073245765)
 COS_COEFS = (0.999999953466542, -4.934792858659144, 4.05841191384421, -1.3318801591805476, 0.219696794464285)
@@ -80,76 +84,56 @@
     return constant, half * (k1 + 2.0 * bent * x1), half * half * bent, half * k2
 
 
-def phase_kernel(coef_hbm, wave_hbm, center_hbm, kind_hbm, phases_ref, coef_ref, wave_ref, center_ref, kind_ref, sems):
-    copies = [
-        pltpu.make_async_copy(source, target, sems.at[index])
-        for index, (source, target) in enumerate(
-            ((coef_hbm, coef_ref), (wave_hbm, wave_ref), (center_hbm, center_ref), (kind_hbm, kind_ref))
-        )
-    ]
-    for copy in copies:
+def pack_kernel(steps, me_ref, weights_hbm, coef_hbm, wave_hbm, center_hbm, kind_hbm, *refs):
+    outs, (coef_ref, wave_ref, center_ref, kind_ref, small_sems, block_sems) = refs[: len(steps)], refs[len(steps) :]
+    small, large = [pltpu.make_async_copy(coef_hbm, coef_ref, small_sems.at[3, 0])], []
+    for index, (step, out) in enumerate(zip(steps, outs)):
+        slot = me_ref[0] ^ step
+        there = pl.ds(pl.multiple_of(slot * LANES, LANES), LANES)
+        here = pl.ds(index * LANES, LANES)
+        small += [
+            pltpu.make_async_copy(wave_hbm.at[:, :, there], wave_ref.at[:, :, here], small_sems.at[0, index]),
+            pltpu.make_async_copy(center_hbm.at[:, :, there], center_ref.at[:, :, here], small_sems.at[1, index]),
+            pltpu.make_async_copy(kind_hbm.at[:, there], kind_ref.at[:, here], small_sems.at[2, index]),
+        ]
+        large.append(pltpu.make_async_copy(weights_hbm.at[:, slot], out.at[pl.ds(0, POINTS)], block_sems.at[index]))
+    for copy in small + large:
         copy.start()
-    for copy in copies:
+    for copy in small:
         copy.wait()
     rows = phase_rows(
         (wave_ref[:, 0, :], wave_ref[:, 1, :]), (center_ref[:, 0, :], center_ref[:, 1, :]), kind_ref[...], coef_ref
     )
-    for index, values in enumerate(rows):
+    for part, values in enumerate(rows):
         for level in range(LEVELS):
-            row = index * LEVELS + level
-            phases_ref[row // 2, row % 2, :] = values[level]
-
-
-def pack_kernel(steps, first, me_ref, weights_hbm, *refs):
-    if first:
-        small, refs = refs[:4], refs[4:]
-        outs, refs = refs[: len(steps)], refs[len(steps) :]
-        phases_ref, block_sems, scratch = refs[0], refs[1], refs[2:]
-    else:
-        phases_ref, outs, block_sems = refs[0], refs[1 : 1 + len(steps)], refs[1 + len(steps)]
-    slots = [me_ref[0] ^ step for step in steps]
-    copies = [
-        pltpu.make_async_copy(weights_hbm.at[:, slot], out.at[pl.ds(0, POINTS)], block_sems.at[index])
-        for index, (slot, out) in enumerate(zip(slots, outs))
-    ]
-    for copy in copies:
-        copy.start()
-    if first:
-        phase_kernel(*small, phases_ref, *scratch)
-    for slot, out in zip(slots, outs):
-        out[POINTS:] = phases_ref[:, :, pl.ds(pl.multiple_of(slot * LANES, LANES), LANES)]
-    for copy in copies:
+            row = part * LEVELS + level
+            for index, out in enumerate(outs):
+                out[POINTS + row // 2, row % 2, :] = values[level, index * LANES : (index + 1) * LANES]
+    for copy in large:
         copy.wait()
 
 
-def pack(steps, me, weights, phases, sources):
-    first = phases is None
-    vmem = pl.BlockSpec(memory_space=pltpu.VMEM)
+def pack(steps, me, weights, sources):
     hbm = pl.BlockSpec(memory_space=pltpu.HBM)
-    out_shape = [jax.ShapeDtypeStruct((ROWS // 2, 2, LANES), jnp.float32) for _ in steps]
-    scratch = [pltpu.SemaphoreType.DMA((len(steps),))]
-    if first:
-        boxes = sources[-1].shape[-1]
-        out_shape.append(jax.ShapeDtypeStruct((PHASE_ROWS // 2, 2, boxes), jnp.float32))
-        scratch += [pltpu.SMEM(sources[0].shape, jnp.float32)]
-        scratch += [pltpu.VMEM(source.shape, source.dtype) for source in sources[1:]]
-        scratch += [pltpu.SemaphoreType.DMA((len(sources),))]
-    operands = sources if first else [phases]
-    *arrays, last = pl.pallas_call(
-        functools.partial(pack_kernel, steps, first),
-        out_shape=out_shape,
-        in_specs=[pl.BlockSpec(memory_space=pltpu.SMEM), hbm] + ([hbm] * len(sources) if first else [vmem]),
-        out_specs=[vmem] * len(out_shape),
-        scratch_shapes=scratch,
+    count = len(steps)
+    arrays = pl.pallas_call(
+        functools.partial(pack_kernel, steps),
+        out_shape=[jax.ShapeDtypeStruct((ROWS // 2, 2, LANES), jnp.float32)] * count,
+        in_specs=[pl.BlockSpec(memory_space=pltpu.SMEM)] + [hbm] * (1 + len(sources)),
+        out_specs=[pl.BlockSpec(memory_space=pltpu.VMEM)] * count,
+        scratch_shapes=[
+            pltpu.SMEM(sources[0].shape, jnp.float32),
+            pltpu.VMEM((LEVELS, 2, count * LANES), jnp.float32),
+            pltpu.VMEM((LEVELS, 2, count * LANES), jnp.float32),
+            pltpu.VMEM((1, count * LANES), jnp.int32),
+            pltpu.SemaphoreType.DMA((4, count)),
+            pltpu.SemaphoreType.DMA((count,)),
+        ],
         compiler_params=pltpu.CompilerParams(vmem_limit_bytes=16 * 2**20),
         cost_estimate=pl.CostEstimate(flops=2**20, bytes_accessed=2**20, transcendentals=0),
         name="pack",
-    )(me, weights, *operands)
-    if first:
-        phases = last
-    else:
-        arrays.append(last)
-    return dict(zip(steps, arrays)), phases
+    )(me, weights, *sources)
+    return dict(zip(steps, arrays))
 
 
 def turn_both_ways(base, step):
@@ -163,7 +147,10 @@
     mid = CHEB // 2
 
     def put(ref, index, pair):
-        ref[index + (0,)], ref[index + (1,)] = pair
+        scale = ROW_SCALE[index[0]]
+        if len(index) > 1:
+            scale = COLUMN_SCALE[index[1] if index[0] == 0 else CHEB - 1 - index[1]]
+        ref[index + (0,)], ref[index + (1,)] = (float(scale) * value for value in pair)
 
     def norm(turns):
         cosine, sine = cos_sin_turns(turns)
@@ -224,9 +211,10 @@
         sums = []
         for part in range(2):
             plus, minus = halves[part]
-            even = plus[0] * float(EVEN_HALF[t, 0])
-            for s in range(1, CHEB):
-                even = even + plus[s] * float(EVEN_HALF[t, s])
+            even = None
+            for s in range(CHEB):
+                term = plus[s] if t == ONES[0] or s == ONES[1] else plus[s] * float(EVEN_HALF[t, s])
+                even = term if even is None else even + term
             if t == mid:
                 sums.append((even,))
                 continue
@@ -299,7 +287,7 @@
 def even_kernel(me_ref, *refs):
     work, last_phases, held, *factor_refs, sems = refs[OCT:]
     factors = [[ref.at[level] for ref in factor_refs] for level in range(LEVELS - 1)]
-    join_chips(me_ref[0], refs, EVEN_ORDER, held, sems, work, last_phases, factors, CHEB)
+    join_chips(me_ref[0], refs, EVEN_ORDER, held, sems, work, last_phases, factors, 3)
 
 
 def odd_kernel(me_ref, even_work, even_phases, *refs):
@@ -415,13 +403,12 @@
         pltpu.with_memory_space_constraint(operand, pltpu.HBM)
         for operand in (weights, phase_coef, wave_vectors, source_centers, phase_kind[None, :])
     ]
-    blocks, phases = {}, None
+    blocks, slot = {}, me
     for steps in PACKS:
         if blocks:
             last = next(reversed(blocks))
-            phases, blocks[last] = lax.optimization_barrier((phases, blocks[last]))
-        packed, phases = pack(steps, me, weights, phases, sources)
-        blocks.update(packed)
+            slot, blocks[last] = lax.optimization_barrier((slot, blocks[last]))
+        blocks.update(pack(steps, slot, weights, sources))
     if direct:
         for step in SENDS:
             if step in WAITS:

time: 45.8 us -> 45.6 us (level)
  waiting for transfers between devices: 8.77 us -> 7.36 us
  Pallas kernels: 13.4 us -> 14.2 us
    ppermute x15, waiting for transfers between devices: 8.77 us -> 7.36 us  [on_device(): lax.ppermute(blocks[step], 'box', [(s, s ^ step) for s in range(SLOTS)])]
    pallas_call x3, Pallas kernels: 3.57 us -> 4.43 us  [pack(): pl.pallas_call(functools.partial(pack_kernel, steps), out_shape=[jax.Shap...]
  transfers between devices with their start and end apart: 15 -> 15, of which waited for: 3 -> 3; matrix products, arithmetic and copies ran while one was open for 0% -> 0% of each run, Pallas kernels for 13% -> 15%
where the time goes in v14:
time: 45.6 us; the launch traced here: 44.9 us
  starting transfers between devices  23.3 us (51%)
  Pallas kernels  14.2 us (31%)
  waiting for transfers between devices  7.36 us (16%)
    ppermute x15, starting transfers between devices, on_device(): lax.ppermute(blocks[step], 'box', [(s, s ^ step) for s in range(SLOTS)])  23.3 us
    ppermute x15, waiting for transfers between devices, on_device(): lax.ppermute(blocks[step], 'box', [(s, s ^ step) for s in range(SLOTS)])  7.36 us
    pallas_call x1, Pallas kernels, combine_odd(): pl.pallas_call(odd_kernel, out_shape=jax.ShapeDtypeStruct((WEIGHT_ROWS *...  6.09 us
    pallas_call x3, Pallas kernels, pack(): pl.pallas_call(functools.partial(pack_kernel, steps), out_shape=[jax.Shap...  4.43 us
    pallas_call x1, Pallas kernels, combine_even(): pl.pallas_call(even_kernel, out_shape=[jax.ShapeDtypeStruct((WEIGHT_ROWS,...  3.63 us
  transfers between devices with their start and end apart: 15, of which 3 were waited for; matrix products, arithmetic and copies ran while one was open for 0% of the time, Pallas kernels for 15%

profile of v14, /device:TPU:0, one launch (start us, length us, event | category | flops | bytes accessed | tf_op | source)
XLA Modules:
  0.0 44.9 jit_solution(6710343217360864821)
XLA Ops:
  0.0 1.3 %pack.3 = (f32[89,2,128]{2,1,0:T(2,128)S(1)}, f32[89,2,128]{2,1,0:T(2,128)S(1)}, f32[89,2,128]{2,1,0:T(2,128)S(1)}, f32[89,2,128]{2,1,0:T(2,128)S(1)}) custom-call(s32[1]{0:T(128)} %bitcast.me_ref, f32[81,16,2,128]{3,2,1,0:T(2,128)} %bitcast.10, f32[4,3]{1,0:T(4,128)} %coef_hbm.5, f32[4,2,2048]{2,1,0:T(2,128)} %wave_hbm.5, f32[4,2,2048]{2,1,0:T(2,128)} %center_hbm.5, ...), custom_call_target="tpu_custom_call" | custom-call | flops 1048576 | bytes 1048576 | tf_op jit(solution)/shard_map/pack/pallas_call | solution.py:119
  1.4 5.1 %collective-permute-start = (f32[89,2,128]{2,1,0:T(2,128)S(1)}, f32[89,2,128]{2,1,0:T(2,128)S(1)}, u32[]{:S(2)}, u32[]{:S(2)}) collective-permute-start(f32[89,2,128]{2,1,0:T(2,128)S(1)} %get-tuple-element.32), channel_id=1, source_target_pairs={{0,10},{1,11},{2,8},{3,9},{4,14},{5,15},{6,12},{7,13},{8,2},{9,3},... | collective-permute-start | bytes 273416 | tf_op jit(solution)/shard_map/ppermute | solution.py:417
  6.4 1.5 %collective-permute-start.1 = (f32[89,2,128]{2,1,0:T(2,128)S(1)}, f32[89,2,128]{2,1,0:T(2,128)S(1)}, u32[]{:S(2)}, u32[]{:S(2)}) collective-permute-start(f32[89,2,128]{2,1,0:T(2,128)S(1)} %get-tuple-element.33), channel_id=1, source_target_pairs={{0,6},{1,7},{2,4},{3,5},{4,2},{5,3},{6,0},{7,1},{8,14},{9,15},{10,... | collective-permute-start | bytes 273416 | tf_op jit(solution)/shard_map/ppermute | solution.py:417
  7.9 0.0 collective-permute-start.2
  8.0 0.9 %collective-permute-start.4 = (f32[89,2,128]{2,1,0:T(2,128)S(1)}, f32[89,2,128]{2,1,0:T(2,128)S(1)}, u32[]{:S(2)}, u32[]{:S(2)}) collective-permute-start(f32[89,2,128]{2,1,0:T(2,128)S(1)} %get-tuple-element.38), channel_id=1, source_target_pairs={{0,4},{1,5},{2,6},{3,7},{4,0},{5,1},{6,2},{7,3},{8,12},{9,13},{10,... | collective-permute-start | bytes 273416 | tf_op jit(solution)/shard_map/ppermute | solution.py:417
  8.8 1.6 %pack.4 = (f32[89,2,128]{2,1,0:T(2,128)S(1)}, f32[89,2,128]{2,1,0:T(2,128)S(1)}, f32[89,2,128]{2,1,0:T(2,128)S(1)}, f32[89,2,128]{2,1,0:T(2,128)S(1)}, f32[89,2,...) custom-call(s32[1]{0:T(128)} %bitcast.me_ref, f32[81,16,2,128]{3,2,1,0:T(2,128)} %bitcast.11, ...), custom_call_target="tpu_custom_call" | custom-call | flops 1048576 | bytes 1048576 | tf_op jit(solution)/shard_map/pack/pallas_call | solution.py:119
  10.5 2.8 %collective-permute-start.8 = (f32[89,2,128]{2,1,0:T(2,128)S(1)}, f32[89,2,128]{2,1,0:T(2,128)S(1)}, u32[]{:S(2)}, u32[]{:S(2)}) collective-permute-start(f32[89,2,128]{2,1,0:T(2,128)S(1)} %get-tuple-element.49), channel_id=1, source_target_pairs={{0,11},{1,10},{2,9},{3,8},{4,15},{5,14},{6,13},{7,12},{8,3},{9,2},... | collective-permute-start | bytes 273416 | tf_op jit(solution)/shard_map/ppermute | solution.py:417
  13.3 0.0 collective-permute-done.refs_0_
  13.3 0.8 %collective-permute-start.6 = (f32[89,2,128]{2,1,0:T(2,128)S(1)}, f32[89,2,128]{2,1,0:T(2,128)S(1)}, u32[]{:S(2)}, u32[]{:S(2)}) collective-permute-start(f32[89,2,128]{2,1,0:T(2,128)S(1)} %get-tuple-element.42), channel_id=1, source_target_pairs={{0,8},{1,9},{2,10},{3,11},{4,12},{5,13},{6,14},{7,15},{8,0},{9,1},... | collective-permute-start | bytes 273416 | tf_op jit(solution)/shard_map/ppermute | solution.py:417
  14.1 0.0 collective-permute-done.1.refs_1_
  14.1 2.3 %collective-permute-start.3 = (f32[89,2,128]{2,1,0:T(2,128)S(1)}, f32[89,2,128]{2,1,0:T(2,128)S(1)}, u32[]{:S(2)}, u32[]{:S(2)}) collective-permute-start(f32[89,2,128]{2,1,0:T(2,128)S(1)} %get-tuple-element.36), channel_id=1, source_target_pairs={{0,14},{1,15},{2,12},{3,13},{4,10},{5,11},{6,8},{7,9},{8,6},{9,7},... | collective-permute-start | bytes 273416 | tf_op jit(solution)/shard_map/ppermute | solution.py:417
  16.5 0.0 collective-permute-done.2.refs_2_
  16.5 1.5 %collective-permute-start.5 = (f32[89,2,128]{2,1,0:T(2,128)S(1)}, f32[89,2,128]{2,1,0:T(2,128)S(1)}, u32[]{:S(2)}, u32[]{:S(2)}) collective-permute-start(f32[89,2,128]{2,1,0:T(2,128)S(1)} %get-tuple-element.40), channel_id=1, source_target_pairs={{0,2},{1,3},{2,0},{3,1},{4,6},{5,7},{6,4},{7,5},{8,10},{9,11},{10,... | collective-permute-start | bytes 273416 | tf_op jit(solution)/shard_map/ppermute | solution.py:417
  18.0 0.0 collective-permute-done.4.refs_4_
  18.0 0.2 collective-permute-start.7
  18.2 4.9 %collective-permute-done.8.refs_1_ = f32[89,2,128]{2,1,0:T(2,128)S(1)} collective-permute-done((f32[89,2,128]{2,1,0:T(2,128)S(1)}, f32[89,2,128]{2,1,0:T(2,128)S(1)}, u32[]{:S(2)}, u32[]{:S(2)}) %collective-permute-start.8) | collective-permute-done | bytes 91168 | tf_op jit(solution)/shard_map/ppermute | solution.py:417
  23.1 3.7 %collective-permute-start.9 = (f32[89,2,128]{2,1,0:T(2,128)S(1)}, f32[89,2,128]{2,1,0:T(2,128)S(1)}, u32[]{:S(2)}, u32[]{:S(2)}) collective-permute-start(f32[89,2,128]{2,1,0:T(2,128)S(1)} %get-tuple-element.51), channel_id=1, source_target_pairs={{0,15},{1,14},{2,13},{3,12},{4,11},{5,10},{6,9},{7,8},{8,7},{9,6},... | collective-permute-start | bytes 273416 | tf_op jit(solution)/shard_map/ppermute | solution.py:417
  26.8 1.4 %pack.5 = (f32[89,2,128]{2,1,0:T(2,128)S(1)}, f32[89,2,128]{2,1,0:T(2,128)S(1)}, f32[89,2,128]{2,1,0:T(2,128)S(1)}, f32[89,2,128]{2,1,0:T(2,128)S(1)}, f32[89,2,128]{2,1,0:T(2,128)S(1)}) custom-call(s32[1]{0:T(128)} %bitcast.me_ref, f32[81,16,2,128]{3,2,1,0:T(2,128)} %bitcast.12, f32[4,3]{1,0:T(4,128)} %coef_hbm.5, f32[4,2,2048]{2,1,0:T(2,128)} %wave_hbm.5, ...), custom_call_target="tpu_custom_call" | custom-call | flops 1048576 | bytes 1048576 | tf_op jit(solution)/shard_map/pack/pallas_call | solution.py:119
  28.3 0.8 %collective-permute-start.11 = (f32[89,2,128]{2,1,0:T(2,128)S(1)}, f32[89,2,128]{2,1,0:T(2,128)S(1)}, u32[]{:S(2)}, u32[]{:S(2)}) collective-permute-start(f32[89,2,128]{2,1,0:T(2,128)S(1)} %get-tuple-element.53), channel_id=1, source_target_pairs={{0,13},{1,12},{2,15},{3,14},{4,9},{5,8},{6,11},{7,10},{8,5},{9,4},... | collective-permute-start | bytes 273416 | tf_op jit(solution)/shard_map/ppermute | solution.py:417
  29.1 0.0 collective-permute-start.13
  29.1 0.0 collective-permute-done.5.refs_5_
  29.1 1.7 %collective-permute-start.14 = (f32[89,2,128]{2,1,0:T(2,128)S(1)}, f32[89,2,128]{2,1,0:T(2,128)S(1)}, u32[]{:S(2)}, u32[]{:S(2)}) collective-permute-start(f32[89,2,128]{2,1,0:T(2,128)S(1)} %get-tuple-element.56), channel_id=1, source_target_pairs={{0,5},{1,4},{2,7},{3,6},{4,1},{5,0},{6,3},{7,2},{8,13},{9,12},{10,... | collective-permute-start | bytes 273416 | tf_op jit(solution)/shard_map/ppermute | solution.py:417
  30.8 0.0 collective-permute-done.7.refs_0_
  30.8 1.8 %collective-permute-start.10 = (f32[89,2,128]{2,1,0:T(2,128)S(1)}, f32[89,2,128]{2,1,0:T(2,128)S(1)}, u32[]{:S(2)}, u32[]{:S(2)}) collective-permute-start(f32[89,2,128]{2,1,0:T(2,128)S(1)} %get-tuple-element.52), channel_id=1, source_target_pairs={{0,9},{1,8},{2,11},{3,10},{4,13},{5,12},{6,15},{7,14},{8,1},{9,0},... | collective-permute-start | bytes 273416 | tf_op jit(solution)/shard_map/ppermute | solution.py:417
  32.6 0.0 collective-permute-start.12
  32.6 3.6 %combine_even.1 = (f32[162,8,128]{2,1,0:T(8,128)S(1)}, f32[4,8,128]{2,1,0:T(8,128)S(1)}) custom-call(s32[1]{0:T(128)} %bitcast.me_ref, f32[89,2,128]{2,1,0:T(2,128)S(1)} %collective-permute-done.refs_0_, f32[89,2,128]{2,1,0:T(2,128)S(1)} %collective-permute-done.1.refs_1_, f32[89,2,128]{2,1,0:T(2,128)S(1)} %collective-permute-done.2.refs_2_, ...), custom_call_target="tpu_custom_call" | custom-call | flops 41943040 | bytes 12582912 | tf_op jit(solution)/shard_map/combine_even/pallas_call | solution.py:353
  36.3 0.0 collective-permute-done.11.refs_4_
  36.3 2.3 %collective-permute-done.13.refs_6_ = f32[89,2,128]{2,1,0:T(2,128)S(1)} collective-permute-done((f32[89,2,128]{2,1,0:T(2,128)S(1)}, f32[89,2,128]{2,1,0:T(2,128)S(1)}, u32[]{:S(2)}, u32[]{:S(2)}) %collective-permute-start.13) | collective-permute-done | bytes 91168 | tf_op jit(solution)/shard_map/ppermute | solution.py:417
  38.6 0.1 collective-permute-done.14.refs_7_
  38.8 0.0 collective-permute-done.10.refs_3_
  38.8 0.0 collective-permute-done.12.refs_5_
  38.8 6.1 %combine_odd.1 = f32[2592,128]{1,0:T(8,128)} custom-call(s32[1]{0:T(128)} %bitcast.me_ref, f32[162,8,128]{2,1,0:T(8,128)S(1)} %get-tuple-element.45.even_work, f32[4,8,128]{2,1,0:T(8,128)S(1)} %get-tuple-element.46.even_phases, f32[89,2,128]{2,1,0:T(2,128)S(1)} %collective-permute-done.7.refs_0_, f32[89,2,128]{2,1,0:T(2,128)S(1)} %collective-permute-done.8.refs_1_, ...), custom_call_target="tpu_custom_call" | custom-call | flops 83886080 | bytes 20971520 | tf_op jit(solution)/shard_map/combine_odd/pallas_call | solution.py:375
  (3 shorter events, 0.0 us)
Async XLA Ops:
  1.4 12.0 %collective-permute-start = (f32[89,2,128]{2,1,0:T(2,128)S(1)}, f32[89,2,128]{2,1,0:T(2,128)S(1)}, u32[]{:S(2)}, u32[]{:S(2)}) collective-permute-start(f32[89,2,128]{2,1,0:T(2,128)S(1)} %get-tuple-element.32), channel_id=1, source_target_pairs={{0,10},{1,11},{2,8},{3,9},{4,14},{5,15},{6,12},{7,13},{8,2},{9,3},... | collective-permute-start | bytes 273416 | tf_op jit(solution)/shard_map/ppermute | solution.py:417
  6.4 7.7 %collective-permute-start.1 = (f32[89,2,128]{2,1,0:T(2,128)S(1)}, f32[89,2,128]{2,1,0:T(2,128)S(1)}, u32[]{:S(2)}, u32[]{:S(2)}) collective-permute-start(f32[89,2,128]{2,1,0:T(2,128)S(1)} %get-tuple-element.33), channel_id=1, source_target_pairs={{0,6},{1,7},{2,4},{3,5},{4,2},{5,3},{6,0},{7,1},{8,14},{9,15},{10,... | collective-permute-start | bytes 273416 | tf_op jit(solution)/shard_map/ppermute | solution.py:417
  7.9 8.5 %collective-permute-start.2 = (f32[89,2,128]{2,1,0:T(2,128)S(1)}, f32[89,2,128]{2,1,0:T(2,128)S(1)}, u32[]{:S(2)}, u32[]{:S(2)}) collective-permute-start(f32[89,2,128]{2,1,0:T(2,128)S(1)} %get-tuple-element.34), channel_id=1, source_target_pairs={{0,12},{1,13},{2,14},{3,15},{4,8},{5,9},{6,10},{7,11},{8,4},{9,5},... | collective-permute-start | bytes 273416 | tf_op jit(solution)/shard_map/ppermute | solution.py:417
  8.0 10.1 %collective-permute-start.4 = (f32[89,2,128]{2,1,0:T(2,128)S(1)}, f32[89,2,128]{2,1,0:T(2,128)S(1)}, u32[]{:S(2)}, u32[]{:S(2)}) collective-permute-start(f32[89,2,128]{2,1,0:T(2,128)S(1)} %get-tuple-element.38), channel_id=1, source_target_pairs={{0,4},{1,5},{2,6},{3,7},{4,0},{5,1},{6,2},{7,3},{8,12},{9,13},{10,... | collective-permute-start | bytes 273416 | tf_op jit(solution)/shard_map/ppermute | solution.py:417
  10.5 12.6 %collective-permute-start.8 = (f32[89,2,128]{2,1,0:T(2,128)S(1)}, f32[89,2,128]{2,1,0:T(2,128)S(1)}, u32[]{:S(2)}, u32[]{:S(2)}) collective-permute-start(f32[89,2,128]{2,1,0:T(2,128)S(1)} %get-tuple-element.49), channel_id=1, source_target_pairs={{0,11},{1,10},{2,9},{3,8},{4,15},{5,14},{6,13},{7,12},{8,3},{9,2},... | collective-permute-start | bytes 273416 | tf_op jit(solution)/shard_map/ppermute | solution.py:417
  13.3 15.0 %collective-permute-start.6 = (f32[89,2,128]{2,1,0:T(2,128)S(1)}, f32[89,2,128]{2,1,0:T(2,128)S(1)}, u32[]{:S(2)}, u32[]{:S(2)}) collective-permute-start(f32[89,2,128]{2,1,0:T(2,128)S(1)} %get-tuple-element.42), channel_id=1, source_target_pairs={{0,8},{1,9},{2,10},{3,11},{4,12},{5,13},{6,14},{7,15},{8,0},{9,1},... | collective-permute-start | bytes 273416 | tf_op jit(solution)/shard_map/ppermute | solution.py:417
  14.1 15.0 %collective-permute-start.3 = (f32[89,2,128]{2,1,0:T(2,128)S(1)}, f32[89,2,128]{2,1,0:T(2,128)S(1)}, u32[]{:S(2)}, u32[]{:S(2)}) collective-permute-start(f32[89,2,128]{2,1,0:T(2,128)S(1)} %get-tuple-element.36), channel_id=1, source_target_pairs={{0,14},{1,15},{2,12},{3,13},{4,10},{5,11},{6,8},{7,9},{8,6},{9,7},... | collective-permute-start | bytes 273416 | tf_op jit(solution)/shard_map/ppermute | solution.py:417
  16.5 12.6 %collective-permute-start.5 = (f32[89,2,128]{2,1,0:T(2,128)S(1)}, f32[89,2,128]{2,1,0:T(2,128)S(1)}, u32[]{:S(2)}, u32[]{:S(2)}) collective-permute-start(f32[89,2,128]{2,1,0:T(2,128)S(1)} %get-tuple-element.40), channel_id=1, source_target_pairs={{0,2},{1,3},{2,0},{3,1},{4,6},{5,7},{6,4},{7,5},{8,10},{9,11},{10,... | collective-permute-start | bytes 273416 | tf_op jit(solution)/shard_map/ppermute | solution.py:417
  18.0 12.8 %collective-permute-start.7 = (f32[89,2,128]{2,1,0:T(2,128)S(1)}, f32[89,2,128]{2,1,0:T(2,128)S(1)}, u32[]{:S(2)}, u32[]{:S(2)}) collective-permute-start(f32[89,2,128]{2,1,0:T(2,128)S(1)} %get-tuple-element.47), channel_id=1, source_target_pairs={{0,3},{1,2},{2,1},{3,0},{4,7},{5,6},{6,5},{7,4},{8,11},{9,10},{10,... | collective-permute-start | bytes 273416 | tf_op jit(solution)/shard_map/ppermute | solution.py:417
  23.1 9.6 %collective-permute-start.9 = (f32[89,2,128]{2,1,0:T(2,128)S(1)}, f32[89,2,128]{2,1,0:T(2,128)S(1)}, u32[]{:S(2)}, u32[]{:S(2)}) collective-permute-start(f32[89,2,128]{2,1,0:T(2,128)S(1)} %get-tuple-element.51), channel_id=1, source_target_pairs={{0,15},{1,14},{2,13},{3,12},{4,11},{5,10},{6,9},{7,8},{8,7},{9,6},... | collective-permute-start | bytes 273416 | tf_op jit(solution)/shard_map/ppermute | solution.py:417
  28.3 8.0 %collective-permute-start.11 = (f32[89,2,128]{2,1,0:T(2,128)S(1)}, f32[89,2,128]{2,1,0:T(2,128)S(1)}, u32[]{:S(2)}, u32[]{:S(2)}) collective-permute-start(f32[89,2,128]{2,1,0:T(2,128)S(1)} %get-tuple-element.53), channel_id=1, source_target_pairs={{0,13},{1,12},{2,15},{3,14},{4,9},{5,8},{6,11},{7,10},{8,5},{9,4},... | collective-permute-start | bytes 273416 | tf_op jit(solution)/shard_map/ppermute | solution.py:417
  29.1 9.6 %collective-permute-start.13 = (f32[89,2,128]{2,1,0:T(2,128)S(1)}, f32[89,2,128]{2,1,0:T(2,128)S(1)}, u32[]{:S(2)}, u32[]{:S(2)}) collective-permute-start(f32[89,2,128]{2,1,0:T(2,128)S(1)} %get-tuple-element.55), channel_id=1, source_target_pairs={{0,7},{1,6},{2,5},{3,4},{4,3},{5,2},{6,1},{7,0},{8,15},{9,14},{10,... | collective-permute-start | bytes 273416 | tf_op jit(solution)/shard_map/ppermute | solution.py:417
  29.1 9.7 %collective-permute-start.14 = (f32[89,2,128]{2,1,0:T(2,128)S(1)}, f32[89,2,128]{2,1,0:T(2,128)S(1)}, u32[]{:S(2)}, u32[]{:S(2)}) collective-permute-start(f32[89,2,128]{2,1,0:T(2,128)S(1)} %get-tuple-element.56), channel_id=1, source_target_pairs={{0,5},{1,4},{2,7},{3,6},{4,1},{5,0},{6,3},{7,2},{8,13},{9,12},{10,... | collective-permute-start | bytes 273416 | tf_op jit(solution)/shard_map/ppermute | solution.py:417
  30.8 8.0 %collective-permute-start.10 = (f32[89,2,128]{2,1,0:T(2,128)S(1)}, f32[89,2,128]{2,1,0:T(2,128)S(1)}, u32[]{:S(2)}, u32[]{:S(2)}) collective-permute-start(f32[89,2,128]{2,1,0:T(2,128)S(1)} %get-tuple-element.52), channel_id=1, source_target_pairs={{0,9},{1,8},{2,11},{3,10},{4,13},{5,12},{6,15},{7,14},{8,1},{9,0},... | collective-permute-start | bytes 273416 | tf_op jit(solution)/shard_map/ppermute | solution.py:417
  32.6 6.1 %collective-permute-start.12 = (f32[89,2,128]{2,1,0:T(2,128)S(1)}, f32[89,2,128]{2,1,0:T(2,128)S(1)}, u32[]{:S(2)}, u32[]{:S(2)}) collective-permute-start(f32[89,2,128]{2,1,0:T(2,128)S(1)} %get-tuple-element.54), channel_id=1, source_target_pairs={{0,1},{1,0},{2,3},{3,2},{4,5},{5,4},{6,7},{7,6},{8,9},{9,8},{10,11... | collective-permute-start | bytes 273416 | tf_op jit(solution)/shard_map/ppermute | solution.py:417

commit v15 on v11

--- a/solution.py
+++ b/solution.py
@@ -22,12 +22,12 @@
 PAIRS = ROWS // 2
 ACROSS_Y = 2
 OCT = SLOTS // 2
-PACKS = (((8, 10), (4, 6), (2,), (1, 3)), ((12,), (5,), (7,), (14,), (9, 11), (15,), (13,), (0,)))
+PACKS = (((8, 10),), ((9, 11), (13,), (15,), (4, 6), (7,), (2,), (14,), (5,), (12,), (1, 3), (0,)))
 ONWARD = {"even": (2, 8, 4), "odd": (9, 1)}
-SENDS = (8, 4, 1, 12, 5, 7, 14, 9, 15, 13, "even", "odd")
-WAITS = {14: 1, 15: 5, 12: 8, 7: 5, 5: 8}
-EVEN_ORDER = (8, 12, 14, 4, "even", 0)
-ODD_ORDER = (1, 13, 15, 7, 5, "odd", 9)
+SENDS = (8, 14, 12, 9, 13, 4, 7, 5, 15, 1, "even", "odd")
+WAITS = {"odd": 4, 15: 4, "even": 5, 14: 8}
+EVEN_ORDER = (14, 4, "even", 8, 12, 0)
+ODD_ORDER = (13, 1, 5, 15, 9, "odd", 7)
 
 NODES = np.cos(math.pi * (2.0 * np.arange(CHEB) + 1.0) / (2.0 * CHEB))
 NODES[CHEB // 2] = 0.0

time: 46.2 us -> 43.7 us (0.946)
  waiting for transfers between devices: 11.2 us -> 7.88 us
  starting transfers between devices: 21.9 us -> 22.8 us
    ppermute x12, waiting for transfers between devices: 11.2 us -> 7.88 us  [on_device(): lax.ppermute(blocks[name], 'box', [(s, s ^ step) for s in range(SLOTS)])]
    ppermute x12, starting transfers between devices: 21.9 us -> 22.8 us  [on_device(): lax.ppermute(blocks[name], 'box', [(s, s ^ step) for s in range(SLOTS)])]
  transfers between devices with their start and end apart: 12 -> 12, of which waited for: 4 -> 2; matrix products, arithmetic and copies ran while one was open for 1% -> 1% of each run, Pallas kernels for 11% -> 12%
where the time goes in v15:
time: 43.7 us; the launch traced here: 43.4 us
  starting transfers between devices  22.8 us (52%)
  Pallas kernels  12.4 us (28%)
  waiting for transfers between devices  7.88 us (18%)
    ppermute x12, starting transfers between devices, on_device(): lax.ppermute(blocks[name], 'box', [(s, s ^ step) for s in range(SLOTS)])  22.8 us
    ppermute x12, waiting for transfers between devices, on_device(): lax.ppermute(blocks[name], 'box', [(s, s ^ step) for s in range(SLOTS)])  7.88 us
    pallas_call x1, Pallas kernels, combine_odd(): pl.pallas_call(functools.partial(odd_kernel, pieces, len(arrays)), out_sh...  6.13 us
    pallas_call x1, Pallas kernels, combine_even(): pl.pallas_call(functools.partial(even_kernel, pieces, len(arrays)), out_s...  3.62 us
    pallas_call x2, Pallas kernels, pack(): pl.pallas_call(functools.partial(pack_kernel, messages, first), out_shape...  2.64 us
  transfers between devices with their start and end apart: 12, of which 2 were waited for; matrix products, arithmetic and copies ran while one was open for 1% of the time, Pallas kernels for 12%

profile of v15, /device:TPU:0, one launch (start us, length us, event | category | flops | bytes accessed | tf_op | source)
XLA Modules:
  0.0 43.4 jit_solution(12496090725004096083)
XLA Ops:
  0.0 1.1 %pack.2 = (f32[178,2,128]{2,1,0:T(2,128)S(1)}, f32[8,2,2048]{2,1,0:T(2,128)S(1)}) custom-call(s32[1]{0:T(128)} %bitcast.me_ref, f32[81,16,2,128]{3,2,1,0:T(2,128)} %bitcast.10, f32[4,3]{1,0:T(4,128)} %refs_0_.1, f32[4,2,2048]{2,1,0:T(2,128)} %refs_1_.1, f32[4,2,2048]{2,1,0:T(2,128)} %refs_2_.1, s32[1,2048]{1,0:T(1,128)} %bitcast.12), custom_call_target="tpu_custom_call" | custom-call | flops 1048576 | bytes 1048576 | tf_op jit(solution)/shard_map/pack/pallas_call | solution.py:146
  1.1 4.1 %collective-permute-start = (f32[178,2,128]{2,1,0:T(2,128)S(1)}, f32[178,2,128]{2,1,0:T(2,128)S(1)}, u32[]{:S(2)}, u32[]{:S(2)}) collective-permute-start(f32[178,2,128]{2,1,0:T(2,128)S(1)} %get-tuple-element.34), channel_id=1, source_target_pairs={{0,8},{1,9},{2,10},{3,11},{4,12},{5,13},{6,14},{7,15},{8,0},{9,1},... | collective-permute-start | bytes 546824 | tf_op jit(solution)/shard_map/ppermute | solution.py:442
  5.2 1.5 %pack.3 = (f32[178,2,128]{2,1,0:T(2,128)S(1)}, f32[89,2,128]{2,1,0:T(2,128)S(1)}, f32[89,2,128]{2,1,0:T(2,128)S(1)}, f32[178,2,128]{2,1,0:T(2,128)S(1)}, f32[89,...) custom-call(s32[1]{0:T(128)} %bitcast.me_ref, ...), custom_call_target="tpu_custom_call" | custom-call | flops 1048576 | bytes 1048576 | tf_op jit(solution)/shard_map/pack/pallas_call | solution.py:146
  6.8 1.6 %collective-permute-start.4 = (f32[178,2,128]{2,1,0:T(2,128)S(1)}, f32[178,2,128]{2,1,0:T(2,128)S(1)}, u32[]{:S(2)}, u32[]{:S(2)}) collective-permute-start(f32[178,2,128]{2,1,0:T(2,128)S(1)} %get-tuple-element.39), channel_id=1, source_target_pairs={{0,4},{1,5},{2,6},{3,7},{4,0},{5,1},{6,2},{7,3},{8,12},{9,13},{10,... | collective-permute-start | bytes 546824 | tf_op jit(solution)/shard_map/ppermute | solution.py:442
  8.4 0.0 collective-permute-start.2
  8.4 0.4 %collective-permute-start.3 = (f32[178,2,128]{2,1,0:T(2,128)S(1)}, f32[178,2,128]{2,1,0:T(2,128)S(1)}, u32[]{:S(2)}, u32[]{:S(2)}) collective-permute-start(f32[178,2,128]{2,1,0:T(2,128)S(1)} %get-tuple-element.37), channel_id=1, source_target_pairs={{0,1},{1,0},{2,3},{3,2},{4,5},{5,4},{6,7},{7,6},{8,9},{9,8},{10,11... | collective-permute-start | bytes 546824 | tf_op jit(solution)/shard_map/ppermute | solution.py:442
  8.9 0.1 collective-permute-start.5
  9.0 6.5 %collective-permute-done.refs_3_ = f32[178,2,128]{2,1,0:T(2,128)S(1)} collective-permute-done((f32[178,2,128]{2,1,0:T(2,128)S(1)}, f32[178,2,128]{2,1,0:T(2,128)S(1)}, u32[]{:S(2)}, u32[]{:S(2)}) %collective-permute-start) | collective-permute-done | bytes 182304 | tf_op jit(solution)/shard_map/ppermute | solution.py:442
  15.5 2.9 %collective-permute-start.7 = (f32[89,2,128]{2,1,0:T(2,128)S(1)}, f32[89,2,128]{2,1,0:T(2,128)S(1)}, u32[]{:S(2)}, u32[]{:S(2)}) collective-permute-start(f32[89,2,128]{2,1,0:T(2,128)S(1)} %get-tuple-element.46), channel_id=1, source_target_pairs={{0,12},{1,13},{2,14},{3,15},{4,8},{5,9},{6,10},{7,11},{8,4},{9,5},... | collective-permute-start | bytes 273416 | tf_op jit(solution)/shard_map/ppermute | solution.py:442
  18.4 0.0 collective-permute-done.4.refs_1_
  18.4 4.2 %collective-permute-start.1 = (f32[89,2,128]{2,1,0:T(2,128)S(1)}, f32[89,2,128]{2,1,0:T(2,128)S(1)}, u32[]{:S(2)}, u32[]{:S(2)}) collective-permute-start(f32[89,2,128]{2,1,0:T(2,128)S(1)} %get-tuple-element.35), channel_id=1, source_target_pairs={{0,14},{1,15},{2,12},{3,13},{4,10},{5,11},{6,8},{7,9},{8,6},{9,7},... | collective-permute-start | bytes 273416 | tf_op jit(solution)/shard_map/ppermute | solution.py:442
  22.7 0.1 pad_maximum_fusion
  22.8 0.0 collective-permute-done.5.refs_2_
  22.8 0.1 collective-permute-start.6
  22.9 0.0 collective-permute-done.2.refs_4_
  22.9 0.0 collective-permute-done.3.refs_1_
  22.9 0.1 pad_maximum_fusion.1
  23.0 2.1 %collective-permute-start.10 = (f32[178,2,128]{2,1,0:T(2,128)S(1)}, f32[178,2,128]{2,1,0:T(2,128)S(1)}, u32[]{:S(2)}, u32[]{:S(2)}) collective-permute-start(f32[178,2,128]{2,1,0:T(2,128)S(1)} %pad_maximum_fusion.1), channel_id=1, source_target_pairs={{0,2},{1,3},{2,0},{3,1},{4,6},{5,7},{6,4},{7,5},{8,10},{9,11},{10,... | collective-permute-start | bytes 546824 | tf_op jit(solution)/shard_map/ppermute | solution.py:442
  25.1 5.1 %collective-permute-start.8 = (f32[89,2,128]{2,1,0:T(2,128)S(1)}, f32[89,2,128]{2,1,0:T(2,128)S(1)}, u32[]{:S(2)}, u32[]{:S(2)}) collective-permute-start(f32[89,2,128]{2,1,0:T(2,128)S(1)} %get-tuple-element.50), channel_id=1, source_target_pairs={{0,13},{1,12},{2,15},{3,14},{4,9},{5,8},{6,11},{7,10},{8,5},{9,4},... | collective-permute-start | bytes 273416 | tf_op jit(solution)/shard_map/ppermute | solution.py:442
  30.2 0.0 collective-permute-done.7.refs_4_
  30.2 0.0 collective-permute-start.11
  30.2 0.0 collective-permute-done.1.refs_0_
  30.2 2.1 %collective-permute-start.9 = (f32[89,2,128]{2,1,0:T(2,128)S(1)}, f32[89,2,128]{2,1,0:T(2,128)S(1)}, u32[]{:S(2)}, u32[]{:S(2)}) collective-permute-start(f32[89,2,128]{2,1,0:T(2,128)S(1)} %get-tuple-element.52), channel_id=1, source_target_pairs={{0,15},{1,14},{2,13},{3,12},{4,11},{5,10},{6,9},{7,8},{8,7},{9,6},... | collective-permute-start | bytes 273416 | tf_op jit(solution)/shard_map/ppermute | solution.py:442
  32.3 0.0 collective-permute-done.6.refs_2_
  32.3 3.6 %combine_even.1 = (f32[162,8,128]{2,1,0:T(8,128)S(1)}, f32[4,8,128]{2,1,0:T(8,128)S(1)}) custom-call(s32[1]{0:T(128)} %bitcast.me_ref, f32[89,2,128]{2,1,0:T(2,128)S(1)} %collective-permute-done.1.refs_0_, f32[178,2,128]{2,1,0:T(2,128)S(1)} %collective-permute-done.4.refs_1_, f32[267,2,128]{2,1,0:T(2,128)S(1)} %collective-permute-done.6.refs_2_, ...), custom_call_target="tpu_custom_call" | custom-call | flops 41943040 | bytes 12582912 | tf_op jit(solution)/shard_map/combine_even/pallas_call | solution.py:369
  35.9 0.0 collective-permute-done.8.refs_0_
  35.9 0.0 collective-permute-done.11.refs_6_
  35.9 1.4 %collective-permute-done.9.refs_3_ = f32[89,2,128]{2,1,0:T(2,128)S(1)} collective-permute-done((f32[89,2,128]{2,1,0:T(2,128)S(1)}, f32[89,2,128]{2,1,0:T(2,128)S(1)}, u32[]{:S(2)}, u32[]{:S(2)}) %collective-permute-start.9) | collective-permute-done | bytes 91168 | tf_op jit(solution)/shard_map/ppermute | solution.py:442
  37.3 0.0 collective-permute-done.10.refs_5_
  37.3 6.1 %combine_odd.1 = f32[2592,128]{1,0:T(8,128)} custom-call(s32[1]{0:T(128)} %bitcast.me_ref, f32[162,8,128]{2,1,0:T(8,128)S(1)} %get-tuple-element.48.even_work, f32[4,8,128]{2,1,0:T(8,128)S(1)} %get-tuple-element.49.even_phases, f32[89,2,128]{2,1,0:T(2,128)S(1)} %collective-permute-done.8.refs_0_, f32[178,2,128]{2,1,0:T(2,128)S(1)} %collective-permute-done.3.refs_1_, ...), custom_call_target="tpu_custom_call" | custom-call | flops 83886080 | bytes 20971520 | tf_op jit(solution)/shard_map/combine_odd/pallas_call | solution.py:391
  (4 shorter events, 0.0 us)
Async XLA Ops:
  1.1 14.3 %collective-permute-start = (f32[178,2,128]{2,1,0:T(2,128)S(1)}, f32[178,2,128]{2,1,0:T(2,128)S(1)}, u32[]{:S(2)}, u32[]{:S(2)}) collective-permute-start(f32[178,2,128]{2,1,0:T(2,128)S(1)} %get-tuple-element.34), channel_id=1, source_target_pairs={{0,8},{1,9},{2,10},{3,11},{4,12},{5,13},{6,14},{7,15},{8,0},{9,1},... | collective-permute-start | bytes 546824 | tf_op jit(solution)/shard_map/ppermute | solution.py:442
  6.8 11.7 %collective-permute-start.4 = (f32[178,2,128]{2,1,0:T(2,128)S(1)}, f32[178,2,128]{2,1,0:T(2,128)S(1)}, u32[]{:S(2)}, u32[]{:S(2)}) collective-permute-start(f32[178,2,128]{2,1,0:T(2,128)S(1)} %get-tuple-element.39), channel_id=1, source_target_pairs={{0,4},{1,5},{2,6},{3,7},{4,0},{5,1},{6,2},{7,3},{8,12},{9,13},{10,... | collective-permute-start | bytes 546824 | tf_op jit(solution)/shard_map/ppermute | solution.py:442
  8.4 14.5 %collective-permute-start.2 = (f32[178,2,128]{2,1,0:T(2,128)S(1)}, f32[178,2,128]{2,1,0:T(2,128)S(1)}, u32[]{:S(2)}, u32[]{:S(2)}) collective-permute-start(f32[178,2,128]{2,1,0:T(2,128)S(1)} %get-tuple-element.36), channel_id=1, source_target_pairs={{0,9},{1,8},{2,11},{3,10},{4,13},{5,12},{6,15},{7,14},{8,1},{9,0},... | collective-permute-start | bytes 546824 | tf_op jit(solution)/shard_map/ppermute | solution.py:442
  8.4 14.5 %collective-permute-start.3 = (f32[178,2,128]{2,1,0:T(2,128)S(1)}, f32[178,2,128]{2,1,0:T(2,128)S(1)}, u32[]{:S(2)}, u32[]{:S(2)}) collective-permute-start(f32[178,2,128]{2,1,0:T(2,128)S(1)} %get-tuple-element.37), channel_id=1, source_target_pairs={{0,1},{1,0},{2,3},{3,2},{4,5},{5,4},{6,7},{7,6},{8,9},{9,8},{10,11... | collective-permute-start | bytes 546824 | tf_op jit(solution)/shard_map/ppermute | solution.py:442
  8.9 14.0 %collective-permute-start.5 = (f32[89,2,128]{2,1,0:T(2,128)S(1)}, f32[89,2,128]{2,1,0:T(2,128)S(1)}, u32[]{:S(2)}, u32[]{:S(2)}) collective-permute-start(f32[89,2,128]{2,1,0:T(2,128)S(1)} %get-tuple-element.44), channel_id=1, source_target_pairs={{0,5},{1,4},{2,7},{3,6},{4,1},{5,0},{6,3},{7,2},{8,13},{9,12},{10,... | collective-permute-start | bytes 273416 | tf_op jit(solution)/shard_map/ppermute | solution.py:442
  15.5 14.7 %collective-permute-start.7 = (f32[89,2,128]{2,1,0:T(2,128)S(1)}, f32[89,2,128]{2,1,0:T(2,128)S(1)}, u32[]{:S(2)}, u32[]{:S(2)}) collective-permute-start(f32[89,2,128]{2,1,0:T(2,128)S(1)} %get-tuple-element.46), channel_id=1, source_target_pairs={{0,12},{1,13},{2,14},{3,15},{4,8},{5,9},{6,10},{7,11},{8,4},{9,5},... | collective-permute-start | bytes 273416 | tf_op jit(solution)/shard_map/ppermute | solution.py:442
  18.4 11.7 %collective-permute-start.1 = (f32[89,2,128]{2,1,0:T(2,128)S(1)}, f32[89,2,128]{2,1,0:T(2,128)S(1)}, u32[]{:S(2)}, u32[]{:S(2)}) collective-permute-start(f32[89,2,128]{2,1,0:T(2,128)S(1)} %get-tuple-element.35), channel_id=1, source_target_pairs={{0,14},{1,15},{2,12},{3,13},{4,10},{5,11},{6,8},{7,9},{8,6},{9,7},... | collective-permute-start | bytes 273416 | tf_op jit(solution)/shard_map/ppermute | solution.py:442
  22.8 9.5 %collective-permute-start.6 = (f32[267,2,128]{2,1,0:T(2,128)S(1)}, f32[267,2,128]{2,1,0:T(2,128)S(1)}, u32[]{:S(2)}, u32[]{:S(2)}) collective-permute-start(f32[267,2,128]{2,1,0:T(2,128)S(1)} %pad_maximum_fusion), channel_id=1, source_target_pairs={{0,2},{1,3},{2,0},{3,1},{4,6},{5,7},{6,4},{7,5},{8,10},{9,11},{10,... | collective-permute-start | bytes 820232 | tf_op jit(solution)/shard_map/ppermute | solution.py:442
  23.0 14.2 %collective-permute-start.10 = (f32[178,2,128]{2,1,0:T(2,128)S(1)}, f32[178,2,128]{2,1,0:T(2,128)S(1)}, u32[]{:S(2)}, u32[]{:S(2)}) collective-permute-start(f32[178,2,128]{2,1,0:T(2,128)S(1)} %pad_maximum_fusion.1), channel_id=1, source_target_pairs={{0,2},{1,3},{2,0},{3,1},{4,6},{5,7},{6,4},{7,5},{8,10},{9,11},{10,... | collective-permute-start | bytes 546824 | tf_op jit(solution)/shard_map/ppermute | solution.py:442
  25.1 10.8 %collective-permute-start.8 = (f32[89,2,128]{2,1,0:T(2,128)S(1)}, f32[89,2,128]{2,1,0:T(2,128)S(1)}, u32[]{:S(2)}, u32[]{:S(2)}) collective-permute-start(f32[89,2,128]{2,1,0:T(2,128)S(1)} %get-tuple-element.50), channel_id=1, source_target_pairs={{0,13},{1,12},{2,15},{3,14},{4,9},{5,8},{6,11},{7,10},{8,5},{9,4},... | collective-permute-start | bytes 273416 | tf_op jit(solution)/shard_map/ppermute | solution.py:442
  30.2 5.8 %collective-permute-start.11 = (f32[89,2,128]{2,1,0:T(2,128)S(1)}, f32[89,2,128]{2,1,0:T(2,128)S(1)}, u32[]{:S(2)}, u32[]{:S(2)}) collective-permute-start(f32[89,2,128]{2,1,0:T(2,128)S(1)} %get-tuple-element.54), channel_id=1, source_target_pairs={{0,7},{1,6},{2,5},{3,4},{4,3},{5,2},{6,1},{7,0},{8,15},{9,14},{10,... | collective-permute-start | bytes 273416 | tf_op jit(solution)/shard_map/ppermute | solution.py:442
  30.2 7.1 %collective-permute-start.9 = (f32[89,2,128]{2,1,0:T(2,128)S(1)}, f32[89,2,128]{2,1,0:T(2,128)S(1)}, u32[]{:S(2)}, u32[]{:S(2)}) collective-permute-start(f32[89,2,128]{2,1,0:T(2,128)S(1)} %get-tuple-element.52), channel_id=1, source_target_pairs={{0,15},{1,14},{2,13},{3,12},{4,11},{5,10},{6,9},{7,8},{8,7},{9,6},... | collective-permute-start | bytes 273416 | tf_op jit(solution)/shard_map/ppermute | solution.py:442
